TPU v7x, 32 devices: a whole 2x2x4 slice. The times are simulated.
32 devices in a mesh: dp: 8 (over z, x), section: 4 (over y, core).
Axes of the slice: x: 2, y: 2, z: 4, core: 2. Of those that a mesh axis runs over, the one named last changes fastest.
Arguments:
- latents: float32 [16, 32, 32, 4], P('dp'), may hold values from -6 to 6
- noise: float32 [16, 32, 32, 4], P('dp'), may hold values from -6 to 6
- timesteps: int32 [16], P('dp'), may hold values from 0 to 999
- labels: int32 [16], P('dp'), may hold values from 0 to 999
- null_mask: int32 [16], P('dp'), may hold values 0 or 1
- valid: int32 [16], P('dp'), may hold values from 0 to 1, as said below
- mod_w: float32 [4, 1152, 3456], P('section', 'dp'), may hold values from -0.1875 to 0.1875
- mod_m: float32 [4, 1152, 3456], P('section', 'dp'), may hold values from -1 to 1
- mod_e: float32 [4, 1152, 3456], P('section', 'dp'), may hold values from -0.1875 to 0.1875
- block_w: float32 [4, 1152, 4608], P('section', 'dp'), may hold values from -2 to 2
- block_m: float32 [4, 1152, 4608], P('section', 'dp'), may hold values from -1 to 1
- block_e: float32 [4, 1152, 4608], P('section', 'dp'), may hold values from -0.1875 to 0.1875
- down_w: float32 [2, 4608, 1152], P(None, None, 'dp'), may hold values from -0.09375 to 0.09375
- down_m: float32 [2, 4608, 1152], P(None, None, 'dp'), may hold values from -1 to 1
- down_e: float32 [2, 4608, 1152], P(None, None, 'dp'), may hold values from -0.09375 to 0.09375
- stem_w: float32 [2425, 1152], P(None, 'dp'), may hold values from -1 to 1
- stem_m: float32 [2425, 1152], P(None, 'dp'), may hold values from -1 to 1
- stem_e: float32 [2425, 1152], P(None, 'dp'), may hold values from -0.1875 to 0.1875
- tail_w: float32 [1152, 2336], P('dp'), may hold values from -0.1875 to 0.1875
- tail_m: float32 [1152, 2336], P('dp'), may hold values from -1 to 1
- tail_e: float32 [1152, 2336], P('dp'), may hold values from -0.1875 to 0.1875
- biases: float32 [40352], replicated, may hold values from -3 to 5
- bias_m: float32 [40352], replicated, may hold values from -1 to 1
- bias_e: float32 [40352], replicated, may hold values from -3 to 3
Outputs:
- loss_sum: float32 [], replicated
- count: float32 [], replicated
- grad_norm: float32 [], replicated
- mod_new: float32 [4, 1152, 3456], P('section', 'dp')
- mod_mom: float32 [4, 1152, 3456], P('section', 'dp')
- mod_avg: float32 [4, 1152, 3456], P('section', 'dp')
- mod_half: bfloat16 [4, 1152, 3456], P('section', 'dp')
- block_new: float32 [4, 1152, 4608], P('section', 'dp')
- block_mom: float32 [4, 1152, 4608], P('section', 'dp')
- block_avg: float32 [4, 1152, 4608], P('section', 'dp')
- block_half: bfloat16 [4, 1152, 4608], P('section', 'dp')
- down_new: float32 [2, 4608, 1152], P(None, None, 'dp')
- down_mom: float32 [2, 4608, 1152], P(None, None, 'dp')
- down_avg: float32 [2, 4608, 1152], P(None, None, 'dp')
- down_half: bfloat16 [2, 4608, 1152], P(None, None, 'dp')
- stem_new: float32 [2425, 1152], P(None, 'dp')
- stem_mom: float32 [2425, 1152], P(None, 'dp')
- stem_avg: float32 [2425, 1152], P(None, 'dp')
- stem_half: bfloat16 [2425, 1152], P(None, 'dp')
- tail_new: float32 [1152, 2336], P('dp')
- tail_mom: float32 [1152, 2336], P('dp')
- tail_avg: float32 [1152, 2336], P('dp')
- tail_half: bfloat16 [1152, 2336], P('dp')
- bias_new: float32 [40352], replicated
- bias_mom: float32 [40352], replicated
- bias_avg: float32 [40352], replicated
- bias_half: bfloat16 [40352], replicated
Inputs may be any that keep to these rules, and one draw needn't show every extreme that they name: `valid`: an image of the i-th of n indices of dp counts with chance (1 + 2 i / (n - 1)) / 3; every image of the last index counts.
All inputs are finite; a program needn't handle non-finite values. No bound on the sum of `null_mask` on one device may be relied on, other than what follows from the above.
Results may differ from a plain program's by a relative error of at most 0.0095.
Values may be sent and summed in bfloat16 or wider, within the bound.
A program may use at most 1.125 GiB of HBM per device.

v0:
```python
from functools import partial
import math

import jax
import jax.numpy as jnp
from jax import lax
from jax.sharding import PartitionSpec as P

HEADS = 16
HEAD_DIM = 72
D = 1152
FF = 4608
NCLS = 1001
FREQ = 256
GRID = 32
PATCHES = 256
PATCH_IN = 16
HEAD_OUT = 32
LAYERS = 2
MICRO = 2
MB_IMG = 1
NBIAS = 40352


epsilon_norm = 1e-06
momentum_rate = 0.9
ema_decay = 0.9
learn_rate = 4000.0
clip_limit = 0.02


def from_behind(array, axis, by):
    peers = lax.axis_size(axis)
    pairs = [(i, i + by) for i in range(peers) if 0 <= i + by < peers]
    return lax.ppermute(array, axis, pairs)


def matmul(left, right):
    return jnp.dot(left, right, preferred_element_type=jnp.float32)


def to_half(value):
    return value.astype(jnp.bfloat16)


def column_sums(value):
    return jnp.sum(value.astype(jnp.float32), axis=0)


def silu_back(value, grad):
    return jax.vjp(jax.nn.silu, value)[1](grad)[0]


def layer_modulate(tokens, shift, scale):
    grouped = tokens.reshape(shift.shape[0], -1, tokens.shape[-1])
    centered = grouped - jnp.mean(grouped, axis=-1, keepdims=True)
    normed = centered * lax.rsqrt(
        jnp.mean(centered * centered, axis=-1, keepdims=True) + epsilon_norm
    )
    return (normed * (1.0 + scale[:, None]) + shift[:, None]).reshape(tokens.shape)


def patchify(field):
    images, side = (field.shape[0], field.shape[1] // 2)
    return (
        field.reshape(images, side, 2, side, 2, 4)
        .transpose(0, 1, 3, 2, 4, 5)
        .reshape(images, side * side, 16)
    )


def sincos_rows(places, width):
    omega = 1.0 / 10000.0 ** (jnp.arange(width // 2, dtype=jnp.float32) / (width // 2))
    angle = places[:, None] * omega[None, :]
    return jnp.concatenate([jnp.sin(angle), jnp.cos(angle)], axis=1)


def position_table(side, width):
    index = jnp.arange(side * side, dtype=jnp.int32)
    column = (index % side).astype(jnp.float32)
    row = (index // side).astype(jnp.float32)
    return jnp.concatenate([sincos_rows(column, width // 2), sincos_rows(row, width // 2)], axis=1)


def time_features(steps):
    half = FREQ // 2
    freqs = jnp.exp(-math.log(10000.0) * jnp.arange(half, dtype=jnp.float32) / half)
    angle = steps[:, None] * freqs[None, :]
    return jnp.concatenate([jnp.cos(angle), jnp.sin(angle)], axis=1)


def noise_levels(steps):
    level = jnp.cos((steps / 1000.0 + 0.008) / 1.008 * (math.pi / 2)) ** 2
    return (jnp.sqrt(level), jnp.sqrt(1.0 - level))


def attention_forward(xm_half, wblk, bblk, images):
    qkv = to_half(matmul(xm_half, wblk[:, : 3 * D]) + bblk[: 3 * D])
    parts = qkv.reshape(images, -1, 3, HEADS, HEAD_DIM)
    scores = jnp.einsum(
        "bqhd,bkhd->bhqk", parts[:, :, 0], parts[:, :, 1], preferred_element_type=jnp.float32
    ) * HEAD_DIM ** (-0.5)
    probs = jax.nn.softmax(scores, axis=-1)
    attended = to_half(
        jnp.einsum(
            "bhqk,bkhd->bqhd", to_half(probs), parts[:, :, 2], preferred_element_type=jnp.float32
        )
    ).reshape(xm_half.shape)
    branch = matmul(attended, wblk[:, 3 * D :]) + bblk[3 * D :]
    return (branch, (parts, probs, attended))


def attention_backward(d_branch, xm_half, saved, wblk, images):
    parts, probs, attended = saved
    grad_half = to_half(d_branch)
    g_out = matmul(attended.T, grad_half)
    d_att = to_half(matmul(grad_half, wblk[:, 3 * D :].T)).reshape(images, -1, HEADS, HEAD_DIM)
    d_value = jnp.einsum(
        "bhqk,bqhd->bkhd", to_half(probs), d_att, preferred_element_type=jnp.float32
    )
    d_probs = jnp.einsum(
        "bqhd,bkhd->bhqk", d_att, parts[:, :, 2], preferred_element_type=jnp.float32
    )
    d_scores = to_half(probs * (d_probs - jnp.sum(probs * d_probs, axis=-1, keepdims=True)))
    d_query = jnp.einsum(
        "bhqk,bkhd->bqhd", d_scores, parts[:, :, 1], preferred_element_type=jnp.float32
    ) * HEAD_DIM ** (-0.5)
    d_key = jnp.einsum(
        "bhqk,bqhd->bkhd", d_scores, parts[:, :, 0], preferred_element_type=jnp.float32
    ) * HEAD_DIM ** (-0.5)
    d_qkv = to_half(jnp.stack([d_query, d_key, d_value], axis=2).reshape(xm_half.shape[0], 3 * D))
    g_qkv = matmul(xm_half.T, d_qkv)
    d_xm = matmul(d_qkv, wblk[:, : 3 * D].T)
    return (
        d_xm,
        jnp.concatenate([g_qkv, g_out], axis=1),
        jnp.concatenate([column_sums(d_qkv), column_sums(grad_half)]),
    )


def mlp_forward(xm_half, wblk, bblk, wdown, bdown):
    pre = matmul(xm_half, wblk) + bblk
    act = to_half(jax.nn.gelu(pre, approximate=True))
    return (matmul(act, wdown) + bdown, (pre, act))


def mlp_backward(d_branch, xm_half, saved, wblk, wdown):
    pre, act = saved
    grad_half = to_half(d_branch)
    g_down = matmul(act.T, grad_half)
    d_act = matmul(grad_half, wdown.T)
    d_pre = to_half(jax.vjp(partial(jax.nn.gelu, approximate=True), pre)[1](d_act)[0])
    g_up = matmul(xm_half.T, d_pre)
    return (matmul(d_pre, wblk.T), g_up, column_sums(d_pre), g_down, column_sums(grad_half))


def block_forward(attention, x_in, cond, weights):
    wmod, bmod, wblk, bblk, wdown, bdown = weights
    images = cond.shape[0]
    silu_half = to_half(jax.nn.silu(cond))
    mod = matmul(silu_half, wmod) + bmod
    xm_half = to_half(layer_modulate(x_in, mod[:, :D], mod[:, D : 2 * D]))
    if attention:
        branch, saved = attention_forward(xm_half, wblk, bblk, images)
    else:
        branch, saved = mlp_forward(xm_half, wblk, bblk, wdown, bdown)
    x_out = x_in + (branch.reshape(images, -1, D) * mod[:, None, 2 * D :]).reshape(x_in.shape)
    return (x_out, (mod, silu_half, xm_half, branch, saved))


def block_backward(attention, d_out, x_in, cond, weights, kept):
    wmod, bmod, wblk, bblk, wdown, bdown = weights
    mod, silu_half, xm_half, branch, saved = kept
    images = cond.shape[0]
    d_grouped = d_out.reshape(images, -1, D)
    d_gate = jnp.sum(d_grouped * branch.reshape(images, -1, D), axis=1)
    d_branch = (d_grouped * mod[:, None, 2 * D :]).reshape(d_out.shape)
    if attention:
        d_xm, g_blk, b_blk = attention_backward(d_branch, xm_half, saved, wblk, images)
        g_down = jnp.zeros((FF, D), jnp.float32)
        b_down = jnp.zeros((D,), jnp.float32)
    else:
        d_xm, g_blk, b_blk, g_down, b_down = mlp_backward(d_branch, xm_half, saved, wblk, wdown)
    pull = jax.vjp(layer_modulate, x_in, mod[:, :D], mod[:, D : 2 * D])[1]
    d_x, d_shift, d_scale = pull(d_xm)
    d_mod = to_half(jnp.concatenate([d_shift, d_scale, d_gate], axis=1))
    g_mod = matmul(silu_half.T, d_mod)
    d_cond = silu_back(cond, matmul(d_mod, wmod.T))
    return (d_out + d_x, d_cond, (g_mod, column_sums(d_mod), g_blk, b_blk, g_down, b_down))


def final_step(x_out, cond, wtail, btail, target_rows, weight_rows, loss_scale):
    silu_half = to_half(jax.nn.silu(cond))
    fmod = matmul(silu_half, wtail[:, : 2 * D]) + btail[: 2 * D]
    xf_half = to_half(layer_modulate(x_out, fmod[:, :D], fmod[:, D:]))
    error = matmul(xf_half, wtail[:, 2 * D :]) + btail[2 * D :] - target_rows
    loss = jnp.sum(weight_rows[:, None] * error * error)
    d_pred = to_half(2.0 * loss_scale * weight_rows[:, None] * error)
    g_head = matmul(xf_half.T, d_pred)
    pull = jax.vjp(layer_modulate, x_out, fmod[:, :D], fmod[:, D:])[1]
    d_x, d_shift, d_scale = pull(matmul(d_pred, wtail[:, 2 * D :].T))
    d_fmod = to_half(jnp.concatenate([d_shift, d_scale], axis=1))
    g_fmod = matmul(silu_half.T, d_fmod)
    d_cond = silu_back(cond, matmul(d_fmod, wtail[:, : 2 * D].T))
    return (
        loss,
        d_x,
        d_cond,
        jnp.concatenate([g_fmod, g_head], axis=1),
        jnp.concatenate([column_sums(d_fmod), column_sums(d_pred)]),
    )


def embed_forward(tok_half, freq_half, classes, wstem, bias_patch, bias_one, bias_two, position):
    table = wstem[:NCLS]
    wpatch = wstem[NCLS : NCLS + PATCH_IN]
    wone = wstem[NCLS + PATCH_IN : NCLS + PATCH_IN + FREQ]
    wtwo = wstem[NCLS + PATCH_IN + FREQ :]
    x_first = matmul(tok_half, wpatch) + bias_patch + position
    pre = matmul(freq_half, wone) + bias_one
    hid_half = to_half(jax.nn.silu(pre))
    picks = (classes[:, None] == jnp.arange(NCLS, dtype=jnp.int32)[None, :]).astype(jnp.bfloat16)
    cond = matmul(hid_half, wtwo) + bias_two + matmul(picks, table)
    return (x_first, cond, (pre, hid_half, picks))


def embed_backward(d_first, d_cond, tok_half, freq_half, kept, wstem):
    pre, hid_half, picks = kept
    wtwo = wstem[NCLS + PATCH_IN + FREQ :]
    dx_half = to_half(d_first)
    dc_half = to_half(d_cond)
    d_pre = to_half(silu_back(pre, matmul(dc_half, wtwo.T)))
    grads = jnp.concatenate(
        [
            matmul(picks.T, dc_half),
            matmul(tok_half.T, dx_half),
            matmul(freq_half.T, d_pre),
            matmul(hid_half.T, dc_half),
        ],
        axis=0,
    )
    return (grads, column_sums(dx_half), column_sums(d_pre), column_sums(dc_half))


def nesterov(weight, moment, average, grad, factor):
    clipped = grad * factor
    moment_new = momentum_rate * moment + clipped
    weight_new = weight - learn_rate * (clipped + momentum_rate * moment_new)
    average_new = ema_decay * average + (1.0 - ema_decay) * weight_new
    return (weight_new, moment_new, average_new, weight_new.astype(jnp.bfloat16))


def body(
    latents,
    noise,
    timesteps,
    labels,
    null_mask,
    valid,
    mod_w,
    mod_m,
    mod_e,
    block_w,
    block_m,
    block_e,
    down_w,
    down_m,
    down_e,
    stem_w,
    stem_m,
    stem_e,
    tail_w,
    tail_m,
    tail_e,
    biases,
    bias_m,
    bias_e,
):
    section = lax.axis_index("section")
    sections = lax.axis_size("section")
    layer = section // 2
    first = section == 0
    final = section == sections - 1
    rows = MB_IMG * PATCHES
    down_local = lax.dynamic_index_in_dim(down_w, layer, 0, keepdims=False)
    wmod, wblk, wdown, wstem, wtail = (
        lax.all_gather(to_half(mod_w[0]), "dp", axis=0, tiled=True),
        lax.all_gather(to_half(block_w[0]), "dp", axis=0, tiled=True),
        lax.all_gather(to_half(down_local), "dp", axis=1, tiled=True),
        lax.all_gather(to_half(stem_w), "dp", axis=1, tiled=True),
        lax.all_gather(to_half(tail_w), "dp", axis=0, tiled=True),
    )
    bmod = lax.dynamic_slice_in_dim(biases, 3 * D * section, 3 * D)
    bblk = lax.dynamic_slice_in_dim(biases, 12 * D + 4 * D * section, 4 * D)
    bdown = lax.dynamic_slice_in_dim(biases, 28 * D + D * layer, D)
    bias_patch = biases[30 * D : 31 * D]
    bias_one = biases[31 * D : 32 * D]
    bias_two = biases[32 * D : 33 * D]
    btail = biases[33 * D :]
    weights = (wmod, bmod, wblk, bblk, wdown, bdown)
    steps_f = timesteps.astype(jnp.float32)
    signal, spread = noise_levels(steps_f)
    signal = signal[:, None, None, None]
    spread = spread[:, None, None, None]
    tok_all = to_half(patchify(signal * latents + spread * noise))
    target_all = jnp.concatenate(
        [patchify(signal * noise - spread * latents), patchify(noise)], axis=2
    )
    freq_all = to_half(time_features(steps_f))
    classes_all = jnp.where(null_mask > 0, NCLS - 1, labels)
    valid_f = valid.astype(jnp.float32)
    position = jnp.tile(position_table(GRID // 2, D), (MB_IMG, 1))
    count = lax.psum(jnp.sum(valid_f), "dp")
    loss_scale = 1.0 / (count * PATCHES * HEAD_OUT)

    def micro_data(index):
        start = index * MB_IMG
        tok = lax.dynamic_slice_in_dim(tok_all, start, MB_IMG, 0).reshape(rows, PATCH_IN)
        freq = lax.dynamic_slice_in_dim(freq_all, start, MB_IMG, 0)
        classes = lax.dynamic_slice_in_dim(classes_all, start, MB_IMG, 0)
        target = lax.dynamic_slice_in_dim(target_all, start, MB_IMG, 0).reshape(rows, HEAD_OUT)
        weight_rows = jnp.repeat(lax.dynamic_slice_in_dim(valid_f, start, MB_IMG, 0), PATCHES)
        return (tok, freq, classes, target, weight_rows)

    def skip_forward(x_in, cond):
        return jnp.zeros_like(x_in)

    def attention_forward_tick(x_in, cond):
        return block_forward(True, x_in, cond, weights)[0]

    def mlp_forward_tick(x_in, cond):
        return block_forward(False, x_in, cond, weights)[0]

    def attention_tick(x_in, cond, d_recv, target, weight_rows):
        kept = block_forward(True, x_in, cond, weights)[1]
        d_in, d_cond, grads = block_backward(True, d_recv, x_in, cond, weights, kept)
        tail_zero = jnp.zeros((D, 2 * D + HEAD_OUT), jnp.float32)
        return (
            (d_in, d_cond)
            + grads
            + (tail_zero, jnp.zeros((2 * D + HEAD_OUT,), jnp.float32), jnp.zeros((), jnp.float32))
        )

    def mlp_tick(x_in, cond, d_recv, target, weight_rows):
        x_out, kept = block_forward(False, x_in, cond, weights)
        loss, d_final, c_final, g_tail, b_tail = final_step(
            x_out, cond, wtail, btail, target, weight_rows, loss_scale
        )
        flag = final.astype(jnp.float32)
        d_out = jnp.where(final, d_final, d_recv)
        d_in, d_cond, grads = block_backward(False, d_out, x_in, cond, weights, kept)
        return (d_in, d_cond + flag * c_final) + grads + (flag * g_tail, flag * b_tail, flag * loss)

    def skip_tick(x_in, cond, d_recv, target, weight_rows):
        return (
            jnp.zeros(x_in.shape, jnp.float32),
            jnp.zeros(cond.shape, jnp.float32),
            jnp.zeros((D, 3 * D), jnp.float32),
            jnp.zeros((3 * D,), jnp.float32),
            jnp.zeros((D, 4 * D), jnp.float32),
            jnp.zeros((4 * D,), jnp.float32),
            jnp.zeros((FF, D), jnp.float32),
            jnp.zeros((D,), jnp.float32),
            jnp.zeros((D, 2 * D + HEAD_OUT), jnp.float32),
            jnp.zeros((2 * D + HEAD_OUT,), jnp.float32),
            jnp.zeros((), jnp.float32),
        )

    ticks = MICRO + sections - 1
    x_store = jnp.zeros((MICRO, rows, D), jnp.float32)
    c_store = jnp.zeros((MICRO, MB_IMG, D), jnp.float32)
    recv_x = jnp.zeros((rows, D), jnp.bfloat16)
    recv_c = jnp.zeros((MB_IMG, D), jnp.bfloat16)
    for tick in range(ticks):
        micro = tick - section
        active = (micro >= 0) & (micro < MICRO)
        index = jnp.clip(micro, 0, MICRO - 1)
        tok, freq, classes, target, weight_rows = micro_data(index)
        x_first, c_first, unused = embed_forward(
            tok, freq, classes, wstem, bias_patch, bias_one, bias_two, position
        )
        x_in = jnp.where(first, x_first, recv_x.astype(jnp.float32))
        cond = jnp.where(first, c_first, recv_c.astype(jnp.float32))
        x_store = lax.dynamic_update_index_in_dim(
            x_store, jnp.where(active, x_in, x_store[index]), index, 0
        )
        c_store = lax.dynamic_update_index_in_dim(
            c_store, jnp.where(active, cond, c_store[index]), index, 0
        )
        branch_id = jnp.where(active, 1 + section % 2, 0)
        x_out = lax.switch(
            branch_id, [skip_forward, attention_forward_tick, mlp_forward_tick], x_in, cond
        )
        recv_x, recv_c = from_behind((to_half(x_out), to_half(cond)), "section", 1)
    recv_dx = jnp.zeros((rows, D), jnp.bfloat16)
    recv_dc = jnp.zeros((MB_IMG, D), jnp.bfloat16)
    totals = None
    bias_grad = jnp.zeros((NBIAS,), jnp.float32)
    loss_total = jnp.zeros((), jnp.float32)
    for tick in range(ticks):
        micro = tick - (sections - 1 - section)
        active = (micro >= 0) & (micro < MICRO)
        index = jnp.clip(micro, 0, MICRO - 1)
        tok, freq, classes, target, weight_rows = micro_data(index)
        x_in = x_store[index]
        cond = c_store[index]
        branch_id = jnp.where(active, 1 + section % 2, 0)
        outputs = lax.switch(
            branch_id,
            [skip_tick, attention_tick, mlp_tick],
            x_in,
            cond,
            recv_dx.astype(jnp.float32),
            target,
            weight_rows,
        )
        d_in, d_cond, g_mod, b_mod, g_blk, b_blk, g_down, b_down, g_tail, b_tail, loss = outputs
        d_cond = jnp.where(active, d_cond + recv_dc.astype(jnp.float32), 0.0)
        on_first = (first & active).astype(jnp.float32)
        unused_x, unused_c, kept = embed_forward(
            tok, freq, classes, wstem, bias_patch, bias_one, bias_two, position
        )
        g_stem, b_patch, b_one, b_two = embed_backward(d_in, d_cond, tok, freq, kept, wstem)
        recv_dx, recv_dc = from_behind((to_half(d_in), to_half(d_cond)), "section", -1)
        piece = (g_mod, g_blk, g_down, on_first * g_stem, g_tail)
        totals = piece if totals is None else jax.tree.map(jnp.add, totals, piece)
        vector = jnp.zeros((NBIAS,), jnp.float32)
        vector = lax.dynamic_update_slice_in_dim(vector, b_mod, 3 * D * section, 0)
        vector = lax.dynamic_update_slice_in_dim(vector, b_blk, 12 * D + 4 * D * section, 0)
        vector = lax.dynamic_update_slice_in_dim(vector, b_down, 28 * D + D * layer, 0)
        vector = lax.dynamic_update_slice_in_dim(
            vector, on_first * jnp.concatenate([b_patch, b_one, b_two]), 30 * D, 0
        )
        vector = lax.dynamic_update_slice_in_dim(vector, b_tail, 33 * D, 0)
        bias_grad = bias_grad + vector
        loss_total = loss_total + loss
    g_mod, g_blk, g_down, g_stem, g_tail = totals
    g_mod, g_blk, g_down, g_stem, g_tail = (
        lax.psum_scatter(g_mod, "dp", scatter_dimension=0, tiled=True),
        lax.psum_scatter(g_blk, "dp", scatter_dimension=0, tiled=True),
        lax.psum_scatter(g_down, "dp", scatter_dimension=1, tiled=True),
        lax.psum_scatter(g_stem, "dp", scatter_dimension=1, tiled=True),
        lax.psum_scatter(g_tail, "dp", scatter_dimension=0, tiled=True),
    )
    down_both = jnp.where((jnp.arange(LAYERS) == layer)[:, None, None], g_down[None], 0.0)
    owned_squares = jnp.sum(g_mod * g_mod) + jnp.sum(g_blk * g_blk)
    down_both, g_stem, g_tail, owned_squares = (
        lax.psum(down_both.astype(jnp.bfloat16), "section").astype(jnp.float32),
        lax.psum(g_stem.astype(jnp.bfloat16), "section").astype(jnp.float32),
        lax.psum(g_tail.astype(jnp.bfloat16), "section").astype(jnp.float32),
        lax.psum(owned_squares.astype(jnp.bfloat16), "section").astype(jnp.float32),
    )
    bias_grad, loss_sum = lax.psum((bias_grad, loss_total), ("dp", "section"))
    on_anchor = (lax.axis_index("dp") == 0).astype(jnp.float32)
    squares = (
        owned_squares
        + jnp.sum(down_both * down_both)
        + jnp.sum(g_stem * g_stem)
        + jnp.sum(g_tail * g_tail)
    )
    squares = squares + on_anchor * jnp.sum(bias_grad * bias_grad)
    grad_norm = jnp.sqrt(lax.psum(squares, "dp"))
    factor = jnp.minimum(1.0, clip_limit / (grad_norm + 1e-06))
    mod_new, mod_mom, mod_avg, mod_half = nesterov(mod_w, mod_m, mod_e, g_mod[None], factor)
    block_new, block_mom, block_avg, block_half = nesterov(
        block_w, block_m, block_e, g_blk[None], factor
    )
    down_new, down_mom, down_avg, down_half = nesterov(down_w, down_m, down_e, down_both, factor)
    stem_new, stem_mom, stem_avg, stem_half = nesterov(stem_w, stem_m, stem_e, g_stem, factor)
    tail_new, tail_mom, tail_avg, tail_half = nesterov(tail_w, tail_m, tail_e, g_tail, factor)
    bias_new, bias_mom, bias_avg, bias_half = nesterov(biases, bias_m, bias_e, bias_grad, factor)
    return (
        loss_sum,
        count,
        grad_norm,
        mod_new,
        mod_mom,
        mod_avg,
        mod_half,
        block_new,
        block_mom,
        block_avg,
        block_half,
        down_new,
        down_mom,
        down_avg,
        down_half,
        stem_new,
        stem_mom,
        stem_avg,
        stem_half,
        tail_new,
        tail_mom,
        tail_avg,
        tail_half,
        bias_new,
        bias_mom,
        bias_avg,
        bias_half,
    )


def solution(mesh):
    placed = (
        P("dp", None, None, None),
        P("dp", None, None, None),
        P("dp"),
        P("dp"),
        P("dp"),
        P("dp"),
        P("section", "dp", None),
        P("section", "dp", None),
        P("section", "dp", None),
        P("section", "dp", None),
        P("section", "dp", None),
        P("section", "dp", None),
        P(None, None, "dp"),
        P(None, None, "dp"),
        P(None, None, "dp"),
        P(None, "dp"),
        P(None, "dp"),
        P(None, "dp"),
        P("dp", None),
        P("dp", None),
        P("dp", None),
        P(),
        P(),
        P(),
    )
    return jax.shard_map(
        body,
        mesh=mesh,
        in_specs=placed,
        out_specs=(
            P(),
            P(),
            P(),
            P("section", "dp", None),
            P("section", "dp", None),
            P("section", "dp", None),
            P("section", "dp", None),
            P("section", "dp", None),
            P("section", "dp", None),
            P("section", "dp", None),
            P("section", "dp", None),
            P(None, None, "dp"),
            P(None, None, "dp"),
            P(None, None, "dp"),
            P(None, None, "dp"),
            P(None, "dp"),
            P(None, "dp"),
            P(None, "dp"),
            P(None, "dp"),
            P("dp", None),
            P("dp", None),
            P("dp", None),
            P("dp", None),
            P(),
            P(),
            P(),
            P(),
        ),
        check_vma=False,
    )
```

profile of v0, /device:TPU:0, one launch (start us, length us, event | category | flops | bytes accessed | tf_op | source)
XLA Modules:
  0.0 3036.2 jit_solution(14242272363512468003)
XLA Ops:
  27.1 24.2 psum.56
  58.6 45.9 %all-gather.9.cloned.1.call-done = bf16[2425,1152]{0,1:T(8,128)(2,1)} async-done(((bf16[2425,144]{0,1:T(8,128)(2,1)}), bf16[2425,1152]{0,1:T(8,128)(2,1)}) %all-gather.9.cloned.1.call-update) | async-done | bytes 5587216 | tf_op jit(solution)/shard_map/all_gather | solution.py:290
  121.1 14.4 collective-permute-start.1
  162.6 62.5 %all-gather.13.cloned.1.call-done = bf16[1,1152,3456]{2,1,0:T(8,128)(2,1)} async-done(((bf16[1,144,3456]{2,1,0:T(8,128)(2,1)}), bf16[1,1152,3456]{2,1,0:T(8,128)(2,1)}) %all-gather.13.cloned.1.call-update) | async-done | bytes 7962640 | tf_op jit(solution)/shard_map/all_gather | solution.py:287
  225.1 153.4 %all-gather.15.cloned.1.call-done = bf16[1,1152,4608]{2,1,0:T(8,128)(2,1)} async-done(((bf16[1,144,4608]{2,1,0:T(8,128)(2,1)}), bf16[1,1152,4608]{2,1,0:T(8,128)(2,1)}) %all-gather.15.cloned.1.call-update) | async-done | bytes 10616848 | tf_op jit(solution)/shard_map/all_gather | solution.py:288
  378.5 153.3 %all-gather.17.cloned.1.call-done = bf16[1,4608,1152]{1,2,0:T(8,128)(2,1)} async-done(((bf16[1,4608,144]{1,2,0:T(8,128)(2,1)}), bf16[1,4608,1152]{1,2,0:T(8,128)(2,1)}) %all-gather.17.cloned.1.call-update) | async-done | bytes 10616848 | tf_op jit(solution)/shard_map/all_gather | solution.py:289
  531.8 30.8 %conditional.9 = (bf16[256,1152]{1,0:T(8,128)(2,1)}) conditional(s32[]{:T(128)} %clamp.28, () %tuple.176, (f32[256,1152]{1,0:T(8,128)S(1)}, f32[1,1152]{1,0:T(1,128)}, bf16[1152,3456]{1,0:T(8,128)(2,1)}, f32[3456]{0:T(1024)S(1)}, bf16[1152,4608]{1,0:T(8,128)(2,1)}, /*index=5*/f32[4608]{0:T(1024)}) %tuple.556, ...), branch_computations={%region_0.1_spmd, %region_1.6_spmd, %region_6.9_spmd} | conditional | flops 5459421696 | bytes 49177128 | solution.py:391
  570.9 32.9 %conditional.10 = (bf16[256,1152]{1,0:T(8,128)(2,1)S(1)}) conditional(s32[]{:T(128)} %clamp.29, () %tuple.179, (f32[256,1152]{1,0:T(8,128)S(1)}, f32[1,1152]{1,0:T(1,128)}, bf16[1152,3456]{1,0:T(8,128)(2,1)}, f32[3456]{0:T(1024)S(1)}, bf16[1152,4608]{1,0:T(8,128)(2,1)}, /*index=5*/f32[4608]{0:T(1024)}) %tuple.585, ...), branch_computations={%region_9.10_spmd, %region_10.15_spmd, %region_15.18_spmd} | conditional | flops 5459421696 | bytes 49148940 | solution.py:391
  614.6 16.5 collective-permute-start.4
  662.4 40.6 %conditional.13 = (bf16[1,1152]{1,0:T(2,128)(2,1)}, f32[1152,3456]{1,0:T(8,128)}, f32[3456]{0:T(1024)}, f32[1152,4608]{1,0:T(8,128)}, f32[4608]{0:T(1024)}, /*in...) conditional(s32[]{:T(128)} %clamp.27, () %tuple.175, ...), branch_computations={%region_38.39_spmd, %region_39.53_spmd, %region_53.72_spmd} | conditional | flops 16471501824 | bytes 369981024 | solution.py:408
  704.4 31.4 %collective-permute-done.8 = bf16[256,1152]{1,0:T(8,128)(2,1)S(1)} collective-permute-done((bf16[256,1152]{1,0:T(8,128)(2,1)S(1)}, bf16[256,1152]{1,0:T(8,128)(2,1)S(1)}, u32[]{:S(2)}, u32[]{:S(2)}) %collective-permute-start.8) | collective-permute-done | bytes 589856 | tf_op jit(solution)/shard_map/ppermute | solution.py:35
  735.9 41.4 %conditional.14 = (f32[1,1152]{1,0:T(1,128)}, f32[1152,3456]{1,0:T(8,128)}, f32[3456]{0:T(1024)}, f32[1152,4608]{1,0:T(8,128)}, f32[4608]{0:T(1024)}, /*index=5*...) conditional(s32[]{:T(128)} %clamp.32, () %tuple.190, ...), branch_computations={%region_72.73_spmd, %region_73.87_spmd, %region_87.106_spmd} | conditional | flops 16471500800 | bytes 369983328 | solution.py:408
  789.5 40.9 %conditional.15 = (f32[1,1152]{1,0:T(1,128)}, f32[1152,3456]{1,0:T(8,128)}, f32[3456]{0:T(1024)}, f32[1152,4608]{1,0:T(8,128)}, f32[4608]{0:T(1024)}, /*index=5*...) conditional(s32[]{:T(128)} %clamp.33, () %tuple.193, ...), branch_computations={%region_106.107_spmd, %region_107.121_spmd, %region_121.140_spmd} | conditional | flops 16471500800 | bytes 369983328 | solution.py:408
  843.7 242.3 %collective-permute-done.10 = bf16[256,1152]{1,0:T(8,128)(2,1)S(1)} collective-permute-done((bf16[256,1152]{1,0:T(8,128)(2,1)S(1)}, bf16[256,1152]{1,0:T(8,128)(2,1)S(1)}, u32[]{:S(2)}, u32[]{:S(2)}) %collective-permute-start.10) | collective-permute-done | bytes 589856 | tf_op jit(solution)/shard_map/ppermute | solution.py:35
  1086.1 109.0 %conditional.16 = (f32[1,1152]{1,0:T(1,128)}, f32[1152,3456]{1,0:T(8,128)}, f32[3456]{0:T(1024)}, f32[1152,4608]{1,0:T(8,128)}, f32[4608]{0:T(1024)}, /*index=5*...) conditional(s32[]{:T(128)} %clamp.34, () %tuple.196, ...), branch_computations={%region_140.141_spmd, %region_141.155_spmd, %region_155.174_spmd} | conditional | flops 16471500800 | bytes 365273440 | solution.py:408
  1218.7 104.0 %conditional.17 = (f32[1,1152]{1,0:T(1,128)}, f32[1152,3456]{1,0:T(8,128)}, f32[3456]{0:T(1024)}, f32[1152,4608]{1,0:T(8,128)}, f32[4608]{0:T(1024)}, /*index=5*...) conditional(s32[]{:T(128)} %clamp.35, () %tuple.199, ...), branch_computations={%region_174.175_spmd, %region_175.189_spmd, %region_189.208_spmd} | conditional | flops 16471500800 | bytes 362895648 | solution.py:408
  1322.7 22.4 add_add_fusion.18
  1390.1 13.6 concatenate.341
  1416.9 13.3 concatenate.339
  1467.2 23.5 multiply_add_fusion.20
  1490.8 41.0 %add_add_fusion.15 = f32[4608,1152]{1,0:T(8,128)} fusion(f32[4608,1152]{1,0:T(8,128)} %get-tuple-element.1049, f32[4608,1152]{1,0:T(8,128)} %get-tuple-element.1048, f32[4608,1152]{1,0:T(8,128)} %get-tuple-element.1047, f32[4608,1152]{1,0:T(8,128)} %get-tuple-element.1045, f32[4608,1152]{1,0:T(8,128)} %get-tuple-element.1046), kind=kLoop, calls=%fused_computation.1097 | loop fusion | flops 21233664 | bytes 127401984 | tf_op jit(solution)/shard_map/add | solution.py:426
  1531.8 21.9 copy.368
  1575.3 32.0 %add_add_fusion.17 = f32[1152,3456]{1,0:T(8,128)} fusion(f32[1152,3456]{1,0:T(8,128)} %get-tuple-element.1039, f32[1152,3456]{1,0:T(8,128)} %get-tuple-element.1038, f32[1152,3456]{1,0:T(8,128)} %get-tuple-element.1037, f32[1152,3456]{1,0:T(8,128)} %get-tuple-element.1035, f32[1152,3456]{1,0:T(8,128)} %get-tuple-element.1036), kind=kLoop, calls=%fused_computation.1099 | loop fusion | flops 15925248 | bytes 95551488 | tf_op jit(solution)/shard_map/add | solution.py:426
  1607.4 42.5 %add_add_fusion.16 = f32[1152,4608]{1,0:T(8,128)} fusion(f32[1152,4608]{1,0:T(8,128)} %get-tuple-element.1044, f32[1152,4608]{1,0:T(8,128)} %get-tuple-element.1043, f32[1152,4608]{1,0:T(8,128)} %get-tuple-element.1042, f32[1152,4608]{1,0:T(8,128)} %get-tuple-element.1040, f32[1152,4608]{1,0:T(8,128)} %get-tuple-element.1041), kind=kLoop, calls=%fused_computation.1098 | loop fusion | flops 21233664 | bytes 127401984 | tf_op jit(solution)/shard_map/add | solution.py:426
  1652.3 71.2 %reduce-scatter.12.cloned.1.call-done = f32[2425,144]{0,1:T(8,128)} async-done(((f32[2425,1152]{0,1:T(8,128)}), f32[2425,144]{0,1:T(8,128)}) %reduce-scatter.12.cloned.1.call-update) | async-done | bytes 1396816 | tf_op jit(solution)/shard_map/reduce_scatter | solution.py:442
  1725.8 348.0 %reduce-scatter.16.cloned.1.call-done = f32[144,4608]{1,0:T(8,128)} async-done(((f32[1152,4608]{1,0:T(8,128)}), f32[144,4608]{1,0:T(8,128)}) %reduce-scatter.16.cloned.1.call-update) | async-done | bytes 2654224
  2077.5 124.5 %all-reduce.4.cloned.1.call-done = f32[40352]{0:T(1024)} async-done(((f32[40352]{0:T(1024)}), f32[40352]{0:T(1024)}) %all-reduce.4.cloned.1.call-update) | async-done | bytes 161424 | tf_op jit(solution)/shard_map/psum | solution.py:453
  2203.5 273.9 %reduce-scatter.8.cloned.1.call-done = f32[144,3456]{1,0:T(8,128)} async-done(((f32[1152,3456]{1,0:T(8,128)}), f32[144,3456]{1,0:T(8,128)}) %reduce-scatter.8.cloned.1.call-update) | async-done | bytes 1990672 | tf_op jit(solution)/shard_map/reduce_scatter | solution.py:439
  2480.1 348.2 %reduce-scatter.10.cloned.1.call-done = f32[144,4608]{1,0:T(8,128)} async-done(((f32[1152,4608]{1,0:T(8,128)}), f32[144,4608]{1,0:T(8,128)}) %reduce-scatter.10.cloned.1.call-update) | async-done | bytes 2654224 | tf_op jit(solution)/shard_map/reduce_scatter | solution.py:440
  2840.8 73.9 %all-reduce.6.cloned.1.call-done = (bf16[2,4608,144]{1,2,0:T(8,128)(2,1)}, bf16[2425,144]{0,1:T(8,128)(2,1)}, bf16[144,2336]{1,0:T(8,128)(2,1)}) async-done(((bf16[2,4608,144]{1,2,0:T(8,128)(2,1)}, bf16[2425,144]{0,1:T(8,128)(2,1)}, bf16[144,2336]{1,0:T(8,128)(2,1)}), (bf16[2,4608,144]{1,2,0:T(8,128)(2,1)}, bf16[2425,144]{0,1:T(8,128)(2,1)}, bf16[144,2336]{1,0:T(8,128)(2,1)})) %all-reduce.6.cloned.1.call-update) | async-done | bytes 4025392 | tf_op jit(solution)/shard_map/psum | solution.py:448
  2924.2 39.4 %psum.57 = f32[]{:T(128)} all-reduce(f32[]{:T(128)S(6)} %add.2273), channel_id=1, replica_groups=mesh['dp'=8,'section'=4] {'dp','section'}, use_global_device_ids=true, to_apply=%region_208.209 | all-reduce | flops 1 | bytes 8 | tf_op jit(solution)/shard_map/psum | solution.py:453
  2963.7 21.8 psum.63
  (771 shorter events, 699.6 us)
Async XLA Ops:
  7.2 97.3 %all-gather.9.cloned.1.call-start = ((), (), s32[]{:S(2)}) async-start(), calls=%async_computation.5 | async-start | bytes 6303744 | tf_op jit(solution)/shard_map/all_gather | solution.py:290
  9.6 215.5 %all-gather.13.cloned.1.call-start = ((), (), s32[]{:S(2)}) async-start(), calls=%async_computation.12 | async-start | bytes 8957952 | tf_op jit(solution)/shard_map/all_gather | solution.py:287
  12.4 366.1 %all-gather.15.cloned.1.call-start = ((), (), s32[]{:S(2)}) async-start(), calls=%async_computation.13 | async-start | bytes 11943936 | tf_op jit(solution)/shard_map/all_gather | solution.py:288
  13.7 518.1 %all-gather.17.cloned.1.call-start = ((), (), s32[]{:S(2)}) async-start(), calls=%async_computation.14 | async-start | bytes 11943936 | tf_op jit(solution)/shard_map/all_gather | solution.py:289
  16.8 645.6 %all-gather.11.cloned.1.call-start = ((), (), s32[]{:S(2)}) async-start(), calls=%async_computation.6 | async-start | bytes 6303744 | tf_op jit(solution)/shard_map/all_gather | solution.py:291
  17.8 1632.2 %reduce-scatter.14.cloned.1.call-start = ((), (), s32[]{:S(2)}) async-start(), calls=%async_computation.10 | async-start | bytes 12607488 | tf_op jit(solution)/shard_map/reduce_scatter | solution.py:443
  23.7 120.6 %copy-start.137 = (bf16[2,256,16]{1,2,0:T(8,128)(2,1)}, bf16[2,256,16]{1,2,0:T(8,128)(2,1)S(1)}, u32[]{:S(2)}) copy-start(bf16[2,256,16]{1,2,0:T(8,128)(2,1)S(1)} %convert_element_type.1408) | copy-start | bytes 49156
  121.1 31.8 %collective-permute-start.1 = (bf16[1,1152]{1,0:T(2,128)(2,1)S(1)}, bf16[1,1152]{1,0:T(2,128)(2,1)S(1)}, u32[]{:S(2)}, u32[]{:S(2)}) collective-permute-start(bf16[1,1152]{1,0:T(2,128)(2,1)S(1)} %convert_element_type.1423), channel_id=1, source_target_pairs={{0,1},{1,2},{2,3},{4,5},{5,6},{6,7},{8,9},{9,10},{10,11},{12,13},{... | collective-permute-start | bytes 6920 | tf_op jit(solution)/shard_map/ppermute | solution.py:35
  153.5 2.1 collective-permute-start.3
  157.4 407.9 %collective-permute-start.5 = (bf16[1,1152]{1,0:T(2,128)(2,1)}, bf16[1,1152]{1,0:T(2,128)(2,1)}, u32[]{:S(2)}, u32[]{:S(2)}) collective-permute-start(bf16[1,1152]{1,0:T(2,128)(2,1)} %convert_element_type.1433), channel_id=1, source_target_pairs={{0,1},{1,2},{2,3},{4,5},{5,6},{6,7},{8,9},{9,10},{10,11},{12,13},{... | collective-permute-start | bytes 6920 | tf_op jit(solution)/shard_map/ppermute | solution.py:35
  562.6 5.8 collective-permute-start
  566.6 64.5 %collective-permute-start.7 = (bf16[1,1152]{1,0:T(2,128)(2,1)}, bf16[1,1152]{1,0:T(2,128)(2,1)}, u32[]{:S(2)}, u32[]{:S(2)}) collective-permute-start(bf16[1,1152]{1,0:T(2,128)(2,1)} %get-tuple-element.1491), channel_id=1, source_target_pairs={{0,1},{1,2},{2,3},{4,5},{5,6},{6,7},{8,9},{9,10},{10,11},{12,13},{... | collective-permute-start | bytes 6920 | tf_op jit(solution)/shard_map/ppermute | solution.py:35
  603.8 3.5 collective-permute-start.2
  614.6 19.2 collective-permute-start.4
  643.7 12.1 collective-permute-start.6
  662.4 73.5 %copy-start.5 = (f32[1,256,1152]{2,1,0:T(8,128)S(1)}, f32[1,256,1152]{2,1,0:T(8,128)}, u32[]{:S(2)}) copy-start(f32[1,256,1152]{2,1,0:T(8,128)} %get-tuple-element.1564) | copy-start | bytes 3538948
  703.0 32.7 %collective-permute-start.8 = (bf16[256,1152]{1,0:T(8,128)(2,1)S(1)}, bf16[256,1152]{1,0:T(8,128)(2,1)S(1)}, u32[]{:S(2)}, u32[]{:S(2)}) collective-permute-start(bf16[256,1152]{1,0:T(8,128)(2,1)S(1)} %get-tuple-element.1027), channel_id=1, source_target_pairs={{1,0},{2,1},{3,2},{5,4},{6,5},{7,6},{9,8},{10,9},{11,10},{13,12},{... | collective-permute-start | bytes 1769480 | tf_op jit(solution)/shard_map/ppermute | solution.py:35
  777.3 12.1 collective-permute-start.9
  789.5 296.6 %copy-start.3 = (f32[1,256,1152]{2,1,0:T(8,128)S(1)}, f32[1,256,1152]{2,1,0:T(8,128)}, u32[]{:S(2)}) copy-start(f32[1,256,1152]{2,1,0:T(8,128)} %get-tuple-element.1562) | copy-start | bytes 3538948
  830.5 255.5 %collective-permute-start.10 = (bf16[256,1152]{1,0:T(8,128)(2,1)S(1)}, bf16[256,1152]{1,0:T(8,128)(2,1)S(1)}, u32[]{:S(2)}, u32[]{:S(2)}) collective-permute-start(bf16[256,1152]{1,0:T(8,128)(2,1)S(1)} %get-tuple-element.1031), channel_id=1, source_target_pairs={{1,0},{2,1},{3,2},{5,4},{6,5},{7,6},{9,8},{10,9},{11,10},{13,12},{... | collective-permute-start | bytes 1769480 | tf_op jit(solution)/shard_map/ppermute | solution.py:35
  1195.2 23.4 collective-permute-start.11
  1345.1 378.5 %reduce-scatter.12.cloned.1.call-start = ((), (), s32[]{:S(2)}) async-start(), calls=%async_computation.9 | async-start | bytes 12607488 | tf_op jit(solution)/shard_map/reduce_scatter | solution.py:442
  1345.2 6.8 collective-permute-start.12
  1352.7 7.1 collective-permute-start.13
  1360.5 6.1 collective-permute-start.14
  1368.0 75.2 %collective-permute-start.15 = (bf16[1,1152]{1,0:T(2,128)(2,1)}, bf16[1,1152]{1,0:T(2,128)(2,1)}, u32[]{:S(2)}, u32[]{:S(2)}) collective-permute-start(bf16[1,1152]{1,0:T(2,128)(2,1)} %get-tuple-element.1488), channel_id=1, source_target_pairs={{1,0},{2,1},{3,2},{5,4},{6,5},{7,6},{9,8},{10,9},{11,10},{13,12},{... | collective-permute-start | bytes 6920 | tf_op jit(solution)/shard_map/ppermute | solution.py:35
  1490.7 583.1 %reduce-scatter.16.cloned.1.call-start = ((), (), s32[]{:S(2)}) async-start(), calls=%async_computation.15 | async-start | bytes 23887872
  1553.9 648.1 %all-reduce.4.cloned.1.call-start = ((), (), s32[]{:S(2)}) async-start(), calls=%async_computation.11 | async-start | bytes 327680 | tf_op jit(solution)/shard_map/psum | solution.py:453
  1575.3 902.2 %reduce-scatter.8.cloned.1.call-start = ((), (), s32[]{:S(2)}) async-start(), calls=%async_computation.7 | async-start | bytes 17915904 | tf_op jit(solution)/shard_map/reduce_scatter | solution.py:439
  1607.3 1220.9 %reduce-scatter.10.cloned.1.call-start = ((), (), s32[]{:S(2)}) async-start(), calls=%async_computation.8 | async-start | bytes 23887872 | tf_op jit(solution)/shard_map/reduce_scatter | solution.py:440
  1650.0 1264.8 %all-reduce.6.cloned.1.call-start = ((), (), s32[]{:S(2)}) async-start(), calls=%async_computation.16 | async-start | bytes 8110080 | tf_op jit(solution)/shard_map/psum | solution.py:448
  2914.7 71.4 %copy-start.26 = (bf16[2,4608,144]{1,2,0:T(8,128)(2,1)S(1)}, bf16[2,4608,144]{1,2,0:T(8,128)(2,1)}, u32[]{:S(2)}) copy-start(bf16[2,4608,144]{1,2,0:T(8,128)(2,1)} %get-tuple-element.1297) | copy-start | bytes 7962628
  (165 other events, 1319.2 us)
Sparse Core Ops, SparseCore 0:
  10.8 93.6 all-gather.8
  107.2 117.7 all-gather.12
  227.8 150.6 all-gather.14
  381.1 150.6 all-gather.16
  534.4 88.8 all-gather.10
  1345.2 186.4 reduce-scatter.13
  1535.9 187.6 reduce-scatter.11
  1727.5 346.3 reduce-scatter.15
  2080.9 120.9 all-reduce.3
  2206.2 271.2 reduce-scatter.7
  2481.8 346.4 reduce-scatter.9
  2831.8 82.8 all-reduce.5
where the time goes:
time: 3050 us; the launch traced here: 3040 us
  waiting for transfers between devices  1950 us (64%)
  other arithmetic  363 us (12%)
  local copies, waits for them, and re-layouts  306 us (10%)
  matrix products  167 us (5%)
  blocking collectives  93 us (3%)
  loops' own time  72.8 us (2%)
  starting transfers between devices  61.6 us (2%)
    unnamed x13, waiting for transfers between devices  348 us
    reduce_scatter x1, waiting for transfers between devices, body(): lax.psum_scatter(g_blk, 'dp', scatter_dimension=0, tiled=True)  348 us
    ppermute x16, waiting for transfers between devices, from_behind(): return lax.ppermute(array, axis, pairs)  294 us
    reduce_scatter x1, waiting for transfers between devices, body(): lax.psum_scatter(g_mod, 'dp', scatter_dimension=0, tiled=True)  274 us
    add x5, other arithmetic, body(): totals = piece if totals is None else jax.tree.map(jnp.add, totals, piece)  161 us
    all_gather x1, waiting for transfers between devices, body(): lax.all_gather(to_half(block_w[0]), 'dp', axis=0, tiled=True)  153 us
    all_gather x1, waiting for transfers between devices, body(): lax.all_gather(to_half(down_local), 'dp', axis=1, tiled=True)  153 us
    dot_general x57, matrix products, matmul(): return jnp.dot(left, right, preferred_element_type=jnp.float32)  141 us
  transfers between devices with their start and end apart: 28, of which 15 were waited for; matrix products, arithmetic and copies ran while one was open for 16% of the time, Pallas kernels for 0%

commit v1 on v0

v1 whole, which is shorter than its diff:
```python
from functools import partial
import math

import jax
import jax.numpy as jnp
from jax import lax
from jax.experimental import pallas as pl
from jax.experimental.pallas import tpu as pltpu
from jax.sharding import PartitionSpec as P

HEADS = 16
HEAD_DIM = 72
D = 1152
FF = 4608
HALF = FF // 2
NCLS = 1001
FREQ = 256
GRID = 32
PATCHES = 256
PATCH_IN = 16
HEAD_OUT = 32
LAYERS = 2
NBIAS = 40352


epsilon_norm = 1e-06
momentum_rate = 0.9
ema_decay = 0.9
learn_rate = 4000.0
clip_limit = 0.02
MESH = pl.DeviceIdType.MESH
BF = jnp.bfloat16


def matmul(left, right):
    return jnp.dot(left, right, preferred_element_type=jnp.float32)


def matmul_nt(left, right):
    return lax.dot_general(
        left, right, (((1,), (1,)), ((), ())), preferred_element_type=jnp.float32
    )


def matmul_tn(left, right):
    return lax.dot_general(
        left, right, (((0,), (0,)), ((), ())), preferred_element_type=jnp.float32
    )


def to_half(value):
    return value.astype(BF)


def column_sums(value):
    return jnp.sum(value.astype(jnp.float32), axis=0)


def silu_back(value, grad):
    return jax.vjp(jax.nn.silu, value)[1](grad)[0]


def layer_modulate(tokens, shift, scale):
    centered = tokens - jnp.mean(tokens, axis=-1, keepdims=True)
    normed = centered * lax.rsqrt(
        jnp.mean(centered * centered, axis=-1, keepdims=True) + epsilon_norm
    )
    return normed * (1.0 + scale) + shift


def patchify(field):
    images, side = (field.shape[0], field.shape[1] // 2)
    return (
        field.reshape(images, side, 2, side, 2, 4)
        .transpose(0, 1, 3, 2, 4, 5)
        .reshape(images, side * side, 16)
    )


def sincos_rows(places, width):
    omega = 1.0 / 10000.0 ** (jnp.arange(width // 2, dtype=jnp.float32) / (width // 2))
    angle = places[:, None] * omega[None, :]
    return jnp.concatenate([jnp.sin(angle), jnp.cos(angle)], axis=1)


def position_table(side, width):
    line = sincos_rows(jnp.arange(side, dtype=jnp.float32), width // 2)
    column = jnp.broadcast_to(line[None], (side, side, width // 2))
    row = jnp.broadcast_to(line[:, None], (side, side, width // 2))
    return jnp.concatenate([column, row], axis=2).reshape(side * side, width)


def time_features(steps):
    half = FREQ // 2
    freqs = jnp.exp(-math.log(10000.0) * jnp.arange(half, dtype=jnp.float32) / half)
    angle = steps[:, None] * freqs[None, :]
    return jnp.concatenate([jnp.cos(angle), jnp.sin(angle)], axis=1)


def noise_levels(steps):
    level = jnp.cos((steps / 1000.0 + 0.008) / 1.008 * (math.pi / 2)) ** 2
    return (jnp.sqrt(level), jnp.sqrt(1.0 - level))


Z, X = 4, 2
PART = 48
GATHER_CHUNKS = ((0, 0, False), (0, 48, False), (0, 96, False), (1, 0, False), (1, 48, False), (1, 96, True))


def ring_fits(n, rows):
    return n == Z * X and rows == 144


def gather_kernel(blk_ref, dn_ref, out_blk, out_dn, up_sem, down_sem, x_sem, sib_sem, recv_sem, sib_recv, own_sem):
    me = lax.axis_index("dp")
    section = lax.axis_index("section")
    z, x = me // X, lax.rem(me, X)
    core = lax.rem(section, 2)
    sibling = section + 1 - 2 * core
    across = me + 1 - 2 * x
    chunks = len(GATHER_CHUNKS)
    has_up, has_down = z < Z - 1, z > 0

    barrier = pltpu.get_barrier_semaphore()
    pl.semaphore_signal(barrier, 1, device_id={"section": sibling}, device_id_type=MESH)
    pl.semaphore_signal(barrier, 1, device_id={"dp": across}, device_id_type=MESH)

    @pl.when(has_up)
    def _():
        pl.semaphore_signal(barrier, 1, device_id={"dp": me + X}, device_id_type=MESH)

    @pl.when(has_down)
    def _():
        pl.semaphore_signal(barrier, 1, device_id={"dp": me - X}, device_id_type=MESH)

    pl.semaphore_wait(barrier, 2 + has_up.astype(jnp.int32) + has_down.astype(jnp.int32))

    def place(owner, k, side):
        which, first, unused = GATHER_CHUNKS[k]
        rows = pl.ds(pl.multiple_of(owner * 144 + first, 16), PART)
        return (out_dn if which else out_blk).at[side, rows]

    def source(owner, k, mine):
        if not mine:
            return place(owner, k, core)
        which, first, unused = GATHER_CHUNKS[k]
        return (dn_ref if which else blk_ref).at[pl.ds(first, PART)]

    def copy(owner, k, mine, sem, target):
        unit = owner * chunks + k
        return pltpu.make_async_remote_copy(
            src_ref=source(owner, k, mine),
            dst_ref=place(owner, k, core),
            send_sem=sem.at[unit],
            recv_sem=recv_sem.at[unit],
            device_id={"dp": target},
            device_id_type=MESH,
        )

    def to_sibling(owner, k, mine):
        unit = owner * chunks + k
        return pltpu.make_async_remote_copy(
            src_ref=source(owner, k, mine),
            dst_ref=place(owner, k, core),
            send_sem=sib_sem.at[unit],
            recv_sem=sib_recv.at[unit],
            device_id={"section": sibling},
            device_id_type=MESH,
        )

    def own_copy(k):
        return pltpu.make_async_copy(source(me, k, True), place(me, k, core), own_sem.at[k])

    def arrived(owner, k):
        copy(owner, k, False, x_sem, across).wait_recv()

    for k in range(chunks):
        @pl.when(has_up)
        def _():
            copy(me, k, True, up_sem, me + X).start()

        @pl.when(has_down)
        def _():
            copy(me, k, True, down_sem, me - X).start()

        copy(me, k, True, x_sem, across).start()
        own_copy(k).start()
        to_sibling(me, k, True).start()

    def along(step, k, first_across):
        shift = 1 - 2 * x if first_across else 0
        crosses = (not first_across) and (not GATHER_CHUNKS[k][2])

        @pl.when(z >= step)
        def _():
            owner = me - X * step + shift
            arrived(owner, k)

            @pl.when(has_up)
            def _():
                copy(owner, k, False, up_sem, me + X).start()

            if crosses:
                copy(owner, k, False, x_sem, across).start()
            to_sibling(owner, k, False).start()

        @pl.when(z + step < Z)
        def _():
            owner = me + X * step + shift
            arrived(owner, k)

            @pl.when(has_down)
            def _():
                copy(owner, k, False, down_sem, me - X).start()

            if crosses:
                copy(owner, k, False, x_sem, across).start()
            to_sibling(owner, k, False).start()

    def crossed(step, k):
        direct = GATHER_CHUNKS[k][2]
        if step == 0:
            owner = across
            arrived(owner, k)
            if direct:
                @pl.when(has_up)
                def _():
                    copy(owner, k, False, up_sem, me + X).start()

                @pl.when(has_down)
                def _():
                    copy(owner, k, False, down_sem, me - X).start()
            to_sibling(owner, k, False).start()
        elif not direct:
            for sign in (-1, 1):
                @pl.when((z >= step) if sign < 0 else (z + step < Z))
                def _():
                    owner = across + sign * X * step
                    arrived(owner, k)
                    to_sibling(owner, k, False).start()

    for step in range(1, Z + 1):
        for k in range(chunks):
            if step < Z:
                along(step, k, False)
            crossed(step - 1, k)
            if step < Z and GATHER_CHUNKS[k][2]:
                along(step, k, True)

    for k in range(chunks):
        direct = GATHER_CHUNKS[k][2]
        own_copy(k).wait()
        for column in range(2):
            base = me if column == 0 else across
            for step in range(0, Z):
                for sign in (-1, 1) if step else (1,):
                    @pl.when((z >= step) if sign < 0 else (z + step < Z))
                    def _():
                        owner = base + sign * X * step
                        mine = column == 0 and step == 0
                        to_sibling(owner, k, mine).wait_send()
                        pltpu.make_async_remote_copy(
                            src_ref=place(owner, k, 1 - core),
                            dst_ref=place(owner, k, 1 - core),
                            send_sem=sib_sem.at[owner * chunks + k],
                            recv_sem=sib_recv.at[owner * chunks + k],
                            device_id={"section": sibling},
                            device_id_type=MESH,
                        ).wait_recv()
                        runs = column == 0 or direct
                        if runs and (step == 0 or sign < 0):
                            @pl.when(has_up)
                            def _():
                                copy(owner, k, mine, up_sem, me + X).wait_send()
                        if runs and (step == 0 or sign > 0):
                            @pl.when(has_down)
                            def _():
                                copy(owner, k, mine, down_sem, me - X).wait_send()
                        if column == 0 and (step == 0 or not direct):
                            copy(owner, k, mine, x_sem, across).wait_send()


def gather_weights(blk, dn):
    n = lax.axis_size("dp")
    if not ring_fits(n, blk.shape[0]):
        blk_all = lax.all_gather(blk, "dp", axis=0, tiled=True)
        dn_all = lax.all_gather(dn, "dp", axis=0, tiled=True)
        pairs = [(k, k ^ 1) for k in range(lax.axis_size("section"))]
        blk_sib, dn_sib = lax.ppermute((blk_all, dn_all), "section", pairs)
        even = lax.rem(lax.axis_index("section"), 2) == 0
        both = lambda a, b: jnp.where(even, jnp.stack([a, b]), jnp.stack([b, a]))
        return (both(blk_all, blk_sib), both(dn_all, dn_sib))
    units = n * len(GATHER_CHUNKS)
    return pl.pallas_call(
        gather_kernel,
        out_shape=(
            jax.ShapeDtypeStruct((2, D, FF), BF),
            jax.ShapeDtypeStruct((2, D, HALF), BF),
        ),
        in_specs=[pl.BlockSpec(memory_space=pl.ANY)] * 2,
        out_specs=(pl.BlockSpec(memory_space=pl.ANY),) * 2,
        scratch_shapes=[pltpu.SemaphoreType.DMA((units,))] * 6
        + [pltpu.SemaphoreType.DMA((len(GATHER_CHUNKS),))],
        compiler_params=pltpu.CompilerParams(collective_id=0, has_side_effects=True),
        name="gather_weights",
    )(blk, dn)


SUM_CHUNKS = ((1, 0, False), (1, 48, False), (1, 96, True), (0, 0, False), (0, 48, False), (0, 96, False))
VMEM_BYTES = 60 * 1024 * 1024


def sum_kernel(
    g_ref, gd_ref, blk_out, dn_out,
    own_b, own_d, other_d, xb, xd, xq, up_b, up_d, up_o, down_b, down_d, down_o, acc,
    load_sem, x_send, x_recv, up_send, up_recv, down_send, down_recv, sib_send, sib_recv, y_send, y_recv,
):
    me = lax.axis_index("dp")
    section = lax.axis_index("section")
    z, x = me // X, lax.rem(me, X)
    core = lax.rem(section, 2)
    sibling = section + 1 - 2 * core
    facing = lax.rem(section + 2, 4)
    across = me + 1 - 2 * x
    chunks = len(SUM_CHUNKS)
    has_up, has_down = z < Z - 1, z > 0

    barrier = pltpu.get_barrier_semaphore()
    for target in ({"section": sibling}, {"section": facing}, {"dp": across}):
        pl.semaphore_signal(barrier, 1, device_id=target, device_id_type=MESH)

    @pl.when(has_up)
    def _():
        pl.semaphore_signal(barrier, 1, device_id={"dp": me + X}, device_id_type=MESH)

    @pl.when(has_down)
    def _():
        pl.semaphore_signal(barrier, 1, device_id={"dp": me - X}, device_id_type=MESH)

    def each(distance, run):
        if distance == 0:
            run(z, None)
            return

        @pl.when(z + distance < Z)
        def _():
            run(z + distance, True)

        @pl.when(z >= distance)
        def _():
            run(z - distance, False)

    def hbm(k, zz, column):
        which, first, unused = SUM_CHUNKS[k]
        rows = pl.ds(pl.multiple_of((zz * X + column) * 144 + first, 16), PART)
        return (gd_ref if which else g_ref).at[rows]

    def own(k, zz):
        which, first, unused = SUM_CHUNKS[k]
        return (own_d if which else own_b).at[zz, pl.ds(first, PART)]

    def from_x(k, zz):
        which, first, direct = SUM_CHUNKS[k]
        if direct:
            return xq
        return (xd if which else xb).at[zz, pl.ds(first, PART)]

    def from_z(k, zz, up, other):
        which, first, unused = SUM_CHUNKS[k]
        if other:
            return (up_o if up else down_o).at[zz]
        if which:
            return (up_d if up else down_d).at[zz, pl.ds(first, PART)]
        return (up_b if up else down_b).at[zz, pl.ds(first, PART)]

    def load(k, zz, other=False):
        index = ((chunks if other else 0) + k) * Z + zz
        return pltpu.make_async_copy(
            hbm(k, zz, (1 - x) if other else x),
            other_d.at[zz] if other else own(k, zz),
            load_sem.at[index],
        )

    def x_copy(k, zz, src):
        unit = k * Z + zz
        return pltpu.make_async_remote_copy(
            src_ref=src, dst_ref=from_x(k, zz), send_sem=x_send.at[unit], recv_sem=x_recv.at[unit],
            device_id={"dp": across}, device_id_type=MESH,
        )

    def z_copy(k, zz, up, other):
        unit = ((chunks if other else 0) + k) * Z + zz
        return pltpu.make_async_remote_copy(
            src_ref=other_d.at[zz] if other else own(k, zz),
            dst_ref=from_z(k, zz, up, other),
            send_sem=(up_send if up else down_send).at[unit],
            recv_sem=(up_recv if up else down_recv).at[unit],
            device_id={"dp": me + X if up else me - X},
            device_id_type=MESH,
        )

    def dn_copy(k, slot, to_sib):
        rows = pl.ds(SUM_CHUNKS[k][1], PART)
        unit = slot * chunks + k
        return pltpu.make_async_remote_copy(
            src_ref=dn_out.at[slot, rows], dst_ref=dn_out.at[slot, rows],
            send_sem=(sib_send if to_sib else y_send).at[unit],
            recv_sem=(sib_recv if to_sib else y_recv).at[unit],
            device_id={"section": sibling if to_sib else facing},
            device_id_type=MESH,
        )

    def total(dst, srcs):
        @pl.loop(0, PART // 16)
        def _(step):
            rows = pl.ds(pl.multiple_of(step * 16, 16), 16)
            value = srcs[0][rows].astype(jnp.float32)
            for src in srcs[1:]:
                value = value + src[rows].astype(jnp.float32)
            dst[rows] = value.astype(dst.dtype)

    for k in range(chunks):
        for distance in (3, 2, 1, 0):
            def run(zz, up):
                load(k, zz).start()
                if SUM_CHUNKS[k][2]:
                    load(k, zz, True).start()
            each(distance, run)

    pl.semaphore_wait(barrier, 3 + has_up.astype(jnp.int32) + has_down.astype(jnp.int32))

    for which in (1, 0):
        for distance in (3, 2, 1, 0):
            for k in range(chunks):
                if SUM_CHUNKS[k][0] == which and not SUM_CHUNKS[k][2]:
                    each(distance, lambda zz, up: x_copy(k, zz, hbm(k, zz, 1 - x)).start())

    def pass_on(k, distance):
        def run(zz, up):
            behind = has_down if up else has_up
            if SUM_CHUNKS[k][2]:
                for other in (False, True):
                    mine = other_d.at[zz] if other else own(k, zz)
                    load(k, zz, other).wait()

                    @pl.when(behind)
                    def _():
                        z_copy(k, zz, up, other).wait_recv()
                        total(mine, [mine, from_z(k, zz, up, other)])

                    z_copy(k, zz, up, other).start()
                return
            load(k, zz).wait()
            x_copy(k, zz, hbm(k, zz, 1 - x)).wait_recv()

            @pl.when(behind)
            def _():
                z_copy(k, zz, up, False).wait_recv()
                total(own(k, zz), [own(k, zz), from_x(k, zz), from_z(k, zz, up, False)])

            @pl.when(jnp.logical_not(behind))
            def _():
                total(own(k, zz), [own(k, zz), from_x(k, zz)])

            z_copy(k, zz, up, False).start()
        each(distance, run)

    def add_z(dst, k, other):
        @pl.when(has_down)
        def _():
            z_copy(k, z, True, other).wait_recv()
            total(dst, [dst, from_z(k, z, True, other)])

        @pl.when(has_up)
        def _():
            z_copy(k, z, False, other).wait_recv()
            total(dst, [dst, from_z(k, z, False, other)])

    def send_direct(k):
        load(k, z, True).wait()
        acc[...] = other_d[z].astype(jnp.float32)
        add_z(acc, k, True)
        other_d[z] = acc[...].astype(BF)
        x_copy(k, z, other_d.at[z]).start()

    def finish(k):
        which, first, direct = SUM_CHUNKS[k]
        rows = pl.ds(first, PART)
        dst = acc if which else blk_out.at[rows]
        load(k, z).wait()
        if direct:
            total(dst, [own(k, z)])
            add_z(dst, k, False)
            x_copy(k, z, other_d.at[z]).wait_recv()
            total(dst, [dst, from_x(k, z)])
        else:
            x_copy(k, z, hbm(k, z, 1 - x)).wait_recv()
            total(dst, [own(k, z), from_x(k, z)])
            add_z(dst, k, False)
        if which:
            total(dn_out.at[section, rows], [acc])
            dn_copy(k, section, True).start()
            dn_copy(k, section, False).start()

    dn_chunks = [k for k in range(chunks) if SUM_CHUNKS[k][0]]
    blk_chunks = [k for k in range(chunks) if not SUM_CHUNKS[k][0]]
    for distance in (3, 2, 1):
        for k in dn_chunks:
            pass_on(k, distance)
    for k in blk_chunks:
        pass_on(k, 3)
    for k in dn_chunks:
        if SUM_CHUNKS[k][2]:
            send_direct(k)
    for k in dn_chunks:
        finish(k)
    for k in blk_chunks:
        pass_on(k, 2)
    for k in dn_chunks:
        dn_copy(k, facing, False).wait_recv()
        dn_copy(k, facing, True).start()
    for k in blk_chunks:
        pass_on(k, 1)
    for k in blk_chunks:
        finish(k)

    for k in range(chunks):
        direct = SUM_CHUNKS[k][2]
        for distance in (3, 2, 1, 0):
            def run(zz, up):
                if not direct:
                    x_copy(k, zz, hbm(k, zz, 1 - x)).wait_send()
                elif distance == 0:
                    x_copy(k, zz, other_d.at[zz]).wait_send()
                if distance:
                    z_copy(k, zz, up, False).wait_send()
                    if direct:
                        z_copy(k, zz, up, True).wait_send()
            each(distance, run)
        if SUM_CHUNKS[k][0]:
            dn_copy(k, section, True).wait_send()
            dn_copy(k, section, False).wait_send()
            dn_copy(k, facing, True).wait_send()
            dn_copy(k, sibling, True).wait_recv()
            dn_copy(k, lax.rem(sibling + 2, 4), True).wait_recv()


def sum_gradients(g_blk, g_dn):
    n = lax.axis_size("dp")
    if not ring_fits(n, D // n):
        blk = lax.psum_scatter(g_blk, "dp", scatter_dimension=0, tiled=True)
        dn = lax.psum_scatter(g_dn, "dp", scatter_dimension=0, tiled=True)
        return (blk.astype(jnp.float32), lax.all_gather(dn, "section"))
    chunks = len(SUM_CHUNKS)
    dma = lambda count: pltpu.SemaphoreType.DMA((count,))
    ring_b = pltpu.VMEM((Z, 144, FF), BF)
    ring_d = pltpu.VMEM((Z, 144, HALF), BF)
    ring_o = pltpu.VMEM((Z, PART, HALF), BF)
    vmem = pl.BlockSpec(memory_space=pltpu.VMEM)
    return pl.pallas_call(
        sum_kernel,
        out_shape=(
            jax.ShapeDtypeStruct((144, FF), jnp.float32),
            jax.ShapeDtypeStruct((4, 144, HALF), BF),
        ),
        in_specs=[pl.BlockSpec(memory_space=pl.ANY)] * 2,
        out_specs=(vmem, vmem),
        scratch_shapes=[
            ring_b, ring_d, ring_o, ring_b, pltpu.VMEM((Z, 96, HALF), BF), pltpu.VMEM((PART, HALF), BF),
            ring_b, ring_d, ring_o, ring_b, ring_d, ring_o, pltpu.VMEM((PART, HALF), jnp.float32),
            dma(2 * chunks * Z), dma(chunks * Z), dma(chunks * Z),
            dma(2 * chunks * Z), dma(2 * chunks * Z), dma(2 * chunks * Z), dma(2 * chunks * Z),
            dma(4 * chunks), dma(4 * chunks), dma(4 * chunks), dma(4 * chunks),
        ],
        compiler_params=pltpu.CompilerParams(
            collective_id=1, has_side_effects=True, vmem_limit_bytes=VMEM_BYTES
        ),
        name="sum_gradients",
    )(g_blk, g_dn)


def heads_of(value):
    return value.reshape(PATCHES, HEADS, HEAD_DIM)


def attention_forward(xm_half, wblk, bblk):
    qkv = to_half(matmul(xm_half, wblk[:, : 3 * D]) + bblk[: 3 * D])
    parts = qkv.reshape(PATCHES, 3, HEADS, HEAD_DIM)
    scores = jnp.einsum(
        "qhd,khd->hqk", parts[:, 0], parts[:, 1], preferred_element_type=jnp.float32
    ) * HEAD_DIM ** (-0.5)
    probs = jax.nn.softmax(scores, axis=-1)
    attended = to_half(
        jnp.einsum("hqk,khd->qhd", to_half(probs), parts[:, 2], preferred_element_type=jnp.float32)
    ).reshape(PATCHES, D)
    branch = matmul(attended, wblk[:, 3 * D :]) + bblk[3 * D :]
    return (branch, (parts, probs, attended))


def attention_backward(grad_half, saved, wblk):
    parts, probs, attended = saved
    d_att = heads_of(to_half(matmul_nt(grad_half, wblk[:, 3 * D :])))
    d_value = jnp.einsum(
        "hqk,qhd->khd", to_half(probs), d_att, preferred_element_type=jnp.float32
    )
    d_probs = jnp.einsum("qhd,khd->hqk", d_att, parts[:, 2], preferred_element_type=jnp.float32)
    d_scores = to_half(probs * (d_probs - jnp.sum(probs * d_probs, axis=-1, keepdims=True)))
    d_query = jnp.einsum(
        "hqk,khd->qhd", d_scores, parts[:, 1], preferred_element_type=jnp.float32
    ) * HEAD_DIM ** (-0.5)
    d_key = jnp.einsum(
        "hqk,qhd->khd", d_scores, parts[:, 0], preferred_element_type=jnp.float32
    ) * HEAD_DIM ** (-0.5)
    d_qkv = to_half(jnp.stack([d_query, d_key, d_value], axis=1).reshape(PATCHES, 3 * D))
    return (matmul_nt(d_qkv, wblk[:, : 3 * D]), d_qkv)


def modulated(x, mod):
    return layer_modulate(x, mod[None, :D], mod[None, D : 2 * D])


def modulated_back(x, mod, d_xm):
    pull = jax.vjp(layer_modulate, x, mod[None, :D], mod[None, D : 2 * D])[1]
    d_x, d_shift, d_scale = pull(d_xm)
    return (d_x, d_shift[0], d_scale[0])


def stage_forward(x_in, weights):
    mod_a, mod_m, w_blk, w_dn, b_attn, b_up, b_down = weights
    xm_a = to_half(modulated(x_in, mod_a))
    branch_a, saved = attention_forward(xm_a, w_blk[0], b_attn)
    x_mid = to_half(x_in + mod_a[None, 2 * D :] * branch_a).astype(jnp.float32)
    xm_m = to_half(modulated(x_mid, mod_m))
    pre = matmul(xm_m, w_blk[1]) + b_up
    act = to_half(jax.nn.gelu(pre, approximate=True))
    branch_m = matmul_nt(act[:, :HALF], w_dn[0]) + matmul_nt(act[:, HALF:], w_dn[1]) + b_down
    x_out = x_mid + mod_m[None, 2 * D :] * branch_m
    return (x_out, (xm_a, branch_a, saved, x_mid, xm_m, pre, act, branch_m))


def mlp_backward(d_out, weights, kept):
    mod_a, mod_m, w_blk, w_dn, b_attn, b_up, b_down = weights
    xm_a, branch_a, saved, x_mid, xm_m, pre, act, branch_m = kept
    d_gate = jnp.sum(d_out * branch_m, axis=0)
    grad_half = to_half(d_out * mod_m[None, 2 * D :])
    d_act = jnp.concatenate([matmul(grad_half, w_dn[0]), matmul(grad_half, w_dn[1])], axis=1)
    d_pre = to_half(jax.vjp(partial(jax.nn.gelu, approximate=True), pre)[1](d_act)[0])
    d_x, d_shift, d_scale = modulated_back(x_mid, mod_m, matmul_nt(d_pre, w_blk[1]))
    d_mod = to_half(jnp.concatenate([d_shift, d_scale, d_gate]))
    return (to_half(d_out + d_x).astype(jnp.float32), d_mod, grad_half, d_pre)


def attn_backward(d_out, x_in, weights, kept):
    mod_a, mod_m, w_blk, w_dn, b_attn, b_up, b_down = weights
    xm_a, branch_a, saved, x_mid, xm_m, pre, act, branch_m = kept
    d_gate = jnp.sum(d_out * branch_a, axis=0)
    grad_half = to_half(d_out * mod_a[None, 2 * D :])
    d_xm, d_qkv = attention_backward(grad_half, saved, w_blk[0])
    d_x, d_shift, d_scale = modulated_back(x_in, mod_a, d_xm)
    d_mod = to_half(jnp.concatenate([d_shift, d_scale, d_gate]))
    return (to_half(d_out + d_x), d_mod, grad_half, d_qkv)


def final_step(x_out, fmod, w_head, b_head, target, counts, loss_scale):
    xf_half = to_half(modulated(x_out, fmod))
    error = matmul(xf_half, w_head) + b_head - target
    loss = counts * jnp.sum(error * error)
    d_pred = to_half(2.0 * loss_scale * counts * error)
    g_head = matmul_tn(xf_half, d_pred)
    d_x, d_shift, d_scale = modulated_back(x_out, fmod, matmul_nt(d_pred, w_head))
    return (loss, d_x, to_half(jnp.concatenate([d_shift, d_scale])), g_head, column_sums(d_pred))


def nesterov(weight, moment, average, grad, factor):
    clipped = grad * factor
    moment_new = momentum_rate * moment + clipped
    weight_new = weight - learn_rate * (clipped + momentum_rate * moment_new)
    average_new = ema_decay * average + (1.0 - ema_decay) * weight_new
    return (weight_new, moment_new, average_new, weight_new.astype(jnp.bfloat16))


def swap(array, by):
    peers = lax.axis_size("section")
    return lax.ppermute(array, "section", [(k, k ^ by) for k in range(peers)])


def pick(parts, index):
    return lax.dynamic_index_in_dim(parts, index, 0, keepdims=False)


def body(
    latents, noise, timesteps, labels, null_mask, valid,
    mod_w, mod_m, mod_e, block_w, block_m, block_e, down_w, down_m, down_e,
    stem_w, stem_m, stem_e, tail_w, tail_m, tail_e, biases, bias_m, bias_e,
):
    place = lax.axis_index("dp")
    section = lax.axis_index("section")
    stage = section // 2
    core = lax.rem(section, 2)
    even = core == 0
    n = lax.axis_size("dp")
    width = D // n

    downs = jnp.swapaxes(down_w, 1, 2)
    blk_half = to_half(block_w[0])
    dn_half = to_half(lax.dynamic_slice(downs, (stage, 0, core * HALF), (1, width, HALF))[0])
    w_blk, w_dn = gather_weights(blk_half, dn_half)

    stems = stem_w.T
    classes_own = jnp.where(null_mask > 0, NCLS - 1, labels)
    meta = lax.all_gather(jnp.stack([timesteps, classes_own, valid], axis=1), "dp", axis=0, tiled=True)
    images = meta.shape[0]
    steps_all = meta[:, 0].astype(jnp.float32)
    picks = (meta[:, 1][:, None] == jnp.arange(NCLS, dtype=jnp.int32)[None, :]).astype(BF)
    count = jnp.sum(meta[:, 2].astype(jnp.float32))
    loss_scale = 1.0 / (count * PATCHES * HEAD_OUT)
    freq = to_half(time_features(steps_all))

    stem_half = to_half(stems)
    table = stem_half[:, :NCLS]
    w_patch = stem_half[:, NCLS : NCLS + PATCH_IN]
    w_one = stem_half[:, NCLS + PATCH_IN : NCLS + PATCH_IN + FREQ]
    w_two = stem_half[:, NCLS + PATCH_IN + FREQ :]
    b_one = lax.dynamic_slice_in_dim(biases, 31 * D + place * width, width)
    b_two = lax.dynamic_slice_in_dim(biases, 32 * D + place * width, width)
    hidden_pre = matmul_nt(w_one, freq) + b_one[:, None]
    hidden = to_half(jax.nn.silu(hidden_pre))
    tail_half = to_half(tail_w)
    small = jnp.concatenate([hidden, w_patch, tail_half[:, 2 * D :]], axis=1)
    small = lax.all_gather(small, "dp", axis=0, tiled=True)
    hidden_all = small[:, :images]
    w_patch_all = small[:, images : images + PATCH_IN]
    w_head_all = small[:, images + PATCH_IN :]
    cond = matmul(w_two, hidden_all) + b_two[:, None] + matmul_nt(table, picks)
    cond_low = to_half(cond).astype(jnp.float32)
    cond_own = jnp.where(section == 0, cond, cond_low)
    silu_own = to_half(jax.nn.silu(cond_own))
    silu_low = to_half(jax.nn.silu(cond_low))
    mod_half_w = to_half(mod_w[0])
    part_mod = matmul_tn(silu_own, mod_half_w)
    part_fm = matmul_tn(silu_low, tail_half[:, : 2 * D])
    parts = jnp.concatenate([part_mod, part_fm], axis=1).reshape(n, images // n, 5 * D)
    mods = jnp.sum(lax.all_to_all(parts, "dp", 0, 0), axis=0)
    own_mod = mods[:, : 3 * D]
    sib_mod = swap(own_mod, 1)
    mod_a = pick(jnp.where(even, own_mod, sib_mod), core)
    mod_b = pick(jnp.where(even, sib_mod, own_mod), core)
    bias_of = lambda first, length: lax.dynamic_slice_in_dim(biases, first, length)
    mod_a = mod_a + bias_of(6 * D * stage, 3 * D)
    mod_b = mod_b + bias_of(6 * D * stage + 3 * D, 3 * D)
    fmod = pick(mods[:, 3 * D :], core) + biases[33 * D : 35 * D]
    weights = (
        mod_a, mod_b, w_blk, w_dn,
        bias_of(12 * D + 8 * D * stage, 4 * D),
        bias_of(16 * D + 8 * D * stage, 4 * D),
        bias_of(28 * D + D * stage, D),
    )

    step = pick(timesteps, core).astype(jnp.float32)
    signal, spread = noise_levels(step)
    lat, noi = pick(latents, core)[None], pick(noise, core)[None]
    counts = pick(valid, core).astype(jnp.float32)
    tok_half = to_half(patchify(signal * lat + spread * noi))[0]
    target = jnp.concatenate([patchify(signal * noi - spread * lat), patchify(noi)], axis=2)[0]
    x_first = matmul_nt(tok_half, w_patch_all) + biases[30 * D : 31 * D] + position_table(GRID // 2, D)

    x_hop = swap(to_half(stage_forward(x_first, weights)[0]), 2)
    x_in = jnp.where(stage == 0, x_first, x_hop.astype(jnp.float32))
    x_out, kept = stage_forward(x_in, weights)
    loss, d_final, d_fmod, g_head, b_head = final_step(
        x_out, fmod, w_head_all, biases[35 * D :], target, counts, loss_scale
    )
    d_mid = mlp_backward(d_final, weights, kept)[0]
    d_hop = swap(attn_backward(d_mid, x_in, weights, kept)[0], 2)
    d_out = jnp.where(stage == 1, d_final, d_hop.astype(jnp.float32))
    d_mid, d_mod_b, d_branch_b, d_pre = mlp_backward(d_out, weights, kept)
    d_first, d_mod_a, d_branch_a, d_qkv = attn_backward(d_mid, x_in, weights, kept)
    xm_a, branch_a, saved, x_mid, xm_b, pre, act, branch_b = kept
    attended = saved[2]

    act_own = jnp.where(even, act[:, :HALF], act[:, HALF:])
    act_sib, branch_sib = swap((jnp.where(even, act[:, HALF:], act[:, :HALF]), d_branch_b), 1)
    g_dn = to_half(matmul_tn(d_branch_b, act_own) + matmul_tn(branch_sib, act_sib))
    d_attn = jnp.concatenate([d_qkv, d_branch_a], axis=1)
    left_sib, last_sib, right_sib = swap(
        (
            jnp.where(even, xm_b, xm_a),
            jnp.where(even, xm_b, attended),
            jnp.where(even, d_pre, d_attn),
        ),
        1,
    )
    left = jnp.concatenate([jnp.where(even, xm_a, xm_b), left_sib], axis=0)
    last = jnp.concatenate([jnp.where(even, attended, xm_b), last_sib], axis=0)
    right = jnp.concatenate([jnp.where(even, d_attn, d_pre), right_sib], axis=0)
    g_blk = jnp.concatenate(
        [
            to_half(matmul_tn(left, right[:, : 3 * D])),
            to_half(matmul_tn(last, right[:, 3 * D :])),
        ],
        axis=1,
    )
    g_blk, g_dn = sum_gradients(g_blk, g_dn)

    last_stage = (stage == 1).astype(jnp.float32)
    first_stage = (stage == 0).astype(jnp.float32)
    d_mod_sib = swap(jnp.where(even, d_mod_b, d_mod_a), 1)
    d_mod_own = jnp.where(even, d_mod_a, d_mod_b)
    d_fmod = jnp.where(stage == 1, d_fmod, jnp.zeros_like(d_fmod))
    d_fmod_sib = swap(d_fmod, 1)
    pair = lambda own, sib: jnp.where(even, jnp.stack([own, sib]), jnp.stack([sib, own]))
    d_fmods = pair(d_fmod, d_fmod_sib)
    d_fmods = d_fmods + swap(d_fmods, 2)
    d_mods = jnp.concatenate([pair(d_mod_own, d_mod_sib), d_fmods], axis=1)
    d_mods = lax.all_gather(d_mods, "dp", axis=0, tiled=True)
    d_mod_all, d_fm_all = d_mods[:, : 3 * D], d_mods[:, 3 * D :]
    g_mod = matmul(silu_own, d_mod_all)
    g_fm = matmul(silu_low, d_fm_all)
    c_own = silu_back(cond_own, matmul_nt(mod_half_w, d_mod_all))
    c_fm = silu_back(cond_low, matmul_nt(tail_half[:, : 2 * D], d_fm_all))
    c_all = lax.all_gather(c_own, "section")
    d_cond = to_half(c_all[3] + c_fm)
    for slot in (2, 1, 0):
        d_cond = to_half(d_cond.astype(jnp.float32) + c_all[slot])
    part_hidden = matmul_tn(w_two, d_cond).reshape(n, width, images)
    d_hidden = jnp.sum(lax.all_to_all(part_hidden, "dp", 0, 0), axis=0)
    d_pre_one = to_half(silu_back(hidden_pre, d_hidden))
    g_table = matmul(d_cond, picks)
    g_one = matmul(d_pre_one, freq)
    g_two = matmul_nt(d_cond, hidden_all)

    row_sums = lambda value: jnp.sum(value.astype(jnp.float32), axis=1)
    anchor = (place == 0).astype(jnp.float32)
    corner = anchor * (section == 0).astype(jnp.float32)
    once = (section == 0).astype(jnp.float32)
    vector = jnp.zeros((NBIAS,), jnp.float32)
    put = lambda vector, piece, start: lax.dynamic_update_slice_in_dim(vector, piece, start, 0)
    vector = put(vector, anchor * column_sums(d_mod_all), 3 * D * section)
    vector = put(
        vector,
        jnp.concatenate([column_sums(d_qkv), column_sums(d_branch_a), column_sums(d_pre)]),
        12 * D + 8 * D * stage,
    )
    vector = put(vector, column_sums(d_branch_b), 28 * D + D * stage)
    vector = put(vector, first_stage * column_sums(d_first), 30 * D)
    vector = put(vector, once * row_sums(d_pre_one), 31 * D + place * width)
    vector = put(vector, once * row_sums(d_cond), 32 * D + place * width)
    vector = put(vector, corner * column_sums(d_fm_all), 33 * D)
    vector = put(vector, last_stage * b_head, 35 * D)
    g_patch = first_stage * matmul_tn(d_first, tok_half)
    ends = jnp.concatenate([g_patch, last_stage * g_head], axis=1)
    ends = lax.psum_scatter(ends, "dp", scatter_dimension=0, tiled=True)
    vector = jnp.concatenate([vector, (last_stage * loss)[None]])
    vector = lax.psum(vector, ("dp", "section"))
    ends = lax.psum(ends, "section")
    bias_grad, loss_sum = vector[:NBIAS], vector[NBIAS]
    g_stem = jnp.concatenate([g_table, ends[:, :PATCH_IN], g_one, g_two], axis=1)
    g_tail = jnp.concatenate([g_fm, ends[:, PATCH_IN:]], axis=1)
    g_dn = g_dn.astype(jnp.float32)
    down_both = jnp.stack(
        [jnp.concatenate([g_dn[0], g_dn[1]], axis=1), jnp.concatenate([g_dn[2], g_dn[3]], axis=1)]
    )

    square = lambda value: jnp.sum(value * value)
    squares = square(g_mod) + square(g_blk)
    squares = squares + once * (square(down_both) + square(g_stem) + square(g_tail))
    squares = squares + corner * square(bias_grad)
    grad_norm = jnp.sqrt(lax.psum(squares, ("dp", "section")))
    factor = jnp.minimum(1.0, clip_limit / (grad_norm + 1e-06))
    mod_out = nesterov(mod_w, mod_m, mod_e, g_mod[None], factor)
    block_out = nesterov(block_w, block_m, block_e, g_blk[None], factor)
    flip = lambda value: jnp.swapaxes(value, 1, 2)
    down_out = tuple(map(flip, nesterov(downs, flip(down_m), flip(down_e), down_both, factor)))
    stem_out = tuple(value.T for value in nesterov(stems, stem_m.T, stem_e.T, g_stem, factor))
    tail_out = nesterov(tail_w, tail_m, tail_e, g_tail, factor)
    bias_out = nesterov(biases, bias_m, bias_e, bias_grad, factor)
    return (
        (loss_sum, count, grad_norm)
        + mod_out + block_out + down_out + stem_out + tail_out + bias_out
    )


def solution(mesh):
    images = (P("dp", None, None, None),) * 2 + (P("dp"),) * 4
    owned = P("section", "dp", None)
    states = (owned,) * 6 + (P(None, None, "dp"),) * 3 + (P(None, "dp"),) * 3 + (P("dp", None),) * 3 + (P(),) * 3
    updates = (owned,) * 8 + (P(None, None, "dp"),) * 4 + (P(None, "dp"),) * 4 + (P("dp", None),) * 4 + (P(),) * 4
    return jax.shard_map(
        body,
        mesh=mesh,
        in_specs=images + states,
        out_specs=(P(), P(), P()) + updates,
        check_vma=False,
    )
```

time: 3050 us -> 1050 us (0.34)
  waiting for transfers between devices: 1950 us -> 138 us
  Pallas kernels: 0 us -> 398 us
  other arithmetic: 363 us -> 98.4 us
  local copies, waits for them, and re-layouts: 306 us -> 64.4 us
  loops' own time: 72.8 us -> 0 us
  blocking collectives: 93 us -> 144 us
  starting transfers between devices: 61.6 us -> 12.7 us
    reduce_scatter x4 -> x1, waiting for transfers between devices: 693 us -> 0.03 us  [body(): ends = lax.psum_scatter(ends, 'dp', scatter_dimension=0, tiled=True)]
    all_gather x5 -> x0, waiting for transfers between devices: 415 us -> none  [the longest x1 153 us: body(): lax.all_gather(to_half(block_w[0]), 'dp', axis=0, tiled=True)]
    pallas_call x0 -> x2, Pallas kernels: none -> 398 us  [the longest x1 223 us: sum_gradients(): pl.pallas_call(sum_kernel, out_shape=(jax.ShapeDtypeStruct((144, FF), jnp...]
    unnamed x13 -> x2, waiting for transfers between devices: 348 us -> 0.03 us
    ppermute x16 -> x11, waiting for transfers between devices: 294 us -> 16.9 us  [swap(): return lax.ppermute(array, 'section', [(k, k ^ by) for k in range(peers)])]
    add x12 -> x4, other arithmetic: 163 us -> 2.13 us  [the longest x1 1.42 us: body(): d_fmods = d_fmods + swap(d_fmods, 2)]
    another operation x49 -> x3, local copies, waits for them, and re-layouts: 132 us -> 0.81 us  [the longest x2 0.71 us: body(): jnp.stack([own, sib])]
    all_gather x0 -> x4, blocking collectives: none -> 88.9 us  [the longest x1 30.7 us: body(): small = lax.all_gather(small, 'dp', axis=0, tiled=True)]
  transfers between devices with their start and end apart: 28 -> 15, of which waited for: 15 -> 6; matrix products, arithmetic and copies ran while one was open for 16% -> 12% of each run, Pallas kernels for 0% -> 17%
where the time goes in v1:
time: 1050 us; the launch traced here: 1030 us
  Pallas kernels  398 us (38%)
  matrix products  154 us (15%)
  blocking collectives  144 us (14%)
  waiting for transfers between devices  138 us (13%)
  other arithmetic  98.4 us (9%)
  local copies, waits for them, and re-layouts  64.4 us (6%)
  between operations  26.5 us (3%)
  starting transfers between devices  12.7 us (1%)
    pallas_call x1, Pallas kernels, sum_gradients(): pl.pallas_call(sum_kernel, out_shape=(jax.ShapeDtypeStruct((144, FF), jnp...  223 us
    pallas_call x1, Pallas kernels, gather_weights(): pl.pallas_call(gather_kernel, out_shape=(jax.ShapeDtypeStruct((2, D, FF),...  175 us
    psum x1, waiting for transfers between devices, body(): vector = lax.psum(vector, ('dp', 'section'))  114 us
    dot_general x16, matrix products, matmul(): return jnp.dot(left, right, preferred_element_type=jnp.float32)  61.7 us
    dot_general x17, matrix products, matmul_nt(): lax.dot_general(left, right, (((1,), (1,)), ((), ())), preferred_element_...  51.6 us
    psum x1, blocking collectives, body(): grad_norm = jnp.sqrt(lax.psum(squares, ('dp', 'section')))  42.4 us
    all_gather x1, blocking collectives, body(): small = lax.all_gather(small, 'dp', axis=0, tiled=True)  30.7 us
    all_gather x1, blocking collectives, body(): d_mods = lax.all_gather(d_mods, 'dp', axis=0, tiled=True)  30.7 us
  transfers between devices with their start and end apart: 15, of which 6 were waited for; matrix products, arithmetic and copies ran while one was open for 12% of the time, Pallas kernels for 17%

profile of v1, /device:TPU:0, one launch (start us, length us, event | category | flops | bytes accessed | tf_op | source)
XLA Modules:
  0.0 1034.8 jit_solution(4368956983641996336)
XLA Ops:
  9.8 22.2 %all-gather.1 = s32[8,2,3]{2,1,0:T(2,128)S(1)} all-gather(s32[1,2,3]{2,1,0:T(2,128)S(1)} %bitcast.378), channel_id=1, replica_groups=mesh['dp'=8,'section'=4] {'dp'}, dimensions={0}, use_global_device_ids=true | all-gather | bytes 216 | tf_op jit(solution)/shard_map/all_gather | solution.py:711
  36.3 30.7 %all-gather.2 = bf16[8,144,64]{1,2,0:T(8,128)(2,1)S(1)} all-gather(bf16[1,144,64]{1,2,0:T(8,128)(2,1)S(1)} %maximum_bitcast_fusion.2), channel_id=1, replica_groups=mesh['dp'=8,'section'=4] {'dp'}, dimensions={0}, use_global_device_ids=true | all-gather | bytes 165888 | tf_op jit(solution)/shard_map/all_gather | solution.py:730
  81.1 174.7 %gather_weights.1 = (bf16[2,1152,4608]{2,1,0:T(8,128)(2,1)}, bf16[2,1152,2304]{2,1,0:T(8,128)(2,1)}) custom-call(bf16[144,4608]{1,0:T(8,128)(2,1)} %convert_bitcast_fusion.1.blk_ref, bf16[144,2304]{1,0:T(8,128)(2,1)} %fusion.181.dn_ref), custom_call_target="tpu_custom_call" | custom-call | tf_op jit(solution)/shard_map/gather_weights/pallas_call | solution.py:294
  255.8 9.9 slice_bitcast_fusion
  271.9 7.2 fusion.38
  279.1 3.9 copy.140
  293.3 8.1 fusion.59
  314.2 7.5 collective-permute-done.1
  322.2 7.2 fusion.39
  338.1 4.1 convert_reduce_fusion.2
  342.5 10.4 %multiply_convert_fusion = (bf16[256,4608]{1,0:T(8,128)(2,1)S(1)}, f32[256,4608]{1,0:T(8,128)}) fusion(f32[4608]{0:T(1024)S(1)} %dynamic_slice.60, bf16[2,1152,4608]{2,1,0:T(8,128)(2,1)} %get-tuple-element.31, bf16[256,1152]{1,0:T(8,128)(2,1)S(1)} %get-tuple-element.90, f32[256]{0:T(256)S(1)} %fusion.266, f32[256]{0:T(256)S(1)} %broadcast_multiply_fusion.1, ...), kind=kOutput, calls=%fused_computation.77 | convolution fusion | flops 2731474944 | bytes 18314240 | tf_op jit(solution)/shard_map/dot_general | solution.py:36
  366.2 10.4 %fusion.151 = (f32[256]{0:T(256)S(1)}, f32[256,1152]{1,0:T(8,128)S(1)}) fusion(bf16[256,1152]{1,0:T(8,128)(2,1)S(1)} %get-tuple-element.90, f32[256]{0:T(256)S(1)} %broadcast_multiply_fusion.1, f32[1152]{0:T(1024)S(1)} %get-tuple-element.123, bf16[2,1152,4608]{2,1,0:T(8,128)(2,1)} %get-tuple-element.31, f32[256,4608]{1,0:T(8,128)} %get-tuple-element.148, ...), kind=kOutput, calls=%fused_computation.216 | convolution fusion | flops 2744155904 | bytes 21830144 | tf_op jit(solution)/shard_map/dot_general | solution.py:40
  402.8 5.9 multiply_reduce_fusion.13
  418.7 8.0 collective-permute-done.5
  430.5 4.5 fusion.30
  435.1 4.6 fusion.22
  439.7 4.2 convert_reduce_fusion
  444.0 8.2 fusion.152
  484.4 5.3 broadcast_select_fusion.1
  492.9 30.7 %all-gather.3 = bf16[8,2,5760]{2,1,0:T(2,128)(2,1)S(1)} all-gather(bf16[1,2,5760]{2,1,0:T(2,128)(2,1)S(1)} %maximum_bitcast_fusion.4), channel_id=1, replica_groups=mesh['dp'=8,'section'=4] {'dp'}, dimensions={0}, use_global_device_ids=true | all-gather | bytes 207360 | tf_op jit(solution)/shard_map/all_gather | solution.py:815
  525.1 5.2 all-gather.4
  537.2 6.6 all-to-all-done.1
  552.8 114.0 %all-reduce.2.cloned.1.call-done = f32[40353]{0:T(1024)} async-done(((f32[40353]{0:T(1024)}), f32[40353]{0:T(1024)}) %all-reduce.2.cloned.1.call-update) | async-done | bytes 161428 | tf_op jit(solution)/shard_map/psum | solution.py:854
  669.1 12.8 %psum.22 = f32[144,48]{1,0:T(8,128)S(1)} all-reduce(f32[144,48]{1,0:T(8,128)} %reduce-scatter.4.cloned.1.call-done), channel_id=1, replica_groups=mesh['dp'=8,'section'=4] {'section'}, use_global_device_ids=true, to_apply=%region_53.54 | all-reduce | flops 6912 | bytes 55296 | tf_op jit(solution)/shard_map/psum | solution.py:855
  688.8 5.2 fusion.2.gd_ref
  694.0 6.2 convolution_convert_fusion
  703.2 4.5 pad_maximum_fusion.g_ref
  707.8 222.9 %sum_gradients.1 = (f32[144,4608]{1,0:T(8,128)}, bf16[4,144,2304]{2,1,0:T(8,128)(2,1)}) custom-call(bf16[1152,4608]{1,0:T(8,128)(2,1)} %pad_maximum_fusion.g_ref, bf16[1152,2304]{1,0:T(8,128)(2,1)} %fusion.2.gd_ref), custom_call_target="tpu_custom_call" | custom-call | tf_op jit(solution)/shard_map/sum_gradients/pallas_call | solution.py:560
  944.2 42.4 %psum.23 = f32[]{:T(128)} all-reduce(f32[]{:T(128)S(6)} %add.554), channel_id=1, replica_groups=mesh['dp'=8,'section'=4] {'dp','section'}, use_global_device_ids=true, to_apply=%region_57.58 | all-reduce | flops 1 | bytes 8 | tf_op jit(solution)/shard_map/psum | solution.py:868
  987.3 4.0 fusion.291
  994.4 7.8 convert_bitcast_fusion
  1012.1 6.1 fusion.21
  (536 shorter events, 202.8 us)
Async XLA Ops:
  8.1 24.3 %copy-start.21 = (f32[144,2336]{1,0:T(8,128)S(1)}, f32[144,2336]{1,0:T(8,128)}, u32[]{:S(2)}) copy-start(f32[144,2336]{1,0:T(8,128)} %param.42) | copy-start | bytes 4036612
  9.7 22.6 %copy-start.45 = (bf16[144,2425]{1,0:T(8,128)(2,1)}, bf16[144,2425]{1,0:T(8,128)(2,1)S(1)}, u32[]{:S(2)}) copy-start(bf16[144,2425]{1,0:T(8,128)(2,1)S(1)} %bitcast_convert_fusion) | copy-start | bytes 2095204
  33.3 37.8 %copy-start.28 = (bf16[144,2336]{0,1:T(8,128)(2,1)}, bf16[144,2336]{0,1:T(8,128)(2,1)S(1)}, u32[]{:S(2)}) copy-start(bf16[144,2336]{0,1:T(8,128)(2,1)S(1)} %copy.137) | copy-start | bytes 2018308
  34.4 36.8 %copy-start.6 = (f32[1,144,3456]{2,1,0:T(8,128)S(1)}, f32[1,144,3456]{2,1,0:T(8,128)}, u32[]{:S(2)}) copy-start(f32[1,144,3456]{2,1,0:T(8,128)} %param.30) | copy-start | bytes 5971972
  72.4 197.8 %all-to-all-start = ((f32[8,2,5760]{2,1,0:T(2,128)}), f32[8,2,5760]{2,1,0:T(2,128)S(1)}, u32[]{:S(2)}, u32[]{:S(2)}) async-start(f32[8,2,5760]{2,1,0:T(2,128)} %reshape.400), calls=%async_computation | async-start | bytes 737280 | tf_op jit(solution)/shard_map/all_to_all | solution.py:743
  270.4 1.3 collective-permute-start
  271.9 50.3 %copy-start.75 = (f32[1152]{0:T(1024)}, f32[1152]{0:T(1024)S(1)}, u32[]{:S(2)}) copy-start(f32[1152]{0:T(1024)S(1)} %get-tuple-element.166) | copy-start | bytes 13828
  271.9 50.3 %copy-start.97 = (f32[1152]{0:T(1024)}, f32[1152]{0:T(1024)S(1)}, u32[]{:S(2)}) copy-start(f32[1152]{0:T(1024)S(1)} %get-tuple-element.167) | copy-start | bytes 13828
  271.9 70.6 %copy-start.95 = (f32[1152]{0:T(1024)}, f32[1152]{0:T(1024)S(1)}, u32[]{:S(2)}) copy-start(f32[1152]{0:T(1024)S(1)} %get-tuple-element.122) | copy-start | bytes 13828
  271.9 82.8 %copy-start.93 = (f32[1152]{0:T(1024)}, f32[1152]{0:T(1024)S(1)}, u32[]{:S(2)}) copy-start(f32[1152]{0:T(1024)S(1)} %get-tuple-element.121) | copy-start | bytes 13828
  305.8 15.8 %collective-permute-start.1 = (bf16[256,1152]{1,0:T(8,128)(2,1)}, bf16[256,1152]{1,0:T(8,128)(2,1)S(1)}, u32[]{:S(2)}, u32[]{:S(2)}) collective-permute-start(bf16[256,1152]{1,0:T(8,128)(2,1)} %fusion.110), channel_id=1, source_target_pairs={{0,2},{1,3},{2,0},{3,1},{4,6},{5,7},{6,4},{7,5},{8,10},{9,11},{10,... | collective-permute-start | bytes 1769480 | tf_op jit(solution)/shard_map/ppermute | solution.py:684
  342.2 35.5 %copy-start.81 = (f32[256]{0:T(256)}, f32[256]{0:T(256)S(1)}, u32[]{:S(2)}) copy-start(f32[256]{0:T(256)S(1)} %broadcast_multiply_fusion.1) | copy-start | bytes 3076
  342.5 35.2 %copy-start.84 = (f32[256]{0:T(256)}, f32[256]{0:T(256)S(1)}, u32[]{:S(2)}) copy-start(f32[256]{0:T(256)S(1)} %fusion.266) | copy-start | bytes 3076
  411.4 16.7 %collective-permute-start.2 = (bf16[256,1152]{1,0:T(8,128)(2,1)}, bf16[256,1152]{1,0:T(8,128)(2,1)S(1)}, u32[]{:S(2)}, u32[]{:S(2)}) collective-permute-start(bf16[256,1152]{1,0:T(8,128)(2,1)} %fusion.149), channel_id=1, source_target_pairs={{0,2},{1,3},{2,0},{3,1},{4,6},{5,7},{6,4},{7,5},{8,10},{9,11},{10,... | collective-permute-start | bytes 1769480 | tf_op jit(solution)/shard_map/ppermute | solution.py:684
  412.9 1.2 collective-permute-start.4
  412.9 272.6 %collective-permute-start.10 = (bf16[256,2304]{1,0:T(8,128)(2,1)}, bf16[256,2304]{1,0:T(8,128)(2,1)}, u32[]{:S(2)}, u32[]{:S(2)}) collective-permute-start(bf16[256,2304]{1,0:T(8,128)(2,1)} %broadcast_select_fusion.2), channel_id=1, source_target_pairs={{0,1},{1,0},{2,3},{3,2},{4,5},{5,4},{6,7},{7,6},{8,9},{9,8},{10,11... | collective-permute-start | bytes 3538952 | tf_op jit(solution)/shard_map/ppermute | solution.py:684
  414.8 11.9 %collective-permute-start.5 = (bf16[2,2304]{1,0:T(2,128)(2,1)}, bf16[2,2304]{1,0:T(2,128)(2,1)}, u32[]{:S(2)}, u32[]{:S(2)}) collective-permute-start(bf16[2,2304]{1,0:T(2,128)(2,1)} %broadcast_select_fusion.12), channel_id=1, source_target_pairs={{0,2},{1,3},{2,0},{3,1},{4,6},{5,7},{6,4},{7,5},{8,10},{9,11},{10,... | collective-permute-start | bytes 27656 | tf_op jit(solution)/shard_map/ppermute | solution.py:684
  417.5 276.5 %collective-permute-start.6 = (bf16[256,1152]{1,0:T(8,128)(2,1)}, bf16[256,1152]{1,0:T(8,128)(2,1)}, u32[]{:S(2)}, u32[]{:S(2)}) collective-permute-start(bf16[256,1152]{1,0:T(8,128)(2,1)} %get-tuple-element.103), channel_id=1, source_target_pairs={{0,1},{1,0},{2,3},{3,2},{4,5},{5,4},{6,7},{7,6},{8,9},{9,8},{10,11... | collective-permute-start | bytes 1769480 | tf_op jit(solution)/shard_map/ppermute | solution.py:684
  417.5 282.7 %collective-permute-start.8 = (bf16[256,1152]{1,0:T(8,128)(2,1)}, bf16[256,1152]{1,0:T(8,128)(2,1)}, u32[]{:S(2)}, u32[]{:S(2)}) collective-permute-start(bf16[256,1152]{1,0:T(8,128)(2,1)} %get-tuple-element.106), channel_id=1, source_target_pairs={{0,1},{1,0},{2,3},{3,2},{4,5},{5,4},{6,7},{7,6},{8,9},{9,8},{10,11... | collective-permute-start | bytes 1769480 | tf_op jit(solution)/shard_map/ppermute | solution.py:684
  481.1 204.4 %collective-permute-start.9 = (bf16[256,1152]{1,0:T(8,128)(2,1)}, bf16[256,1152]{1,0:T(8,128)(2,1)}, u32[]{:S(2)}, u32[]{:S(2)}) collective-permute-start(bf16[256,1152]{1,0:T(8,128)(2,1)} %get-tuple-element.71), channel_id=1, source_target_pairs={{0,1},{1,0},{2,3},{3,2},{4,5},{5,4},{6,7},{7,6},{8,9},{9,8},{10,11... | collective-permute-start | bytes 1769480 | tf_op jit(solution)/shard_map/ppermute | solution.py:684
  483.8 8.2 collective-permute-start.3
  484.4 39.3 %copy-start.7 = (f32[1,144,3456]{2,1,0:T(8,128)S(1)}, f32[1,144,3456]{2,1,0:T(8,128)}, u32[]{:S(2)}) copy-start(f32[1,144,3456]{2,1,0:T(8,128)} %param.30) | copy-start | bytes 5971972
  489.8 40.5 %copy-start.29 = (bf16[144,2336]{0,1:T(8,128)(2,1)S(1)}, bf16[144,2336]{0,1:T(8,128)(2,1)}, u32[]{:S(2)}) copy-start(bf16[144,2336]{0,1:T(8,128)(2,1)} %copy-done.28) | copy-start | bytes 2018308
  523.7 22.3 %copy-start.33 = (bf16[16,5760]{1,0:T(8,128)(2,1)}, bf16[16,5760]{1,0:T(8,128)(2,1)S(1)}, u32[]{:S(2)}) copy-start(bf16[16,5760]{1,0:T(8,128)(2,1)S(1)} %reshape.431) | copy-start | bytes 552964
  525.0 18.8 %copy-start.122 = (f32[144,16]{0,1:T(8,128)S(1)}, f32[144,16]{0,1:T(8,128)}, u32[]{:S(2)}) copy-start(f32[144,16]{0,1:T(8,128)} %get-tuple-element.137) | copy-start | bytes 27652
  525.0 19.1 %copy-start.135 = (f32[32]{0:T(128)S(1)}, f32[32]{0:T(128)}, u32[]{:S(2)}) copy-start(f32[32]{0:T(128)} %get-tuple-element.62) | copy-start | bytes 388
  532.7 11.1 %all-to-all-start.1 = ((f32[8,144,16]{1,2,0:T(8,128)}), f32[8,144,16]{1,2,0:T(8,128)S(1)}, u32[]{:S(2)}, u32[]{:S(2)}) async-start(f32[8,144,16]{1,2,0:T(8,128)} %copy.156), calls=%async_computation.1 | async-start | bytes 262144 | tf_op jit(solution)/shard_map/all_to_all | solution.py:826
  536.3 130.6 %all-reduce.2.cloned.1.call-start = ((), (), s32[]{:S(2)}) async-start(), calls=%async_computation.3 | async-start | bytes 327680 | tf_op jit(solution)/shard_map/psum | solution.py:854
  544.9 124.2 %reduce-scatter.4.cloned.1.call-start = ((), (), s32[]{:S(2)}) async-start(), calls=%async_computation.4 | async-start | bytes 663552 | tf_op jit(solution)/shard_map/reduce_scatter | solution.py:852
  546.0 148.0 %collective-permute-start.7 = (bf16[256,4608]{1,0:T(8,128)(2,1)}, bf16[256,4608]{1,0:T(8,128)(2,1)}, u32[]{:S(2)}, u32[]{:S(2)}) collective-permute-start(bf16[256,4608]{1,0:T(8,128)(2,1)} %get-tuple-element.99), channel_id=1, source_target_pairs={{0,1},{1,0},{2,3},{3,2},{4,5},{5,4},{6,7},{7,6},{8,9},{9,8},{10,11... | collective-permute-start | bytes 7077896 | tf_op jit(solution)/shard_map/ppermute | solution.py:684
  546.5 137.1 %copy-start.14 = (f32[144,2304]{1,0:T(8,128)}, f32[144,2304]{1,0:T(8,128)S(1)}, u32[]{:S(2)}) copy-start(f32[144,2304]{1,0:T(8,128)S(1)} %fusion.209) | copy-start | bytes 3981316
  991.3 17.4 %copy-start.23 = (f32[144,2336]{1,0:T(8,128)}, f32[144,2336]{1,0:T(8,128)S(1)}, u32[]{:S(2)}) copy-start(f32[144,2336]{1,0:T(8,128)S(1)} %get-tuple-element.50) | copy-start | bytes 4036612
  (133 other events, 669.8 us)
Sparse Core Ops, SparseCore 0:
  545.0 121.8 all-reduce.1
Sparse Core Ops, SparseCore 1:
  549.2 60.4 reduce-scatter.3

commit v2 on v1

--- a/solution.py
+++ b/solution.py
@@ -579,6 +579,96 @@
     )(g_blk, g_dn)
 
 
+def exchange_kernel(axes, modes, *refs):
+    count = len(modes)
+    ins, outs = refs[:count], refs[count : 2 * count]
+    send_sem, recv_sem, own_sem = refs[2 * count :]
+    dp, section = lax.axis_index("dp"), lax.axis_index("section")
+    n, sections = lax.axis_size("dp"), lax.axis_size("section")
+    if axes == "dp":
+        size, me, where = n, dp, lambda p: {"dp": p}
+    elif axes == "section":
+        size, me, where = sections, section, lambda p: {"section": p}
+    elif axes == "stage":
+        low = section - lax.rem(section, 2)
+        size, me = 2 * n, dp * 2 + lax.rem(section, 2)
+        where = lambda p: {"dp": p // 2, "section": low + lax.rem(p, 2)}
+    else:
+        size, me = n * sections, dp * sections + section
+        where = lambda p: {"dp": p // sections, "section": lax.rem(p, sections)}
+
+    def part(k, p):
+        if modes[k] == "all":
+            return ins[k]
+        index = {"each": p, "dp": p // 2, "core": lax.rem(p, 2)}[modes[k]]
+        return ins[k].at[index]
+
+    def copy(k, step, src, slot, p):
+        return pltpu.make_async_remote_copy(
+            src_ref=src, dst_ref=outs[k].at[slot],
+            send_sem=send_sem.at[k, step], recv_sem=recv_sem.at[k, step],
+            device_id=where(p), device_id_type=MESH,
+        )
+
+    barrier = pltpu.get_barrier_semaphore()
+
+    @pl.loop(1, size)
+    def _(step):
+        pl.semaphore_signal(barrier, 1, device_id=where(lax.rem(me + step, size)), device_id_type=MESH)
+
+    for k in range(count):
+        pltpu.make_async_copy(part(k, me), outs[k].at[me], own_sem.at[k]).start()
+    pl.semaphore_wait(barrier, size - 1)
+
+    @pl.loop(1, size)
+    def _(step):
+        p = lax.rem(me + step, size)
+        for k in range(count):
+            copy(k, step, part(k, p), me, p).start()
+
+    for k in range(count):
+        pltpu.make_async_copy(part(k, me), outs[k].at[me], own_sem.at[k]).wait()
+
+    @pl.loop(1, size)
+    def _(step):
+        p = lax.rem(me + size - step, size)
+        for k in range(count):
+            copy(k, step, part(k, p), p, p).wait_recv()
+            copy(k, step, part(k, p), p, p).wait_send()
+
+
+def exchange(ident, axes, modes, *arrays):
+    n, sections = lax.axis_size("dp"), lax.axis_size("section")
+    size = {"dp": n, "section": sections, "stage": 2 * n, "every": n * sections}[axes]
+    blocks = [a.shape if mode == "all" else a.shape[1:] for a, mode in zip(arrays, modes)]
+    count = len(arrays)
+    vmem = pl.BlockSpec(memory_space=pltpu.VMEM)
+    return pl.pallas_call(
+        partial(exchange_kernel, axes, modes),
+        out_shape=tuple(jax.ShapeDtypeStruct((size,) + b, a.dtype) for a, b in zip(arrays, blocks)),
+        in_specs=[vmem] * count,
+        out_specs=(vmem,) * count,
+        scratch_shapes=[
+            pltpu.SemaphoreType.DMA((count, size)),
+            pltpu.SemaphoreType.DMA((count, size)),
+            pltpu.SemaphoreType.DMA((count,)),
+        ],
+        compiler_params=pltpu.CompilerParams(
+            collective_id=ident, has_side_effects=True, vmem_limit_bytes=VMEM_BYTES
+        ),
+        name="exchange_" + axes,
+    )(*arrays)
+
+
+def rows_of(value, size):
+    value = value.reshape(-1)
+    return jnp.pad(value, (0, size * 128 - value.shape[0])).reshape(size, 128)
+
+
+def row_count(length, unit=8):
+    return -(-length // (128 * unit)) * unit
+
+
 def heads_of(value):
     return value.reshape(PATCHES, HEADS, HEAD_DIM)
 
@@ -708,7 +798,22 @@
 
     stems = stem_w.T
     classes_own = jnp.where(null_mask > 0, NCLS - 1, labels)
-    meta = lax.all_gather(jnp.stack([timesteps, classes_own, valid], axis=1), "dp", axis=0, tiled=True)
+    meta = jnp.stack([timesteps, classes_own, valid], axis=1)
+    images_own = meta.shape[0]
+    meta = jnp.pad(meta, ((0, 8 - images_own), (0, 125)))
+    stem_half = to_half(stems)
+    tail_half = to_half(tail_w)
+    table = stem_half[:, :NCLS]
+    w_two = stem_half[:, NCLS + PATCH_IN + FREQ :]
+    ends = NCLS, NCLS + PATCH_IN + FREQ
+    small = jnp.concatenate([stem_half[:, ends[0] : ends[1]], tail_half[:, 2 * D :]], axis=1)
+    small = jnp.pad(small, ((0, -width % 16), (0, -small.shape[1] % 128)))
+    meta, small = exchange(2, "dp", ("all", "all"), meta, small)
+    meta = meta[:, :images_own].reshape(n * images_own, 128)
+    small = small[:, :width].reshape(D, -1)
+    w_patch_all = small[:, :PATCH_IN]
+    w_one_all = small[:, PATCH_IN : PATCH_IN + FREQ]
+    w_head_all = small[:, PATCH_IN + FREQ : PATCH_IN + FREQ + HEAD_OUT]
     images = meta.shape[0]
     steps_all = meta[:, 0].astype(jnp.float32)
     picks = (meta[:, 1][:, None] == jnp.arange(NCLS, dtype=jnp.int32)[None, :]).astype(BF)
@@ -716,21 +821,9 @@
     loss_scale = 1.0 / (count * PATCHES * HEAD_OUT)
     freq = to_half(time_features(steps_all))
 
-    stem_half = to_half(stems)
-    table = stem_half[:, :NCLS]
-    w_patch = stem_half[:, NCLS : NCLS + PATCH_IN]
-    w_one = stem_half[:, NCLS + PATCH_IN : NCLS + PATCH_IN + FREQ]
-    w_two = stem_half[:, NCLS + PATCH_IN + FREQ :]
-    b_one = lax.dynamic_slice_in_dim(biases, 31 * D + place * width, width)
     b_two = lax.dynamic_slice_in_dim(biases, 32 * D + place * width, width)
-    hidden_pre = matmul_nt(w_one, freq) + b_one[:, None]
-    hidden = to_half(jax.nn.silu(hidden_pre))
-    tail_half = to_half(tail_w)
-    small = jnp.concatenate([hidden, w_patch, tail_half[:, 2 * D :]], axis=1)
-    small = lax.all_gather(small, "dp", axis=0, tiled=True)
-    hidden_all = small[:, :images]
-    w_patch_all = small[:, images : images + PATCH_IN]
-    w_head_all = small[:, images + PATCH_IN :]
+    hidden_pre = matmul_nt(w_one_all, freq) + biases[31 * D : 32 * D, None]
+    hidden_all = to_half(jax.nn.silu(hidden_pre))
     cond = matmul(w_two, hidden_all) + b_two[:, None] + matmul_nt(table, picks)
     cond_low = to_half(cond).astype(jnp.float32)
     cond_own = jnp.where(section == 0, cond, cond_low)
@@ -739,16 +832,13 @@
     mod_half_w = to_half(mod_w[0])
     part_mod = matmul_tn(silu_own, mod_half_w)
     part_fm = matmul_tn(silu_low, tail_half[:, : 2 * D])
-    parts = jnp.concatenate([part_mod, part_fm], axis=1).reshape(n, images // n, 5 * D)
-    mods = jnp.sum(lax.all_to_all(parts, "dp", 0, 0), axis=0)
-    own_mod = mods[:, : 3 * D]
-    sib_mod = swap(own_mod, 1)
-    mod_a = pick(jnp.where(even, own_mod, sib_mod), core)
-    mod_b = pick(jnp.where(even, sib_mod, own_mod), core)
+    parts = jnp.concatenate([part_mod, part_fm, jnp.zeros((images, 384), jnp.float32)], axis=1)
+    (mods,) = exchange(3, "stage", ("each",), parts.reshape(images, 48, 128))
+    mods = jnp.sum(mods.reshape(n, 2, 48 * 128), axis=0)
     bias_of = lambda first, length: lax.dynamic_slice_in_dim(biases, first, length)
-    mod_a = mod_a + bias_of(6 * D * stage, 3 * D)
-    mod_b = mod_b + bias_of(6 * D * stage + 3 * D, 3 * D)
-    fmod = pick(mods[:, 3 * D :], core) + biases[33 * D : 35 * D]
+    mod_a = mods[0, : 3 * D] + bias_of(6 * D * stage, 3 * D)
+    mod_b = mods[1, : 3 * D] + bias_of(6 * D * stage + 3 * D, 3 * D)
+    fmod = mods[0, 3 * D : 5 * D] + biases[33 * D : 35 * D]
     weights = (
         mod_a, mod_b, w_blk, w_dn,
         bias_of(12 * D + 8 * D * stage, 4 * D),
@@ -803,69 +893,90 @@
     g_blk, g_dn = sum_gradients(g_blk, g_dn)
 
     last_stage = (stage == 1).astype(jnp.float32)
-    first_stage = (stage == 0).astype(jnp.float32)
-    d_mod_sib = swap(jnp.where(even, d_mod_b, d_mod_a), 1)
-    d_mod_own = jnp.where(even, d_mod_a, d_mod_b)
-    d_fmod = jnp.where(stage == 1, d_fmod, jnp.zeros_like(d_fmod))
-    d_fmod_sib = swap(d_fmod, 1)
-    pair = lambda own, sib: jnp.where(even, jnp.stack([own, sib]), jnp.stack([sib, own]))
-    d_fmods = pair(d_fmod, d_fmod_sib)
-    d_fmods = d_fmods + swap(d_fmods, 2)
-    d_mods = jnp.concatenate([pair(d_mod_own, d_mod_sib), d_fmods], axis=1)
-    d_mods = lax.all_gather(d_mods, "dp", axis=0, tiled=True)
-    d_mod_all, d_fm_all = d_mods[:, : 3 * D], d_mods[:, 3 * D :]
+    zeros_fm = jnp.zeros((2 * D + 384,), BF)
+    d_fmod = jnp.concatenate([jnp.where(stage == 1, d_fmod, zeros_fm[: 2 * D]), zeros_fm[2 * D :]])
+    d_mods = jnp.stack([jnp.concatenate([d_mod_a, d_fmod]), jnp.concatenate([d_mod_b, d_fmod])])
+    last_own = jnp.where(stage == 0, column_sums(d_first), jnp.pad(b_head, (0, D - HEAD_OUT)))
+    own_biases = jnp.concatenate(
+        [
+            column_sums(d_qkv), column_sums(d_branch_a), column_sums(d_pre), column_sums(d_branch_b),
+            last_own, loss[None],
+        ]
+    )
+    piece = row_count(-(-own_biases.shape[0] // (2 * n)))
+    own_biases = rows_of(own_biases, 2 * n * piece).reshape(2 * n, piece, 128)
+    g_patch = jnp.pad(matmul_tn(d_first, tok_half), ((0, 0), (0, HEAD_OUT - PATCH_IN)))
+    end_rows = row_count(width * HEAD_OUT)
+    own_ends = jnp.where(stage == 0, g_patch, g_head).reshape(n, width * HEAD_OUT)
+    own_ends = jnp.pad(own_ends, ((0, 0), (0, end_rows * 128 - width * HEAD_OUT))).reshape(n, end_rows, 128)
+    d_mods, own_biases, own_ends = exchange(
+        4, "stage", ("core", "each", "dp"), d_mods.reshape(2, 48, 128), own_biases, own_ends
+    )
+    d_mods = d_mods.reshape(images, 48 * 128)
+    bias_piece = jnp.sum(own_biases, axis=0)
+    own_ends = jnp.sum(own_ends, axis=0)
+    d_mod_all, d_fm_all = d_mods[:, : 3 * D], d_mods[:, 3 * D : 5 * D]
     g_mod = matmul(silu_own, d_mod_all)
+    c_own = matmul_nt(mod_half_w, d_mod_all)
+    c_own = c_own + matmul_nt(tail_half[:, : 2 * D], jnp.where(section == 3, d_fm_all, jnp.zeros_like(d_fm_all)))
+    c_own = silu_back(cond_own, c_own)
+    cond_rows = row_count(width * images)
+    c_all, end_pair, d_fm_all = exchange(
+        5, "section", ("all", "all", "all"), rows_of(c_own, cond_rows), own_ends, d_fm_all
+    )
+    d_fm_all = d_fm_all[3]
+    ends = [end_pair[k].reshape(-1)[: width * HEAD_OUT].reshape(width, HEAD_OUT) for k in (0, 3)]
     g_fm = matmul(silu_low, d_fm_all)
-    c_own = silu_back(cond_own, matmul_nt(mod_half_w, d_mod_all))
-    c_fm = silu_back(cond_low, matmul_nt(tail_half[:, : 2 * D], d_fm_all))
-    c_all = lax.all_gather(c_own, "section")
-    d_cond = to_half(c_all[3] + c_fm)
+    c_all = [c_all[k].reshape(-1)[: width * images].reshape(width, images) for k in range(4)]
+    d_cond = to_half(c_all[3])
     for slot in (2, 1, 0):
         d_cond = to_half(d_cond.astype(jnp.float32) + c_all[slot])
-    part_hidden = matmul_tn(w_two, d_cond).reshape(n, width, images)
-    d_hidden = jnp.sum(lax.all_to_all(part_hidden, "dp", 0, 0), axis=0)
-    d_pre_one = to_half(silu_back(hidden_pre, d_hidden))
+    part_hidden = matmul_tn(w_two, d_cond).reshape(n, width * images)
+    part_hidden = jnp.pad(part_hidden, ((0, 0), (0, cond_rows * 128 - width * images)))
+    (d_hidden,) = exchange(6, "dp", ("each",), part_hidden.reshape(n, cond_rows, 128))
+    d_hidden = jnp.sum(d_hidden, axis=0).reshape(-1)[: width * images].reshape(width, images)
+    pre_own = lax.dynamic_slice_in_dim(hidden_pre, place * width, width)
+    d_pre_one = to_half(silu_back(pre_own, d_hidden))
     g_table = matmul(d_cond, picks)
     g_one = matmul(d_pre_one, freq)
     g_two = matmul_nt(d_cond, hidden_all)
-
-    row_sums = lambda value: jnp.sum(value.astype(jnp.float32), axis=1)
-    anchor = (place == 0).astype(jnp.float32)
-    corner = anchor * (section == 0).astype(jnp.float32)
-    once = (section == 0).astype(jnp.float32)
-    vector = jnp.zeros((NBIAS,), jnp.float32)
-    put = lambda vector, piece, start: lax.dynamic_update_slice_in_dim(vector, piece, start, 0)
-    vector = put(vector, anchor * column_sums(d_mod_all), 3 * D * section)
-    vector = put(
-        vector,
-        jnp.concatenate([column_sums(d_qkv), column_sums(d_branch_a), column_sums(d_pre)]),
-        12 * D + 8 * D * stage,
-    )
-    vector = put(vector, column_sums(d_branch_b), 28 * D + D * stage)
-    vector = put(vector, first_stage * column_sums(d_first), 30 * D)
-    vector = put(vector, once * row_sums(d_pre_one), 31 * D + place * width)
-    vector = put(vector, once * row_sums(d_cond), 32 * D + place * width)
-    vector = put(vector, corner * column_sums(d_fm_all), 33 * D)
-    vector = put(vector, last_stage * b_head, 35 * D)
-    g_patch = first_stage * matmul_tn(d_first, tok_half)
-    ends = jnp.concatenate([g_patch, last_stage * g_head], axis=1)
-    ends = lax.psum_scatter(ends, "dp", scatter_dimension=0, tiled=True)
-    vector = jnp.concatenate([vector, (last_stage * loss)[None]])
-    vector = lax.psum(vector, ("dp", "section"))
-    ends = lax.psum(ends, "section")
-    bias_grad, loss_sum = vector[:NBIAS], vector[NBIAS]
-    g_stem = jnp.concatenate([g_table, ends[:, :PATCH_IN], g_one, g_two], axis=1)
-    g_tail = jnp.concatenate([g_fm, ends[:, PATCH_IN:]], axis=1)
+    g_stem = jnp.concatenate([g_table, ends[0][:, :PATCH_IN], g_one, g_two], axis=1)
+    g_tail = jnp.concatenate([g_fm, ends[1]], axis=1)
     g_dn = g_dn.astype(jnp.float32)
     down_both = jnp.stack(
         [jnp.concatenate([g_dn[0], g_dn[1]], axis=1), jnp.concatenate([g_dn[2], g_dn[3]], axis=1)]
     )
 
     square = lambda value: jnp.sum(value * value)
+    once = (section == 0).astype(jnp.float32)
     squares = square(g_mod) + square(g_blk)
     squares = squares + once * (square(down_both) + square(g_stem) + square(g_tail))
-    squares = squares + corner * square(bias_grad)
-    grad_norm = jnp.sqrt(lax.psum(squares, ("dp", "section")))
+    row_sums = lambda value: jnp.sum(value.astype(jnp.float32), axis=1)
+    mod_piece = 3 * D // n
+    mod_rows, slice_rows = row_count(mod_piece, 1), row_count(2 * width, 1)
+    bias_mod = lax.dynamic_slice_in_dim(column_sums(d_mod_all), place * mod_piece, mod_piece)
+    slices = jnp.concatenate([row_sums(d_pre_one), row_sums(d_cond)])
+    news = jnp.concatenate(
+        [bias_piece, rows_of(bias_mod, mod_rows), rows_of(slices, slice_rows), rows_of(squares[None], 1)]
+    )
+    news = jnp.pad(news, ((0, -news.shape[0] % 8), (0, 0)))
+    (news,) = exchange(7, "every", ("all",), news)
+    news = news.reshape(n, 4, -1, 128)
+    first, second = piece + mod_rows, piece + mod_rows + slice_rows
+    stages = [news[:, 2 * k : 2 * k + 2, :piece].reshape(-1) for k in range(2)]
+    bias_mods = news[:, :, piece:first].reshape(n, 4, mod_rows * 128)[:, :, :mod_piece]
+    bias_mods = bias_mods.transpose(1, 0, 2).reshape(-1)
+    slices = news[:, 0, first:second].reshape(n, slice_rows * 128)[:, : 2 * width]
+    bias_grad = jnp.concatenate(
+        [bias_mods]
+        + [part[: 8 * D] for part in stages]
+        + [part[8 * D : 9 * D] for part in stages]
+        + [stages[0][9 * D : 10 * D]]
+        + [slices[:, :width].reshape(-1), slices[:, width:].reshape(-1)]
+        + [column_sums(d_fm_all), stages[1][9 * D : 9 * D + HEAD_OUT]]
+    )
+    loss_sum = stages[1][10 * D]
+    grad_norm = jnp.sqrt(jnp.sum(news[:, :, second, 0]) + square(bias_grad))
     factor = jnp.minimum(1.0, clip_limit / (grad_norm + 1e-06))
     mod_out = nesterov(mod_w, mod_m, mod_e, g_mod[None], factor)
     block_out = nesterov(block_w, block_m, block_e, g_blk[None], factor)

time: 1050 us -> 870 us (0.83)
  blocking collectives: 144 us -> 0 us
  waiting for transfers between devices: 138 us -> 14.6 us
  Pallas kernels: 398 us -> 490 us
  local copies, waits for them, and re-layouts: 64.4 us -> 79.6 us
  between operations: 26.5 us -> 11.5 us
    psum x1 -> x0, waiting for transfers between devices: 114 us -> none  [body(): vector = lax.psum(vector, ('dp', 'section'))]
    pallas_call x0 -> x6, Pallas kernels: none -> 89.1 us  [exchange(): pl.pallas_call(partial(exchange_kernel, axes, modes), out_shape=tuple((ja...]
    all_gather x4 -> x0, blocking collectives: 88.9 us -> none  [the longest x1 30.7 us: body(): small = lax.all_gather(small, 'dp', axis=0, tiled=True)]
    psum x2 -> x0, blocking collectives: 55.2 us -> none  [the longest x1 42.4 us: body(): grad_norm = jnp.sqrt(lax.psum(squares, ('dp', 'section')))]
    unnamed x307 -> x326, local copies, waits for them, and re-layouts: 18.1 us -> 25.5 us
  transfers between devices with their start and end apart: 15 -> 7, of which waited for: 6 -> 2; matrix products, arithmetic and copies ran while one was open for 12% -> 12% of each run, Pallas kernels for 17% -> 4%
where the time goes in v2:
time: 870 us; the launch traced here: 859 us
  Pallas kernels  490 us (56%)
  matrix products  153 us (18%)
  other arithmetic  106 us (12%)
  local copies, waits for them, and re-layouts  79.6 us (9%)
  waiting for transfers between devices  14.6 us (2%)
  between operations  11.5 us (1%)
    pallas_call x1, Pallas kernels, sum_gradients(): pl.pallas_call(sum_kernel, out_shape=(jax.ShapeDtypeStruct((144, FF), jnp...  224 us
    pallas_call x1, Pallas kernels, gather_weights(): pl.pallas_call(gather_kernel, out_shape=(jax.ShapeDtypeStruct((2, D, FF),...  177 us
    pallas_call x6, Pallas kernels, exchange(): pl.pallas_call(partial(exchange_kernel, axes, modes), out_shape=tuple((ja...  89.1 us
    dot_general x16, matrix products, matmul(): return jnp.dot(left, right, preferred_element_type=jnp.float32)  60 us
    dot_general x17, matrix products, matmul_nt(): lax.dot_general(left, right, (((1,), (1,)), ((), ())), preferred_element_...  55.1 us
    unnamed x326, local copies, waits for them, and re-layouts  25.5 us
    dot_general x9, matrix products, matmul_tn(): lax.dot_general(left, right, (((0,), (0,)), ((), ())), preferred_element_...  19.7 us
  transfers between devices with their start and end apart: 7, of which 2 were waited for; matrix products, arithmetic and copies ran while one was open for 12% of the time, Pallas kernels for 4%

profile of v2, /device:TPU:0, one launch (start us, length us, event | category | flops | bytes accessed | tf_op | source)
XLA Modules:
  0.0 858.9 jit_solution(393094252838237621)
XLA Ops:
  12.2 22.9 %exchange_dp.2 = (s32[8,8,128]{2,1,0:T(8,128)}, bf16[8,144,384]{2,1,0:T(8,128)(2,1)}) custom-call(s32[8,128]{1,0:T(8,128)} %pad.44.refs_0_, bf16[144,384]{1,0:T(8,128)(2,1)} %fusion.209.refs_1_), custom_call_target="tpu_custom_call" | custom-call | tf_op jit(solution)/shard_map/exchange_dp/pallas_call | solution.py:646
  45.5 18.2 %exchange_stage.2 = f32[16,48,128]{2,1,0:T(8,128)} custom-call(f32[16,48,128]{2,1,0:T(8,128)} %bitcast.362), custom_call_target="tpu_custom_call" | custom-call | tf_op jit(solution)/shard_map/exchange_stage/pallas_call | solution.py:646
  68.5 177.4 %gather_weights.1 = (bf16[2,1152,4608]{2,1,0:T(8,128)(2,1)}, bf16[2,1152,2304]{2,1,0:T(8,128)(2,1)}) custom-call(bf16[144,4608]{1,0:T(8,128)(2,1)} %convert_bitcast_fusion.1.blk_ref, bf16[144,2304]{1,0:T(8,128)(2,1)} %fusion.179.dn_ref), custom_call_target="tpu_custom_call" | custom-call | tf_op jit(solution)/shard_map/gather_weights/pallas_call | solution.py:294
  246.0 9.9 %slice_bitcast_fusion = bf16[1152,4608]{1,0:T(8,128)(2,1)} fusion(bf16[2,1152,4608]{2,1,0:T(8,128)(2,1)} %get-tuple-element.41), kind=kLoop, calls=%fused_computation.14 | loop fusion | bytes 21233664 | tf_op jit(solution)/shard_map/squeeze | solution.py:721
  261.1 7.2 fusion.38
  268.3 3.9 copy.85
  282.6 8.0 fusion.59
  290.6 4.2 fusion.28
  294.9 5.1 fusion.110
  307.7 8.1 collective-permute-done
  316.4 7.2 fusion.39
  332.3 4.1 convert_reduce_fusion.2
  336.8 10.4 %multiply_convert_fusion = (bf16[256,4608]{1,0:T(8,128)(2,1)S(1)}, f32[256,4608]{1,0:T(8,128)}) fusion(f32[4608]{0:T(1024)S(1)} %dynamic_slice.49, bf16[2,1152,4608]{2,1,0:T(8,128)(2,1)} %get-tuple-element.41, bf16[256,1152]{1,0:T(8,128)(2,1)S(1)} %get-tuple-element.106, f32[256]{0:T(256)S(1)} %fusion.243, f32[256]{0:T(256)S(1)} %broadcast_multiply_fusion.1, ...), kind=kOutput, calls=%fused_computation.77 | convolution fusion | flops 2731474944 | bytes 18314240 | tf_op jit(solution)/shard_map/dot_general | solution.py:36
  361.1 10.4 %fusion.151 = (f32[256]{0:T(256)S(1)}, f32[256,1152]{1,0:T(8,128)S(1)}) fusion(bf16[256,1152]{1,0:T(8,128)(2,1)S(1)} %get-tuple-element.106, f32[256]{0:T(256)S(1)} %broadcast_multiply_fusion.1, f32[1152]{0:T(1024)S(1)} %copy-done.72, bf16[2,1152,4608]{2,1,0:T(8,128)(2,1)} %get-tuple-element.41, f32[256,4608]{1,0:T(8,128)} %get-tuple-element.166, ...), kind=kOutput, calls=%fused_computation.216 | convolution fusion | flops 2744155904 | bytes 21830144 | tf_op jit(solution)/shard_map/dot_general | solution.py:40
  393.2 5.9 multiply_reduce_fusion.13
  410.3 6.5 collective-permute-done.1
  419.6 4.5 fusion.30
  424.1 4.6 fusion.22
  428.8 4.2 convert_reduce_fusion
  433.0 8.2 fusion.152
  474.0 15.6 %exchange_stage.3 = (bf16[16,48,128]{2,1,0:T(8,128)(2,1)}, f32[16,8,128]{2,1,0:T(8,128)}, f32[16,40,128]{2,1,0:T(8,128)}) custom-call(bf16[2,48,128]{2,1,0:T(8,128)(2,1)} %pad_maximum_fusion.11.refs_0_, f32[16,8,128]{2,1,0:T(8,128)} %pad_bitcast_fusion.2.refs_1_, f32[8,40,128]{2,1,0:T(8,128)} %bitcast.372), custom_call_target="tpu_custom_call" | custom-call | tf_op jit(solution)/shard_map/exchange_stage/pallas_call | solution.py:646
  493.4 8.8 %exchange_section.1 = (f32[4,24,128]{2,1,0:T(8,128)}, f32[4,40,128]{2,1,0:T(8,128)}, bf16[4,16,2304]{2,1,0:T(8,128)(2,1)}) custom-call(f32[24,128]{1,0:T(8,128)} %pad_bitcast_fusion.3.refs_0_, f32[40,128]{1,0:T(8,128)} %reduce_sum.621.refs_1_, bf16[16,2304]{1,0:T(8,128)(2,1)} %slice.420.refs_2_), custom_call_target="tpu_custom_call" | custom-call | tf_op jit(solution)/shard_map/exchange_section/pallas_call | solution.py:646
  511.8 11.3 %exchange_dp.3 = f32[8,24,128]{2,1,0:T(8,128)} custom-call(f32[8,24,128]{2,1,0:T(8,128)} %bitcast.378), custom_call_target="tpu_custom_call" | custom-call | tf_op jit(solution)/shard_map/exchange_dp/pallas_call | solution.py:646
  526.4 4.6 broadcast_select_fusion.1
  541.9 5.2 fusion.2.gd_ref
  547.1 6.2 convolution_convert_fusion
  556.3 4.6 pad_maximum_fusion.g_ref
  560.9 223.8 %sum_gradients.1 = (f32[144,4608]{1,0:T(8,128)}, bf16[4,144,2304]{2,1,0:T(8,128)(2,1)}) custom-call(bf16[1152,4608]{1,0:T(8,128)(2,1)} %pad_maximum_fusion.g_ref, bf16[1152,2304]{1,0:T(8,128)(2,1)} %fusion.2.gd_ref), custom_call_target="tpu_custom_call" | custom-call | tf_op jit(solution)/shard_map/sum_gradients/pallas_call | solution.py:560
  798.3 12.3 %exchange_every.1 = f32[32,16,128]{2,1,0:T(8,128)} custom-call(f32[16,128]{1,0:T(8,128)} %pad_maximum_fusion.13.refs_0_), custom_call_target="tpu_custom_call" | custom-call | tf_op jit(solution)/shard_map/exchange_every/pallas_call | solution.py:646
  819.5 4.0 fusion.271
  826.6 7.8 convert_bitcast_fusion
  843.7 6.1 fusion.21
  (553 shorter events, 206.2 us)
Async XLA Ops:
  3.3 39.9 %copy-start.45 = (bf16[144,2425]{1,0:T(8,128)(2,1)}, bf16[144,2425]{1,0:T(8,128)(2,1)S(1)}, u32[]{:S(2)}) copy-start(bf16[144,2425]{1,0:T(8,128)(2,1)S(1)} %bitcast_convert_fusion) | copy-start | bytes 2095204
  3.3 36.5 %copy-start.57 = (f32[40352]{0:T(1024)S(1)}, f32[40352]{0:T(1024)}, u32[]{:S(2)}) copy-start(f32[40352]{0:T(1024)} %param.45) | copy-start | bytes 484228
  4.1 40.4 %copy-start.32 = (bf16[144,2336]{1,0:T(8,128)(2,1)}, bf16[144,2336]{1,0:T(8,128)(2,1)S(1)}, u32[]{:S(2)}) copy-start(bf16[144,2336]{1,0:T(8,128)(2,1)S(1)} %convert_element_type.354) | copy-start | bytes 2018308
  4.1 40.1 %copy-start.6 = (f32[1,144,3456]{2,1,0:T(8,128)S(1)}, f32[1,144,3456]{2,1,0:T(8,128)}, u32[]{:S(2)}) copy-start(f32[1,144,3456]{2,1,0:T(8,128)} %param.30) | copy-start | bytes 5971972
  44.5 20.5 %copy-start.15 = (f32[1,144,4608]{2,1,0:T(8,128)S(1)}, f32[1,144,4608]{2,1,0:T(8,128)}, u32[]{:S(2)}) copy-start(f32[1,144,4608]{2,1,0:T(8,128)} %param.33) | copy-start | bytes 7962628
  261.0 55.3 %copy-start.81 = (f32[1152]{0:T(1024)}, f32[1152]{0:T(1024)S(1)}, u32[]{:S(2)}) copy-start(f32[1152]{0:T(1024)S(1)} %get-tuple-element.182) | copy-start | bytes 13828
  261.1 55.3 %copy-start.99 = (f32[1152]{0:T(1024)}, f32[1152]{0:T(1024)S(1)}, u32[]{:S(2)}) copy-start(f32[1152]{0:T(1024)S(1)} %get-tuple-element.183) | copy-start | bytes 13828
  261.1 71.2 %copy-start.60 = (f32[1152]{0:T(1024)}, f32[1152]{0:T(1024)S(1)}, u32[]{:S(2)}) copy-start(f32[1152]{0:T(1024)S(1)} %get-tuple-element.184) | copy-start | bytes 13828
  261.1 75.6 %copy-start.71 = (f32[1152]{0:T(1024)}, f32[1152]{0:T(1024)S(1)}, u32[]{:S(2)}) copy-start(f32[1152]{0:T(1024)S(1)} %get-tuple-element.142) | copy-start | bytes 13828
  261.1 75.6 %copy-start.97 = (f32[1152]{0:T(1024)}, f32[1152]{0:T(1024)S(1)}, u32[]{:S(2)}) copy-start(f32[1152]{0:T(1024)S(1)} %get-tuple-element.141) | copy-start | bytes 13828
  261.1 87.8 %copy-start.94 = (f32[1152]{0:T(1024)}, f32[1152]{0:T(1024)S(1)}, u32[]{:S(2)}) copy-start(f32[1152]{0:T(1024)S(1)} %get-tuple-element.140) | copy-start | bytes 13828
  300.0 15.8 %collective-permute-start = (bf16[256,1152]{1,0:T(8,128)(2,1)}, bf16[256,1152]{1,0:T(8,128)(2,1)S(1)}, u32[]{:S(2)}, u32[]{:S(2)}) collective-permute-start(bf16[256,1152]{1,0:T(8,128)(2,1)} %fusion.110), channel_id=1, source_target_pairs={{0,2},{1,3},{2,0},{3,1},{4,6},{5,7},{6,4},{7,5},{8,10},{9,11},{10,... | collective-permute-start | bytes 1769480 | tf_op jit(solution)/shard_map/ppermute | solution.py:774
  332.3 14.9 %slice-start.5 = ((s8[10616832]{0:T(1024)(128)(4,1)}), s8[4194304]{0:T(1024)(128)(4,1)S(1)}, s32[]{:S(2)}) async-start(s8[10616832]{0:T(1024)(128)(4,1)} %bitcast.398), calls=%async_computation.5 | async-start | bytes 8388608
  336.4 36.1 %copy-start.89 = (f32[256]{0:T(256)}, f32[256]{0:T(256)S(1)}, u32[]{:S(2)}) copy-start(f32[256]{0:T(256)S(1)} %broadcast_multiply_fusion.1) | copy-start | bytes 3076
  336.7 35.8 %copy-start.92 = (f32[256]{0:T(256)}, f32[256]{0:T(256)S(1)}, u32[]{:S(2)}) copy-start(f32[256]{0:T(256)S(1)} %fusion.243) | copy-start | bytes 3076
  355.9 16.6 %copy-start.110 = (f32[256]{0:T(256)}, f32[256]{0:T(256)S(1)}, u32[]{:S(2)}) copy-start(f32[256]{0:T(256)S(1)} %negate_multiply_fusion.4) | copy-start | bytes 3076
  401.7 15.1 %collective-permute-start.1 = (bf16[256,1152]{1,0:T(8,128)(2,1)}, bf16[256,1152]{1,0:T(8,128)(2,1)}, u32[]{:S(2)}, u32[]{:S(2)}) collective-permute-start(bf16[256,1152]{1,0:T(8,128)(2,1)} %fusion.149), channel_id=1, source_target_pairs={{0,2},{1,3},{2,0},{3,1},{4,6},{5,7},{6,4},{7,5},{8,10},{9,11},{10,... | collective-permute-start | bytes 1769480 | tf_op jit(solution)/shard_map/ppermute | solution.py:774
  406.8 131.8 %collective-permute-start.6 = (bf16[256,2304]{1,0:T(8,128)(2,1)}, bf16[256,2304]{1,0:T(8,128)(2,1)}, u32[]{:S(2)}, u32[]{:S(2)}) collective-permute-start(bf16[256,2304]{1,0:T(8,128)(2,1)} %broadcast_select_fusion.2), channel_id=1, source_target_pairs={{0,1},{1,0},{2,3},{3,2},{4,5},{5,4},{6,7},{7,6},{8,9},{9,8},{10,11... | collective-permute-start | bytes 3538952 | tf_op jit(solution)/shard_map/ppermute | solution.py:774
  409.2 137.9 %collective-permute-start.2 = (bf16[256,1152]{1,0:T(8,128)(2,1)}, bf16[256,1152]{1,0:T(8,128)(2,1)}, u32[]{:S(2)}, u32[]{:S(2)}) collective-permute-start(bf16[256,1152]{1,0:T(8,128)(2,1)} %get-tuple-element.119), channel_id=1, source_target_pairs={{0,1},{1,0},{2,3},{3,2},{4,5},{5,4},{6,7},{7,6},{8,9},{9,8},{10,11... | collective-permute-start | bytes 1769480 | tf_op jit(solution)/shard_map/ppermute | solution.py:774
  409.6 143.7 %collective-permute-start.4 = (bf16[256,1152]{1,0:T(8,128)(2,1)}, bf16[256,1152]{1,0:T(8,128)(2,1)}, u32[]{:S(2)}, u32[]{:S(2)}) collective-permute-start(bf16[256,1152]{1,0:T(8,128)(2,1)} %get-tuple-element.122), channel_id=1, source_target_pairs={{0,1},{1,0},{2,3},{3,2},{4,5},{5,4},{6,7},{7,6},{8,9},{9,8},{10,11... | collective-permute-start | bytes 1769480 | tf_op jit(solution)/shard_map/ppermute | solution.py:774
  467.7 22.9 %copy-start.7 = (f32[1,144,3456]{2,1,0:T(8,128)S(1)}, f32[1,144,3456]{2,1,0:T(8,128)}, u32[]{:S(2)}) copy-start(f32[1,144,3456]{2,1,0:T(8,128)} %param.30) | copy-start | bytes 5971972
  469.3 22.4 %copy-start.33 = (bf16[144,2336]{1,0:T(8,128)(2,1)S(1)}, bf16[144,2336]{1,0:T(8,128)(2,1)}, u32[]{:S(2)}) copy-start(bf16[144,2336]{1,0:T(8,128)(2,1)} %copy-done.32) | copy-start | bytes 2018308
  469.3 22.4 %copy-start.63 = (f32[144,16]{0,1:T(8,128)S(1)}, f32[144,16]{0,1:T(8,128)}, u32[]{:S(2)}) copy-start(f32[144,16]{0,1:T(8,128)} %copy-done.62) | copy-start | bytes 27652
  491.7 14.8 %copy-start.24 = (bf16[256,3,16,72]{0,3,2,1:T(8,128)(2,1)S(1)}, bf16[256,3,16,72]{0,3,2,1:T(8,128)(2,1)}, u32[]{:S(2)}) copy-start(bf16[256,3,16,72]{0,3,2,1:T(8,128)(2,1)} %copy-done.23) | copy-start | bytes 5308420
  505.7 32.9 %collective-permute-start.5 = (bf16[256,1152]{1,0:T(8,128)(2,1)}, bf16[256,1152]{1,0:T(8,128)(2,1)}, u32[]{:S(2)}, u32[]{:S(2)}) collective-permute-start(bf16[256,1152]{1,0:T(8,128)(2,1)} %get-tuple-element.87), channel_id=1, source_target_pairs={{0,1},{1,0},{2,3},{3,2},{4,5},{5,4},{6,7},{7,6},{8,9},{9,8},{10,11... | collective-permute-start | bytes 1769480 | tf_op jit(solution)/shard_map/ppermute | solution.py:774
  508.7 16.9 %copy-start.118 = (bf16[16,128]{1,0:T(8,128)(2,1)S(1)}, bf16[16,128]{1,0:T(8,128)(2,1)}, u32[]{:S(2)}) copy-start(bf16[16,128]{1,0:T(8,128)(2,1)} %copy-done.117) | copy-start | bytes 12292
  508.7 17.8 %copy-start.20 = (bf16[256,4608]{1,0:T(8,128)(2,1)S(1)}, bf16[256,4608]{1,0:T(8,128)(2,1)}, u32[]{:S(2)}) copy-start(bf16[256,4608]{1,0:T(8,128)(2,1)} %copy-done.19) | copy-start | bytes 7077892
  531.1 16.0 %collective-permute-start.3 = (bf16[256,4608]{1,0:T(8,128)(2,1)}, bf16[256,4608]{1,0:T(8,128)(2,1)}, u32[]{:S(2)}, u32[]{:S(2)}) collective-permute-start(bf16[256,4608]{1,0:T(8,128)(2,1)} %get-tuple-element.115), channel_id=1, source_target_pairs={{0,1},{1,0},{2,3},{3,2},{4,5},{5,4},{6,7},{7,6},{8,9},{9,8},{10,11... | collective-permute-start | bytes 7077896 | tf_op jit(solution)/shard_map/ppermute | solution.py:774
  793.3 22.2 %copy-start.51 = (f32[40352]{0:T(1024)S(1)}, f32[40352]{0:T(1024)}, u32[]{:S(2)}) copy-start(f32[40352]{0:T(1024)} %custom-call) | copy-start | bytes 484228
  793.3 24.6 %copy-start.58 = (f32[40352]{0:T(1024)S(1)}, f32[40352]{0:T(1024)}, u32[]{:S(2)}) copy-start(f32[40352]{0:T(1024)} %param.45) | copy-start | bytes 484228
  819.5 19.4 %copy-start.52 = (f32[40352]{0:T(1024)}, f32[40352]{0:T(1024)S(1)}, u32[]{:S(2)}) copy-start(f32[40352]{0:T(1024)S(1)} %get-tuple-element.63) | copy-start | bytes 484228
  823.5 16.5 %copy-start.27 = (f32[144,2336]{1,0:T(8,128)}, f32[144,2336]{1,0:T(8,128)S(1)}, u32[]{:S(2)}) copy-start(f32[144,2336]{1,0:T(8,128)S(1)} %get-tuple-element.66) | copy-start | bytes 4036612
  (123 other events, 511.7 us)

commit v3 on v2

--- a/solution.py
+++ b/solution.py
@@ -103,22 +103,21 @@
 
 
 Z, X = 4, 2
-PART = 48
-GATHER_CHUNKS = ((0, 0, False), (0, 48, False), (0, 96, False), (1, 0, False), (1, 48, False), (1, 96, True))
+CHUNKS = ((0, 16, True), (16, 32, False), (48, 32, False), (80, 32, False), (112, 32, False))
 
 
 def ring_fits(n, rows):
     return n == Z * X and rows == 144
 
 
-def gather_kernel(blk_ref, dn_ref, out_blk, out_dn, up_sem, down_sem, x_sem, sib_sem, recv_sem, sib_recv, own_sem):
+def gather_kernel(blk_ref, out_blk, up_sem, down_sem, x_sem, sib_sem, recv_sem, sib_recv, own_sem):
     me = lax.axis_index("dp")
     section = lax.axis_index("section")
     z, x = me // X, lax.rem(me, X)
     core = lax.rem(section, 2)
     sibling = section + 1 - 2 * core
     across = me + 1 - 2 * x
-    chunks = len(GATHER_CHUNKS)
+    chunks = len(CHUNKS)
     has_up, has_down = z < Z - 1, z > 0
 
     barrier = pltpu.get_barrier_semaphore()
@@ -136,15 +135,14 @@
     pl.semaphore_wait(barrier, 2 + has_up.astype(jnp.int32) + has_down.astype(jnp.int32))
 
     def place(owner, k, side):
-        which, first, unused = GATHER_CHUNKS[k]
-        rows = pl.ds(pl.multiple_of(owner * 144 + first, 16), PART)
-        return (out_dn if which else out_blk).at[side, rows]
+        first, rows, unused = CHUNKS[k]
+        return out_blk.at[side, pl.ds(pl.multiple_of(owner * 144 + first, 16), rows)]
 
     def source(owner, k, mine):
         if not mine:
             return place(owner, k, core)
-        which, first, unused = GATHER_CHUNKS[k]
-        return (dn_ref if which else blk_ref).at[pl.ds(first, PART)]
+        first, rows, unused = CHUNKS[k]
+        return blk_ref.at[pl.ds(first, rows)]
 
     def copy(owner, k, mine, sem, target):
         unit = owner * chunks + k
@@ -189,7 +187,7 @@
 
     def along(step, k, first_across):
         shift = 1 - 2 * x if first_across else 0
-        crosses = (not first_across) and (not GATHER_CHUNKS[k][2])
+        crosses = (not first_across) and (not CHUNKS[k][2])
 
         @pl.when(z >= step)
         def _():
@@ -218,7 +216,7 @@
             to_sibling(owner, k, False).start()
 
     def crossed(step, k):
-        direct = GATHER_CHUNKS[k][2]
+        direct = CHUNKS[k][2]
         if step == 0:
             owner = across
             arrived(owner, k)
@@ -244,11 +242,11 @@
             if step < Z:
                 along(step, k, False)
             crossed(step - 1, k)
-            if step < Z and GATHER_CHUNKS[k][2]:
+            if step < Z and CHUNKS[k][2]:
                 along(step, k, True)
 
     for k in range(chunks):
-        direct = GATHER_CHUNKS[k][2]
+        direct = CHUNKS[k][2]
         own_copy(k).wait()
         for column in range(2):
             base = me if column == 0 else across
@@ -280,54 +278,42 @@
                             copy(owner, k, mine, x_sem, across).wait_send()
 
 
-def gather_weights(blk, dn):
+def gather_weights(half):
     n = lax.axis_size("dp")
-    if not ring_fits(n, blk.shape[0]):
-        blk_all = lax.all_gather(blk, "dp", axis=0, tiled=True)
-        dn_all = lax.all_gather(dn, "dp", axis=0, tiled=True)
-        pairs = [(k, k ^ 1) for k in range(lax.axis_size("section"))]
-        blk_sib, dn_sib = lax.ppermute((blk_all, dn_all), "section", pairs)
+    if not ring_fits(n, half.shape[0]):
+        own = lax.all_gather(half, "dp", axis=0, tiled=True)
+        sib = swap(own, 1)
         even = lax.rem(lax.axis_index("section"), 2) == 0
-        both = lambda a, b: jnp.where(even, jnp.stack([a, b]), jnp.stack([b, a]))
-        return (both(blk_all, blk_sib), both(dn_all, dn_sib))
-    units = n * len(GATHER_CHUNKS)
+        return jnp.where(even, jnp.stack([own, sib]), jnp.stack([sib, own]))
+    units = n * len(CHUNKS)
     return pl.pallas_call(
         gather_kernel,
-        out_shape=(
-            jax.ShapeDtypeStruct((2, D, FF), BF),
-            jax.ShapeDtypeStruct((2, D, HALF), BF),
-        ),
-        in_specs=[pl.BlockSpec(memory_space=pl.ANY)] * 2,
-        out_specs=(pl.BlockSpec(memory_space=pl.ANY),) * 2,
+        out_shape=jax.ShapeDtypeStruct((2, D, HALF), BF),
+        in_specs=[pl.BlockSpec(memory_space=pl.ANY)],
+        out_specs=pl.BlockSpec(memory_space=pl.ANY),
         scratch_shapes=[pltpu.SemaphoreType.DMA((units,))] * 6
-        + [pltpu.SemaphoreType.DMA((len(GATHER_CHUNKS),))],
+        + [pltpu.SemaphoreType.DMA((len(CHUNKS),))],
         compiler_params=pltpu.CompilerParams(collective_id=0, has_side_effects=True),
+        cost_estimate=pl.CostEstimate(flops=0, bytes_accessed=200_000_000, transcendentals=0),
         name="gather_weights",
-    )(blk, dn)
-
-
-SUM_CHUNKS = ((1, 0, False), (1, 48, False), (1, 96, True), (0, 0, False), (0, 48, False), (0, 96, False))
+    )(half)
+
+
 VMEM_BYTES = 60 * 1024 * 1024
 
 
 def sum_kernel(
-    g_ref, gd_ref, blk_out, dn_out,
-    own_b, own_d, other_d, xb, xd, xq, up_b, up_d, up_o, down_b, down_d, down_o, acc,
-    load_sem, x_send, x_recv, up_send, up_recv, down_send, down_recv, sib_send, sib_recv, y_send, y_recv,
+    g_ref, out, own_b, other_d, xb, xq, up_b, up_o, down_b, down_o, acc,
+    load_sem, x_send, x_recv, up_send, up_recv, down_send, down_recv,
 ):
     me = lax.axis_index("dp")
-    section = lax.axis_index("section")
     z, x = me // X, lax.rem(me, X)
-    core = lax.rem(section, 2)
-    sibling = section + 1 - 2 * core
-    facing = lax.rem(section + 2, 4)
     across = me + 1 - 2 * x
-    chunks = len(SUM_CHUNKS)
+    chunks = len(CHUNKS)
     has_up, has_down = z < Z - 1, z > 0
 
     barrier = pltpu.get_barrier_semaphore()
-    for target in ({"section": sibling}, {"section": facing}, {"dp": across}):
-        pl.semaphore_signal(barrier, 1, device_id=target, device_id_type=MESH)
+    pl.semaphore_signal(barrier, 1, device_id={"dp": across}, device_id_type=MESH)
 
     @pl.when(has_up)
     def _():
@@ -350,28 +336,23 @@
         def _():
             run(z - distance, False)
 
+    def part(k):
+        return pl.ds(CHUNKS[k][0], CHUNKS[k][1])
+
     def hbm(k, zz, column):
-        which, first, unused = SUM_CHUNKS[k]
-        rows = pl.ds(pl.multiple_of((zz * X + column) * 144 + first, 16), PART)
-        return (gd_ref if which else g_ref).at[rows]
+        start = pl.multiple_of((zz * X + column) * 144 + CHUNKS[k][0], 16)
+        return g_ref.at[pl.ds(start, CHUNKS[k][1])]
 
     def own(k, zz):
-        which, first, unused = SUM_CHUNKS[k]
-        return (own_d if which else own_b).at[zz, pl.ds(first, PART)]
+        return own_b.at[zz, part(k)]
 
     def from_x(k, zz):
-        which, first, direct = SUM_CHUNKS[k]
-        if direct:
-            return xq
-        return (xd if which else xb).at[zz, pl.ds(first, PART)]
+        return xq if CHUNKS[k][2] else xb.at[zz, part(k)]
 
     def from_z(k, zz, up, other):
-        which, first, unused = SUM_CHUNKS[k]
         if other:
             return (up_o if up else down_o).at[zz]
-        if which:
-            return (up_d if up else down_d).at[zz, pl.ds(first, PART)]
-        return (up_b if up else down_b).at[zz, pl.ds(first, PART)]
+        return (up_b if up else down_b).at[zz, part(k)]
 
     def load(k, zz, other=False):
         index = ((chunks if other else 0) + k) * Z + zz
@@ -399,19 +380,8 @@
             device_id_type=MESH,
         )
 
-    def dn_copy(k, slot, to_sib):
-        rows = pl.ds(SUM_CHUNKS[k][1], PART)
-        unit = slot * chunks + k
-        return pltpu.make_async_remote_copy(
-            src_ref=dn_out.at[slot, rows], dst_ref=dn_out.at[slot, rows],
-            send_sem=(sib_send if to_sib else y_send).at[unit],
-            recv_sem=(sib_recv if to_sib else y_recv).at[unit],
-            device_id={"section": sibling if to_sib else facing},
-            device_id_type=MESH,
-        )
-
-    def total(dst, srcs):
-        @pl.loop(0, PART // 16)
+    def total(k, dst, srcs):
+        @pl.loop(0, CHUNKS[k][1] // 16)
         def _(step):
             rows = pl.ds(pl.multiple_of(step * 16, 16), 16)
             value = srcs[0][rows].astype(jnp.float32)
@@ -419,26 +389,25 @@
                 value = value + src[rows].astype(jnp.float32)
             dst[rows] = value.astype(dst.dtype)
 
-    for k in range(chunks):
-        for distance in (3, 2, 1, 0):
+    for distance in (3, 2, 1, 0):
+        for k in range(chunks):
             def run(zz, up):
                 load(k, zz).start()
-                if SUM_CHUNKS[k][2]:
+                if CHUNKS[k][2]:
                     load(k, zz, True).start()
             each(distance, run)
 
-    pl.semaphore_wait(barrier, 3 + has_up.astype(jnp.int32) + has_down.astype(jnp.int32))
-
-    for which in (1, 0):
-        for distance in (3, 2, 1, 0):
-            for k in range(chunks):
-                if SUM_CHUNKS[k][0] == which and not SUM_CHUNKS[k][2]:
-                    each(distance, lambda zz, up: x_copy(k, zz, hbm(k, zz, 1 - x)).start())
+    pl.semaphore_wait(barrier, 1 + has_up.astype(jnp.int32) + has_down.astype(jnp.int32))
+
+    for distance in (3, 2, 1, 0):
+        for k in range(chunks):
+            if not CHUNKS[k][2]:
+                each(distance, lambda zz, up: x_copy(k, zz, hbm(k, zz, 1 - x)).start())
 
     def pass_on(k, distance):
         def run(zz, up):
             behind = has_down if up else has_up
-            if SUM_CHUNKS[k][2]:
+            if CHUNKS[k][2]:
                 for other in (False, True):
                     mine = other_d.at[zz] if other else own(k, zz)
                     load(k, zz, other).wait()
@@ -446,7 +415,7 @@
                     @pl.when(behind)
                     def _():
                         z_copy(k, zz, up, other).wait_recv()
-                        total(mine, [mine, from_z(k, zz, up, other)])
+                        total(k, mine, [mine, from_z(k, zz, up, other)])
 
                     z_copy(k, zz, up, other).start()
                 return
@@ -456,11 +425,11 @@
             @pl.when(behind)
             def _():
                 z_copy(k, zz, up, False).wait_recv()
-                total(own(k, zz), [own(k, zz), from_x(k, zz), from_z(k, zz, up, False)])
+                total(k, own(k, zz), [own(k, zz), from_x(k, zz), from_z(k, zz, up, False)])
 
             @pl.when(jnp.logical_not(behind))
             def _():
-                total(own(k, zz), [own(k, zz), from_x(k, zz)])
+                total(k, own(k, zz), [own(k, zz), from_x(k, zz)])
 
             z_copy(k, zz, up, False).start()
         each(distance, run)
@@ -469,114 +438,83 @@
         @pl.when(has_down)
         def _():
             z_copy(k, z, True, other).wait_recv()
-            total(dst, [dst, from_z(k, z, True, other)])
+            total(k, dst, [dst, from_z(k, z, True, other)])
 
         @pl.when(has_up)
         def _():
             z_copy(k, z, False, other).wait_recv()
-            total(dst, [dst, from_z(k, z, False, other)])
+            total(k, dst, [dst, from_z(k, z, False, other)])
 
     def send_direct(k):
         load(k, z, True).wait()
-        acc[...] = other_d[z].astype(jnp.float32)
+        total(k, acc, [other_d.at[z]])
         add_z(acc, k, True)
-        other_d[z] = acc[...].astype(BF)
+        total(k, other_d.at[z], [acc])
         x_copy(k, z, other_d.at[z]).start()
 
     def finish(k):
-        which, first, direct = SUM_CHUNKS[k]
-        rows = pl.ds(first, PART)
-        dst = acc if which else blk_out.at[rows]
+        dst = out.at[part(k)]
         load(k, z).wait()
-        if direct:
-            total(dst, [own(k, z)])
+        if CHUNKS[k][2]:
+            total(k, dst, [own(k, z)])
             add_z(dst, k, False)
             x_copy(k, z, other_d.at[z]).wait_recv()
-            total(dst, [dst, from_x(k, z)])
+            total(k, dst, [dst, from_x(k, z)])
         else:
             x_copy(k, z, hbm(k, z, 1 - x)).wait_recv()
-            total(dst, [own(k, z), from_x(k, z)])
+            total(k, dst, [own(k, z), from_x(k, z)])
             add_z(dst, k, False)
-        if which:
-            total(dn_out.at[section, rows], [acc])
-            dn_copy(k, section, True).start()
-            dn_copy(k, section, False).start()
-
-    dn_chunks = [k for k in range(chunks) if SUM_CHUNKS[k][0]]
-    blk_chunks = [k for k in range(chunks) if not SUM_CHUNKS[k][0]]
+
+    straight = [k for k in range(chunks) if not CHUNKS[k][2]]
+    direct = [k for k in range(chunks) if CHUNKS[k][2]]
     for distance in (3, 2, 1):
-        for k in dn_chunks:
+        for k in range(chunks):
             pass_on(k, distance)
-    for k in blk_chunks:
-        pass_on(k, 3)
-    for k in dn_chunks:
-        if SUM_CHUNKS[k][2]:
-            send_direct(k)
-    for k in dn_chunks:
+    for k in direct:
+        send_direct(k)
+    for k in straight + direct:
         finish(k)
-    for k in blk_chunks:
-        pass_on(k, 2)
-    for k in dn_chunks:
-        dn_copy(k, facing, False).wait_recv()
-        dn_copy(k, facing, True).start()
-    for k in blk_chunks:
-        pass_on(k, 1)
-    for k in blk_chunks:
-        finish(k)
 
     for k in range(chunks):
-        direct = SUM_CHUNKS[k][2]
         for distance in (3, 2, 1, 0):
             def run(zz, up):
-                if not direct:
+                if not CHUNKS[k][2]:
                     x_copy(k, zz, hbm(k, zz, 1 - x)).wait_send()
                 elif distance == 0:
                     x_copy(k, zz, other_d.at[zz]).wait_send()
                 if distance:
                     z_copy(k, zz, up, False).wait_send()
-                    if direct:
+                    if CHUNKS[k][2]:
                         z_copy(k, zz, up, True).wait_send()
             each(distance, run)
-        if SUM_CHUNKS[k][0]:
-            dn_copy(k, section, True).wait_send()
-            dn_copy(k, section, False).wait_send()
-            dn_copy(k, facing, True).wait_send()
-            dn_copy(k, sibling, True).wait_recv()
-            dn_copy(k, lax.rem(sibling + 2, 4), True).wait_recv()
-
-
-def sum_gradients(g_blk, g_dn):
+
+
+def sum_gradients(grad):
     n = lax.axis_size("dp")
     if not ring_fits(n, D // n):
-        blk = lax.psum_scatter(g_blk, "dp", scatter_dimension=0, tiled=True)
-        dn = lax.psum_scatter(g_dn, "dp", scatter_dimension=0, tiled=True)
-        return (blk.astype(jnp.float32), lax.all_gather(dn, "section"))
-    chunks = len(SUM_CHUNKS)
+        return lax.psum_scatter(grad, "dp", scatter_dimension=0, tiled=True).astype(jnp.float32)
+    chunks = len(CHUNKS)
     dma = lambda count: pltpu.SemaphoreType.DMA((count,))
-    ring_b = pltpu.VMEM((Z, 144, FF), BF)
-    ring_d = pltpu.VMEM((Z, 144, HALF), BF)
-    ring_o = pltpu.VMEM((Z, PART, HALF), BF)
-    vmem = pl.BlockSpec(memory_space=pltpu.VMEM)
+    ring = pltpu.VMEM((Z, 144, HALF), BF)
+    short = [rows for first, rows, direct in CHUNKS if direct][0]
+    ring_o = pltpu.VMEM((Z, short, HALF), BF)
     return pl.pallas_call(
         sum_kernel,
-        out_shape=(
-            jax.ShapeDtypeStruct((144, FF), jnp.float32),
-            jax.ShapeDtypeStruct((4, 144, HALF), BF),
-        ),
-        in_specs=[pl.BlockSpec(memory_space=pl.ANY)] * 2,
-        out_specs=(vmem, vmem),
+        out_shape=jax.ShapeDtypeStruct((144, HALF), jnp.float32),
+        in_specs=[pl.BlockSpec(memory_space=pl.ANY)],
+        out_specs=pl.BlockSpec(memory_space=pltpu.VMEM),
         scratch_shapes=[
-            ring_b, ring_d, ring_o, ring_b, pltpu.VMEM((Z, 96, HALF), BF), pltpu.VMEM((PART, HALF), BF),
-            ring_b, ring_d, ring_o, ring_b, ring_d, ring_o, pltpu.VMEM((PART, HALF), jnp.float32),
+            ring, ring_o, ring, pltpu.VMEM((short, HALF), BF),
+            ring, ring_o, ring, ring_o, pltpu.VMEM((short, HALF), jnp.float32),
             dma(2 * chunks * Z), dma(chunks * Z), dma(chunks * Z),
             dma(2 * chunks * Z), dma(2 * chunks * Z), dma(2 * chunks * Z), dma(2 * chunks * Z),
-            dma(4 * chunks), dma(4 * chunks), dma(4 * chunks), dma(4 * chunks),
         ],
         compiler_params=pltpu.CompilerParams(
             collective_id=1, has_side_effects=True, vmem_limit_bytes=VMEM_BYTES
         ),
+        cost_estimate=pl.CostEstimate(flops=0, bytes_accessed=200_000_000, transcendentals=0),
         name="sum_gradients",
-    )(g_blk, g_dn)
+    )(grad)
 
 
 def exchange_kernel(axes, modes, *refs):
@@ -656,6 +594,7 @@
         compiler_params=pltpu.CompilerParams(
             collective_id=ident, has_side_effects=True, vmem_limit_bytes=VMEM_BYTES
         ),
+        cost_estimate=pl.CostEstimate(flops=0, bytes_accessed=30_000_000, transcendentals=0),
         name="exchange_" + axes,
     )(*arrays)
 
@@ -673,36 +612,41 @@
     return value.reshape(PATCHES, HEADS, HEAD_DIM)
 
 
-def attention_forward(xm_half, wblk, bblk):
-    qkv = to_half(matmul(xm_half, wblk[:, : 3 * D]) + bblk[: 3 * D])
-    parts = qkv.reshape(PATCHES, 3, HEADS, HEAD_DIM)
+def attention_forward(xm_half, w_attn, bblk):
+    pair = to_half(matmul(xm_half, w_attn[0]) + bblk[:HALF])
+    value = heads_of(to_half(matmul(xm_half, w_attn[1][:, :D]) + bblk[HALF : 3 * D]))
+    query, key = heads_of(pair[:, :D]), heads_of(pair[:, D:])
     scores = jnp.einsum(
-        "qhd,khd->hqk", parts[:, 0], parts[:, 1], preferred_element_type=jnp.float32
+        "qhd,khd->hqk", query, key, preferred_element_type=jnp.float32
     ) * HEAD_DIM ** (-0.5)
     probs = jax.nn.softmax(scores, axis=-1)
     attended = to_half(
-        jnp.einsum("hqk,khd->qhd", to_half(probs), parts[:, 2], preferred_element_type=jnp.float32)
+        jnp.einsum("hqk,khd->qhd", to_half(probs), value, preferred_element_type=jnp.float32)
     ).reshape(PATCHES, D)
-    branch = matmul(attended, wblk[:, 3 * D :]) + bblk[3 * D :]
-    return (branch, (parts, probs, attended))
-
-
-def attention_backward(grad_half, saved, wblk):
-    parts, probs, attended = saved
-    d_att = heads_of(to_half(matmul_nt(grad_half, wblk[:, 3 * D :])))
-    d_value = jnp.einsum(
-        "hqk,qhd->khd", to_half(probs), d_att, preferred_element_type=jnp.float32
-    )
-    d_probs = jnp.einsum("qhd,khd->hqk", d_att, parts[:, 2], preferred_element_type=jnp.float32)
+    branch = matmul(attended, w_attn[1][:, D:]) + bblk[3 * D :]
+    return (branch, (query, key, value, probs, attended))
+
+
+def attention_backward(grad_half, saved, w_attn):
+    query, key, value, probs, attended = saved
+    d_att = heads_of(to_half(matmul_nt(grad_half, w_attn[1][:, D:])))
+    flat = lambda grad: to_half(grad).reshape(PATCHES, D)
+    d_value = flat(
+        jnp.einsum("hqk,qhd->khd", to_half(probs), d_att, preferred_element_type=jnp.float32)
+    )
+    d_probs = jnp.einsum("qhd,khd->hqk", d_att, value, preferred_element_type=jnp.float32)
     d_scores = to_half(probs * (d_probs - jnp.sum(probs * d_probs, axis=-1, keepdims=True)))
-    d_query = jnp.einsum(
-        "hqk,khd->qhd", d_scores, parts[:, 1], preferred_element_type=jnp.float32
-    ) * HEAD_DIM ** (-0.5)
-    d_key = jnp.einsum(
-        "hqk,qhd->khd", d_scores, parts[:, 0], preferred_element_type=jnp.float32
-    ) * HEAD_DIM ** (-0.5)
-    d_qkv = to_half(jnp.stack([d_query, d_key, d_value], axis=1).reshape(PATCHES, 3 * D))
-    return (matmul_nt(d_qkv, wblk[:, : 3 * D]), d_qkv)
+    d_query = flat(
+        jnp.einsum("hqk,khd->qhd", d_scores, key, preferred_element_type=jnp.float32)
+        * HEAD_DIM ** (-0.5)
+    )
+    d_key = flat(
+        jnp.einsum("hqk,qhd->khd", d_scores, query, preferred_element_type=jnp.float32)
+        * HEAD_DIM ** (-0.5)
+    )
+    d_pair = jnp.concatenate([d_query, d_key], axis=1)
+    d_xm = matmul_nt(d_pair, w_attn[0]) + matmul_nt(d_value, w_attn[1][:, :D])
+    return (d_xm, d_query, d_key, d_value)
 
 
 def modulated(x, mod):
@@ -716,39 +660,40 @@
 
 
 def stage_forward(x_in, weights):
-    mod_a, mod_m, w_blk, w_dn, b_attn, b_up, b_down = weights
+    mod_a, mod_m, w_attn, w_up, w_dn, b_attn, b_up, b_down = weights
     xm_a = to_half(modulated(x_in, mod_a))
-    branch_a, saved = attention_forward(xm_a, w_blk[0], b_attn)
+    branch_a, saved = attention_forward(xm_a, w_attn, b_attn)
     x_mid = to_half(x_in + mod_a[None, 2 * D :] * branch_a).astype(jnp.float32)
     xm_m = to_half(modulated(x_mid, mod_m))
-    pre = matmul(xm_m, w_blk[1]) + b_up
-    act = to_half(jax.nn.gelu(pre, approximate=True))
-    branch_m = matmul_nt(act[:, :HALF], w_dn[0]) + matmul_nt(act[:, HALF:], w_dn[1]) + b_down
+    pre = [matmul(xm_m, w_up[k]) + b_up[k] for k in range(2)]
+    act = [to_half(jax.nn.gelu(half, approximate=True)) for half in pre]
+    branch_m = matmul_nt(act[0], w_dn[0]) + matmul_nt(act[1], w_dn[1]) + b_down
     x_out = x_mid + mod_m[None, 2 * D :] * branch_m
     return (x_out, (xm_a, branch_a, saved, x_mid, xm_m, pre, act, branch_m))
 
 
 def mlp_backward(d_out, weights, kept):
-    mod_a, mod_m, w_blk, w_dn, b_attn, b_up, b_down = weights
+    mod_a, mod_m, w_attn, w_up, w_dn, b_attn, b_up, b_down = weights
     xm_a, branch_a, saved, x_mid, xm_m, pre, act, branch_m = kept
     d_gate = jnp.sum(d_out * branch_m, axis=0)
     grad_half = to_half(d_out * mod_m[None, 2 * D :])
-    d_act = jnp.concatenate([matmul(grad_half, w_dn[0]), matmul(grad_half, w_dn[1])], axis=1)
-    d_pre = to_half(jax.vjp(partial(jax.nn.gelu, approximate=True), pre)[1](d_act)[0])
-    d_x, d_shift, d_scale = modulated_back(x_mid, mod_m, matmul_nt(d_pre, w_blk[1]))
+    gelu_back = lambda half, grad: jax.vjp(partial(jax.nn.gelu, approximate=True), half)[1](grad)[0]
+    d_pre = [to_half(gelu_back(pre[k], matmul(grad_half, w_dn[k]))) for k in range(2)]
+    d_xm = matmul_nt(d_pre[0], w_up[0]) + matmul_nt(d_pre[1], w_up[1])
+    d_x, d_shift, d_scale = modulated_back(x_mid, mod_m, d_xm)
     d_mod = to_half(jnp.concatenate([d_shift, d_scale, d_gate]))
     return (to_half(d_out + d_x).astype(jnp.float32), d_mod, grad_half, d_pre)
 
 
 def attn_backward(d_out, x_in, weights, kept):
-    mod_a, mod_m, w_blk, w_dn, b_attn, b_up, b_down = weights
+    mod_a, mod_m, w_attn, w_up, w_dn, b_attn, b_up, b_down = weights
     xm_a, branch_a, saved, x_mid, xm_m, pre, act, branch_m = kept
     d_gate = jnp.sum(d_out * branch_a, axis=0)
     grad_half = to_half(d_out * mod_a[None, 2 * D :])
-    d_xm, d_qkv = attention_backward(grad_half, saved, w_blk[0])
+    d_xm, d_query, d_key, d_value = attention_backward(grad_half, saved, w_attn)
     d_x, d_shift, d_scale = modulated_back(x_in, mod_a, d_xm)
     d_mod = to_half(jnp.concatenate([d_shift, d_scale, d_gate]))
-    return (to_half(d_out + d_x), d_mod, grad_half, d_qkv)
+    return (to_half(d_out + d_x), d_mod, grad_half, (d_query, d_key, d_value))
 
 
 def final_step(x_out, fmod, w_head, b_head, target, counts, loss_scale):
@@ -793,8 +738,15 @@
 
     downs = jnp.swapaxes(down_w, 1, 2)
     blk_half = to_half(block_w[0])
+    crossing = swap(jnp.where(even, blk_half[:, HALF:], blk_half[:, :HALF]), 1)
+    attn_half = jnp.where(even, blk_half[:, :HALF], crossing)
+    up_half = jnp.where(even, crossing, blk_half[:, HALF:])
     dn_half = to_half(lax.dynamic_slice(downs, (stage, 0, core * HALF), (1, width, HALF))[0])
-    w_blk, w_dn = gather_weights(blk_half, dn_half)
+    up_own = lax.all_gather(up_half, "dp", axis=0, tiled=True)
+    dn_own = lax.all_gather(dn_half, "dp", axis=0, tiled=True)
+    w_up = (up_own, swap(up_own, 1))
+    w_dn = (dn_own, swap(dn_own, 1))
+    w_attn = gather_weights(attn_half)
 
     stems = stem_w.T
     classes_own = jnp.where(null_mask > 0, NCLS - 1, labels)
@@ -840,9 +792,9 @@
     mod_b = mods[1, : 3 * D] + bias_of(6 * D * stage + 3 * D, 3 * D)
     fmod = mods[0, 3 * D : 5 * D] + biases[33 * D : 35 * D]
     weights = (
-        mod_a, mod_b, w_blk, w_dn,
+        mod_a, mod_b, w_attn, w_up, w_dn,
         bias_of(12 * D + 8 * D * stage, 4 * D),
-        bias_of(16 * D + 8 * D * stage, 4 * D),
+        [bias_of(16 * D + 8 * D * stage + HALF * half, HALF) for half in (core, 1 - core)],
         bias_of(28 * D + D * stage, D),
     )
 
@@ -863,43 +815,63 @@
     d_mid = mlp_backward(d_final, weights, kept)[0]
     d_hop = swap(attn_backward(d_mid, x_in, weights, kept)[0], 2)
     d_out = jnp.where(stage == 1, d_final, d_hop.astype(jnp.float32))
+    xm_a, branch_a, saved, x_mid, xm_b, pre, act, branch_b = kept
+    attended = saved[-1]
+
     d_mid, d_mod_b, d_branch_b, d_pre = mlp_backward(d_out, weights, kept)
+    act_sib, branch_sib, xm_sib, pre_sib = swap((act[1], d_branch_b, xm_b, d_pre[1]), 1)
+    g_dn = to_half(matmul_tn(d_branch_b, act[0]) + matmul_tn(branch_sib, act_sib))
+    g_up = to_half(matmul_tn(xm_b, d_pre[0]) + matmul_tn(xm_sib, pre_sib))
+    g_dn = lax.psum_scatter(g_dn, "dp", scatter_dimension=0, tiled=True)
+    g_up = lax.psum_scatter(g_up, "dp", scatter_dimension=0, tiled=True)
+
     d_first, d_mod_a, d_branch_a, d_qkv = attn_backward(d_mid, x_in, weights, kept)
-    xm_a, branch_a, saved, x_mid, xm_b, pre, act, branch_b = kept
-    attended = saved[2]
-
-    act_own = jnp.where(even, act[:, :HALF], act[:, HALF:])
-    act_sib, branch_sib = swap((jnp.where(even, act[:, HALF:], act[:, :HALF]), d_branch_b), 1)
-    g_dn = to_half(matmul_tn(d_branch_b, act_own) + matmul_tn(branch_sib, act_sib))
-    d_attn = jnp.concatenate([d_qkv, d_branch_a], axis=1)
-    left_sib, last_sib, right_sib = swap(
+    d_query, d_key, d_value = d_qkv
+    xa_sib, last_sib, one_sib, two_sib = swap(
         (
-            jnp.where(even, xm_b, xm_a),
-            jnp.where(even, xm_b, attended),
-            jnp.where(even, d_pre, d_attn),
+            xm_a,
+            jnp.where(even, attended, xm_a),
+            jnp.where(even, d_value, d_query),
+            jnp.where(even, d_branch_a, d_key),
         ),
         1,
     )
-    left = jnp.concatenate([jnp.where(even, xm_a, xm_b), left_sib], axis=0)
-    last = jnp.concatenate([jnp.where(even, attended, xm_b), last_sib], axis=0)
-    right = jnp.concatenate([jnp.where(even, d_attn, d_pre), right_sib], axis=0)
-    g_blk = jnp.concatenate(
+    last = jnp.where(even, xm_a, attended)
+    one = jnp.where(even, d_query, d_value)
+    two = jnp.where(even, d_key, d_branch_a)
+    g_attn = jnp.concatenate(
         [
-            to_half(matmul_tn(left, right[:, : 3 * D])),
-            to_half(matmul_tn(last, right[:, 3 * D :])),
+            to_half(matmul_tn(xm_a, one) + matmul_tn(xa_sib, one_sib)),
+            to_half(matmul_tn(last, two) + matmul_tn(last_sib, two_sib)),
         ],
         axis=1,
     )
-    g_blk, g_dn = sum_gradients(g_blk, g_dn)
+    g_attn = sum_gradients(g_attn)
+    crossing = swap(jnp.where(even, g_up, to_half(g_attn)), 1).astype(jnp.float32)
+    g_up = g_up.astype(jnp.float32)
+    g_blk = jnp.concatenate(
+        [jnp.where(even, g_attn, crossing), jnp.where(even, crossing, g_up)], axis=1
+    )
+    g_facing = swap(g_dn, 2)
+    g_sib, g_corner = swap((g_dn, g_facing), 1)
+    in_core = lambda own, sib: jnp.concatenate(
+        [jnp.where(even, own, sib), jnp.where(even, sib, own)], axis=1
+    ).astype(jnp.float32)
+    here, there = in_core(g_dn, g_sib), in_core(g_facing, g_corner)
+    down_both = jnp.where(stage == 0, jnp.stack([here, there]), jnp.stack([there, here]))
 
     last_stage = (stage == 1).astype(jnp.float32)
     zeros_fm = jnp.zeros((2 * D + 384,), BF)
     d_fmod = jnp.concatenate([jnp.where(stage == 1, d_fmod, zeros_fm[: 2 * D]), zeros_fm[2 * D :]])
     d_mods = jnp.stack([jnp.concatenate([d_mod_a, d_fmod]), jnp.concatenate([d_mod_b, d_fmod])])
     last_own = jnp.where(stage == 0, column_sums(d_first), jnp.pad(b_head, (0, D - HEAD_OUT)))
+    in_order = lambda own, sib: jnp.where(
+        even, jnp.concatenate([own, sib]), jnp.concatenate([sib, own])
+    )
     own_biases = jnp.concatenate(
         [
-            column_sums(d_qkv), column_sums(d_branch_a), column_sums(d_pre), column_sums(d_branch_b),
+            *map(column_sums, d_qkv), column_sums(d_branch_a), in_order(*map(column_sums, d_pre)),
+            column_sums(d_branch_b),
             last_own, loss[None],
         ]
     )
@@ -942,10 +914,6 @@
     g_two = matmul_nt(d_cond, hidden_all)
     g_stem = jnp.concatenate([g_table, ends[0][:, :PATCH_IN], g_one, g_two], axis=1)
     g_tail = jnp.concatenate([g_fm, ends[1]], axis=1)
-    g_dn = g_dn.astype(jnp.float32)
-    down_both = jnp.stack(
-        [jnp.concatenate([g_dn[0], g_dn[1]], axis=1), jnp.concatenate([g_dn[2], g_dn[3]], axis=1)]
-    )
 
     square = lambda value: jnp.sum(value * value)
     once = (section == 0).astype(jnp.float32)

time: 870 us -> 770 us (0.89)
  Pallas kernels: 490 us -> 321 us
  matrix products: 153 us -> 185 us
  waiting for transfers between devices: 14.6 us -> 46.1 us
  other arithmetic: 106 us -> 85.7 us
  between operations: 11.5 us -> 25.2 us
  local copies, waits for them, and re-layouts: 79.6 us -> 91 us
    pallas_call x2, Pallas kernels: 401 us -> 205 us  [the longest x1 128 us: gather_weights(): pl.pallas_call(gather_kernel, out_shape=jax.ShapeDtypeStruct((2, D, HALF)...]
    pallas_call x6, Pallas kernels: 89.1 us -> 116 us  [exchange(): pl.pallas_call(partial(exchange_kernel, axes, modes), out_shape=tuple((ja...]
    ppermute x7 -> x17, waiting for transfers between devices: 14.6 us -> 36.4 us  [swap(): return lax.ppermute(array, 'section', [(k, k ^ by) for k in range(peers)])]
    unnamed x326 -> x417, local copies, waits for them, and re-layouts: 25.5 us -> 44.6 us
    dot_general x17 -> x21, matrix products: 55.1 us -> 73.4 us  [matmul_nt(): lax.dot_general(left, right, (((1,), (1,)), ((), ())), preferred_element_...]
    dot_general x9 -> x13, matrix products: 19.7 us -> 33.1 us  [matmul_tn(): lax.dot_general(left, right, (((0,), (0,)), ((), ())), preferred_element_...]
    all_gather x0 -> x2, waiting for transfers between devices: none -> 9.65 us  [the longest x1 9.63 us: body(): up_own = lax.all_gather(up_half, 'dp', axis=0, tiled=True)]
    dot_general x16, matrix products: 60 us -> 50.8 us  [matmul(): return jnp.dot(left, right, preferred_element_type=jnp.float32)]
  transfers between devices with their start and end apart: 7 -> 21, of which waited for: 2 -> 6; matrix products, arithmetic and copies ran while one was open for 12% -> 25% of each run, Pallas kernels for 4% -> 41%
where the time goes in v3:
time: 770 us; the launch traced here: 762 us
  Pallas kernels  321 us (42%)
  matrix products  185 us (24%)
  local copies, waits for them, and re-layouts  91 us (12%)
  other arithmetic  85.7 us (11%)
  waiting for transfers between devices  46.1 us (6%)
  between operations  25.2 us (3%)
    pallas_call x1, Pallas kernels, gather_weights(): pl.pallas_call(gather_kernel, out_shape=jax.ShapeDtypeStruct((2, D, HALF)...  128 us
    pallas_call x6, Pallas kernels, exchange(): pl.pallas_call(partial(exchange_kernel, axes, modes), out_shape=tuple((ja...  116 us
    pallas_call x1, Pallas kernels, sum_gradients(): pl.pallas_call(sum_kernel, out_shape=jax.ShapeDtypeStruct((144, HALF), jn...  76.9 us
    dot_general x21, matrix products, matmul_nt(): lax.dot_general(left, right, (((1,), (1,)), ((), ())), preferred_element_...  73.4 us
    dot_general x16, matrix products, matmul(): return jnp.dot(left, right, preferred_element_type=jnp.float32)  50.8 us
    unnamed x417, local copies, waits for them, and re-layouts  44.6 us
    ppermute x17, waiting for transfers between devices, swap(): return lax.ppermute(array, 'section', [(k, k ^ by) for k in range(peers)])  36.4 us
    dot_general x13, matrix products, matmul_tn(): lax.dot_general(left, right, (((0,), (0,)), ((), ())), preferred_element_...  33.1 us
  transfers between devices with their start and end apart: 21, of which 6 were waited for; matrix products, arithmetic and copies ran while one was open for 25% of the time, Pallas kernels for 41%

profile of v3, /device:TPU:0, one launch (start us, length us, event | category | flops | bytes accessed | tf_op | source)
XLA Modules:
  0.0 762.2 jit_solution(11560344759942855824)
XLA Ops:
  18.5 34.7 %exchange_dp.2 = (s32[8,8,128]{2,1,0:T(8,128)}, bf16[8,144,384]{2,1,0:T(8,128)(2,1)}) custom-call(s32[8,128]{1,0:T(8,128)} %pad.44.refs_0_, bf16[144,384]{1,0:T(8,128)(2,1)} %fusion.190.refs_1_), custom_call_target="tpu_custom_call" | custom-call | bytes 30000000 | tf_op jit(solution)/shard_map/exchange_dp/pallas_call | solution.py:584
  60.4 32.4 %exchange_stage.2 = f32[16,48,128]{2,1,0:T(8,128)} custom-call(f32[16,48,128]{2,1,0:T(8,128)} %bitcast.360), custom_call_target="tpu_custom_call" | custom-call | bytes 30000000 | tf_op jit(solution)/shard_map/exchange_stage/pallas_call | solution.py:584
  101.1 128.5 %gather_weights.1 = bf16[2,1152,2304]{2,1,0:T(8,128)(2,1)} custom-call(bf16[144,2304]{1,0:T(8,128)(2,1)} %get-tuple-element.102.blk_ref), custom_call_target="tpu_custom_call" | custom-call | bytes 200000000 | tf_op jit(solution)/shard_map/gather_weights/pallas_call | solution.py:289
  229.7 4.5 fusion.25
  235.4 9.6 %all-gather.4.cloned.1.call-done = bf16[1152,2304]{1,0:T(8,128)(2,1)} async-done(((bf16[144,2304]{1,0:T(8,128)(2,1)}), bf16[1152,2304]{1,0:T(8,128)(2,1)}) %all-gather.4.cloned.1.call-update) | async-done | bytes 5308432 | tf_op jit(solution)/shard_map/all_gather | solution.py:745
  261.1 8.6 %fusion.146 = f32[256,1152]{1,0:T(8,128)} fusion(bf16[1152,2304]{1,0:T(8,128)(2,1)} %all-gather.4.cloned.1.call-done, f32[2304]{0:T(1024)S(1)} %copy-done.145, f32[256,1152]{1,0:T(8,128)S(1)} %get-tuple-element.154, f32[1152]{0:T(1024)S(1)} %copy-done.127, f32[1152]{0:T(1024)S(1)} %copy-done.92, f32[256]{0:T(256)S(1)} %add_rsqrt_fusion, ...), kind=kOutput, calls=%fused_computation.264 | convolution fusion | flops 2725281792 | bytes 12996608 | tf_op jit(solution)/shard_map/dot_general | solution.py:40
  269.8 9.0 %fusion.58 = bf16[256,1152]{1,0:T(8,128)(2,1)} fusion(f32[256,1152]{1,0:T(8,128)S(1)} %get-tuple-element.154, f32[256,1152]{1,0:T(8,128)} %fusion.146, bf16[1152,2304]{1,0:T(8,128)(2,1)} %collective-permute-done.2, bf16[1152,2304]{1,0:T(8,128)(2,1)} %collective-permute-done.1, f32[2304]{0:T(1024)S(1)} %copy-done.143, f32[1152]{0:T(1024)S(1)} %copy-done.152, ...), kind=kOutput, calls=%fused_computation.87 | convolution fusion | flops 2726756352 | bytes 13595648 | tf_op jit(solution)/shard_map/dot_general | solution.py:40
  287.7 7.0 collective-permute-done.3
  296.4 4.7 fusion.22
  306.2 4.2 fusion.302
  313.1 4.1 convert_reduce_fusion.2
  319.2 4.7 convolution_add_fusion.5
  324.0 7.4 multiply_convert_fusion.2
  333.5 5.7 fusion.288
  344.0 9.6 %fusion.137 = f32[256,1152]{1,0:T(8,128)} fusion(bf16[1152,2304]{1,0:T(8,128)(2,1)} %collective-permute-done.1, f32[256,2304]{1,0:T(8,128)} %get-tuple-element.159, bf16[1152,2304]{1,0:T(8,128)(2,1)} %collective-permute-done.2, f32[256,1152]{1,0:T(8,128)S(1)} %get-tuple-element.92, f32[256]{0:T(256)} %negate_multiply_fusion.4, f32[1152]{0:T(1024)} %get-tuple-element.133), kind=kOutput, calls=%fused_computation.250 | convolution fusion | flops 2730590208 | bytes 15341056 | tf_op jit(solution)/shard_map/dot_general | solution.py:40
  353.6 10.7 %fusion.120 = (f32[256]{0:T(256)}, f32[256,1152]{1,0:T(8,128)}) fusion(bf16[256,1152]{1,0:T(8,128)(2,1)S(1)} %get-tuple-element.96, f32[256]{0:T(256)} %copy-done.114, f32[1152]{0:T(1024)S(1)} %copy-done.94, f32[256,1152]{1,0:T(8,128)} %fusion.137, bf16[1152,2304]{1,0:T(8,128)(2,1)} %all-gather.4.cloned.1.call-done, f32[256,2304]{1,0:T(8,128)} %copy-done.57, ...), kind=kOutput, calls=%fused_computation.205 | convolution fusion | flops 2732359424 | bytes 17117184 | tf_op jit(solution)/shard_map/dot_general | solution.py:40
  391.5 13.7 %collective-permute-done.4 = bf16[256,1152]{1,0:T(8,128)(2,1)S(1)} collective-permute-done((bf16[256,1152]{1,0:T(8,128)(2,1)}, bf16[256,1152]{1,0:T(8,128)(2,1)S(1)}, u32[]{:S(2)}, u32[]{:S(2)}) %collective-permute-start.4) | collective-permute-done | bytes 589856 | tf_op jit(solution)/shard_map/ppermute | solution.py:719
  421.3 8.0 %convert_reduce_fusion = (f32[2304]{0:T(1024)}, bf16[256,2304]{1,0:T(8,128)(2,1)}) fusion(f32[256,2304]{1,0:T(8,128)} %get-tuple-element.159, bf16[256,1152]{1,0:T(8,128)(2,1)S(1)} %copy-done.44, bf16[1152,2304]{1,0:T(8,128)(2,1)} %collective-permute-done.2), kind=kOutput, calls=%fused_computation.114 | convolution fusion | flops 1371928320 | bytes 9446400 | tf_op jit(solution)/shard_map/dot_general | solution.py:36
  429.7 4.8 fusion.305
  434.6 6.0 convert_reduce_fusion.1
  468.2 5.5 fusion.2
  474.8 5.8 multiply_reduce_fusion.8
  513.9 16.3 %exchange_stage.3 = (bf16[16,48,128]{2,1,0:T(8,128)(2,1)}, f32[16,8,128]{2,1,0:T(8,128)}, f32[16,40,128]{2,1,0:T(8,128)}) custom-call(bf16[2,48,128]{2,1,0:T(8,128)(2,1)} %pad_maximum_fusion.4.refs_0_, f32[16,8,128]{2,1,0:T(8,128)} %pad_bitcast_fusion.2.refs_1_, f32[8,40,128]{2,1,0:T(8,128)} %bitcast.370), custom_call_target="tpu_custom_call" | custom-call | bytes 30000000 | tf_op jit(solution)/shard_map/exchange_stage/pallas_call | solution.py:584
  535.1 8.9 %exchange_section.1 = (f32[4,24,128]{2,1,0:T(8,128)}, f32[4,40,128]{2,1,0:T(8,128)}, bf16[4,16,2304]{2,1,0:T(8,128)(2,1)}) custom-call(f32[24,128]{1,0:T(8,128)} %pad_bitcast_fusion.3.refs_0_, f32[40,128]{1,0:T(8,128)} %reduce_sum.657.refs_1_, bf16[16,2304]{1,0:T(8,128)(2,1)} %slice.363.refs_2_), custom_call_target="tpu_custom_call" | custom-call | bytes 30000000 | tf_op jit(solution)/shard_map/exchange_section/pallas_call | solution.py:584
  547.3 12.3 %exchange_dp.3 = f32[8,24,128]{2,1,0:T(8,128)} custom-call(f32[8,24,128]{2,1,0:T(8,128)} %bitcast.386), custom_call_target="tpu_custom_call" | custom-call | bytes 30000000 | tf_op jit(solution)/shard_map/exchange_dp/pallas_call | solution.py:584
  572.2 4.5 fusion.153
  578.2 4.5 fusion.150
  584.6 4.1 fusion.4
  593.8 76.9 %sum_gradients.1 = f32[144,2304]{1,0:T(8,128)} custom-call(bf16[1152,2304]{1,0:T(8,128)(2,1)} %pad_maximum_fusion.g_ref), custom_call_target="tpu_custom_call" | custom-call | bytes 200000000 | tf_op jit(solution)/shard_map/sum_gradients/pallas_call | solution.py:501
  674.2 11.8 %collective-permute-done.15 = bf16[144,2304]{1,0:T(8,128)(2,1)S(1)} collective-permute-done((bf16[144,2304]{1,0:T(8,128)(2,1)}, bf16[144,2304]{1,0:T(8,128)(2,1)S(1)}, u32[]{:S(2)}, u32[]{:S(2)}) %collective-permute-start.15) | collective-permute-done | bytes 663584 | tf_op jit(solution)/shard_map/ppermute | solution.py:719
  698.8 11.5 %exchange_every.1 = f32[32,16,128]{2,1,0:T(8,128)} custom-call(f32[16,128]{1,0:T(8,128)} %pad_maximum_fusion.6.refs_0_), custom_call_target="tpu_custom_call" | custom-call | bytes 30000000 | tf_op jit(solution)/shard_map/exchange_every/pallas_call | solution.py:584
  725.3 7.9 %convert_bitcast_fusion = (bf16[2,4608,144]{1,2,0:T(8,128)(2,1)}, f32[2,144,4608]{2,1,0:T(8,128)S(1)}, f32[2,4608,144]{1,2,0:T(8,128)}) fusion(f32[2,4608,144]{1,2,0:T(8,128)} %param.37, f32[]{:T(128)S(6)} %min.3, f32[1,144,4608]{2,1,0:T(8,128)S(1)} %get-tuple-element.183, f32[1,144,4608]{2,1,0:T(8,128)S(1)} %copy-done.1, pred[]{:T(512)S(6)} %eq.35, ...), kind=kLoop, calls=%fused_computation.79 | loop fusion | flops 14598144 | bytes 29196292 | tf_op jit(solution)/shard_map/transpose | solution.py:951
  (702 shorter events, 249.1 us)
Async XLA Ops:
  7.2 227.7 %all-gather.6.cloned.1.call-start = ((), (), s32[]{:S(2)}) async-start(), calls=%async_computation.5 | async-start | bytes 5971968 | tf_op jit(solution)/shard_map/all_gather | solution.py:746
  9.5 235.4 %all-gather.4.cloned.1.call-start = ((), (), s32[]{:S(2)}) async-start(), calls=%async_computation.2 | async-start | bytes 5971968 | tf_op jit(solution)/shard_map/all_gather | solution.py:745
  11.6 2.3 collective-permute-start
  15.1 655.6 %reduce-scatter.5.cloned.1.call-start = ((), (), s32[]{:S(2)}) async-start(), calls=%async_computation.4 | async-start | bytes 5971968 | tf_op jit(solution)/shard_map/reduce_scatter | solution.py:825
  15.3 43.4 %copy-start.62 = (bf16[144,2425]{1,0:T(8,128)(2,1)}, bf16[144,2425]{1,0:T(8,128)(2,1)S(1)}, u32[]{:S(2)}) copy-start(bf16[144,2425]{1,0:T(8,128)(2,1)S(1)} %bitcast_convert_fusion) | copy-start | bytes 2095204
  16.7 42.7 %copy-start.45 = (bf16[144,2336]{1,0:T(8,128)(2,1)}, bf16[144,2336]{1,0:T(8,128)(2,1)S(1)}, u32[]{:S(2)}) copy-start(bf16[144,2336]{1,0:T(8,128)(2,1)S(1)} %convert_element_type.440) | copy-start | bytes 2018308
  99.4 130.2 %copy-start.156 = (f32[256]{0:T(256)}, f32[256]{0:T(256)S(1)}, u32[]{:S(2)}) copy-start(f32[256]{0:T(256)S(1)} %broadcast_multiply_fusion.4) | copy-start | bytes 3076
  99.7 129.9 %copy-start.163 = (f32[256]{0:T(256)}, f32[256]{0:T(256)S(1)}, u32[]{:S(2)}) copy-start(f32[256]{0:T(256)S(1)} %add_rsqrt_fusion.1) | copy-start | bytes 3076
  99.8 129.8 %copy-start.88 = (f32[1152]{0:T(1024)}, f32[1152]{0:T(1024)S(1)}, u32[]{:S(2)}) copy-start(f32[1152]{0:T(1024)S(1)} %get-tuple-element.138) | copy-start | bytes 13828
  99.8 129.8 %copy-start.104 = (f32[1152]{0:T(1024)}, f32[1152]{0:T(1024)S(1)}, u32[]{:S(2)}) copy-start(f32[1152]{0:T(1024)S(1)} %get-tuple-element.137) | copy-start | bytes 13828
  101.1 128.5 %copy-start.147 = (f32[2304]{0:T(1024)}, f32[2304]{0:T(1024)S(1)}, u32[]{:S(2)}) copy-start(f32[2304]{0:T(1024)S(1)} %get-tuple-element.119) | copy-start | bytes 27652
  234.9 34.8 %collective-permute-start.2 = (bf16[1152,2304]{1,0:T(8,128)(2,1)}, bf16[1152,2304]{1,0:T(8,128)(2,1)}, u32[]{:S(2)}, u32[]{:S(2)}) collective-permute-start(bf16[1152,2304]{1,0:T(8,128)(2,1)} %bitcast.406), channel_id=1, source_target_pairs={{0,1},{1,0},{2,3},{3,2},{4,5},{5,4},{6,7},{7,6},{8,9},{9,8},{10,11... | collective-permute-start | bytes 15925256 | tf_op jit(solution)/shard_map/ppermute | solution.py:719
  245.0 24.7 %collective-permute-start.1 = (bf16[1152,2304]{1,0:T(8,128)(2,1)}, bf16[1152,2304]{1,0:T(8,128)(2,1)}, u32[]{:S(2)}, u32[]{:S(2)}) collective-permute-start(bf16[1152,2304]{1,0:T(8,128)(2,1)} %all-gather.4.cloned.1.call-done), channel_id=1, source_target_pairs={{0,1},{1,0},{2,3},{3,2},{4,5},{5,4},{6,7},{7,6},{8,9},{9,8},{10,11... | collective-permute-start | bytes 15925256 | tf_op jit(solution)/shard_map/ppermute | solution.py:719
  278.8 16.0 %collective-permute-start.3 = (bf16[256,1152]{1,0:T(8,128)(2,1)}, bf16[256,1152]{1,0:T(8,128)(2,1)S(1)}, u32[]{:S(2)}, u32[]{:S(2)}) collective-permute-start(bf16[256,1152]{1,0:T(8,128)(2,1)} %fusion.58), channel_id=1, source_target_pairs={{0,2},{1,3},{2,0},{3,1},{4,6},{5,7},{6,4},{7,5},{8,10},{9,11},{10,... | collective-permute-start | bytes 1769480 | tf_op jit(solution)/shard_map/ppermute | solution.py:719
  304.7 75.8 %copy-start.28 = (bf16[256,1152]{0,1:T(8,128)(2,1)}, bf16[256,1152]{0,1:T(8,128)(2,1)S(1)}, u32[]{:S(2)}) copy-start(bf16[256,1152]{0,1:T(8,128)(2,1)S(1)} %copy.101) | copy-start | bytes 1769476
  390.0 15.2 %collective-permute-start.4 = (bf16[256,1152]{1,0:T(8,128)(2,1)}, bf16[256,1152]{1,0:T(8,128)(2,1)S(1)}, u32[]{:S(2)}, u32[]{:S(2)}) collective-permute-start(bf16[256,1152]{1,0:T(8,128)(2,1)} %fusion.118), channel_id=1, source_target_pairs={{0,2},{1,3},{2,0},{3,1},{4,6},{5,7},{6,4},{7,5},{8,10},{9,11},{10,... | collective-permute-start | bytes 1769480 | tf_op jit(solution)/shard_map/ppermute | solution.py:719
  391.5 17.3 %collective-permute-start.13 = (bf16[256,2304]{1,0:T(8,128)(2,1)}, bf16[256,2304]{1,0:T(8,128)(2,1)}, u32[]{:S(2)}, u32[]{:S(2)}) collective-permute-start(bf16[256,2304]{1,0:T(8,128)(2,1)} %get-tuple-element.158), channel_id=1, source_target_pairs={{0,1},{1,0},{2,3},{3,2},{4,5},{5,4},{6,7},{7,6},{8,9},{9,8},{10,11... | collective-permute-start | bytes 3538952 | tf_op jit(solution)/shard_map/ppermute | solution.py:719
  406.8 2.0 collective-permute-start.12
  415.9 256.2 %reduce-scatter.3.cloned.1.call-start = ((), (), s32[]{:S(2)}) async-start(), calls=%async_computation.3 | async-start | bytes 5971968 | tf_op jit(solution)/shard_map/reduce_scatter | solution.py:826
  416.0 52.2 %collective-permute-start.9 = (bf16[256,1152]{1,0:T(8,128)(2,1)}, bf16[256,1152]{1,0:T(8,128)(2,1)}, u32[]{:S(2)}, u32[]{:S(2)}) collective-permute-start(bf16[256,1152]{1,0:T(8,128)(2,1)} %fusion.115), channel_id=1, source_target_pairs={{0,1},{1,0},{2,3},{3,2},{4,5},{5,4},{6,7},{7,6},{8,9},{9,8},{10,11... | collective-permute-start | bytes 1769480 | tf_op jit(solution)/shard_map/ppermute | solution.py:719
  416.2 168.3 %collective-permute-start.5 = (bf16[256,1152]{1,0:T(8,128)(2,1)}, bf16[256,1152]{1,0:T(8,128)(2,1)}, u32[]{:S(2)}, u32[]{:S(2)}) collective-permute-start(bf16[256,1152]{1,0:T(8,128)(2,1)} %add_convert_fusion.9), channel_id=1, source_target_pairs={{0,1},{1,0},{2,3},{3,2},{4,5},{5,4},{6,7},{7,6},{8,9},{9,8},{10,11... | collective-permute-start | bytes 1769480 | tf_op jit(solution)/shard_map/ppermute | solution.py:719
  420.6 168.1 %collective-permute-start.7 = (bf16[256,1152]{1,0:T(8,128)(2,1)}, bf16[256,1152]{1,0:T(8,128)(2,1)}, u32[]{:S(2)}, u32[]{:S(2)}) collective-permute-start(bf16[256,1152]{1,0:T(8,128)(2,1)} %broadcast_select_fusion.3), channel_id=1, source_target_pairs={{0,1},{1,0},{2,3},{3,2},{4,5},{5,4},{6,7},{7,6},{8,9},{9,8},{10,11... | collective-permute-start | bytes 1769480 | tf_op jit(solution)/shard_map/ppermute | solution.py:719
  429.3 38.9 %collective-permute-start.10 = (bf16[256,2304]{1,0:T(8,128)(2,1)}, bf16[256,2304]{1,0:T(8,128)(2,1)}, u32[]{:S(2)}, u32[]{:S(2)}) collective-permute-start(bf16[256,2304]{1,0:T(8,128)(2,1)} %get-tuple-element.83), channel_id=1, source_target_pairs={{0,1},{1,0},{2,3},{3,2},{4,5},{5,4},{6,7},{7,6},{8,9},{9,8},{10,11... | collective-permute-start | bytes 3538952 | tf_op jit(solution)/shard_map/ppermute | solution.py:719
  461.7 100.4 %copy-start.35 = (bf16[256,1152]{1,0:T(8,128)(2,1)}, bf16[256,1152]{1,0:T(8,128)(2,1)S(1)}, u32[]{:S(2)}) copy-start(bf16[256,1152]{1,0:T(8,128)(2,1)S(1)} %copy.122) | copy-start | bytes 1769476
  482.1 49.8 %copy-start.5 = (f32[1,144,3456]{2,1,0:T(8,128)S(1)}, f32[1,144,3456]{2,1,0:T(8,128)}, u32[]{:S(2)}) copy-start(f32[1,144,3456]{2,1,0:T(8,128)} %param.30) | copy-start | bytes 5971972
  484.7 47.6 %copy-start.81 = (f32[144,16]{0,1:T(8,128)S(1)}, f32[144,16]{0,1:T(8,128)}, u32[]{:S(2)}) copy-start(f32[144,16]{0,1:T(8,128)} %copy-done.80) | copy-start | bytes 27652
  563.0 21.6 %collective-permute-start.6 = (bf16[256,1152]{1,0:T(8,128)(2,1)}, bf16[256,1152]{1,0:T(8,128)(2,1)}, u32[]{:S(2)}, u32[]{:S(2)}) collective-permute-start(bf16[256,1152]{1,0:T(8,128)(2,1)} %broadcast_select_fusion.5), channel_id=1, source_target_pairs={{0,1},{1,0},{2,3},{3,2},{4,5},{5,4},{6,7},{7,6},{8,9},{9,8},{10,11... | collective-permute-start | bytes 1769480 | tf_op jit(solution)/shard_map/ppermute | solution.py:719
  577.9 10.8 %collective-permute-start.8 = (bf16[256,1152]{1,0:T(8,128)(2,1)}, bf16[256,1152]{1,0:T(8,128)(2,1)}, u32[]{:S(2)}, u32[]{:S(2)}) collective-permute-start(bf16[256,1152]{1,0:T(8,128)(2,1)} %broadcast_select_fusion.4), channel_id=1, source_target_pairs={{0,1},{1,0},{2,3},{3,2},{4,5},{5,4},{6,7},{7,6},{8,9},{9,8},{10,11... | collective-permute-start | bytes 1769480 | tf_op jit(solution)/shard_map/ppermute | solution.py:719
  670.7 15.3 %collective-permute-start.15 = (bf16[144,2304]{1,0:T(8,128)(2,1)}, bf16[144,2304]{1,0:T(8,128)(2,1)S(1)}, u32[]{:S(2)}, u32[]{:S(2)}) collective-permute-start(bf16[144,2304]{1,0:T(8,128)(2,1)} %reduce-scatter.5.cloned.1.call-done), channel_id=1, source_target_pairs={{0,2},{1,3},{2,0},{3,1},{4,6},{5,7},{6,4},{7,5},{8,10},{9,11},{10,... | collective-permute-start | bytes 1990664 | tf_op jit(solution)/shard_map/ppermute | solution.py:719
  672.1 13.9 %collective-permute-start.14 = (bf16[144,2304]{1,0:T(8,128)(2,1)}, bf16[144,2304]{1,0:T(8,128)(2,1)S(1)}, u32[]{:S(2)}, u32[]{:S(2)}) collective-permute-start(bf16[144,2304]{1,0:T(8,128)(2,1)} %reduce-scatter.5.cloned.1.call-done), channel_id=1, source_target_pairs={{0,1},{1,0},{2,3},{3,2},{4,5},{5,4},{6,7},{7,6},{8,9},{9,8},{10,11... | collective-permute-start | bytes 1990664 | tf_op jit(solution)/shard_map/ppermute | solution.py:719
  673.8 13.2 %collective-permute-start.11 = (bf16[144,2304]{1,0:T(8,128)(2,1)S(1)}, bf16[144,2304]{1,0:T(8,128)(2,1)S(1)}, u32[]{:S(2)}, u32[]{:S(2)}) collective-permute-start(bf16[144,2304]{1,0:T(8,128)(2,1)S(1)} %convert_select_fusion.4), channel_id=1, source_target_pairs={{0,1},{1,0},{2,3},{3,2},{4,5},{5,4},{6,7},{7,6},{8,9},{9,8},{10,11... | collective-permute-start | bytes 1990664 | tf_op jit(solution)/shard_map/ppermute | solution.py:719
  686.0 4.8 collective-permute-start.16
  (182 other events, 1236.1 us)
Sparse Core Ops, SparseCore 0:
  10.8 123.9 all-gather.5
  137.5 107.4 all-gather.3
  416.1 104.2 reduce-scatter.4
  524.8 125.8 reduce-scatter.2

commit v4 on v3

--- a/solution.py
+++ b/solution.py
@@ -58,14 +58,6 @@
 
 def silu_back(value, grad):
     return jax.vjp(jax.nn.silu, value)[1](grad)[0]
-
-
-def layer_modulate(tokens, shift, scale):
-    centered = tokens - jnp.mean(tokens, axis=-1, keepdims=True)
-    normed = centered * lax.rsqrt(
-        jnp.mean(centered * centered, axis=-1, keepdims=True) + epsilon_norm
-    )
-    return normed * (1.0 + scale) + shift
 
 
 def patchify(field):
@@ -300,16 +292,18 @@
 
 
 VMEM_BYTES = 60 * 1024 * 1024
+SUM_CHUNKS = tuple((which,) + chunk for which in range(2) for chunk in CHUNKS)
 
 
 def sum_kernel(
-    g_ref, out, own_b, other_d, xb, xq, up_b, up_o, down_b, down_o, acc,
+    g_first, g_second, out, own_b, other_d, xb, xq, up_b, up_o, down_b, down_o, acc,
     load_sem, x_send, x_recv, up_send, up_recv, down_send, down_recv,
 ):
     me = lax.axis_index("dp")
     z, x = me // X, lax.rem(me, X)
     across = me + 1 - 2 * x
-    chunks = len(CHUNKS)
+    sources = (g_first, g_second)
+    chunks = len(SUM_CHUNKS)
     has_up, has_down = z < Z - 1, z > 0
 
     barrier = pltpu.get_barrier_semaphore()
@@ -337,28 +331,31 @@
             run(z - distance, False)
 
     def part(k):
-        return pl.ds(CHUNKS[k][0], CHUNKS[k][1])
+        return pl.ds(SUM_CHUNKS[k][1], SUM_CHUNKS[k][2])
 
     def hbm(k, zz, column):
-        start = pl.multiple_of((zz * X + column) * 144 + CHUNKS[k][0], 16)
-        return g_ref.at[pl.ds(start, CHUNKS[k][1])]
+        start = pl.multiple_of((zz * X + column) * 144 + SUM_CHUNKS[k][1], 16)
+        return sources[SUM_CHUNKS[k][0]].at[pl.ds(start, SUM_CHUNKS[k][2])]
 
     def own(k, zz):
-        return own_b.at[zz, part(k)]
+        return own_b.at[SUM_CHUNKS[k][0], zz, part(k)]
 
     def from_x(k, zz):
-        return xq if CHUNKS[k][2] else xb.at[zz, part(k)]
+        return xq.at[SUM_CHUNKS[k][0]] if SUM_CHUNKS[k][3] else xb.at[SUM_CHUNKS[k][0], zz, part(k)]
 
     def from_z(k, zz, up, other):
         if other:
-            return (up_o if up else down_o).at[zz]
-        return (up_b if up else down_b).at[zz, part(k)]
+            return (up_o if up else down_o).at[SUM_CHUNKS[k][0], zz]
+        return (up_b if up else down_b).at[SUM_CHUNKS[k][0], zz, part(k)]
+
+    def other_of(k, zz):
+        return other_d.at[SUM_CHUNKS[k][0], zz]
 
     def load(k, zz, other=False):
         index = ((chunks if other else 0) + k) * Z + zz
         return pltpu.make_async_copy(
             hbm(k, zz, (1 - x) if other else x),
-            other_d.at[zz] if other else own(k, zz),
+            other_of(k, zz) if other else own(k, zz),
             load_sem.at[index],
         )
 
@@ -372,7 +369,7 @@
     def z_copy(k, zz, up, other):
         unit = ((chunks if other else 0) + k) * Z + zz
         return pltpu.make_async_remote_copy(
-            src_ref=other_d.at[zz] if other else own(k, zz),
+            src_ref=other_of(k, zz) if other else own(k, zz),
             dst_ref=from_z(k, zz, up, other),
             send_sem=(up_send if up else down_send).at[unit],
             recv_sem=(up_recv if up else down_recv).at[unit],
@@ -381,7 +378,7 @@
         )
 
     def total(k, dst, srcs):
-        @pl.loop(0, CHUNKS[k][1] // 16)
+        @pl.loop(0, SUM_CHUNKS[k][2] // 16)
         def _(step):
             rows = pl.ds(pl.multiple_of(step * 16, 16), 16)
             value = srcs[0][rows].astype(jnp.float32)
@@ -393,23 +390,24 @@
         for k in range(chunks):
             def run(zz, up):
                 load(k, zz).start()
-                if CHUNKS[k][2]:
+                if SUM_CHUNKS[k][3]:
                     load(k, zz, True).start()
             each(distance, run)
 
     pl.semaphore_wait(barrier, 1 + has_up.astype(jnp.int32) + has_down.astype(jnp.int32))
 
-    for distance in (3, 2, 1, 0):
-        for k in range(chunks):
-            if not CHUNKS[k][2]:
-                each(distance, lambda zz, up: x_copy(k, zz, hbm(k, zz, 1 - x)).start())
+    for which in range(2):
+        for distance in (3, 2, 1, 0):
+            for k in range(chunks):
+                if SUM_CHUNKS[k][0] == which and not SUM_CHUNKS[k][3]:
+                    each(distance, lambda zz, up: x_copy(k, zz, hbm(k, zz, 1 - x)).start())
 
     def pass_on(k, distance):
         def run(zz, up):
             behind = has_down if up else has_up
-            if CHUNKS[k][2]:
+            if SUM_CHUNKS[k][3]:
                 for other in (False, True):
-                    mine = other_d.at[zz] if other else own(k, zz)
+                    mine = other_of(k, zz) if other else own(k, zz)
                     load(k, zz, other).wait()
 
                     @pl.when(behind)
@@ -447,64 +445,67 @@
 
     def send_direct(k):
         load(k, z, True).wait()
-        total(k, acc, [other_d.at[z]])
+        total(k, acc, [other_of(k, z)])
         add_z(acc, k, True)
-        total(k, other_d.at[z], [acc])
-        x_copy(k, z, other_d.at[z]).start()
+        total(k, other_of(k, z), [acc])
+        x_copy(k, z, other_of(k, z)).start()
 
     def finish(k):
-        dst = out.at[part(k)]
+        dst = out.at[SUM_CHUNKS[k][0], part(k)]
         load(k, z).wait()
-        if CHUNKS[k][2]:
+        if SUM_CHUNKS[k][3]:
             total(k, dst, [own(k, z)])
             add_z(dst, k, False)
-            x_copy(k, z, other_d.at[z]).wait_recv()
+            x_copy(k, z, other_of(k, z)).wait_recv()
             total(k, dst, [dst, from_x(k, z)])
         else:
             x_copy(k, z, hbm(k, z, 1 - x)).wait_recv()
             total(k, dst, [own(k, z), from_x(k, z)])
             add_z(dst, k, False)
 
-    straight = [k for k in range(chunks) if not CHUNKS[k][2]]
-    direct = [k for k in range(chunks) if CHUNKS[k][2]]
-    for distance in (3, 2, 1):
-        for k in range(chunks):
-            pass_on(k, distance)
-    for k in direct:
-        send_direct(k)
+    straight = [k for k in range(chunks) if not SUM_CHUNKS[k][3]]
+    direct = [k for k in range(chunks) if SUM_CHUNKS[k][3]]
+    for which in range(2):
+        of = lambda group: [k for k in group if SUM_CHUNKS[k][0] == which]
+        for distance in (3, 2, 1):
+            for k in of(range(chunks)):
+                pass_on(k, distance)
+        for k in of(direct):
+            send_direct(k)
     for k in straight + direct:
         finish(k)
 
     for k in range(chunks):
         for distance in (3, 2, 1, 0):
             def run(zz, up):
-                if not CHUNKS[k][2]:
+                if not SUM_CHUNKS[k][3]:
                     x_copy(k, zz, hbm(k, zz, 1 - x)).wait_send()
                 elif distance == 0:
-                    x_copy(k, zz, other_d.at[zz]).wait_send()
+                    x_copy(k, zz, other_of(k, zz)).wait_send()
                 if distance:
                     z_copy(k, zz, up, False).wait_send()
-                    if CHUNKS[k][2]:
+                    if SUM_CHUNKS[k][3]:
                         z_copy(k, zz, up, True).wait_send()
             each(distance, run)
 
 
-def sum_gradients(grad):
+def sum_gradients(first, second):
     n = lax.axis_size("dp")
     if not ring_fits(n, D // n):
-        return lax.psum_scatter(grad, "dp", scatter_dimension=0, tiled=True).astype(jnp.float32)
-    chunks = len(CHUNKS)
+        total = lambda grad: lax.psum_scatter(grad, "dp", scatter_dimension=0, tiled=True)
+        return jnp.stack([total(first), total(second)]).astype(jnp.float32)
+    chunks = len(SUM_CHUNKS)
     dma = lambda count: pltpu.SemaphoreType.DMA((count,))
-    ring = pltpu.VMEM((Z, 144, HALF), BF)
-    short = [rows for first, rows, direct in CHUNKS if direct][0]
-    ring_o = pltpu.VMEM((Z, short, HALF), BF)
+    ring = pltpu.VMEM((2, Z, 144, HALF), BF)
+    short = [rows for start, rows, direct in CHUNKS if direct][0]
+    ring_o = pltpu.VMEM((2, Z, short, HALF), BF)
     return pl.pallas_call(
         sum_kernel,
-        out_shape=jax.ShapeDtypeStruct((144, HALF), jnp.float32),
-        in_specs=[pl.BlockSpec(memory_space=pl.ANY)],
+        out_shape=jax.ShapeDtypeStruct((2, 144, HALF), jnp.float32),
+        in_specs=[pl.BlockSpec(memory_space=pl.ANY)] * 2,
         out_specs=pl.BlockSpec(memory_space=pltpu.VMEM),
         scratch_shapes=[
-            ring, ring_o, ring, pltpu.VMEM((short, HALF), BF),
+            ring, ring_o, ring, pltpu.VMEM((2, short, HALF), BF),
             ring, ring_o, ring, ring_o, pltpu.VMEM((short, HALF), jnp.float32),
             dma(2 * chunks * Z), dma(chunks * Z), dma(chunks * Z),
             dma(2 * chunks * Z), dma(2 * chunks * Z), dma(2 * chunks * Z), dma(2 * chunks * Z),
@@ -512,9 +513,9 @@
         compiler_params=pltpu.CompilerParams(
             collective_id=1, has_side_effects=True, vmem_limit_bytes=VMEM_BYTES
         ),
-        cost_estimate=pl.CostEstimate(flops=0, bytes_accessed=200_000_000, transcendentals=0),
+        cost_estimate=pl.CostEstimate(flops=0, bytes_accessed=300_000_000, transcendentals=0),
         name="sum_gradients",
-    )(grad)
+    )(first, second)
 
 
 def exchange_kernel(axes, modes, *refs):
@@ -608,6 +609,197 @@
     return -(-length // (128 * unit)) * unit
 
 
+TILE = 768
+STEPS = HALF // TILE
+GELU_SCALE = math.sqrt(2.0 / math.pi)
+
+
+def mean_rows(value):
+    return jnp.mean(value, axis=-1, keepdims=True)
+
+
+def normalized(x):
+    centered = x - mean_rows(x)
+    inverse = lax.rsqrt(mean_rows(centered * centered) + epsilon_norm)
+    return (centered * inverse, inverse)
+
+
+def modulated_back(normed, inverse, scale, d_xm):
+    d_normed = d_xm * (1.0 + scale)
+    d_x = inverse * (d_normed - mean_rows(d_normed) - normed * mean_rows(d_normed * normed))
+    return (d_x, jnp.sum(d_xm, axis=0), jnp.sum(d_xm * normed, axis=0))
+
+
+def mlp_forward_kernel(
+    x_ref, mod_ref, b_up_ref, b_down_ref, up_a, up_b, dn_a, dn_b,
+    out_ref, xm_ref, branch_ref, pre_ref, act_ref, acc,
+):
+    step = pl.program_id(0)
+
+    @pl.when(step == 0)
+    def _():
+        normed, unused = normalized(x_ref[...])
+        xm_ref[...] = to_half(normed * (1.0 + mod_ref[1:2]) + mod_ref[0:1])
+        acc[...] = jnp.zeros_like(acc)
+
+    def tile(up, dn):
+        pre = matmul(xm_ref[...], up[...]) + b_up_ref[...]
+        cube = pre + 0.044715 * (pre * pre * pre)
+        act = to_half(pre * (0.5 * (1.0 + jnp.tanh(GELU_SCALE * cube))))
+        pre_ref[...] = pre
+        act_ref[...] = act
+        acc[...] += matmul_nt(act, dn[...])
+
+    @pl.when(step < STEPS)
+    def _():
+        tile(up_a, dn_a)
+
+    @pl.when(step >= STEPS)
+    def _():
+        tile(up_b, dn_b)
+
+    @pl.when(step == 2 * STEPS - 1)
+    def _():
+        branch = acc[...] + b_down_ref[...]
+        branch_ref[...] = branch
+        out_ref[...] = x_ref[...] + mod_ref[2:3] * branch
+
+
+def mlp_backward_kernel(
+    d_ref, x_ref, mod_ref, branch_ref, pre_ref, up_a, up_b, dn_a, dn_b,
+    d_in_ref, d_mod_ref, grad_ref, d_pre_ref, acc,
+):
+    step = pl.program_id(0)
+
+    @pl.when(step == 0)
+    def _():
+        grad_ref[...] = to_half(d_ref[...] * mod_ref[2:3])
+        acc[...] = jnp.zeros_like(acc)
+
+    def tile(up, dn):
+        d_act = matmul(grad_ref[...], dn[...])
+        pre = pre_ref[...]
+        square = pre * pre
+        tanh = jnp.tanh(GELU_SCALE * (pre + 0.044715 * (square * pre)))
+        slope = 0.5 * (1.0 + tanh) + (0.5 * pre) * (1.0 - tanh * tanh) * (
+            GELU_SCALE * (1.0 + (3.0 * 0.044715) * square)
+        )
+        d_pre = to_half(d_act * slope)
+        d_pre_ref[...] = d_pre
+        acc[...] += matmul_nt(d_pre, up[...])
+
+    @pl.when(step < STEPS)
+    def _():
+        tile(up_a, dn_a)
+
+    @pl.when(step >= STEPS)
+    def _():
+        tile(up_b, dn_b)
+
+    @pl.when(step == 2 * STEPS - 1)
+    def _():
+        normed, inverse = normalized(x_ref[...])
+        d_x, d_shift, d_scale = modulated_back(normed, inverse, mod_ref[1:2], acc[...])
+        d_in_ref[...] = to_half(d_ref[...] + d_x)
+        d_mod_ref[0:1] = d_shift[None]
+        d_mod_ref[1:2] = d_scale[None]
+        d_mod_ref[2:3] = jnp.sum(d_ref[...] * branch_ref[...], axis=0)[None]
+
+
+def whole_spec(shape):
+    return pl.BlockSpec(shape, lambda step: (0,) * len(shape))
+
+
+def tile_specs():
+    first = lambda step: (0, jnp.minimum(step, STEPS - 1))
+    second = lambda step: (0, jnp.maximum(step - STEPS, 0))
+    return [pl.BlockSpec((D, TILE), first), pl.BlockSpec((D, TILE), second)] * 2
+
+
+def mlp_forward(x, mod, b_up, b_down, w_up, w_dn):
+    token = whole_spec((PATCHES, D))
+    hidden = pl.BlockSpec((PATCHES, TILE), lambda step: (0, step))
+    f32 = jax.ShapeDtypeStruct((PATCHES, D), jnp.float32)
+    return pl.pallas_call(
+        mlp_forward_kernel,
+        grid=(2 * STEPS,),
+        out_shape=(
+            f32, jax.ShapeDtypeStruct((PATCHES, D), BF), f32,
+            jax.ShapeDtypeStruct((PATCHES, FF), jnp.float32), jax.ShapeDtypeStruct((PATCHES, FF), BF),
+        ),
+        in_specs=[
+            token, whole_spec((3, D)), pl.BlockSpec((1, TILE), lambda step: (0, step)), whole_spec((1, D)),
+        ] + tile_specs(),
+        out_specs=(token, token, token, hidden, hidden),
+        scratch_shapes=[pltpu.VMEM((PATCHES, D), jnp.float32)],
+        compiler_params=pltpu.CompilerParams(vmem_limit_bytes=VMEM_BYTES),
+        cost_estimate=pl.CostEstimate(
+            flops=4 * PATCHES * D * FF, bytes_accessed=4 * D * FF, transcendentals=PATCHES * FF
+        ),
+        name="mlp_forward",
+    )(x, mod, b_up, b_down, *w_up, *w_dn)
+
+
+def mlp_backward(d_out, x, mod, branch, pre, w_up, w_dn):
+    token = whole_spec((PATCHES, D))
+    hidden = pl.BlockSpec((PATCHES, TILE), lambda step: (0, step))
+    half = jax.ShapeDtypeStruct((PATCHES, D), BF)
+    return pl.pallas_call(
+        mlp_backward_kernel,
+        grid=(2 * STEPS,),
+        out_shape=(
+            half, jax.ShapeDtypeStruct((3, D), jnp.float32), half,
+            jax.ShapeDtypeStruct((PATCHES, FF), BF),
+        ),
+        in_specs=[token, token, whole_spec((3, D)), token, hidden] + tile_specs(),
+        out_specs=(token, whole_spec((3, D)), token, hidden),
+        scratch_shapes=[pltpu.VMEM((PATCHES, D), jnp.float32)],
+        compiler_params=pltpu.CompilerParams(vmem_limit_bytes=VMEM_BYTES),
+        cost_estimate=pl.CostEstimate(
+            flops=4 * PATCHES * D * FF, bytes_accessed=4 * D * FF, transcendentals=PATCHES * FF
+        ),
+        name="mlp_backward",
+    )(d_out, x, mod, branch, pre, *w_up, *w_dn)
+
+
+SUM_ROWS = 16
+
+
+def collect_kernel(peers, flags_ref, *refs):
+    tokens, d_pre_ref, mods, fm_ref, extra_ref = refs[:6], refs[6], refs[7:9], refs[9], refs[10]
+    sums_ref, mods_ref = refs[11:]
+    core, stage = flags_ref[0], flags_ref[1]
+    ones = jnp.ones((8, PATCHES), BF)
+    total = lambda value: matmul(ones, value)[0:1]
+    sums_ref[...] = jnp.zeros_like(sums_ref)
+    rows = [total(ref[...]) for ref in tokens]
+    halves = [[total(d_pre_ref[:, D * k : D * (k + 1)]) for k in range(4)]]
+    own = halves[0]
+    order = [jnp.where(core == 0, own[k], own[(k + 2) % 4]) for k in range(4)]
+    last = jnp.where(stage == 0, rows[5], extra_ref[0:1])
+    for place, row in enumerate(rows[:4] + order + [rows[4], last, extra_ref[1:2]]):
+        sums_ref[place : place + 1, :D] = row
+    for k in range(2):
+        block = jnp.concatenate([mods[k][...], fm_ref[...]], axis=0)
+        mods_ref[k] = to_half(jnp.concatenate([block, jnp.zeros((16 - 5, D), jnp.float32)], axis=0))
+
+
+def collect(flags, tokens, d_pre, mods, fm, extra):
+    peers = 2 * lax.axis_size("dp")
+    vmem = pl.BlockSpec(memory_space=pltpu.VMEM)
+    return pl.pallas_call(
+        partial(collect_kernel, peers),
+        out_shape=(
+            jax.ShapeDtypeStruct((SUM_ROWS, 128 * max(peers, 9)), jnp.float32),
+            jax.ShapeDtypeStruct((2, 16, D), BF),
+        ),
+        in_specs=[pl.BlockSpec(memory_space=pltpu.SMEM)] + [vmem] * 11,
+        out_specs=(vmem, vmem),
+        compiler_params=pltpu.CompilerParams(vmem_limit_bytes=VMEM_BYTES),
+        name="collect",
+    )(flags, *tokens, d_pre, *mods, fm, extra)
+
+
 def heads_of(value):
     return value.reshape(PATCHES, HEADS, HEAD_DIM)
 
@@ -649,61 +841,37 @@
     return (d_xm, d_query, d_key, d_value)
 
 
-def modulated(x, mod):
-    return layer_modulate(x, mod[None, :D], mod[None, D : 2 * D])
-
-
-def modulated_back(x, mod, d_xm):
-    pull = jax.vjp(layer_modulate, x, mod[None, :D], mod[None, D : 2 * D])[1]
-    d_x, d_shift, d_scale = pull(d_xm)
-    return (d_x, d_shift[0], d_scale[0])
-
-
 def stage_forward(x_in, weights):
     mod_a, mod_m, w_attn, w_up, w_dn, b_attn, b_up, b_down = weights
-    xm_a = to_half(modulated(x_in, mod_a))
+    normed, inverse = normalized(x_in)
+    xm_a = to_half(normed * (1.0 + mod_a[1:2]) + mod_a[0:1])
     branch_a, saved = attention_forward(xm_a, w_attn, b_attn)
-    x_mid = to_half(x_in + mod_a[None, 2 * D :] * branch_a).astype(jnp.float32)
-    xm_m = to_half(modulated(x_mid, mod_m))
-    pre = [matmul(xm_m, w_up[k]) + b_up[k] for k in range(2)]
-    act = [to_half(jax.nn.gelu(half, approximate=True)) for half in pre]
-    branch_m = matmul_nt(act[0], w_dn[0]) + matmul_nt(act[1], w_dn[1]) + b_down
-    x_out = x_mid + mod_m[None, 2 * D :] * branch_m
-    return (x_out, (xm_a, branch_a, saved, x_mid, xm_m, pre, act, branch_m))
-
-
-def mlp_backward(d_out, weights, kept):
-    mod_a, mod_m, w_attn, w_up, w_dn, b_attn, b_up, b_down = weights
-    xm_a, branch_a, saved, x_mid, xm_m, pre, act, branch_m = kept
-    d_gate = jnp.sum(d_out * branch_m, axis=0)
-    grad_half = to_half(d_out * mod_m[None, 2 * D :])
-    gelu_back = lambda half, grad: jax.vjp(partial(jax.nn.gelu, approximate=True), half)[1](grad)[0]
-    d_pre = [to_half(gelu_back(pre[k], matmul(grad_half, w_dn[k]))) for k in range(2)]
-    d_xm = matmul_nt(d_pre[0], w_up[0]) + matmul_nt(d_pre[1], w_up[1])
-    d_x, d_shift, d_scale = modulated_back(x_mid, mod_m, d_xm)
-    d_mod = to_half(jnp.concatenate([d_shift, d_scale, d_gate]))
-    return (to_half(d_out + d_x).astype(jnp.float32), d_mod, grad_half, d_pre)
+    x_mid = to_half(x_in + mod_a[2:3] * branch_a).astype(jnp.float32)
+    x_out, xm_m, branch_m, pre, act = mlp_forward(x_mid, mod_m, b_up, b_down, w_up, w_dn)
+    return (x_out, (xm_a, branch_a, saved, x_mid, xm_m, branch_m, pre, act))
 
 
 def attn_backward(d_out, x_in, weights, kept):
     mod_a, mod_m, w_attn, w_up, w_dn, b_attn, b_up, b_down = weights
-    xm_a, branch_a, saved, x_mid, xm_m, pre, act, branch_m = kept
+    branch_a, saved = kept[1:3]
     d_gate = jnp.sum(d_out * branch_a, axis=0)
-    grad_half = to_half(d_out * mod_a[None, 2 * D :])
+    grad_half = to_half(d_out * mod_a[2:3])
     d_xm, d_query, d_key, d_value = attention_backward(grad_half, saved, w_attn)
-    d_x, d_shift, d_scale = modulated_back(x_in, mod_a, d_xm)
-    d_mod = to_half(jnp.concatenate([d_shift, d_scale, d_gate]))
+    normed, inverse = normalized(x_in)
+    d_x, d_shift, d_scale = modulated_back(normed, inverse, mod_a[1:2], d_xm)
+    d_mod = jnp.stack([d_shift, d_scale, d_gate])
     return (to_half(d_out + d_x), d_mod, grad_half, (d_query, d_key, d_value))
 
 
 def final_step(x_out, fmod, w_head, b_head, target, counts, loss_scale):
-    xf_half = to_half(modulated(x_out, fmod))
+    normed, inverse = normalized(x_out)
+    xf_half = to_half(normed * (1.0 + fmod[1:2]) + fmod[0:1])
     error = matmul(xf_half, w_head) + b_head - target
     loss = counts * jnp.sum(error * error)
     d_pred = to_half(2.0 * loss_scale * counts * error)
     g_head = matmul_tn(xf_half, d_pred)
-    d_x, d_shift, d_scale = modulated_back(x_out, fmod, matmul_nt(d_pred, w_head))
-    return (loss, d_x, to_half(jnp.concatenate([d_shift, d_scale])), g_head, column_sums(d_pred))
+    d_x, d_shift, d_scale = modulated_back(normed, inverse, fmod[1:2], matmul_nt(d_pred, w_head))
+    return (loss, d_x, jnp.stack([d_shift, d_scale]), g_head, column_sums(d_pred))
 
 
 def nesterov(weight, moment, average, grad, factor):
@@ -788,14 +956,16 @@
     (mods,) = exchange(3, "stage", ("each",), parts.reshape(images, 48, 128))
     mods = jnp.sum(mods.reshape(n, 2, 48 * 128), axis=0)
     bias_of = lambda first, length: lax.dynamic_slice_in_dim(biases, first, length)
-    mod_a = mods[0, : 3 * D] + bias_of(6 * D * stage, 3 * D)
-    mod_b = mods[1, : 3 * D] + bias_of(6 * D * stage + 3 * D, 3 * D)
-    fmod = mods[0, 3 * D : 5 * D] + biases[33 * D : 35 * D]
+    mod_a = (mods[0, : 3 * D] + bias_of(6 * D * stage, 3 * D)).reshape(3, D)
+    mod_b = (mods[1, : 3 * D] + bias_of(6 * D * stage + 3 * D, 3 * D)).reshape(3, D)
+    fmod = (mods[0, 3 * D : 5 * D] + biases[33 * D : 35 * D]).reshape(2, D)
     weights = (
         mod_a, mod_b, w_attn, w_up, w_dn,
         bias_of(12 * D + 8 * D * stage, 4 * D),
-        [bias_of(16 * D + 8 * D * stage + HALF * half, HALF) for half in (core, 1 - core)],
-        bias_of(28 * D + D * stage, D),
+        jnp.concatenate(
+            [bias_of(16 * D + 8 * D * stage + HALF * half, HALF)[None] for half in (core, 1 - core)], axis=1
+        ),
+        bias_of(28 * D + D * stage, D)[None],
     )
 
     step = pick(timesteps, core).astype(jnp.float32)
@@ -812,18 +982,19 @@
     loss, d_final, d_fmod, g_head, b_head = final_step(
         x_out, fmod, w_head_all, biases[35 * D :], target, counts, loss_scale
     )
-    d_mid = mlp_backward(d_final, weights, kept)[0]
+    xm_a, branch_a, saved, x_mid, xm_b, branch_b, pre, act = kept
+    attended = saved[-1]
+    back = lambda d_out: mlp_backward(d_out, x_mid, mod_b, branch_b, pre, w_up, w_dn)
+    d_mid = back(d_final)[0].astype(jnp.float32)
     d_hop = swap(attn_backward(d_mid, x_in, weights, kept)[0], 2)
     d_out = jnp.where(stage == 1, d_final, d_hop.astype(jnp.float32))
-    xm_a, branch_a, saved, x_mid, xm_b, pre, act, branch_b = kept
-    attended = saved[-1]
-
-    d_mid, d_mod_b, d_branch_b, d_pre = mlp_backward(d_out, weights, kept)
-    act_sib, branch_sib, xm_sib, pre_sib = swap((act[1], d_branch_b, xm_b, d_pre[1]), 1)
-    g_dn = to_half(matmul_tn(d_branch_b, act[0]) + matmul_tn(branch_sib, act_sib))
-    g_up = to_half(matmul_tn(xm_b, d_pre[0]) + matmul_tn(xm_sib, pre_sib))
+
+    d_mid, d_mod_b, d_branch_b, d_pre = back(d_out)
+    d_mid = d_mid.astype(jnp.float32)
+    act_sib, branch_sib, xm_sib, pre_sib = swap((act[:, HALF:], d_branch_b, xm_b, d_pre[:, HALF:]), 1)
+    g_dn = to_half(matmul_tn(d_branch_b, act[:, :HALF]) + matmul_tn(branch_sib, act_sib))
+    g_up = to_half(matmul_tn(xm_b, d_pre[:, :HALF]) + matmul_tn(xm_sib, pre_sib))
     g_dn = lax.psum_scatter(g_dn, "dp", scatter_dimension=0, tiled=True)
-    g_up = lax.psum_scatter(g_up, "dp", scatter_dimension=0, tiled=True)
 
     d_first, d_mod_a, d_branch_a, d_qkv = attn_backward(d_mid, x_in, weights, kept)
     d_query, d_key, d_value = d_qkv
@@ -846,9 +1017,8 @@
         ],
         axis=1,
     )
-    g_attn = sum_gradients(g_attn)
-    crossing = swap(jnp.where(even, g_up, to_half(g_attn)), 1).astype(jnp.float32)
-    g_up = g_up.astype(jnp.float32)
+    g_up, g_attn = sum_gradients(g_up, g_attn)
+    crossing = swap(to_half(jnp.where(even, g_up, g_attn)), 1).astype(jnp.float32)
     g_blk = jnp.concatenate(
         [jnp.where(even, g_attn, crossing), jnp.where(even, crossing, g_up)], axis=1
     )
@@ -860,34 +1030,24 @@
     here, there = in_core(g_dn, g_sib), in_core(g_facing, g_corner)
     down_both = jnp.where(stage == 0, jnp.stack([here, there]), jnp.stack([there, here]))
 
-    last_stage = (stage == 1).astype(jnp.float32)
-    zeros_fm = jnp.zeros((2 * D + 384,), BF)
-    d_fmod = jnp.concatenate([jnp.where(stage == 1, d_fmod, zeros_fm[: 2 * D]), zeros_fm[2 * D :]])
-    d_mods = jnp.stack([jnp.concatenate([d_mod_a, d_fmod]), jnp.concatenate([d_mod_b, d_fmod])])
-    last_own = jnp.where(stage == 0, column_sums(d_first), jnp.pad(b_head, (0, D - HEAD_OUT)))
-    in_order = lambda own, sib: jnp.where(
-        even, jnp.concatenate([own, sib]), jnp.concatenate([sib, own])
-    )
-    own_biases = jnp.concatenate(
-        [
-            *map(column_sums, d_qkv), column_sums(d_branch_a), in_order(*map(column_sums, d_pre)),
-            column_sums(d_branch_b),
-            last_own, loss[None],
-        ]
-    )
-    piece = row_count(-(-own_biases.shape[0] // (2 * n)))
-    own_biases = rows_of(own_biases, 2 * n * piece).reshape(2 * n, piece, 128)
+    flags = jnp.stack([core, stage]).astype(jnp.int32)
+    extra = jnp.stack([jnp.pad(b_head, (0, D - HEAD_OUT)), jnp.pad(loss[None], (0, D - 1))])
+    d_fmod = jnp.where(stage == 1, d_fmod, jnp.zeros_like(d_fmod))
+    own_biases, d_mods = collect(
+        flags, d_qkv + (d_branch_a, d_branch_b, d_first), d_pre, (d_mod_a, d_mod_b), d_fmod, extra
+    )
     g_patch = jnp.pad(matmul_tn(d_first, tok_half), ((0, 0), (0, HEAD_OUT - PATCH_IN)))
     end_rows = row_count(width * HEAD_OUT)
     own_ends = jnp.where(stage == 0, g_patch, g_head).reshape(n, width * HEAD_OUT)
     own_ends = jnp.pad(own_ends, ((0, 0), (0, end_rows * 128 - width * HEAD_OUT))).reshape(n, end_rows, 128)
+    own_biases = own_biases.reshape(SUM_ROWS, -1, 128).transpose(1, 0, 2)[: 2 * n]
     d_mods, own_biases, own_ends = exchange(
-        4, "stage", ("core", "each", "dp"), d_mods.reshape(2, 48, 128), own_biases, own_ends
-    )
-    d_mods = d_mods.reshape(images, 48 * 128)
+        4, "stage", ("core", "each", "dp"), d_mods, own_biases, own_ends
+    )
     bias_piece = jnp.sum(own_biases, axis=0)
     own_ends = jnp.sum(own_ends, axis=0)
-    d_mod_all, d_fm_all = d_mods[:, : 3 * D], d_mods[:, 3 * D : 5 * D]
+    d_mod_all = d_mods[:, :3].reshape(images, 3 * D)
+    d_fm_all = d_mods[:, 3:5].reshape(images, 2 * D)
     g_mod = matmul(silu_own, d_mod_all)
     c_own = matmul_nt(mod_half_w, d_mod_all)
     c_own = c_own + matmul_nt(tail_half[:, : 2 * D], jnp.where(section == 3, d_fm_all, jnp.zeros_like(d_fm_all)))
@@ -930,8 +1090,12 @@
     news = jnp.pad(news, ((0, -news.shape[0] % 8), (0, 0)))
     (news,) = exchange(7, "every", ("all",), news)
     news = news.reshape(n, 4, -1, 128)
+    piece = SUM_ROWS
     first, second = piece + mod_rows, piece + mod_rows + slice_rows
-    stages = [news[:, 2 * k : 2 * k + 2, :piece].reshape(-1) for k in range(2)]
+    stages = []
+    for k in range(2):
+        pieces = news[:, 2 * k : 2 * k + 2, :piece].reshape(2 * n, SUM_ROWS, 128)[: D // 128]
+        stages.append(pieces.transpose(1, 0, 2).reshape(-1))
     bias_mods = news[:, :, piece:first].reshape(n, 4, mod_rows * 128)[:, :, :mod_piece]
     bias_mods = bias_mods.transpose(1, 0, 2).reshape(-1)
     slices = news[:, 0, first:second].reshape(n, slice_rows * 128)[:, : 2 * width]

time: 770 us -> 877 us (1.14)
  waiting for transfers between devices: 46.1 us -> 140 us
  Pallas kernels: 321 us -> 405 us
  matrix products: 185 us -> 119 us
    pallas_call x1 -> x6, Pallas kernels: 76.9 us -> 194 us  [the longest x1 113 us: sum_gradients(): pl.pallas_call(sum_kernel, out_shape=jax.ShapeDtypeStruct((2, 144, HALF),...]
    all_gather x1, waiting for transfers between devices: 9.63 us -> 88.9 us  [body(): up_own = lax.all_gather(up_half, 'dp', axis=0, tiled=True)]
    pallas_call x1, Pallas kernels: 128 us -> 63.9 us  [gather_weights(): pl.pallas_call(gather_kernel, out_shape=jax.ShapeDtypeStruct((2, D, HALF)...]
    dot_general x21 -> x13, matrix products: 73.4 us -> 25.9 us  [matmul_nt(): lax.dot_general(left, right, (((1,), (1,)), ((), ())), preferred_element_...]
    pallas_call x6, Pallas kernels: 116 us -> 147 us  [exchange(): pl.pallas_call(partial(exchange_kernel, axes, modes), out_shape=tuple((ja...]
    all_gather x1, waiting for transfers between devices: 0.02 us -> 24.9 us  [body(): dn_own = lax.all_gather(dn_half, 'dp', axis=0, tiled=True)]
    unnamed x417 -> x244, local copies, waits for them, and re-layouts: 44.6 us -> 23 us
    dot_general x16 -> x12, matrix products: 50.8 us -> 31.1 us  [matmul(): return jnp.dot(left, right, preferred_element_type=jnp.float32)]
  transfers between devices with their start and end apart: 21 -> 20, of which waited for: 6 -> 7; matrix products, arithmetic and copies ran while one was open for 25% -> 19% of each run, Pallas kernels for 41% -> 39%
where the time goes in v4:
time: 877 us; the launch traced here: 869 us
  Pallas kernels  405 us (46%)
  waiting for transfers between devices  140 us (16%)
  matrix products  119 us (14%)
  other arithmetic  85.8 us (10%)
  local copies, waits for them, and re-layouts  85.7 us (10%)
  between operations  24.4 us (3%)
    pallas_call x6, Pallas kernels, exchange(): pl.pallas_call(partial(exchange_kernel, axes, modes), out_shape=tuple((ja...  147 us
    pallas_call x1, Pallas kernels, sum_gradients(): pl.pallas_call(sum_kernel, out_shape=jax.ShapeDtypeStruct((2, 144, HALF),...  113 us
    all_gather x1, waiting for transfers between devices, body(): up_own = lax.all_gather(up_half, 'dp', axis=0, tiled=True)  88.9 us
    pallas_call x1, Pallas kernels, gather_weights(): pl.pallas_call(gather_kernel, out_shape=jax.ShapeDtypeStruct((2, D, HALF)...  63.9 us
    pallas_call x2, Pallas kernels, mlp_backward(): pl.pallas_call(mlp_backward_kernel, grid=(2 * STEPS,), out_shape=(half, j...  38.8 us
    pallas_call x2, Pallas kernels, mlp_forward(): pl.pallas_call(mlp_forward_kernel, grid=(2 * STEPS,), out_shape=(f32, jax...  37.2 us
    dot_general x13, matrix products, matmul_tn(): lax.dot_general(left, right, (((0,), (0,)), ((), ())), preferred_element_...  34.2 us
    dot_general x12, matrix products, matmul(): return jnp.dot(left, right, preferred_element_type=jnp.float32)  31.1 us
  transfers between devices with their start and end apart: 20, of which 7 were waited for; matrix products, arithmetic and copies ran while one was open for 19% of the time, Pallas kernels for 39%

profile of v4, /device:TPU:0, one launch (start us, length us, event | category | flops | bytes accessed | tf_op | source)
XLA Modules:
  0.0 868.8 jit_solution(4740395816417845180)
XLA Ops:
  22.0 35.7 %exchange_dp.2 = (s32[8,8,128]{2,1,0:T(8,128)}, bf16[8,144,384]{2,1,0:T(8,128)(2,1)}) custom-call(s32[8,128]{1,0:T(8,128)} %pad.44.refs_0_, bf16[144,384]{1,0:T(8,128)(2,1)} %fusion.128.refs_1_), custom_call_target="tpu_custom_call" | custom-call | bytes 30000000 | tf_op jit(solution)/shard_map/exchange_dp/pallas_call | solution.py:585
  66.2 28.1 %exchange_stage.2 = f32[16,48,128]{2,1,0:T(8,128)} custom-call(f32[16,48,128]{2,1,0:T(8,128)} %bitcast.343), custom_call_target="tpu_custom_call" | custom-call | bytes 30000000 | tf_op jit(solution)/shard_map/exchange_stage/pallas_call | solution.py:585
  99.9 24.9 %all-gather.6.cloned.1.call-done = bf16[1,1152,2304]{2,1,0:T(8,128)(2,1)} async-done(((bf16[1,144,2304]{2,1,0:T(8,128)(2,1)}), bf16[1,1152,2304]{2,1,0:T(8,128)(2,1)}) %all-gather.6.cloned.1.call-update) | async-done | bytes 5308432 | tf_op jit(solution)/shard_map/all_gather | solution.py:914
  124.8 88.9 %all-gather.4.cloned.1.call-done.up_a = bf16[1152,2304]{1,0:T(8,128)(2,1)} async-done(((bf16[144,2304]{1,0:T(8,128)(2,1)}), bf16[1152,2304]{1,0:T(8,128)(2,1)}) %all-gather.4.cloned.1.call-update) | async-done | bytes 5308432 | tf_op jit(solution)/shard_map/all_gather | solution.py:913
  213.8 63.9 %gather_weights.1 = bf16[2,1152,2304]{2,1,0:T(8,128)(2,1)} custom-call(bf16[144,2304]{1,0:T(8,128)(2,1)} %get-tuple-element.108.blk_ref), custom_call_target="tpu_custom_call" | custom-call | bytes 200000000 | tf_op jit(solution)/shard_map/gather_weights/pallas_call | solution.py:281
  277.7 4.3 fusion.25
  296.6 4.8 fusion.193
  308.1 18.6 %mlp_forward.2 = (f32[256,1152]{1,0:T(8,128)}, bf16[256,1152]{1,0:T(8,128)(2,1)}, f32[256,1152]{1,0:T(8,128)}, f32[256,4608]{1,0:T(8,128)}, bf16[256,4608]{1,0:T(8,128)(2,1)}) custom-call(f32[256,1152]{1,0:T(8,128)} %fusion.52.x_ref, f32[3,1152]{1,0:T(4,128)} %reshape.452.mod_ref, f32[1,4608]{1,0:T(1,128)} %copy-done.79, ...), custom_call_target="tpu_custom_call" | custom-call | flops 5435817984 | bytes 21233664 | tf_op jit(solution)/shard_map/mlp_forward/pallas_call | solution.py:723
  339.5 5.2 collective-permute-done.3
  353.8 5.4 fusion.22
  367.9 4.8 fusion.194
  375.6 4.5 fusion.99
  380.1 18.6 %mlp_forward.3 = (f32[256,1152]{1,0:T(8,128)}, bf16[256,1152]{1,0:T(8,128)(2,1)}, f32[256,1152]{1,0:T(8,128)}, f32[256,4608]{1,0:T(8,128)}, bf16[256,4608]{1,0:T(8,128)(2,1)}) custom-call(f32[256,1152]{1,0:T(8,128)} %get-tuple-element.157.x_ref, f32[3,1152]{1,0:T(4,128)} %reshape.452.mod_ref, f32[1,4608]{1,0:T(1,128)} %copy-done.79, ...), custom_call_target="tpu_custom_call" | custom-call | flops 5435817984 | bytes 21233664 | tf_op jit(solution)/shard_map/mlp_forward/pallas_call | solution.py:723
  405.2 19.5 %mlp_backward.2 = (bf16[256,1152]{1,0:T(8,128)(2,1)}, f32[3,1152]{1,0:T(4,128)}, bf16[256,1152]{1,0:T(8,128)(2,1)}, bf16[256,4608]{1,0:T(8,128)(2,1)}) custom-call(f32[256,1152]{1,0:T(8,128)} %subtract_multiply_fusion.d_ref, f32[256,1152]{1,0:T(8,128)} %get-tuple-element.157.x_ref, f32[3,1152]{1,0:T(4,128)} %reshape.452.mod_ref, ...), custom_call_target="tpu_custom_call" | custom-call | flops 5435817984 | bytes 21233664 | tf_op jit(solution)/shard_map/mlp_backward/pallas_call | solution.py:747
  424.7 3.9 convolution_convert_fusion.1
  443.2 4.6 fusion.177
  457.4 7.6 collective-permute-done.4
  467.2 19.2 %mlp_backward.3 = (bf16[256,1152]{1,0:T(8,128)(2,1)}, f32[3,1152]{1,0:T(4,128)}, bf16[256,1152]{1,0:T(8,128)(2,1)}, bf16[256,4608]{1,0:T(8,128)(2,1)}) custom-call(f32[256,1152]{1,0:T(8,128)} %convert_select_fusion.2.d_ref, f32[256,1152]{1,0:T(8,128)} %get-tuple-element.157.x_ref, f32[3,1152]{1,0:T(4,128)} %reshape.452.mod_ref, ...), custom_call_target="tpu_custom_call" | custom-call | flops 5435817984 | bytes 21233664 | tf_op jit(solution)/shard_map/mlp_backward/pallas_call | solution.py:747
  511.5 4.0 fusion.3
  527.4 4.8 collect.1
  533.8 35.6 %exchange_stage.3 = (bf16[16,16,1152]{2,1,0:T(8,128)(2,1)}, f32[16,16,128]{2,1,0:T(8,128)}, f32[16,40,128]{2,1,0:T(8,128)}) custom-call(bf16[2,16,1152]{2,1,0:T(8,128)(2,1)} %get-tuple-element.59.refs_0_, f32[16,16,128]{2,1,0:T(8,128)} %bitcast_bitcast_fusion.refs_1_, f32[8,40,128]{2,1,0:T(8,128)} %bitcast.351), custom_call_target="tpu_custom_call" | custom-call | bytes 30000000 | tf_op jit(solution)/shard_map/exchange_stage/pallas_call | solution.py:585
  573.7 9.0 %exchange_section.1 = (f32[4,24,128]{2,1,0:T(8,128)}, f32[4,40,128]{2,1,0:T(8,128)}, bf16[4,16,2304]{2,1,0:T(8,128)(2,1)}) custom-call(f32[24,128]{1,0:T(8,128)} %pad_bitcast_fusion.2.refs_0_, f32[40,128]{1,0:T(8,128)} %reduce_sum.397.refs_1_, bf16[16,2304]{1,0:T(8,128)(2,1)} %bitcast.378), custom_call_target="tpu_custom_call" | custom-call | bytes 30000000 | tf_op jit(solution)/shard_map/exchange_section/pallas_call | solution.py:585
  586.0 26.5 %exchange_dp.3 = f32[8,24,128]{2,1,0:T(8,128)} custom-call(f32[8,24,128]{2,1,0:T(8,128)} %bitcast.374), custom_call_target="tpu_custom_call" | custom-call | bytes 30000000 | tf_op jit(solution)/shard_map/exchange_dp/pallas_call | solution.py:585
  621.3 4.8 fusion.105
  626.3 4.7 fusion.102
  635.4 4.3 fusion.4
  647.6 5.0 fusion.2.g_first
  652.6 113.2 %sum_gradients.1 = f32[2,144,2304]{2,1,0:T(8,128)} custom-call(bf16[1152,2304]{1,0:T(8,128)(2,1)} %fusion.2.g_first, bf16[1152,2304]{1,0:T(8,128)(2,1)} %pad_maximum_fusion.g_second), custom_call_target="tpu_custom_call" | custom-call | bytes 300000000 | tf_op jit(solution)/shard_map/sum_gradients/pallas_call | solution.py:502
  780.0 11.0 %collective-permute-done.15 = bf16[144,2304]{1,0:T(8,128)(2,1)S(1)} collective-permute-done((bf16[144,2304]{1,0:T(8,128)(2,1)}, bf16[144,2304]{1,0:T(8,128)(2,1)S(1)}, u32[]{:S(2)}, u32[]{:S(2)}) %collective-permute-start.15) | collective-permute-done | bytes 663584 | tf_op jit(solution)/shard_map/ppermute | solution.py:887
  799.7 12.5 %exchange_every.1 = f32[32,24,128]{2,1,0:T(8,128)} custom-call(f32[24,128]{1,0:T(8,128)} %pad_maximum_fusion.5.refs_0_), custom_call_target="tpu_custom_call" | custom-call | bytes 30000000 | tf_op jit(solution)/shard_map/exchange_every/pallas_call | solution.py:585
  824.8 4.0 fusion.179
  831.8 7.9 convert_bitcast_fusion
  (513 shorter events, 234.7 us)
Async XLA Ops:
  7.2 117.6 %all-gather.6.cloned.1.call-start = ((), (), s32[]{:S(2)}) async-start(), calls=%async_computation.3 | async-start | bytes 5971968 | tf_op jit(solution)/shard_map/all_gather | solution.py:914
  9.5 204.2 %all-gather.4.cloned.1.call-start = ((), (), s32[]{:S(2)}) async-start(), calls=%async_computation.1 | async-start | bytes 5971968 | tf_op jit(solution)/shard_map/all_gather | solution.py:913
  11.6 2.3 collective-permute-start
  15.1 758.6 %reduce-scatter.2.cloned.1.call-start = ((), (), s32[]{:S(2)}) async-start(), calls=%async_computation.2 | async-start | bytes 5971968 | tf_op jit(solution)/shard_map/reduce_scatter | solution.py:997
  18.3 40.4 %copy-start.71 = (f32[40352]{0:T(1024)S(1)}, f32[40352]{0:T(1024)}, u32[]{:S(2)}) copy-start(f32[40352]{0:T(1024)} %param.45) | copy-start | bytes 484228
  20.3 44.7 %copy-start.5 = (f32[1,144,3456]{2,1,0:T(8,128)S(1)}, f32[1,144,3456]{2,1,0:T(8,128)}, u32[]{:S(2)}) copy-start(f32[1,144,3456]{2,1,0:T(8,128)} %param.30) | copy-start | bytes 5971972
  99.9 177.7 %copy-start.91 = (f32[2304]{0:T(1024)}, f32[2304]{0:T(1024)S(1)}, u32[]{:S(2)}) copy-start(f32[2304]{0:T(1024)S(1)} %get-tuple-element.124) | copy-start | bytes 27652
  124.8 183.3 %collective-permute-start.2 = (bf16[1152,2304]{1,0:T(8,128)(2,1)}, bf16[1152,2304]{1,0:T(8,128)(2,1)}, u32[]{:S(2)}, u32[]{:S(2)}) collective-permute-start(bf16[1152,2304]{1,0:T(8,128)(2,1)} %bitcast.311), channel_id=1, source_target_pairs={{0,1},{1,0},{2,3},{3,2},{4,5},{5,4},{6,7},{7,6},{8,9},{9,8},{10,11... | collective-permute-start | bytes 15925256 | tf_op jit(solution)/shard_map/ppermute | solution.py:887
  213.7 94.3 %collective-permute-start.1 = (bf16[1152,2304]{1,0:T(8,128)(2,1)}, bf16[1152,2304]{1,0:T(8,128)(2,1)}, u32[]{:S(2)}, u32[]{:S(2)}) collective-permute-start(bf16[1152,2304]{1,0:T(8,128)(2,1)} %all-gather.4.cloned.1.call-done.up_a), channel_id=1, source_target_pairs={{0,1},{1,0},{2,3},{3,2},{4,5},{5,4},{6,7},{7,6},{8,9},{9,8},{10,11... | collective-permute-start | bytes 15925256 | tf_op jit(solution)/shard_map/ppermute | solution.py:887
  213.8 63.9 %copy-start.79 = (f32[1,4608]{1,0:T(1,128)}, f32[1,4608]{1,0:T(1,128)S(1)}, u32[]{:S(2)}) copy-start(f32[1,4608]{1,0:T(1,128)S(1)} %reshape_dynamic-update-slice_fusion.b_up_ref) | copy-start | bytes 55300
  308.1 23.4 %copy-start.76 = (f32[1,32,32,4]{2,3,1,0:T(4,128)S(1)}, f32[1,32,32,4]{2,3,1,0:T(4,128)}, u32[]{:S(2)}) copy-start(f32[1,32,32,4]{2,3,1,0:T(4,128)} %get-tuple-element.121) | copy-start | bytes 49156
  328.9 15.9 %collective-permute-start.3 = (bf16[256,1152]{1,0:T(8,128)(2,1)}, bf16[256,1152]{1,0:T(8,128)(2,1)}, u32[]{:S(2)}, u32[]{:S(2)}) collective-permute-start(bf16[256,1152]{1,0:T(8,128)(2,1)} %convert_element_type.389), channel_id=1, source_target_pairs={{0,2},{1,3},{2,0},{3,1},{4,6},{5,7},{6,4},{7,5},{8,10},{9,11},{10,... | collective-permute-start | bytes 1769480 | tf_op jit(solution)/shard_map/ppermute | solution.py:887
  438.9 195.7 %collective-permute-start.7 = (bf16[256,1152]{1,0:T(8,128)(2,1)}, bf16[256,1152]{1,0:T(8,128)(2,1)}, u32[]{:S(2)}, u32[]{:S(2)}) collective-permute-start(bf16[256,1152]{1,0:T(8,128)(2,1)} %get-tuple-element.101), channel_id=1, source_target_pairs={{0,1},{1,0},{2,3},{3,2},{4,5},{5,4},{6,7},{7,6},{8,9},{9,8},{10,11... | collective-permute-start | bytes 1769480 | tf_op jit(solution)/shard_map/ppermute | solution.py:887
  449.0 16.1 %collective-permute-start.4 = (bf16[256,1152]{1,0:T(8,128)(2,1)}, bf16[256,1152]{1,0:T(8,128)(2,1)}, u32[]{:S(2)}, u32[]{:S(2)}) collective-permute-start(bf16[256,1152]{1,0:T(8,128)(2,1)} %fusion.78), channel_id=1, source_target_pairs={{0,2},{1,3},{2,0},{3,1},{4,6},{5,7},{6,4},{7,5},{8,10},{9,11},{10,... | collective-permute-start | bytes 1769480 | tf_op jit(solution)/shard_map/ppermute | solution.py:887
  453.7 54.8 %collective-permute-start.13 = (bf16[256,2304]{1,0:T(8,128)(2,1)}, bf16[256,2304]{1,0:T(8,128)(2,1)}, u32[]{:S(2)}, u32[]{:S(2)}) collective-permute-start(bf16[256,2304]{1,0:T(8,128)(2,1)} %slice.327), channel_id=1, source_target_pairs={{0,1},{1,0},{2,3},{3,2},{4,5},{5,4},{6,7},{7,6},{8,9},{9,8},{10,11... | collective-permute-start | bytes 3538952 | tf_op jit(solution)/shard_map/ppermute | solution.py:887
  454.8 184.9 %collective-permute-start.9 = (bf16[256,1152]{1,0:T(8,128)(2,1)}, bf16[256,1152]{1,0:T(8,128)(2,1)}, u32[]{:S(2)}, u32[]{:S(2)}) collective-permute-start(bf16[256,1152]{1,0:T(8,128)(2,1)} %broadcast_select_fusion.3), channel_id=1, source_target_pairs={{0,1},{1,0},{2,3},{3,2},{4,5},{5,4},{6,7},{7,6},{8,9},{9,8},{10,11... | collective-permute-start | bytes 1769480 | tf_op jit(solution)/shard_map/ppermute | solution.py:887
  456.2 188.6 %collective-permute-start.5 = (bf16[256,1152]{1,0:T(8,128)(2,1)}, bf16[256,1152]{1,0:T(8,128)(2,1)}, u32[]{:S(2)}, u32[]{:S(2)}) collective-permute-start(bf16[256,1152]{1,0:T(8,128)(2,1)} %get-tuple-element.65), channel_id=1, source_target_pairs={{0,1},{1,0},{2,3},{3,2},{4,5},{5,4},{6,7},{7,6},{8,9},{9,8},{10,11... | collective-permute-start | bytes 1769480 | tf_op jit(solution)/shard_map/ppermute | solution.py:887
  505.4 3.0 collective-permute-start.12
  532.2 39.8 %copy-start.44 = (bf16[144,2336]{1,0:T(8,128)(2,1)S(1)}, bf16[144,2336]{1,0:T(8,128)(2,1)}, u32[]{:S(2)}) copy-start(bf16[144,2336]{1,0:T(8,128)(2,1)} %copy-done.43) | copy-start | bytes 2018308
  571.9 41.7 %copy-start.24 = (bf16[256,1152]{1,0:T(8,128)(2,1)S(1)}, bf16[256,1152]{1,0:T(8,128)(2,1)}, u32[]{:S(2)}) copy-start(bf16[256,1152]{1,0:T(8,128)(2,1)} %copy.118.refs_2_) | copy-start | bytes 1769476
  571.9 41.7 %copy-start.25 = (bf16[256,1152]{1,0:T(8,128)(2,1)S(1)}, bf16[256,1152]{1,0:T(8,128)(2,1)}, u32[]{:S(2)}) copy-start(bf16[256,1152]{1,0:T(8,128)(2,1)} %copy.116.refs_0_) | copy-start | bytes 1769476
  584.9 30.5 %copy-start.23 = (bf16[256,1152]{1,0:T(8,128)(2,1)S(1)}, bf16[256,1152]{1,0:T(8,128)(2,1)}, u32[]{:S(2)}) copy-start(bf16[256,1152]{1,0:T(8,128)(2,1)} %copy.117.refs_1_) | copy-start | bytes 1769476
  584.9 30.5 %copy-start.40 = (bf16[256,1152]{1,0:T(8,128)(2,1)S(1)}, bf16[256,1152]{1,0:T(8,128)(2,1)}, u32[]{:S(2)}) copy-start(bf16[256,1152]{1,0:T(8,128)(2,1)} %get-tuple-element.55) | copy-start | bytes 1769476
  614.5 20.9 %collective-permute-start.8 = (bf16[256,1152]{1,0:T(8,128)(2,1)}, bf16[256,1152]{1,0:T(8,128)(2,1)}, u32[]{:S(2)}, u32[]{:S(2)}) collective-permute-start(bf16[256,1152]{1,0:T(8,128)(2,1)} %broadcast_select_fusion.5), channel_id=1, source_target_pairs={{0,1},{1,0},{2,3},{3,2},{4,5},{5,4},{6,7},{7,6},{8,9},{9,8},{10,11... | collective-permute-start | bytes 1769480 | tf_op jit(solution)/shard_map/ppermute | solution.py:887
  616.4 23.3 %collective-permute-start.10 = (bf16[256,1152]{1,0:T(8,128)(2,1)}, bf16[256,1152]{1,0:T(8,128)(2,1)}, u32[]{:S(2)}, u32[]{:S(2)}) collective-permute-start(bf16[256,1152]{1,0:T(8,128)(2,1)} %broadcast_select_fusion.4), channel_id=1, source_target_pairs={{0,1},{1,0},{2,3},{3,2},{4,5},{5,4},{6,7},{7,6},{8,9},{9,8},{10,11... | collective-permute-start | bytes 1769480 | tf_op jit(solution)/shard_map/ppermute | solution.py:887
  634.7 10.1 %collective-permute-start.6 = (bf16[256,2304]{1,0:T(8,128)(2,1)}, bf16[256,2304]{1,0:T(8,128)(2,1)S(1)}, u32[]{:S(2)}, u32[]{:S(2)}) collective-permute-start(bf16[256,2304]{1,0:T(8,128)(2,1)} %slice.325), channel_id=1, source_target_pairs={{0,1},{1,0},{2,3},{3,2},{4,5},{5,4},{6,7},{7,6},{8,9},{9,8},{10,11... | collective-permute-start | bytes 3538952 | tf_op jit(solution)/shard_map/ppermute | solution.py:887
  768.6 6.5 collective-permute-start.11
  773.7 17.4 %collective-permute-start.15 = (bf16[144,2304]{1,0:T(8,128)(2,1)}, bf16[144,2304]{1,0:T(8,128)(2,1)S(1)}, u32[]{:S(2)}, u32[]{:S(2)}) collective-permute-start(bf16[144,2304]{1,0:T(8,128)(2,1)} %reduce-scatter.2.cloned.1.call-done), channel_id=1, source_target_pairs={{0,2},{1,3},{2,0},{3,1},{4,6},{5,7},{6,4},{7,5},{8,10},{9,11},{10,... | collective-permute-start | bytes 1990664 | tf_op jit(solution)/shard_map/ppermute | solution.py:887
  775.0 16.0 %collective-permute-start.14 = (bf16[144,2304]{1,0:T(8,128)(2,1)}, bf16[144,2304]{1,0:T(8,128)(2,1)}, u32[]{:S(2)}, u32[]{:S(2)}) collective-permute-start(bf16[144,2304]{1,0:T(8,128)(2,1)} %reduce-scatter.2.cloned.1.call-done), channel_id=1, source_target_pairs={{0,1},{1,0},{2,3},{3,2},{4,5},{5,4},{6,7},{7,6},{8,9},{9,8},{10,11... | collective-permute-start | bytes 1990664 | tf_op jit(solution)/shard_map/ppermute | solution.py:887
  791.0 2.1 collective-permute-start.16
  797.1 23.3 %copy-start.83 = (f32[2304]{0:T(1024)S(1)}, f32[2304]{0:T(1024)}, u32[]{:S(2)}) copy-start(f32[2304]{0:T(1024)} %convert_reduce_fusion.1) | copy-start | bytes 27652
  797.1 26.0 %copy-start.72 = (f32[40352]{0:T(1024)S(1)}, f32[40352]{0:T(1024)}, u32[]{:S(2)}) copy-start(f32[40352]{0:T(1024)} %param.45) | copy-start | bytes 484228
  (100 other events, 475.1 us)
Sparse Core Ops, SparseCore 0:
  10.8 113.9 all-gather.5
  127.6 86.1 all-gather.3
  515.7 127.1 reduce-scatter.1

commit v5 on v4

--- a/solution.py
+++ b/solution.py
@@ -95,46 +95,93 @@
 
 
 Z, X = 4, 2
+GATHER_CHUNKS = (
+    (0, 0, 16, True), (0, 16, 32, False), (0, 48, 32, False), (0, 80, 32, False), (0, 112, 32, False),
+    (1, 0, 48, True), (1, 48, 48, False), (1, 96, 48, False),
+)
 CHUNKS = ((0, 16, True), (16, 32, False), (48, 32, False), (80, 32, False), (112, 32, False))
+META = 1280
+PIECE = 768
 
 
 def ring_fits(n, rows):
     return n == Z * X and rows == 144
 
 
-def gather_kernel(blk_ref, out_blk, up_sem, down_sem, x_sem, sib_sem, recv_sem, sib_recv, own_sem):
+def gather_kernel(
+    blk_ref, dn_ref, meta_ref, small_ref, two_ref, table_ref, mod_ref, fm_ref, b_one, b_two,
+    out_blk, out_dn, meta_out, small_out, pre_out, cond_out, mods_out,
+    part, parts, arrived_parts, meta_send, meta_recv, small_send, small_recv, part_send, part_recv, local_sem,
+    up_sem, down_sem, x_sem, sib_sem, recv_sem, sib_recv, own_sem,
+):
     me = lax.axis_index("dp")
     section = lax.axis_index("section")
     z, x = me // X, lax.rem(me, X)
     core = lax.rem(section, 2)
     sibling = section + 1 - 2 * core
     across = me + 1 - 2 * x
-    chunks = len(CHUNKS)
+    chunks = len(GATHER_CHUNKS)
+    low = section - core
+    group, place_in = Z * X * 2, me * 2 + core
+    where = lambda p: {"dp": p // 2, "section": low + lax.rem(p, 2)}
     has_up, has_down = z < Z - 1, z > 0
 
     barrier = pltpu.get_barrier_semaphore()
-    pl.semaphore_signal(barrier, 1, device_id={"section": sibling}, device_id_type=MESH)
-    pl.semaphore_signal(barrier, 1, device_id={"dp": across}, device_id_type=MESH)
-
-    @pl.when(has_up)
-    def _():
-        pl.semaphore_signal(barrier, 1, device_id={"dp": me + X}, device_id_type=MESH)
-
-    @pl.when(has_down)
-    def _():
-        pl.semaphore_signal(barrier, 1, device_id={"dp": me - X}, device_id_type=MESH)
-
-    pl.semaphore_wait(barrier, 2 + has_up.astype(jnp.int32) + has_down.astype(jnp.int32))
+
+    @pl.loop(1, group)
+    def _(step):
+        pl.semaphore_signal(
+            barrier, 1, device_id=where(lax.rem(place_in + step, group)), device_id_type=MESH
+        )
+
+    pl.semaphore_wait(barrier, group - 1)
+
+    def news(step, p, slot):
+        copies = []
+        for src, dst, send, recv in (
+            (meta_ref, meta_out, meta_send, meta_recv), (small_ref, small_out, small_send, small_recv)
+        ):
+            copies.append(
+                pltpu.make_async_remote_copy(
+                    src_ref=src, dst_ref=dst.at[slot], send_sem=send.at[step], recv_sem=recv.at[step],
+                    device_id={"dp": p}, device_id_type=MESH,
+                )
+            )
+        return copies
+
+    def own_news():
+        return [
+            pltpu.make_async_copy(meta_ref, meta_out.at[me], local_sem.at[0]),
+            pltpu.make_async_copy(small_ref, small_out.at[me], local_sem.at[1]),
+        ]
+
+    def part_copy(step, p, slot):
+        return pltpu.make_async_remote_copy(
+            src_ref=parts.at[p], dst_ref=arrived_parts.at[slot],
+            send_sem=part_send.at[step], recv_sem=part_recv.at[step],
+            device_id=where(p), device_id_type=MESH,
+        )
+
+    own_part = pltpu.make_async_copy(parts.at[place_in], arrived_parts.at[place_in], local_sem.at[2])
+
+    for copy_in in own_news():
+        copy_in.start()
+
+    @pl.loop(1, Z * X)
+    def _(step):
+        p = lax.rem(me + step, Z * X)
+        for copy_out in news(step, p, me):
+            copy_out.start()
 
     def place(owner, k, side):
-        first, rows, unused = CHUNKS[k]
-        return out_blk.at[side, pl.ds(pl.multiple_of(owner * 144 + first, 16), rows)]
+        which, first, rows, unused = GATHER_CHUNKS[k]
+        return (out_dn if which else out_blk).at[side, pl.ds(pl.multiple_of(owner * 144 + first, 16), rows)]
 
     def source(owner, k, mine):
         if not mine:
             return place(owner, k, core)
-        first, rows, unused = CHUNKS[k]
-        return blk_ref.at[pl.ds(first, rows)]
+        which, first, rows, unused = GATHER_CHUNKS[k]
+        return (dn_ref if which else blk_ref).at[pl.ds(first, rows)]
 
     def copy(owner, k, mine, sem, target):
         unit = owner * chunks + k
@@ -177,9 +224,44 @@
         own_copy(k).start()
         to_sibling(me, k, True).start()
 
+    for copy_in in own_news():
+        copy_in.wait()
+
+    @pl.loop(1, Z * X)
+    def _(step):
+        p = lax.rem(me + Z * X - step, Z * X)
+        for copy_in in news(step, p, p):
+            copy_in.wait_recv()
+            copy_in.wait_send()
+
+    rows_all = Z * X * 8
+    meta = to_half(meta_out[...].reshape(rows_all, META))
+    one = small_out[:, :, :FREQ].reshape(D, FREQ)
+    pre = matmul_nt(meta[:, :FREQ], one) + b_one[...]
+    pre_out[...] = pre
+    hidden = to_half(jax.nn.silu(pre))
+    cond = matmul_nt(hidden, two_ref[...]) + b_two[...] + matmul_nt(meta[:, FREQ:], table_ref[...])
+    cond_out[...] = cond
+    cond_low = to_half(cond).astype(jnp.float32)
+    own_cond = jnp.where(section == 0, cond, cond_low)
+    part[:, : 3 * D] = matmul(to_half(jax.nn.silu(own_cond)), mod_ref[...])
+    part[:, 3 * D : 5 * D] = matmul(to_half(jax.nn.silu(cond_low)), fm_ref[...])
+    part[:, 5 * D :] = jnp.zeros((rows_all, 8 * PIECE - 5 * D), jnp.float32)
+    for index in range(Z * X):
+        for image in range(2):
+            row = 8 * index + image
+            for k in range(8):
+                parts[2 * index + image, k : k + 1] = part[row : row + 1, PIECE * k : PIECE * (k + 1)]
+    own_part.start()
+
+    @pl.loop(1, group)
+    def _(step):
+        p = lax.rem(place_in + step, group)
+        part_copy(step, p, place_in).start()
+
     def along(step, k, first_across):
         shift = 1 - 2 * x if first_across else 0
-        crosses = (not first_across) and (not CHUNKS[k][2])
+        crosses = (not first_across) and (not GATHER_CHUNKS[k][3])
 
         @pl.when(z >= step)
         def _():
@@ -208,7 +290,7 @@
             to_sibling(owner, k, False).start()
 
     def crossed(step, k):
-        direct = CHUNKS[k][2]
+        direct = GATHER_CHUNKS[k][3]
         if step == 0:
             owner = across
             arrived(owner, k)
@@ -234,11 +316,25 @@
             if step < Z:
                 along(step, k, False)
             crossed(step - 1, k)
-            if step < Z and CHUNKS[k][2]:
+            if step < Z and GATHER_CHUNKS[k][3]:
                 along(step, k, True)
 
+    own_part.wait()
+
+    @pl.loop(1, group)
+    def _(step):
+        p = lax.rem(place_in + group - step, group)
+        part_copy(step, p, p).wait_recv()
+        part_copy(step, p, p).wait_send()
+
+    for source_core in range(2):
+        total = arrived_parts[source_core]
+        for index in range(1, Z * X):
+            total = total + arrived_parts[2 * index + source_core]
+        mods_out[source_core] = total
+
     for k in range(chunks):
-        direct = CHUNKS[k][2]
+        direct = GATHER_CHUNKS[k][3]
         own_copy(k).wait()
         for column in range(2):
             base = me if column == 0 else across
@@ -270,25 +366,60 @@
                             copy(owner, k, mine, x_sem, across).wait_send()
 
 
-def gather_weights(half):
-    n = lax.axis_size("dp")
-    if not ring_fits(n, half.shape[0]):
-        own = lax.all_gather(half, "dp", axis=0, tiled=True)
-        sib = swap(own, 1)
-        even = lax.rem(lax.axis_index("section"), 2) == 0
-        return jnp.where(even, jnp.stack([own, sib]), jnp.stack([sib, own]))
-    units = n * len(CHUNKS)
+def gather_weights(blk, dn, meta, small, w_two, table, w_mod, w_fm, b_one, b_two):
+    n, width = lax.axis_size("dp"), blk.shape[0]
+    section = lax.axis_index("section")
+    if not ring_fits(n, width):
+        both = lambda own, sib: jnp.where(
+            lax.rem(section, 2) == 0, jnp.stack([own, sib]), jnp.stack([sib, own])
+        )
+        blk = lax.all_gather(blk, "dp", axis=0, tiled=True)
+        dn = lax.all_gather(dn, "dp", axis=0, tiled=True)
+        small = jnp.pad(small, ((0, -width % 16), (0, 0)))
+        meta, small = exchange(2, "dp", ("all", "all"), meta, small)
+        small = small[:, :width]
+        rows = to_half(meta.reshape(-1, META))
+        pre = matmul_nt(rows[:, :FREQ], small[:, :, :FREQ].reshape(D, FREQ)) + b_one
+        hidden = to_half(jax.nn.silu(pre))
+        cond = matmul_nt(hidden, w_two) + b_two + matmul_nt(rows[:, FREQ:], table)
+        cond_low = to_half(cond).astype(jnp.float32)
+        own_cond = jnp.where(section == 0, cond, cond_low)
+        parts = [
+            matmul(to_half(jax.nn.silu(own_cond)), w_mod),
+            matmul(to_half(jax.nn.silu(cond_low)), w_fm),
+        ]
+        parts = jnp.pad(jnp.concatenate(parts, axis=1), ((0, 0), (0, 8 * PIECE - 5 * D)))
+        parts = parts.reshape(n, 8, 8, PIECE)[:, :2].reshape(2 * n, 8, PIECE)
+        (parts,) = exchange(3, "stage", ("each",), parts)
+        mods = jnp.sum(parts.reshape(n, 2, 8, PIECE), axis=0)
+        return (both(blk, swap(blk, 1)), both(dn, swap(dn, 1)), meta, small, pre, cond, mods)
+    units = n * len(GATHER_CHUNKS)
+    hbm, vmem = pl.BlockSpec(memory_space=pl.ANY), pl.BlockSpec(memory_space=pltpu.VMEM)
+    dma = lambda count: pltpu.SemaphoreType.DMA((count,))
+    f32 = jnp.float32
     return pl.pallas_call(
         gather_kernel,
-        out_shape=jax.ShapeDtypeStruct((2, D, HALF), BF),
-        in_specs=[pl.BlockSpec(memory_space=pl.ANY)],
-        out_specs=pl.BlockSpec(memory_space=pl.ANY),
-        scratch_shapes=[pltpu.SemaphoreType.DMA((units,))] * 6
-        + [pltpu.SemaphoreType.DMA((len(CHUNKS),))],
-        compiler_params=pltpu.CompilerParams(collective_id=0, has_side_effects=True),
-        cost_estimate=pl.CostEstimate(flops=0, bytes_accessed=200_000_000, transcendentals=0),
+        out_shape=(
+            jax.ShapeDtypeStruct((2, D, FF), BF), jax.ShapeDtypeStruct((2, D, HALF), BF),
+            jax.ShapeDtypeStruct((n, 8, META), f32), jax.ShapeDtypeStruct((n,) + small.shape, BF),
+            jax.ShapeDtypeStruct((n * 8, D), f32), jax.ShapeDtypeStruct((n * 8, width), f32),
+            jax.ShapeDtypeStruct((2, 8, PIECE), f32),
+        ),
+        in_specs=[hbm] * 2 + [vmem] * 8,
+        out_specs=(hbm, hbm) + (vmem,) * 5,
+        scratch_shapes=[
+            pltpu.VMEM((n * 8, 8 * PIECE), f32),
+            pltpu.VMEM((2 * n, 8, PIECE), f32), pltpu.VMEM((2 * n, 8, PIECE), f32),
+            dma(n), dma(n), dma(n), dma(n), dma(2 * n), dma(2 * n), dma(3),
+        ]
+        + [dma(units)] * 6
+        + [dma(len(GATHER_CHUNKS))],
+        compiler_params=pltpu.CompilerParams(
+            collective_id=0, has_side_effects=True, vmem_limit_bytes=VMEM_BYTES
+        ),
+        cost_estimate=pl.CostEstimate(flops=0, bytes_accessed=400_000_000, transcendentals=0),
         name="gather_weights",
-    )(half)
+    )(blk, dn, meta, small, w_two, table, w_mod, w_fm, b_one, b_two)
 
 
 VMEM_BYTES = 60 * 1024 * 1024
@@ -612,6 +743,7 @@
 TILE = 768
 STEPS = HALF // TILE
 GELU_SCALE = math.sqrt(2.0 / math.pi)
+SCALE = HEAD_DIM ** (-0.5)
 
 
 def mean_rows(value):
@@ -630,149 +762,232 @@
     return (d_x, jnp.sum(d_xm, axis=0), jnp.sum(d_xm * normed, axis=0))
 
 
-def mlp_forward_kernel(
-    x_ref, mod_ref, b_up_ref, b_down_ref, up_a, up_b, dn_a, dn_b,
-    out_ref, xm_ref, branch_ref, pre_ref, act_ref, acc,
+def window(head):
+    low = HEAD_DIM * head // 128 * 128
+    high = -(-HEAD_DIM * (head + 1) // 128) * 128
+    lane = lax.broadcasted_iota(jnp.int32, (PATCHES, high - low), 1) + low
+    return slice(low, high), (lane >= HEAD_DIM * head) & (lane < HEAD_DIM * (head + 1))
+
+
+def own_lanes(mask, value):
+    return jnp.where(mask, value, jnp.zeros_like(value))
+
+
+def softmax_rows(scores):
+    shifted = jnp.exp(scores - jnp.max(scores, axis=-1, keepdims=True))
+    return shifted / jnp.sum(shifted, axis=-1, keepdims=True)
+
+
+def half_of(ref, which, side):
+    return ref.at[which, :, pl.ds(pl.multiple_of(side * HALF, 128) if which else side * HALF, HALF)]
+
+
+def weight_copies(sources, targets, sem):
+    return [pltpu.make_async_copy(src, dst, sem.at[k]) for k, (src, dst) in enumerate(zip(sources, targets))]
+
+
+def forward_kernel(
+    save, flags, x_ref, mod_a, mod_m, b_attn, b_up, b_down, w_blk, w_dn, out_ref, *refs
 ):
-    step = pl.program_id(0)
-
-    @pl.when(step == 0)
-    def _():
-        normed, unused = normalized(x_ref[...])
-        xm_ref[...] = to_half(normed * (1.0 + mod_ref[1:2]) + mod_ref[0:1])
-        acc[...] = jnp.zeros_like(acc)
-
-    def tile(up, dn):
-        pre = matmul(xm_ref[...], up[...]) + b_up_ref[...]
-        cube = pre + 0.044715 * (pre * pre * pre)
-        act = to_half(pre * (0.5 * (1.0 + jnp.tanh(GELU_SCALE * cube))))
-        pre_ref[...] = pre
-        act_ref[...] = act
-        acc[...] += matmul_nt(act, dn[...])
-
-    @pl.when(step < STEPS)
-    def _():
-        tile(up_a, dn_a)
-
-    @pl.when(step >= STEPS)
-    def _():
-        tile(up_b, dn_b)
-
-    @pl.when(step == 2 * STEPS - 1)
-    def _():
-        branch = acc[...] + b_down_ref[...]
-        branch_ref[...] = branch
-        out_ref[...] = x_ref[...] + mod_ref[2:3] * branch
-
-
-def mlp_backward_kernel(
-    d_ref, x_ref, mod_ref, branch_ref, pre_ref, up_a, up_b, dn_a, dn_b,
-    d_in_ref, d_mod_ref, grad_ref, d_pre_ref, acc,
+    if save:
+        xm_ref, qkv_ref, att_ref, branch_a_ref, mid_ref, xm2_ref, branch_m_ref, pre_ref, act_ref = refs[:9]
+        wa, wu, wd, acc, sem = refs[9:]
+    else:
+        xm_ref, qkv_ref, att_ref, mid_ref, xm2_ref, wa, wu, wd, acc, sem = refs
+    copies = weight_copies(
+        [half_of(w_blk, 0, 0), half_of(w_blk, 0, 1)]
+        + [ref for side in (flags[0], 1 - flags[0]) for ref in (half_of(w_blk, 1, side), w_dn.at[side])],
+        (wa.at[0], wa.at[1], wu.at[0], wd.at[0], wu.at[1], wd.at[1]),
+        sem,
+    )
+    for copy in copies:
+        copy.start()
+    normed, unused = normalized(x_ref[...])
+    xm_ref[...] = to_half(normed * (1.0 + mod_a[1:2]) + mod_a[0:1])
+    acc[...] = jnp.zeros_like(acc)
+    for k in range(3):
+        if k != 1:
+            copies[k // 2].wait()
+        half, first = (0, D * k) if k < 2 else (1, 0)
+        part = slice(D * k, D * (k + 1))
+        qkv_ref[:, part] = to_half(
+            matmul(xm_ref[...], wa[half, :, first : first + D]) + b_attn[:, part]
+        )
+    for head in range(HEADS):
+        lanes, mask = window(head)
+        at = lambda k: slice(D * k + lanes.start, D * k + lanes.stop)
+        query = own_lanes(mask, qkv_ref[:, at(0)])
+        probs = softmax_rows(matmul_nt(query, qkv_ref[:, at(1)]) * SCALE)
+        acc[:, lanes] += own_lanes(mask, matmul(to_half(probs), qkv_ref[:, at(2)]))
+    att_ref[...] = to_half(acc[...])
+    branch = matmul(att_ref[...], wa[1, :, D:]) + b_attn[:, 3 * D :]
+    if save:
+        branch_a_ref[...] = branch
+    mid_ref[...] = to_half(x_ref[...] + mod_a[2:3] * branch).astype(jnp.float32)
+    normed, unused = normalized(mid_ref[...])
+    xm2_ref[...] = to_half(normed * (1.0 + mod_m[1:2]) + mod_m[0:1])
+    acc[...] = jnp.broadcast_to(b_down[...], acc.shape)
+    for half in range(2):
+        copies[2 + 2 * half].wait()
+        copies[3 + 2 * half].wait()
+        for step in range(STEPS):
+            own = slice(TILE * step, TILE * (step + 1))
+            part = slice(HALF * half + TILE * step, HALF * half + TILE * (step + 1))
+            pre = matmul(xm2_ref[...], wu[half, :, own]) + b_up[:, part]
+            cube = pre + 0.044715 * (pre * pre * pre)
+            act = to_half(pre * (0.5 * (1.0 + jnp.tanh(GELU_SCALE * cube))))
+            if save:
+                pre_ref[:, part] = pre
+                act_ref[:, part] = act
+            acc[...] += matmul_nt(act, wd[half, :, own])
+    if save:
+        branch_m_ref[...] = acc[...]
+    out = mid_ref[...] + mod_m[2:3] * acc[...]
+    out_ref[...] = out.astype(out_ref.dtype)
+
+
+def backward_kernel(
+    flags, d_ref, x_ref, mid_ref, mod_a, mod_m, branch_a, branch_m, qkv_ref, pre_hbm, w_blk, w_dn,
+    d_in_ref, d_mod_a, d_mod_m, grad_a, grad_m, d_pre_ref, d_qkv_ref,
+    wa, wu, wd, pre_ref, acc, d_acc, d_att, sem,
 ):
-    step = pl.program_id(0)
-
-    @pl.when(step == 0)
-    def _():
-        grad_ref[...] = to_half(d_ref[...] * mod_ref[2:3])
-        acc[...] = jnp.zeros_like(acc)
-
-    def tile(up, dn):
-        d_act = matmul(grad_ref[...], dn[...])
-        pre = pre_ref[...]
-        square = pre * pre
-        tanh = jnp.tanh(GELU_SCALE * (pre + 0.044715 * (square * pre)))
-        slope = 0.5 * (1.0 + tanh) + (0.5 * pre) * (1.0 - tanh * tanh) * (
-            GELU_SCALE * (1.0 + (3.0 * 0.044715) * square)
-        )
-        d_pre = to_half(d_act * slope)
-        d_pre_ref[...] = d_pre
-        acc[...] += matmul_nt(d_pre, up[...])
-
-    @pl.when(step < STEPS)
-    def _():
-        tile(up_a, dn_a)
-
-    @pl.when(step >= STEPS)
-    def _():
-        tile(up_b, dn_b)
-
-    @pl.when(step == 2 * STEPS - 1)
-    def _():
-        normed, inverse = normalized(x_ref[...])
-        d_x, d_shift, d_scale = modulated_back(normed, inverse, mod_ref[1:2], acc[...])
-        d_in_ref[...] = to_half(d_ref[...] + d_x)
-        d_mod_ref[0:1] = d_shift[None]
-        d_mod_ref[1:2] = d_scale[None]
-        d_mod_ref[2:3] = jnp.sum(d_ref[...] * branch_ref[...], axis=0)[None]
-
-
-def whole_spec(shape):
-    return pl.BlockSpec(shape, lambda step: (0,) * len(shape))
-
-
-def tile_specs():
-    first = lambda step: (0, jnp.minimum(step, STEPS - 1))
-    second = lambda step: (0, jnp.maximum(step - STEPS, 0))
-    return [pl.BlockSpec((D, TILE), first), pl.BlockSpec((D, TILE), second)] * 2
-
-
-def mlp_forward(x, mod, b_up, b_down, w_up, w_dn):
-    token = whole_spec((PATCHES, D))
-    hidden = pl.BlockSpec((PATCHES, TILE), lambda step: (0, step))
-    f32 = jax.ShapeDtypeStruct((PATCHES, D), jnp.float32)
+    copies = weight_copies(
+        (
+            w_dn.at[flags[0]], pre_hbm, half_of(w_blk, 1, flags[0]),
+            w_dn.at[1 - flags[0]], half_of(w_blk, 1, 1 - flags[0]),
+            half_of(w_blk, 0, 1), half_of(w_blk, 0, 0),
+        ),
+        (wd.at[0], pre_ref, wu.at[0], wd.at[1], wu.at[1], wa.at[1], wa.at[0]),
+        sem,
+    )
+    for copy in copies:
+        copy.start()
+    grad_m[...] = to_half(d_ref[...] * mod_m[2:3])
+    d_mod_m[2:3] = jnp.sum(d_ref[...] * branch_m[...], axis=0)[None]
+    acc[...] = jnp.zeros_like(acc)
+    for half in range(2):
+        copies[0 if half == 0 else 3].wait()
+        if half == 0:
+            copies[1].wait()
+        copies[2 if half == 0 else 4].wait()
+        for step in range(STEPS):
+            own = slice(TILE * step, TILE * (step + 1))
+            part = slice(HALF * half + TILE * step, HALF * half + TILE * (step + 1))
+            d_act = matmul(grad_m[...], wd[half, :, own])
+            pre = pre_ref[:, part]
+            square = pre * pre
+            tanh = jnp.tanh(GELU_SCALE * (pre + 0.044715 * (square * pre)))
+            slope = 0.5 * (1.0 + tanh) + (0.5 * pre) * (1.0 - tanh * tanh) * (
+                GELU_SCALE * (1.0 + (3.0 * 0.044715) * square)
+            )
+            d_pre = to_half(d_act * slope)
+            d_pre_ref[:, part] = d_pre
+            acc[...] += matmul_nt(d_pre, wu[half, :, own])
+    normed, inverse = normalized(mid_ref[...])
+    d_x, d_shift, d_scale = modulated_back(normed, inverse, mod_m[1:2], acc[...])
+    d_mod_m[0:1] = d_shift[None]
+    d_mod_m[1:2] = d_scale[None]
+    acc[...] = to_half(d_ref[...] + d_x).astype(jnp.float32)
+
+    d_mod_a[2:3] = jnp.sum(acc[...] * branch_a[...], axis=0)[None]
+    grad_a[...] = to_half(acc[...] * mod_a[2:3])
+    copies[5].wait()
+    d_att[...] = to_half(matmul_nt(grad_a[...], wa[1, :, D:]))
+    d_acc[...] = jnp.zeros_like(d_acc)
+    for head in range(HEADS):
+        lanes, mask = window(head)
+        at = lambda k: slice(D * k + lanes.start, D * k + lanes.stop)
+        query, key, value = (qkv_ref[:, at(k)] for k in range(3))
+        probs = softmax_rows(matmul_nt(own_lanes(mask, query), key) * SCALE)
+        outer = d_att[:, lanes]
+        d_acc[:, at(2)] += own_lanes(mask, matmul_tn(to_half(probs), outer))
+        d_probs = matmul_nt(own_lanes(mask, outer), value)
+        d_scores = to_half(probs * (d_probs - jnp.sum(probs * d_probs, axis=-1, keepdims=True)))
+        d_acc[:, at(0)] += own_lanes(mask, matmul(d_scores, key) * SCALE)
+        d_acc[:, at(1)] += own_lanes(mask, matmul_tn(d_scores, query) * SCALE)
+    d_qkv_ref[...] = to_half(d_acc[...])
+    copies[6].wait()
+    d_xm = matmul_nt(d_qkv_ref[:, 2 * D :], wa[1, :, :D]) + matmul_nt(d_qkv_ref[:, : 2 * D], wa[0])
+    normed, inverse = normalized(x_ref[...])
+    d_x, d_shift, d_scale = modulated_back(normed, inverse, mod_a[1:2], d_xm)
+    d_mod_a[0:1] = d_shift[None]
+    d_mod_a[1:2] = d_scale[None]
+    d_in_ref[...] = to_half(acc[...] + d_x)
+
+
+def weight_scratch():
+    return [pltpu.VMEM((2, D, HALF), BF)] * 3
+
+
+def stage_cost():
+    flops = 2 * PATCHES * D * 12 * D + 4 * PATCHES * PATCHES * D
+    return pl.CostEstimate(flops=2 * flops, bytes_accessed=24 * D * D, transcendentals=2 * PATCHES * FF)
+
+
+def stage_forward(save, x_in, weights):
+    flags, mod_a, mod_m, w_blk, w_dn, b_attn, b_up, b_down = weights
+    vmem, hbm = pl.BlockSpec(memory_space=pltpu.VMEM), pl.BlockSpec(memory_space=pl.ANY)
+    smem = pl.BlockSpec(memory_space=pltpu.SMEM)
+    like = lambda columns, kind: jax.ShapeDtypeStruct((PATCHES, columns), kind)
+    tokens, wide = pltpu.VMEM((PATCHES, D), BF), pltpu.VMEM((PATCHES, 3 * D), BF)
+    total = pltpu.VMEM((PATCHES, D), jnp.float32)
+    f32 = jnp.float32
+    if save:
+        shapes = [like(D, f32), like(D, BF), like(3 * D, BF), like(D, BF), like(D, f32), like(D, f32)]
+        shapes += [like(D, BF), like(D, f32), like(FF, f32), like(FF, BF)]
+        scratch = []
+    else:
+        shapes, scratch = [like(D, BF)], [tokens, wide, tokens, total, tokens]
     return pl.pallas_call(
-        mlp_forward_kernel,
-        grid=(2 * STEPS,),
-        out_shape=(
-            f32, jax.ShapeDtypeStruct((PATCHES, D), BF), f32,
-            jax.ShapeDtypeStruct((PATCHES, FF), jnp.float32), jax.ShapeDtypeStruct((PATCHES, FF), BF),
-        ),
-        in_specs=[
-            token, whole_spec((3, D)), pl.BlockSpec((1, TILE), lambda step: (0, step)), whole_spec((1, D)),
-        ] + tile_specs(),
-        out_specs=(token, token, token, hidden, hidden),
-        scratch_shapes=[pltpu.VMEM((PATCHES, D), jnp.float32)],
+        partial(forward_kernel, save),
+        out_shape=tuple(shapes),
+        in_specs=[smem] + [vmem] * 6 + [hbm] * 2,
+        out_specs=(vmem,) * len(shapes),
+        scratch_shapes=scratch + weight_scratch() + [total, pltpu.SemaphoreType.DMA((6,))],
         compiler_params=pltpu.CompilerParams(vmem_limit_bytes=VMEM_BYTES),
-        cost_estimate=pl.CostEstimate(
-            flops=4 * PATCHES * D * FF, bytes_accessed=4 * D * FF, transcendentals=PATCHES * FF
-        ),
-        name="mlp_forward",
-    )(x, mod, b_up, b_down, *w_up, *w_dn)
-
-
-def mlp_backward(d_out, x, mod, branch, pre, w_up, w_dn):
-    token = whole_spec((PATCHES, D))
-    hidden = pl.BlockSpec((PATCHES, TILE), lambda step: (0, step))
-    half = jax.ShapeDtypeStruct((PATCHES, D), BF)
+        cost_estimate=stage_cost(),
+        name="stage_forward",
+    )(flags, x_in, mod_a, mod_m, b_attn, b_up, b_down, w_blk, w_dn)
+
+
+def stage_backward(d_out, x_in, weights, kept):
+    flags, mod_a, mod_m, w_blk, w_dn, b_attn, b_up, b_down = weights
+    xm_a, qkv, att, branch_a, x_mid, xm_m, branch_m, pre, act = kept
+    vmem, hbm = pl.BlockSpec(memory_space=pltpu.VMEM), pl.BlockSpec(memory_space=pl.ANY)
+    smem = pl.BlockSpec(memory_space=pltpu.SMEM)
+    like = lambda columns, kind: jax.ShapeDtypeStruct((PATCHES, columns), kind)
+    mods = jax.ShapeDtypeStruct((3, D), jnp.float32)
     return pl.pallas_call(
-        mlp_backward_kernel,
-        grid=(2 * STEPS,),
-        out_shape=(
-            half, jax.ShapeDtypeStruct((3, D), jnp.float32), half,
-            jax.ShapeDtypeStruct((PATCHES, FF), BF),
-        ),
-        in_specs=[token, token, whole_spec((3, D)), token, hidden] + tile_specs(),
-        out_specs=(token, whole_spec((3, D)), token, hidden),
-        scratch_shapes=[pltpu.VMEM((PATCHES, D), jnp.float32)],
+        backward_kernel,
+        out_shape=(like(D, BF), mods, mods, like(D, BF), like(D, BF), like(FF, BF), like(3 * D, BF)),
+        in_specs=[smem] + [vmem] * 8 + [hbm] * 3,
+        out_specs=(vmem,) * 7,
+        scratch_shapes=weight_scratch()
+        + [
+            pltpu.VMEM((PATCHES, FF), jnp.float32),
+            pltpu.VMEM((PATCHES, D), jnp.float32),
+            pltpu.VMEM((PATCHES, 3 * D), jnp.float32),
+            pltpu.VMEM((PATCHES, D), BF),
+            pltpu.SemaphoreType.DMA((7,)),
+        ],
         compiler_params=pltpu.CompilerParams(vmem_limit_bytes=VMEM_BYTES),
-        cost_estimate=pl.CostEstimate(
-            flops=4 * PATCHES * D * FF, bytes_accessed=4 * D * FF, transcendentals=PATCHES * FF
-        ),
-        name="mlp_backward",
-    )(d_out, x, mod, branch, pre, *w_up, *w_dn)
+        cost_estimate=stage_cost(),
+        name="stage_backward",
+    )(flags, d_out, x_in, x_mid, mod_a, mod_m, branch_a, branch_m, qkv, pre, w_blk, w_dn)
 
 
 SUM_ROWS = 16
 
 
 def collect_kernel(peers, flags_ref, *refs):
-    tokens, d_pre_ref, mods, fm_ref, extra_ref = refs[:6], refs[6], refs[7:9], refs[9], refs[10]
-    sums_ref, mods_ref = refs[11:]
+    tokens, d_pre_ref, mods, fm_ref, extra_ref = refs[:4], refs[4], refs[5:7], refs[7], refs[8]
+    sums_ref, mods_ref = refs[9:]
     core, stage = flags_ref[0], flags_ref[1]
     ones = jnp.ones((8, PATCHES), BF)
     total = lambda value: matmul(ones, value)[0:1]
     sums_ref[...] = jnp.zeros_like(sums_ref)
-    rows = [total(ref[...]) for ref in tokens]
+    rows = [total(tokens[0][:, D * k : D * (k + 1)]) for k in range(3)]
+    rows += [total(ref[...]) for ref in tokens[1:]]
     halves = [[total(d_pre_ref[:, D * k : D * (k + 1)]) for k in range(4)]]
     own = halves[0]
     order = [jnp.where(core == 0, own[k], own[(k + 2) % 4]) for k in range(4)]
@@ -793,74 +1008,11 @@
             jax.ShapeDtypeStruct((SUM_ROWS, 128 * max(peers, 9)), jnp.float32),
             jax.ShapeDtypeStruct((2, 16, D), BF),
         ),
-        in_specs=[pl.BlockSpec(memory_space=pltpu.SMEM)] + [vmem] * 11,
+        in_specs=[pl.BlockSpec(memory_space=pltpu.SMEM)] + [vmem] * 9,
         out_specs=(vmem, vmem),
         compiler_params=pltpu.CompilerParams(vmem_limit_bytes=VMEM_BYTES),
         name="collect",
     )(flags, *tokens, d_pre, *mods, fm, extra)
-
-
-def heads_of(value):
-    return value.reshape(PATCHES, HEADS, HEAD_DIM)
-
-
-def attention_forward(xm_half, w_attn, bblk):
-    pair = to_half(matmul(xm_half, w_attn[0]) + bblk[:HALF])
-    value = heads_of(to_half(matmul(xm_half, w_attn[1][:, :D]) + bblk[HALF : 3 * D]))
-    query, key = heads_of(pair[:, :D]), heads_of(pair[:, D:])
-    scores = jnp.einsum(
-        "qhd,khd->hqk", query, key, preferred_element_type=jnp.float32
-    ) * HEAD_DIM ** (-0.5)
-    probs = jax.nn.softmax(scores, axis=-1)
-    attended = to_half(
-        jnp.einsum("hqk,khd->qhd", to_half(probs), value, preferred_element_type=jnp.float32)
-    ).reshape(PATCHES, D)
-    branch = matmul(attended, w_attn[1][:, D:]) + bblk[3 * D :]
-    return (branch, (query, key, value, probs, attended))
-
-
-def attention_backward(grad_half, saved, w_attn):
-    query, key, value, probs, attended = saved
-    d_att = heads_of(to_half(matmul_nt(grad_half, w_attn[1][:, D:])))
-    flat = lambda grad: to_half(grad).reshape(PATCHES, D)
-    d_value = flat(
-        jnp.einsum("hqk,qhd->khd", to_half(probs), d_att, preferred_element_type=jnp.float32)
-    )
-    d_probs = jnp.einsum("qhd,khd->hqk", d_att, value, preferred_element_type=jnp.float32)
-    d_scores = to_half(probs * (d_probs - jnp.sum(probs * d_probs, axis=-1, keepdims=True)))
-    d_query = flat(
-        jnp.einsum("hqk,khd->qhd", d_scores, key, preferred_element_type=jnp.float32)
-        * HEAD_DIM ** (-0.5)
-    )
-    d_key = flat(
-        jnp.einsum("hqk,qhd->khd", d_scores, query, preferred_element_type=jnp.float32)
-        * HEAD_DIM ** (-0.5)
-    )
-    d_pair = jnp.concatenate([d_query, d_key], axis=1)
-    d_xm = matmul_nt(d_pair, w_attn[0]) + matmul_nt(d_value, w_attn[1][:, :D])
-    return (d_xm, d_query, d_key, d_value)
-
-
-def stage_forward(x_in, weights):
-    mod_a, mod_m, w_attn, w_up, w_dn, b_attn, b_up, b_down = weights
-    normed, inverse = normalized(x_in)
-    xm_a = to_half(normed * (1.0 + mod_a[1:2]) + mod_a[0:1])
-    branch_a, saved = attention_forward(xm_a, w_attn, b_attn)
-    x_mid = to_half(x_in + mod_a[2:3] * branch_a).astype(jnp.float32)
-    x_out, xm_m, branch_m, pre, act = mlp_forward(x_mid, mod_m, b_up, b_down, w_up, w_dn)
-    return (x_out, (xm_a, branch_a, saved, x_mid, xm_m, branch_m, pre, act))
-
-
-def attn_backward(d_out, x_in, weights, kept):
-    mod_a, mod_m, w_attn, w_up, w_dn, b_attn, b_up, b_down = weights
-    branch_a, saved = kept[1:3]
-    d_gate = jnp.sum(d_out * branch_a, axis=0)
-    grad_half = to_half(d_out * mod_a[2:3])
-    d_xm, d_query, d_key, d_value = attention_backward(grad_half, saved, w_attn)
-    normed, inverse = normalized(x_in)
-    d_x, d_shift, d_scale = modulated_back(normed, inverse, mod_a[1:2], d_xm)
-    d_mod = jnp.stack([d_shift, d_scale, d_gate])
-    return (to_half(d_out + d_x), d_mod, grad_half, (d_query, d_key, d_value))
 
 
 def final_step(x_out, fmod, w_head, b_head, target, counts, loss_scale):
@@ -904,69 +1056,61 @@
     n = lax.axis_size("dp")
     width = D // n
 
-    downs = jnp.swapaxes(down_w, 1, 2)
-    blk_half = to_half(block_w[0])
-    crossing = swap(jnp.where(even, blk_half[:, HALF:], blk_half[:, :HALF]), 1)
-    attn_half = jnp.where(even, blk_half[:, :HALF], crossing)
-    up_half = jnp.where(even, crossing, blk_half[:, HALF:])
+    flags = jnp.stack([core, stage]).astype(jnp.int32)
+    downs, stems = jnp.swapaxes(down_w, 1, 2), stem_w.T
+    stem_half, tail_half, mod_half_w = to_half(stems), to_half(tail_w), to_half(mod_w[0])
     dn_half = to_half(lax.dynamic_slice(downs, (stage, 0, core * HALF), (1, width, HALF))[0])
-    up_own = lax.all_gather(up_half, "dp", axis=0, tiled=True)
-    dn_own = lax.all_gather(dn_half, "dp", axis=0, tiled=True)
-    w_up = (up_own, swap(up_own, 1))
-    w_dn = (dn_own, swap(dn_own, 1))
-    w_attn = gather_weights(attn_half)
-
-    stems = stem_w.T
-    classes_own = jnp.where(null_mask > 0, NCLS - 1, labels)
-    meta = jnp.stack([timesteps, classes_own, valid], axis=1)
-    images_own = meta.shape[0]
-    meta = jnp.pad(meta, ((0, 8 - images_own), (0, 125)))
-    stem_half = to_half(stems)
-    tail_half = to_half(tail_w)
-    table = stem_half[:, :NCLS]
-    w_two = stem_half[:, NCLS + PATCH_IN + FREQ :]
-    ends = NCLS, NCLS + PATCH_IN + FREQ
-    small = jnp.concatenate([stem_half[:, ends[0] : ends[1]], tail_half[:, 2 * D :]], axis=1)
-    small = jnp.pad(small, ((0, -width % 16), (0, -small.shape[1] % 128)))
-    meta, small = exchange(2, "dp", ("all", "all"), meta, small)
-    meta = meta[:, :images_own].reshape(n * images_own, 128)
-    small = small[:, :width].reshape(D, -1)
-    w_patch_all = small[:, :PATCH_IN]
-    w_one_all = small[:, PATCH_IN : PATCH_IN + FREQ]
-    w_head_all = small[:, PATCH_IN + FREQ : PATCH_IN + FREQ + HEAD_OUT]
-    images = meta.shape[0]
-    steps_all = meta[:, 0].astype(jnp.float32)
-    picks = (meta[:, 1][:, None] == jnp.arange(NCLS, dtype=jnp.int32)[None, :]).astype(BF)
-    count = jnp.sum(meta[:, 2].astype(jnp.float32))
+    at_one, at_two = NCLS + PATCH_IN, NCLS + PATCH_IN + FREQ
+    w_two = stem_half[:, at_two:]
+    table = jnp.pad(stem_half[:, :NCLS], ((0, 0), (0, META - FREQ - NCLS)))
+    w_fm = tail_half[:, : 2 * D]
+    small = jnp.concatenate(
+        [stem_half[:, at_one:at_two], stem_half[:, NCLS:at_one], tail_half[:, 2 * D :]], axis=1
+    )
+    small = jnp.pad(small, ((0, 0), (0, -small.shape[1] % 128)))
+    classes = jnp.where(null_mask > 0, NCLS - 1, labels)
+    lanes = jnp.arange(META - FREQ, dtype=jnp.int32)[None, :]
+    picks = (classes[:, None] == lanes).astype(jnp.float32)
+    picks = jnp.where(lanes == META - FREQ - 1, valid.astype(jnp.float32)[:, None], picks)
+    freq = to_half(time_features(timesteps.astype(jnp.float32))).astype(jnp.float32)
+    meta = jnp.concatenate([freq, picks], axis=1)
+    meta = jnp.pad(meta, ((0, 8 - meta.shape[0]), (0, 0)))
+    b_two = lax.dynamic_slice_in_dim(biases, 32 * D + place * width, width)
+    w_blk, w_dn, meta, small, pre, cond, mods = gather_weights(
+        to_half(block_w[0]), dn_half, meta, small, w_two, table, mod_half_w, w_fm,
+        biases[None, 31 * D : 32 * D], b_two[None],
+    )
+    small = small.reshape(D, -1)
+    w_patch_all = small[:, FREQ : FREQ + PATCH_IN]
+    w_head_all = small[:, FREQ + PATCH_IN : FREQ + PATCH_IN + HEAD_OUT]
+    of_images = lambda value: value.reshape(n, 8, -1)[:, :2].reshape(2 * n, -1)
+    images = 2 * n
+    meta = of_images(meta)
+    count = jnp.sum(meta[:, META - 1])
     loss_scale = 1.0 / (count * PATCHES * HEAD_OUT)
-    freq = to_half(time_features(steps_all))
-
-    b_two = lax.dynamic_slice_in_dim(biases, 32 * D + place * width, width)
-    hidden_pre = matmul_nt(w_one_all, freq) + biases[31 * D : 32 * D, None]
-    hidden_all = to_half(jax.nn.silu(hidden_pre))
-    cond = matmul(w_two, hidden_all) + b_two[:, None] + matmul_nt(table, picks)
-    cond_low = to_half(cond).astype(jnp.float32)
-    cond_own = jnp.where(section == 0, cond, cond_low)
-    silu_own = to_half(jax.nn.silu(cond_own))
-    silu_low = to_half(jax.nn.silu(cond_low))
-    mod_half_w = to_half(mod_w[0])
-    part_mod = matmul_tn(silu_own, mod_half_w)
-    part_fm = matmul_tn(silu_low, tail_half[:, : 2 * D])
-    parts = jnp.concatenate([part_mod, part_fm, jnp.zeros((images, 384), jnp.float32)], axis=1)
-    (mods,) = exchange(3, "stage", ("each",), parts.reshape(images, 48, 128))
-    mods = jnp.sum(mods.reshape(n, 2, 48 * 128), axis=0)
+    mods = mods.reshape(2, 8 * PIECE)
     bias_of = lambda first, length: lax.dynamic_slice_in_dim(biases, first, length)
     mod_a = (mods[0, : 3 * D] + bias_of(6 * D * stage, 3 * D)).reshape(3, D)
     mod_b = (mods[1, : 3 * D] + bias_of(6 * D * stage + 3 * D, 3 * D)).reshape(3, D)
     fmod = (mods[0, 3 * D : 5 * D] + biases[33 * D : 35 * D]).reshape(2, D)
     weights = (
-        mod_a, mod_b, w_attn, w_up, w_dn,
-        bias_of(12 * D + 8 * D * stage, 4 * D),
+        flags, mod_a, mod_b, w_blk, w_dn,
+        bias_of(12 * D + 8 * D * stage, 4 * D)[None],
         jnp.concatenate(
             [bias_of(16 * D + 8 * D * stage + HALF * half, HALF)[None] for half in (core, 1 - core)], axis=1
         ),
         bias_of(28 * D + D * stage, D)[None],
     )
+
+    freq = to_half(meta[:, :FREQ])
+    picks = to_half(meta[:, FREQ : FREQ + NCLS])
+    hidden_pre = of_images(pre).T
+    hidden_all = to_half(jax.nn.silu(hidden_pre))
+    cond = of_images(cond).T
+    cond_low = to_half(cond).astype(jnp.float32)
+    cond_own = jnp.where(section == 0, cond, cond_low)
+    silu_own = to_half(jax.nn.silu(cond_own))
+    silu_low = to_half(jax.nn.silu(cond_low))
 
     step = pick(timesteps, core).astype(jnp.float32)
     signal, spread = noise_levels(step)
@@ -976,28 +1120,25 @@
     target = jnp.concatenate([patchify(signal * noi - spread * lat), patchify(noi)], axis=2)[0]
     x_first = matmul_nt(tok_half, w_patch_all) + biases[30 * D : 31 * D] + position_table(GRID // 2, D)
 
-    x_hop = swap(to_half(stage_forward(x_first, weights)[0]), 2)
+    x_hop = swap(stage_forward(False, x_first, weights)[0], 2)
     x_in = jnp.where(stage == 0, x_first, x_hop.astype(jnp.float32))
-    x_out, kept = stage_forward(x_in, weights)
+    x_out, *kept = stage_forward(True, x_in, weights)
     loss, d_final, d_fmod, g_head, b_head = final_step(
         x_out, fmod, w_head_all, biases[35 * D :], target, counts, loss_scale
     )
-    xm_a, branch_a, saved, x_mid, xm_b, branch_b, pre, act = kept
-    attended = saved[-1]
-    back = lambda d_out: mlp_backward(d_out, x_mid, mod_b, branch_b, pre, w_up, w_dn)
-    d_mid = back(d_final)[0].astype(jnp.float32)
-    d_hop = swap(attn_backward(d_mid, x_in, weights, kept)[0], 2)
+    xm_a, qkv, attended, branch_a, x_mid, xm_b, branch_b, pre, act = kept
+    d_hop = swap(stage_backward(d_final, x_in, weights, kept)[0], 2)
     d_out = jnp.where(stage == 1, d_final, d_hop.astype(jnp.float32))
-
-    d_mid, d_mod_b, d_branch_b, d_pre = back(d_out)
-    d_mid = d_mid.astype(jnp.float32)
+    d_first, d_mod_a, d_mod_b, d_branch_a, d_branch_b, d_pre, d_qkv = stage_backward(
+        d_out, x_in, weights, kept
+    )
+    d_query, d_key, d_value = (d_qkv[:, D * k : D * (k + 1)] for k in range(3))
+
     act_sib, branch_sib, xm_sib, pre_sib = swap((act[:, HALF:], d_branch_b, xm_b, d_pre[:, HALF:]), 1)
     g_dn = to_half(matmul_tn(d_branch_b, act[:, :HALF]) + matmul_tn(branch_sib, act_sib))
     g_up = to_half(matmul_tn(xm_b, d_pre[:, :HALF]) + matmul_tn(xm_sib, pre_sib))
     g_dn = lax.psum_scatter(g_dn, "dp", scatter_dimension=0, tiled=True)
 
-    d_first, d_mod_a, d_branch_a, d_qkv = attn_backward(d_mid, x_in, weights, kept)
-    d_query, d_key, d_value = d_qkv
     xa_sib, last_sib, one_sib, two_sib = swap(
         (
             xm_a,
@@ -1030,11 +1171,10 @@
     here, there = in_core(g_dn, g_sib), in_core(g_facing, g_corner)
     down_both = jnp.where(stage == 0, jnp.stack([here, there]), jnp.stack([there, here]))
 
-    flags = jnp.stack([core, stage]).astype(jnp.int32)
     extra = jnp.stack([jnp.pad(b_head, (0, D - HEAD_OUT)), jnp.pad(loss[None], (0, D - 1))])
     d_fmod = jnp.where(stage == 1, d_fmod, jnp.zeros_like(d_fmod))
     own_biases, d_mods = collect(
-        flags, d_qkv + (d_branch_a, d_branch_b, d_first), d_pre, (d_mod_a, d_mod_b), d_fmod, extra
+        flags, (d_qkv, d_branch_a, d_branch_b, d_first), d_pre, (d_mod_a, d_mod_b), d_fmod, extra
     )
     g_patch = jnp.pad(matmul_tn(d_first, tok_half), ((0, 0), (0, HEAD_OUT - PATCH_IN)))
     end_rows = row_count(width * HEAD_OUT)

time: 877 us -> 765 us (0.87)
  Pallas kernels: 405 us -> 524 us
  waiting for transfers between devices: 140 us -> 32.1 us
  matrix products: 119 us -> 36.8 us
  local copies, waits for them, and re-layouts: 85.7 us -> 53.5 us
    pallas_call x5, Pallas kernels: 140 us -> 322 us  [the longest x1 220 us: gather_weights(): pl.pallas_call(gather_kernel, out_shape=(jax.ShapeDtypeStruct((2, D, FF),...]
    all_gather x2 -> x0, waiting for transfers between devices: 114 us -> none  [the longest x1 88.9 us: body(): up_own = lax.all_gather(up_half, 'dp', axis=0, tiled=True)]
    pallas_call x6 -> x4, Pallas kernels: 147 us -> 83.5 us  [exchange(): pl.pallas_call(partial(exchange_kernel, axes, modes), out_shape=tuple((ja...]
    dot_general x12 -> x5, matrix products: 31.1 us -> 6.04 us  [matmul(): return jnp.dot(left, right, preferred_element_type=jnp.float32)]
    dot_general x13 -> x5, matrix products: 25.9 us -> 6.68 us  [matmul_nt(): lax.dot_general(left, right, (((1,), (1,)), ((), ())), preferred_element_...]
    dot_general x10 -> x0, matrix products: 18.8 us -> none  [the longest x2 5.77 us: attention_forward(): jnp.einsum('hqk,khd->qhd', to_half(probs), value, preferred_element_type=...]
    dot_general x13 -> x11, matrix products: 34.2 us -> 24.1 us  [matmul_tn(): lax.dot_general(left, right, (((0,), (0,)), ((), ())), preferred_element_...]
    sub x2 -> x0, matrix products: 9.57 us -> none  [attention_forward(): probs = jax.nn.softmax(scores, axis=-1)]
  transfers between devices with their start and end apart: 20 -> 15, of which waited for: 7 -> 4; matrix products, arithmetic and copies ran while one was open for 19% -> 10% of each run, Pallas kernels for 39% -> 29%
where the time goes in v5:
time: 765 us; the launch traced here: 758 us
  Pallas kernels  524 us (68%)
  other arithmetic  80.7 us (11%)
  local copies, waits for them, and re-layouts  53.5 us (7%)
  matrix products  36.8 us (5%)
  waiting for transfers between devices  32.1 us (4%)
  between operations  24.1 us (3%)
    pallas_call x1, Pallas kernels, gather_weights(): pl.pallas_call(gather_kernel, out_shape=(jax.ShapeDtypeStruct((2, D, FF),...  220 us
    pallas_call x1, Pallas kernels, sum_gradients(): pl.pallas_call(sum_kernel, out_shape=jax.ShapeDtypeStruct((2, 144, HALF),...  114 us
    pallas_call x4, Pallas kernels, exchange(): pl.pallas_call(partial(exchange_kernel, axes, modes), out_shape=tuple((ja...  83.5 us
    pallas_call x2, Pallas kernels, stage_backward(): pl.pallas_call(backward_kernel, out_shape=(like(D, BF), mods, mods, like(...  62.3 us
    pallas_call x2, Pallas kernels, stage_forward(): pl.pallas_call(partial(forward_kernel, save), out_shape=tuple(shapes), in...  39.6 us
    ppermute x14, waiting for transfers between devices, swap(): return lax.ppermute(array, 'section', [(k, k ^ by) for k in range(peers)])  32 us
    dot_general x11, matrix products, matmul_tn(): lax.dot_general(left, right, (((0,), (0,)), ((), ())), preferred_element_...  24.1 us
  transfers between devices with their start and end apart: 15, of which 4 were waited for; matrix products, arithmetic and copies ran while one was open for 10% of the time, Pallas kernels for 29%

profile of v5, /device:TPU:0, one launch (start us, length us, event | category | flops | bytes accessed | tf_op | source)
XLA Modules:
  0.0 757.8 jit_solution(9658601288582560659)
XLA Ops:
  19.0 2.6 convert_bitcast_fusion.2.mod_ref
  26.2 2.2 fusion.17.dn_ref
  30.1 219.8 %gather_weights.1 = (bf16[2,1152,4608]{2,1,0:T(8,128)(2,1)}, bf16[2,1152,2304]{2,1,0:T(8,128)(2,1)}, f32[8,8,1280]{2,1,0:T(8,128)}, bf16[8,144,384]{2,1,0:T(8,12...) custom-call(bf16[144,4608]{1,0:T(8,128)(2,1)} %convert_bitcast_fusion.1.blk_ref, ...), custom_call_target="tpu_custom_call" | custom-call | bytes 400000000 | tf_op jit(solution)/shard_map/gather_weights/pallas_call | solution.py:400
  256.9 2.3 fusion.6.x_ref
  259.3 18.5 %stage_forward.2 = bf16[256,1152]{1,0:T(8,128)(2,1)} custom-call(s32[2]{0:T(128)} %get-tuple-element.157.flags.flags_ref, f32[256,1152]{1,0:T(8,128)} %fusion.6.x_ref, f32[3,1152]{1,0:T(4,128)} %reshape.358.mod_a, f32[3,1152]{1,0:T(4,128)} %reshape.359.mod_m, f32[1,4608]{1,0:T(1,128)} %broadcast_in_dim.86.b_attn, f32[1,4608]{1,0:T(1,128)} %copy-done.63, ...), custom_call_target="tpu_custom_call" | custom-call | flops 16911433728 | bytes 31850496 | tf_op jit(solution)/shard_map/stage_forward/pallas_call | solution.py:941
  284.8 8.8 %collective-permute-done = bf16[256,1152]{1,0:T(8,128)(2,1)S(1)} collective-permute-done((bf16[256,1152]{1,0:T(8,128)(2,1)}, bf16[256,1152]{1,0:T(8,128)(2,1)S(1)}, u32[]{:S(2)}, u32[]{:S(2)}) %collective-permute-start) | collective-permute-done | bytes 589856 | tf_op jit(solution)/shard_map/ppermute | solution.py:1039
  294.8 21.1 %stage_forward.3 = (f32[256,1152]{1,0:T(8,128)}, bf16[256,1152]{1,0:T(8,128)(2,1)}, bf16[256,3456]{1,0:T(8,128)(2,1)}, bf16[256,1152]{1,0:T(8,128)(2,1)}, f32[25...) custom-call(s32[2]{0:T(128)} %get-tuple-element.157.flags.flags_ref,, ...), custom_call_target="tpu_custom_call" | custom-call | flops 16911433728 | bytes 31850496 | tf_op jit(solution)/shard_map/stage_forward/pallas_call | solution.py:941
  322.1 31.0 %stage_backward.2 = (bf16[256,1152]{1,0:T(8,128)(2,1)}, f32[3,1152]{1,0:T(4,128)}, f32[3,1152]{1,0:T(4,128)}, bf16[256,1152]{1,0:T(8,128)(2,1)}, bf16[256,1152]{...) custom-call(s32[2]{0:T(128)} %get-tuple-element.157.flags.flags_ref, ...), custom_call_target="tpu_custom_call" | custom-call | flops 16911433728 | bytes 31850496 | tf_op jit(solution)/shard_map/stage_backward/pallas_call | solution.py:960
  354.7 2.4 slice.253
  357.2 10.9 %collective-permute-done.1 = bf16[256,1152]{1,0:T(8,128)(2,1)S(1)} collective-permute-done((bf16[256,1152]{1,0:T(8,128)(2,1)}, bf16[256,1152]{1,0:T(8,128)(2,1)S(1)}, u32[]{:S(2)}, u32[]{:S(2)}) %collective-permute-start.1) | collective-permute-done | bytes 589856 | tf_op jit(solution)/shard_map/ppermute | solution.py:1039
  369.2 31.3 %stage_backward.3 = (bf16[256,1152]{1,0:T(8,128)(2,1)}, f32[3,1152]{1,0:T(4,128)}, f32[3,1152]{1,0:T(4,128)}, bf16[256,1152]{1,0:T(8,128)(2,1)}, bf16[256,1152]{...) custom-call(s32[2]{0:T(128)} %get-tuple-element.157.flags.flags_ref, ...), custom_call_target="tpu_custom_call" | custom-call | flops 16911433728 | bytes 31850496 | tf_op jit(solution)/shard_map/stage_backward/pallas_call | solution.py:960
  404.6 3.1 fusion.100
  407.8 4.0 fusion.1
  417.5 4.5 collect.1
  423.6 36.0 %exchange_stage.1 = (bf16[16,16,1152]{2,1,0:T(8,128)(2,1)}, f32[16,16,128]{2,1,0:T(8,128)}, f32[16,40,128]{2,1,0:T(8,128)}) custom-call(bf16[2,16,1152]{2,1,0:T(8,128)(2,1)} %get-tuple-element.79.refs_0_, f32[16,16,128]{2,1,0:T(8,128)} %bitcast_bitcast_fusion.refs_1_, f32[8,40,128]{2,1,0:T(8,128)} %bitcast.270), custom_call_target="tpu_custom_call" | custom-call | bytes 30000000 | tf_op jit(solution)/shard_map/exchange_stage/pallas_call | solution.py:716
  466.1 9.0 %exchange_section.1 = (f32[4,24,128]{2,1,0:T(8,128)}, f32[4,40,128]{2,1,0:T(8,128)}, bf16[4,16,2304]{2,1,0:T(8,128)(2,1)}) custom-call(f32[24,128]{1,0:T(8,128)} %pad_bitcast_fusion.2.refs_0_, f32[40,128]{1,0:T(8,128)} %reduce_sum.221.refs_1_, bf16[16,2304]{1,0:T(8,128)(2,1)} %bitcast.281), custom_call_target="tpu_custom_call" | custom-call | bytes 30000000 | tf_op jit(solution)/shard_map/exchange_section/pallas_call | solution.py:716
  478.9 26.4 %exchange_dp.1 = f32[8,24,128]{2,1,0:T(8,128)} custom-call(f32[8,24,128]{2,1,0:T(8,128)} %bitcast.274), custom_call_target="tpu_custom_call" | custom-call | bytes 30000000 | tf_op jit(solution)/shard_map/exchange_dp/pallas_call | solution.py:716
  516.5 2.4 concatenate.100
  522.6 2.2 fusion.99
  526.9 2.2 fusion.3
  529.2 2.7 pad_maximum_fusion.g_second
  531.9 2.8 fusion.98
  534.8 4.0 fusion.g_first
  538.8 113.8 %sum_gradients.1 = f32[2,144,2304]{2,1,0:T(8,128)} custom-call(bf16[1152,2304]{1,0:T(8,128)(2,1)} %fusion.g_first, bf16[1152,2304]{1,0:T(8,128)(2,1)} %pad_maximum_fusion.g_second), custom_call_target="tpu_custom_call" | custom-call | bytes 300000000 | tf_op jit(solution)/shard_map/sum_gradients/pallas_call | solution.py:633
  652.6 2.8 fusion.11
  657.5 2.3 multiply_reduce_fusion.1
  665.9 11.4 %collective-permute-done.12 = bf16[144,2304]{1,0:T(8,128)(2,1)} collective-permute-done((bf16[144,2304]{1,0:T(8,128)(2,1)}, bf16[144,2304]{1,0:T(8,128)(2,1)}, u32[]{:S(2)}, u32[]{:S(2)}) %collective-permute-start.12) | collective-permute-done | bytes 663584 | tf_op jit(solution)/shard_map/ppermute | solution.py:1039
  687.3 12.2 %exchange_every.1 = f32[32,24,128]{2,1,0:T(8,128)} custom-call(f32[24,128]{1,0:T(8,128)} %pad_maximum_fusion.4.refs_0_), custom_call_target="tpu_custom_call" | custom-call | bytes 30000000 | tf_op jit(solution)/shard_map/exchange_every/pallas_call | solution.py:716
  713.5 4.0 fusion.88
  720.6 7.9 %convert_bitcast_fusion = (bf16[2,4608,144]{1,2,0:T(8,128)(2,1)}, f32[2,144,4608]{2,1,0:T(8,128)S(1)}, f32[2,4608,144]{1,2,0:T(8,128)}) fusion(f32[2,4608,144]{1,2,0:T(8,128)} %param.37, f32[]{:T(128)S(6)} %min.3, f32[1,144,4608]{2,1,0:T(8,128)S(1)} %maximum_convert_fusion, f32[1,144,4608]{2,1,0:T(8,128)S(1)} %copy-done.1, pred[]{:T(512)S(6)} %eq.44, ...), kind=kLoop, calls=%fused_computation.21 | loop fusion | flops 14598144 | bytes 29196292 | tf_op jit(solution)/shard_map/transpose | solution.py:1255
  733.0 3.8 fusion.4
  738.2 2.6 fusion.89
  (347 shorter events, 122.5 us)
Async XLA Ops:
  7.2 652.7 %reduce-scatter.2.cloned.1.call-start = ((), (), s32[]{:S(2)}) async-start(), calls=%async_computation.1 | async-start | bytes 5971968 | tf_op jit(solution)/shard_map/reduce_scatter | solution.py:1140
  30.1 222.3 %copy-start.64 = (s32[2]{0:T(128)S(1)}, s32[2]{0:T(128)}, u32[]{:S(2)}) copy-start(s32[2]{0:T(128)} %param.26) | copy-start | bytes 28
  30.1 223.7 %copy-start.58 = (f32[2,32,32,4]{2,3,1,0:T(4,128)S(1)}, f32[2,32,32,4]{2,3,1,0:T(4,128)}, u32[]{:S(2)}) copy-start(f32[2,32,32,4]{2,3,1,0:T(4,128)} %param.24) | copy-start | bytes 98308
  30.1 223.7 %copy-start.59 = (f32[2,32,32,4]{2,3,1,0:T(4,128)S(1)}, f32[2,32,32,4]{2,3,1,0:T(4,128)}, u32[]{:S(2)}) copy-start(f32[2,32,32,4]{2,3,1,0:T(4,128)} %param.25) | copy-start | bytes 98308
  30.1 225.5 %copy-start.57 = (f32[1152]{0:T(1024)S(1)}, f32[1152]{0:T(1024)}, u32[]{:S(2)}) copy-start(f32[1152]{0:T(1024)} %get-tuple-element.136) | copy-start | bytes 13828
  259.3 20.1 %copy-start.65 = (s32[2]{0:T(128)S(1)}, s32[2]{0:T(128)}, u32[]{:S(2)}) copy-start(s32[2]{0:T(128)} %param.29) | copy-start | bytes 28
  277.8 15.9 %copy-start.27 = (f32[256,1152]{1,0:T(8,128)S(1)}, f32[256,1152]{1,0:T(8,128)}, u32[]{:S(2)}) copy-start(f32[256,1152]{1,0:T(8,128)} %fusion.6.x_ref) | copy-start | bytes 3538948
  277.8 15.9 %collective-permute-start = (bf16[256,1152]{1,0:T(8,128)(2,1)}, bf16[256,1152]{1,0:T(8,128)(2,1)S(1)}, u32[]{:S(2)}, u32[]{:S(2)}) collective-permute-start(bf16[256,1152]{1,0:T(8,128)(2,1)} %stage_forward.2), channel_id=1, source_target_pairs={{0,2},{1,3},{2,0},{3,1},{4,6},{5,7},{6,4},{7,5},{8,10},{9,11},{10,... | collective-permute-start | bytes 1769480 | tf_op jit(solution)/shard_map/ppermute | solution.py:1039
  353.1 15.1 %copy-start.28 = (f32[256,1152]{1,0:T(8,128)S(1)}, f32[256,1152]{1,0:T(8,128)}, u32[]{:S(2)}) copy-start(f32[256,1152]{1,0:T(8,128)} %subtract_multiply_fusion.d_ref) | copy-start | bytes 3538948
  353.1 15.1 %collective-permute-start.1 = (bf16[256,1152]{1,0:T(8,128)(2,1)}, bf16[256,1152]{1,0:T(8,128)(2,1)S(1)}, u32[]{:S(2)}, u32[]{:S(2)}) collective-permute-start(bf16[256,1152]{1,0:T(8,128)(2,1)} %get-tuple-element.71), channel_id=1, source_target_pairs={{0,2},{1,3},{2,0},{3,1},{4,6},{5,7},{6,4},{7,5},{8,10},{9,11},{10,... | collective-permute-start | bytes 1769480 | tf_op jit(solution)/shard_map/ppermute | solution.py:1039
  357.0 47.6 %collective-permute-start.10 = (bf16[256,2304]{1,0:T(8,128)(2,1)}, bf16[256,2304]{1,0:T(8,128)(2,1)}, u32[]{:S(2)}, u32[]{:S(2)}) collective-permute-start(bf16[256,2304]{1,0:T(8,128)(2,1)} %slice.253), channel_id=1, source_target_pairs={{0,1},{1,0},{2,3},{3,2},{4,5},{5,4},{6,7},{7,6},{8,9},{9,8},{10,11... | collective-permute-start | bytes 3538952 | tf_op jit(solution)/shard_map/ppermute | solution.py:1039
  369.2 34.7 %copy-start.62 = (f32[1152]{0:T(1024)S(1)}, f32[1152]{0:T(1024)}, u32[]{:S(2)}) copy-start(f32[1152]{0:T(1024)} %get-tuple-element.96) | copy-start | bytes 13828
  369.2 34.8 %copy-start.61 = (f32[1152]{0:T(1024)S(1)}, f32[1152]{0:T(1024)}, u32[]{:S(2)}) copy-start(f32[1152]{0:T(1024)} %get-tuple-element.93) | copy-start | bytes 13828
  400.6 4.0 collective-permute-start.9
  401.5 60.5 %copy-start.53 = (f32[16,144]{1,0:T(8,128)}, f32[16,144]{1,0:T(8,128)S(1)}, u32[]{:S(2)}) copy-start(f32[16,144]{1,0:T(8,128)S(1)} %reshape.371) | copy-start | bytes 27652
  404.1 118.2 %collective-permute-start.4 = (bf16[256,1152]{1,0:T(8,128)(2,1)}, bf16[256,1152]{1,0:T(8,128)(2,1)}, u32[]{:S(2)}, u32[]{:S(2)}) collective-permute-start(bf16[256,1152]{1,0:T(8,128)(2,1)} %get-tuple-element.88), channel_id=1, source_target_pairs={{0,1},{1,0},{2,3},{3,2},{4,5},{5,4},{6,7},{7,6},{8,9},{9,8},{10,11... | collective-permute-start | bytes 1769480 | tf_op jit(solution)/shard_map/ppermute | solution.py:1039
  413.7 113.2 %collective-permute-start.6 = (bf16[256,1152]{1,0:T(8,128)(2,1)}, bf16[256,1152]{1,0:T(8,128)(2,1)}, u32[]{:S(2)}, u32[]{:S(2)}) collective-permute-start(bf16[256,1152]{1,0:T(8,128)(2,1)} %broadcast_select_fusion), channel_id=1, source_target_pairs={{0,1},{1,0},{2,3},{3,2},{4,5},{5,4},{6,7},{7,6},{8,9},{9,8},{10,11... | collective-permute-start | bytes 1769480 | tf_op jit(solution)/shard_map/ppermute | solution.py:1039
  414.7 117.3 %collective-permute-start.2 = (bf16[256,1152]{1,0:T(8,128)(2,1)}, bf16[256,1152]{1,0:T(8,128)(2,1)}, u32[]{:S(2)}, u32[]{:S(2)}) collective-permute-start(bf16[256,1152]{1,0:T(8,128)(2,1)} %get-tuple-element.87), channel_id=1, source_target_pairs={{0,1},{1,0},{2,3},{3,2},{4,5},{5,4},{6,7},{7,6},{8,9},{9,8},{10,11... | collective-permute-start | bytes 1769480 | tf_op jit(solution)/shard_map/ppermute | solution.py:1039
  417.5 44.1 %copy-start.18 = (bf16[144,3456]{1,0:T(8,128)(2,1)S(1)}, bf16[144,3456]{1,0:T(8,128)(2,1)}, u32[]{:S(2)}) copy-start(bf16[144,3456]{1,0:T(8,128)(2,1)} %convert_bitcast_fusion.2.mod_ref) | copy-start | bytes 2985988
  462.0 44.4 %copy-start.7 = (bf16[256,3456]{1,0:T(8,128)(2,1)S(1)}, bf16[256,3456]{1,0:T(8,128)(2,1)}, u32[]{:S(2)}) copy-start(bf16[256,3456]{1,0:T(8,128)(2,1)} %get-tuple-element.72.refs_0_) | copy-start | bytes 5308420
  462.0 44.4 %copy-start.26 = (bf16[256,1152]{1,0:T(8,128)(2,1)S(1)}, bf16[256,1152]{1,0:T(8,128)(2,1)}, u32[]{:S(2)}) copy-start(bf16[256,1152]{1,0:T(8,128)(2,1)} %get-tuple-element.73.refs_1_) | copy-start | bytes 1769476
  507.6 15.0 %collective-permute-start.5 = (bf16[256,1152]{1,0:T(8,128)(2,1)}, bf16[256,1152]{1,0:T(8,128)(2,1)}, u32[]{:S(2)}, u32[]{:S(2)}) collective-permute-start(bf16[256,1152]{1,0:T(8,128)(2,1)} %get-tuple-element.123), channel_id=1, source_target_pairs={{0,1},{1,0},{2,3},{3,2},{4,5},{5,4},{6,7},{7,6},{8,9},{9,8},{10,11... | collective-permute-start | bytes 1769480 | tf_op jit(solution)/shard_map/ppermute | solution.py:1039
  515.4 11.6 %collective-permute-start.7 = (bf16[256,1152]{1,0:T(8,128)(2,1)}, bf16[256,1152]{1,0:T(8,128)(2,1)}, u32[]{:S(2)}, u32[]{:S(2)}) collective-permute-start(bf16[256,1152]{1,0:T(8,128)(2,1)} %get-tuple-element.124), channel_id=1, source_target_pairs={{0,1},{1,0},{2,3},{3,2},{4,5},{5,4},{6,7},{7,6},{8,9},{9,8},{10,11... | collective-permute-start | bytes 1769480 | tf_op jit(solution)/shard_map/ppermute | solution.py:1039
  522.2 9.7 %collective-permute-start.3 = (bf16[256,2304]{1,0:T(8,128)(2,1)S(1)}, bf16[256,2304]{1,0:T(8,128)(2,1)S(1)}, u32[]{:S(2)}, u32[]{:S(2)}) collective-permute-start(bf16[256,2304]{1,0:T(8,128)(2,1)S(1)} %copy-done.42), channel_id=1, source_target_pairs={{0,1},{1,0},{2,3},{3,2},{4,5},{5,4},{6,7},{7,6},{8,9},{9,8},{10,11... | collective-permute-start | bytes 3538952 | tf_op jit(solution)/shard_map/ppermute | solution.py:1039
  655.4 5.6 collective-permute-start.8
  659.9 17.5 %collective-permute-start.12 = (bf16[144,2304]{1,0:T(8,128)(2,1)}, bf16[144,2304]{1,0:T(8,128)(2,1)}, u32[]{:S(2)}, u32[]{:S(2)}) collective-permute-start(bf16[144,2304]{1,0:T(8,128)(2,1)} %reduce-scatter.2.cloned.1.call-done), channel_id=1, source_target_pairs={{0,2},{1,3},{2,0},{3,1},{4,6},{5,7},{6,4},{7,5},{8,10},{9,11},{10,... | collective-permute-start | bytes 1990664 | tf_op jit(solution)/shard_map/ppermute | solution.py:1039
  660.9 16.5 %collective-permute-start.11 = (bf16[144,2304]{1,0:T(8,128)(2,1)}, bf16[144,2304]{1,0:T(8,128)(2,1)}, u32[]{:S(2)}, u32[]{:S(2)}) collective-permute-start(bf16[144,2304]{1,0:T(8,128)(2,1)} %reduce-scatter.2.cloned.1.call-done), channel_id=1, source_target_pairs={{0,1},{1,0},{2,3},{3,2},{4,5},{5,4},{6,7},{7,6},{8,9},{9,8},{10,11... | collective-permute-start | bytes 1990664 | tf_op jit(solution)/shard_map/ppermute | solution.py:1039
  662.3 15.1 %copy-start.43 = (bf16[144,2304]{1,0:T(8,128)(2,1)S(1)}, bf16[144,2304]{1,0:T(8,128)(2,1)}, u32[]{:S(2)}) copy-start(bf16[144,2304]{1,0:T(8,128)(2,1)} %reduce-scatter.2.cloned.1.call-done) | copy-start | bytes 1990660
  677.4 2.3 collective-permute-start.13
  684.6 22.2 %copy-start.44 = (f32[40352]{0:T(1024)S(1)}, f32[40352]{0:T(1024)}, u32[]{:S(2)}) copy-start(f32[40352]{0:T(1024)} %custom-call) | copy-start | bytes 484228
  684.6 27.2 %copy-start.48 = (f32[40352]{0:T(1024)S(1)}, f32[40352]{0:T(1024)}, u32[]{:S(2)}) copy-start(f32[40352]{0:T(1024)} %param.45) | copy-start | bytes 484228
  717.5 15.4 %slice-start = ((s8[5308416]{0:T(1024)(128)(4,1)}), s8[4194304]{0:T(1024)(128)(4,1)S(1)}, s32[]{:S(2)}) async-start(s8[5308416]{0:T(1024)(128)(4,1)} %bitcast.258), calls=%async_computation.2 | async-start | bytes 8388608
  (51 other events, 211.9 us)
Sparse Core Ops, SparseCore 0:
  411.9 126.4 reduce-scatter.1

commit v6 on v5

--- a/solution.py
+++ b/solution.py
@@ -96,11 +96,13 @@
 
 Z, X = 4, 2
 GATHER_CHUNKS = (
-    (0, 0, 16, True), (0, 16, 32, False), (0, 48, 32, False), (0, 80, 32, False), (0, 112, 32, False),
-    (1, 0, 48, True), (1, 48, 48, False), (1, 96, 48, False),
+    (0, 0, 48, False), (0, 48, 48, False), (0, 96, 48, False),
+    (1, 0, 48, False), (1, 48, 48, False), (1, 96, 48, False),
 )
 CHUNKS = ((0, 16, True), (16, 32, False), (48, 32, False), (80, 32, False), (112, 32, False))
-META = 1280
+META = 384
+WIDE = 256
+ROWS_END = PATCH_IN + HEAD_OUT
 PIECE = 768
 
 
@@ -108,10 +110,16 @@
     return n == Z * X and rows == 144
 
 
+def one_hot(classes, width):
+    lane = lax.broadcasted_iota(jnp.int32, (classes.shape[0], width), 1).astype(jnp.float32)
+    return to_half(jnp.maximum(1.0 - jnp.abs(lane - classes), 0.0))
+
+
 def gather_kernel(
-    blk_ref, dn_ref, meta_ref, small_ref, two_ref, table_ref, mod_ref, fm_ref, b_one, b_two,
-    out_blk, out_dn, meta_out, small_out, pre_out, cond_out, mods_out,
-    part, parts, arrived_parts, meta_send, meta_recv, small_send, small_recv, part_send, part_recv, local_sem,
+    blk_ref, dn_ref, meta_ref, ends_ref, one_ref, two_ref, table_ref, mod_ref, fm_ref, b_one, b_two,
+    out_blk, out_dn, meta_out, ends_out, pre_out, hidden_out, cond_out, mods_out,
+    metas, hidden, part, parts, arrived_parts,
+    meta_send, meta_recv, ends_send, ends_recv, hid_send, hid_recv, part_send, part_recv, local_sem,
     up_sem, down_sem, x_sem, sib_sem, recv_sem, sib_recv, own_sem,
 ):
     me = lax.axis_index("dp")
@@ -136,24 +144,15 @@
 
     pl.semaphore_wait(barrier, group - 1)
 
-    def news(step, p, slot):
-        copies = []
-        for src, dst, send, recv in (
-            (meta_ref, meta_out, meta_send, meta_recv), (small_ref, small_out, small_send, small_recv)
-        ):
-            copies.append(
-                pltpu.make_async_remote_copy(
-                    src_ref=src, dst_ref=dst.at[slot], send_sem=send.at[step], recv_sem=recv.at[step],
-                    device_id={"dp": p}, device_id_type=MESH,
-                )
-            )
-        return copies
-
-    def own_news():
-        return [
-            pltpu.make_async_copy(meta_ref, meta_out.at[me], local_sem.at[0]),
-            pltpu.make_async_copy(small_ref, small_out.at[me], local_sem.at[1]),
-        ]
+    def to_dp(src, dst, send, recv, step, p, slot):
+        return pltpu.make_async_remote_copy(
+            src_ref=src, dst_ref=dst.at[slot], send_sem=send.at[step], recv_sem=recv.at[step],
+            device_id={"dp": p}, device_id_type=MESH,
+        )
+
+    meta_copy = partial(to_dp, meta_ref, metas, meta_send, meta_recv)
+    ends_copy = partial(to_dp, ends_ref, ends_out, ends_send, ends_recv)
+    hidden_copy = partial(to_dp, hidden, hidden_out, hid_send, hid_recv)
 
     def part_copy(step, p, slot):
         return pltpu.make_async_remote_copy(
@@ -162,16 +161,26 @@
             device_id=where(p), device_id_type=MESH,
         )
 
-    own_part = pltpu.make_async_copy(parts.at[place_in], arrived_parts.at[place_in], local_sem.at[2])
-
-    for copy_in in own_news():
-        copy_in.start()
-
-    @pl.loop(1, Z * X)
-    def _(step):
-        p = lax.rem(me + step, Z * X)
-        for copy_out in news(step, p, me):
-            copy_out.start()
+    own_meta = pltpu.make_async_copy(meta_ref, metas.at[me], local_sem.at[0])
+    own_ends = pltpu.make_async_copy(ends_ref, ends_out.at[me], local_sem.at[1])
+    own_hidden = pltpu.make_async_copy(hidden, hidden_out.at[me], local_sem.at[2])
+    own_part = pltpu.make_async_copy(parts.at[place_in], arrived_parts.at[place_in], local_sem.at[3])
+
+    def send_all(copy_to, size, index):
+        @pl.loop(1, size)
+        def _(step):
+            copy_to(step, lax.rem(index + step, size), index).start()
+
+    def wait_all(copy_to, size, index):
+        @pl.loop(1, size)
+        def _(step):
+            p = lax.rem(index + size - step, size)
+            copy_to(step, p, p).wait_recv()
+            copy_to(step, p, p).wait_send()
+
+    own_meta.start()
+    own_ends.start()
+    send_all(meta_copy, Z * X, me)
 
     def place(owner, k, side):
         which, first, rows, unused = GATHER_CHUNKS[k]
@@ -224,40 +233,36 @@
         own_copy(k).start()
         to_sibling(me, k, True).start()
 
-    for copy_in in own_news():
-        copy_in.wait()
-
-    @pl.loop(1, Z * X)
-    def _(step):
-        p = lax.rem(me + Z * X - step, Z * X)
-        for copy_in in news(step, p, p):
-            copy_in.wait_recv()
-            copy_in.wait_send()
-
-    rows_all = Z * X * 8
-    meta = to_half(meta_out[...].reshape(rows_all, META))
-    one = small_out[:, :, :FREQ].reshape(D, FREQ)
-    pre = matmul_nt(meta[:, :FREQ], one) + b_one[...]
-    pre_out[...] = pre
-    hidden = to_half(jax.nn.silu(pre))
-    cond = matmul_nt(hidden, two_ref[...]) + b_two[...] + matmul_nt(meta[:, FREQ:], table_ref[...])
-    cond_out[...] = cond
-    cond_low = to_half(cond).astype(jnp.float32)
-    own_cond = jnp.where(section == 0, cond, cond_low)
-    part[:, : 3 * D] = matmul(to_half(jax.nn.silu(own_cond)), mod_ref[...])
-    part[:, 3 * D : 5 * D] = matmul(to_half(jax.nn.silu(cond_low)), fm_ref[...])
-    part[:, 5 * D :] = jnp.zeros((rows_all, 8 * PIECE - 5 * D), jnp.float32)
-    for index in range(Z * X):
-        for image in range(2):
-            row = 8 * index + image
+    send_all(ends_copy, Z * X, me)
+
+    def make_hidden():
+        own_meta.wait()
+        wait_all(meta_copy, Z * X, me)
+        for index in range(Z * X):
+            meta_out[2 * index : 2 * index + 2] = metas[index]
+        pre = matmul_nt(to_half(meta_out[:, :FREQ]), one_ref[...]) + b_one[...]
+        pre_out[...] = pre
+        hidden[...] = to_half(jax.nn.silu(pre))
+        own_hidden.start()
+        send_all(hidden_copy, Z * X, me)
+
+    def make_parts():
+        own_hidden.wait()
+        wait_all(hidden_copy, Z * X, me)
+        cond = matmul_nt(one_hot(meta_out[:, FREQ : FREQ + 1], table_ref.shape[1]), table_ref[...]) + b_two[...]
+        for index in range(Z * X):
+            cond = cond + matmul_nt(hidden_out[index], two_ref[index])
+        cond_out[...] = cond
+        cond_low = to_half(cond).astype(jnp.float32)
+        own_cond = jnp.where(section == 0, cond, cond_low)
+        part[:, : 3 * D] = matmul(to_half(jax.nn.silu(own_cond)), mod_ref[...])
+        part[:, 3 * D : 5 * D] = matmul(to_half(jax.nn.silu(cond_low)), fm_ref[...])
+        part[:, 5 * D :] = jnp.zeros((group, 8 * PIECE - 5 * D), jnp.float32)
+        for row in range(group):
             for k in range(8):
-                parts[2 * index + image, k : k + 1] = part[row : row + 1, PIECE * k : PIECE * (k + 1)]
-    own_part.start()
-
-    @pl.loop(1, group)
-    def _(step):
-        p = lax.rem(place_in + step, group)
-        part_copy(step, p, place_in).start()
+                parts[row, k : k + 1] = part[row : row + 1, PIECE * k : PIECE * (k + 1)]
+        own_part.start()
+        send_all(part_copy, group, place_in)
 
     def along(step, k, first_across):
         shift = 1 - 2 * x if first_across else 0
@@ -318,15 +323,15 @@
             crossed(step - 1, k)
             if step < Z and GATHER_CHUNKS[k][3]:
                 along(step, k, True)
+        if step == 1:
+            make_hidden()
+        if step == 2:
+            make_parts()
 
     own_part.wait()
-
-    @pl.loop(1, group)
-    def _(step):
-        p = lax.rem(place_in + group - step, group)
-        part_copy(step, p, p).wait_recv()
-        part_copy(step, p, p).wait_send()
-
+    wait_all(part_copy, group, place_in)
+    own_ends.wait()
+    wait_all(ends_copy, Z * X, me)
     for source_core in range(2):
         total = arrived_parts[source_core]
         for index in range(1, Z * X):
@@ -366,7 +371,7 @@
                             copy(owner, k, mine, x_sem, across).wait_send()
 
 
-def gather_weights(blk, dn, meta, small, w_two, table, w_mod, w_fm, b_one, b_two):
+def gather_weights(blk, dn, meta, ends, w_one, w_two, table, w_mod, w_fm, b_one, b_two):
     n, width = lax.axis_size("dp"), blk.shape[0]
     section = lax.axis_index("section")
     if not ring_fits(n, width):
@@ -375,13 +380,12 @@
         )
         blk = lax.all_gather(blk, "dp", axis=0, tiled=True)
         dn = lax.all_gather(dn, "dp", axis=0, tiled=True)
-        small = jnp.pad(small, ((0, -width % 16), (0, 0)))
-        meta, small = exchange(2, "dp", ("all", "all"), meta, small)
-        small = small[:, :width]
-        rows = to_half(meta.reshape(-1, META))
-        pre = matmul_nt(rows[:, :FREQ], small[:, :, :FREQ].reshape(D, FREQ)) + b_one
-        hidden = to_half(jax.nn.silu(pre))
-        cond = matmul_nt(hidden, w_two) + b_two + matmul_nt(rows[:, FREQ:], table)
+        meta, ends = exchange(2, "dp", ("all", "all"), meta, ends)
+        meta = meta.reshape(2 * n, META)
+        pre = matmul_nt(to_half(meta[:, :FREQ]), w_one) + b_one
+        (hidden,) = exchange(8, "dp", ("all",), to_half(jax.nn.silu(pre)))
+        cond = matmul_nt(one_hot(meta[:, FREQ : FREQ + 1], table.shape[1]), table) + b_two
+        cond = cond + jnp.einsum("jik,jwk->iw", hidden, w_two, preferred_element_type=jnp.float32)
         cond_low = to_half(cond).astype(jnp.float32)
         own_cond = jnp.where(section == 0, cond, cond_low)
         parts = [
@@ -389,11 +393,10 @@
             matmul(to_half(jax.nn.silu(cond_low)), w_fm),
         ]
         parts = jnp.pad(jnp.concatenate(parts, axis=1), ((0, 0), (0, 8 * PIECE - 5 * D)))
-        parts = parts.reshape(n, 8, 8, PIECE)[:, :2].reshape(2 * n, 8, PIECE)
-        (parts,) = exchange(3, "stage", ("each",), parts)
+        (parts,) = exchange(3, "stage", ("each",), parts.reshape(2 * n, 8, PIECE))
         mods = jnp.sum(parts.reshape(n, 2, 8, PIECE), axis=0)
-        return (both(blk, swap(blk, 1)), both(dn, swap(dn, 1)), meta, small, pre, cond, mods)
-    units = n * len(GATHER_CHUNKS)
+        return (both(blk, swap(blk, 1)), both(dn, swap(dn, 1)), meta, ends, pre, hidden, cond, mods)
+    units, images = n * len(GATHER_CHUNKS), 2 * n
     hbm, vmem = pl.BlockSpec(memory_space=pl.ANY), pl.BlockSpec(memory_space=pltpu.VMEM)
     dma = lambda count: pltpu.SemaphoreType.DMA((count,))
     f32 = jnp.float32
@@ -401,16 +404,17 @@
         gather_kernel,
         out_shape=(
             jax.ShapeDtypeStruct((2, D, FF), BF), jax.ShapeDtypeStruct((2, D, HALF), BF),
-            jax.ShapeDtypeStruct((n, 8, META), f32), jax.ShapeDtypeStruct((n,) + small.shape, BF),
-            jax.ShapeDtypeStruct((n * 8, D), f32), jax.ShapeDtypeStruct((n * 8, width), f32),
-            jax.ShapeDtypeStruct((2, 8, PIECE), f32),
+            jax.ShapeDtypeStruct((images, META), f32), jax.ShapeDtypeStruct((n,) + ends.shape, BF),
+            jax.ShapeDtypeStruct((images, WIDE), f32), jax.ShapeDtypeStruct((n, images, WIDE), BF),
+            jax.ShapeDtypeStruct((images, width), f32), jax.ShapeDtypeStruct((2, 8, PIECE), f32),
         ),
-        in_specs=[hbm] * 2 + [vmem] * 8,
-        out_specs=(hbm, hbm) + (vmem,) * 5,
+        in_specs=[hbm] * 2 + [vmem] * 9,
+        out_specs=(hbm, hbm) + (vmem,) * 6,
         scratch_shapes=[
-            pltpu.VMEM((n * 8, 8 * PIECE), f32),
-            pltpu.VMEM((2 * n, 8, PIECE), f32), pltpu.VMEM((2 * n, 8, PIECE), f32),
-            dma(n), dma(n), dma(n), dma(n), dma(2 * n), dma(2 * n), dma(3),
+            pltpu.VMEM((n, 2, META), f32), pltpu.VMEM((images, WIDE), BF),
+            pltpu.VMEM((images, 8 * PIECE), f32),
+            pltpu.VMEM((images, 8, PIECE), f32), pltpu.VMEM((images, 8, PIECE), f32),
+            dma(n), dma(n), dma(n), dma(n), dma(n), dma(n), dma(images), dma(images), dma(4),
         ]
         + [dma(units)] * 6
         + [dma(len(GATHER_CHUNKS))],
@@ -419,34 +423,196 @@
         ),
         cost_estimate=pl.CostEstimate(flops=0, bytes_accessed=400_000_000, transcendentals=0),
         name="gather_weights",
-    )(blk, dn, meta, small, w_two, table, w_mod, w_fm, b_one, b_two)
+    )(blk, dn, meta, ends, w_one, w_two, table, w_mod, w_fm, b_one, b_two)
 
 
 VMEM_BYTES = 60 * 1024 * 1024
-SUM_CHUNKS = tuple((which,) + chunk for which in range(2) for chunk in CHUNKS)
+SUM_CHUNKS = tuple((which,) + chunk for which in range(3) for chunk in CHUNKS)
+
+
+def silu_slope(value):
+    gate = jax.nn.sigmoid(value)
+    return gate * (1.0 + value * (1.0 - gate))
 
 
 def sum_kernel(
-    g_first, g_second, out, own_b, other_d, xb, xq, up_b, up_o, down_b, down_o, acc,
+    g_dn, g_up, g_attn, dm_ref, bp_ref, en_ref, mod_ref, fm_ref, two_ref, cond_ref, pre_ref, hid_ref, meta_ref,
+    out, cross_out, dn_out, gmod_out, gfm_out, gtab_out, gone_out, gtwo_out,
+    ends_all, news_out, cs_all, fmsum_out, sq_all,
+    own_b, other_d, xb, xq, up_b, up_o, down_b, down_o, acc, acc_dn,
+    dm_in, bp_in, en_in, dmat, ends_src, c_src, c_in, fmd_src, fmd_in, cs_src, dcond, ph, ph_in, news_src,
+    sq_src, sq_rows, cross_src,
     load_sem, x_send, x_recv, up_send, up_recv, down_send, down_recv,
+    sib_send, sib_recv, y_send, y_recv, group_send, group_recv, sect_send, sect_recv,
+    ph_send, ph_recv, news_send, news_recv, sq_send, sq_recv, cross_sem, local_sem,
 ):
     me = lax.axis_index("dp")
+    section = lax.axis_index("section")
     z, x = me // X, lax.rem(me, X)
+    core = lax.rem(section, 2)
+    low, sibling, facing = section - core, section + 1 - 2 * core, lax.rem(section + 2, 4)
     across = me + 1 - 2 * x
-    sources = (g_first, g_second)
+    sources = (g_dn, g_up, g_attn)
     chunks = len(SUM_CHUNKS)
     has_up, has_down = z < Z - 1, z > 0
+    devices, group = Z * X * 4, Z * X * 2
+    me_all, me_group = me * 4 + section, me * 2 + core
+    in_all = lambda p: {"dp": p // 4, "section": lax.rem(p, 4)}
+    in_group = lambda p: {"dp": p // 2, "section": low + lax.rem(p, 2)}
+    in_section = lambda p: {"section": p}
+    in_dp = lambda p: {"dp": p}
+    f32 = jnp.float32
 
     barrier = pltpu.get_barrier_semaphore()
-    pl.semaphore_signal(barrier, 1, device_id={"dp": across}, device_id_type=MESH)
-
-    @pl.when(has_up)
-    def _():
-        pl.semaphore_signal(barrier, 1, device_id={"dp": me + X}, device_id_type=MESH)
-
-    @pl.when(has_down)
-    def _():
-        pl.semaphore_signal(barrier, 1, device_id={"dp": me - X}, device_id_type=MESH)
+
+    @pl.loop(1, devices)
+    def _(step):
+        pl.semaphore_signal(
+            barrier, 1, device_id=in_all(lax.rem(me_all + step, devices)), device_id_type=MESH
+        )
+
+    def small(src_of, dst, send, recv, where, size, index):
+        def copy(step, p, slot):
+            return pltpu.make_async_remote_copy(
+                src_ref=src_of(p), dst_ref=dst.at[slot], send_sem=send.at[step], recv_sem=recv.at[step],
+                device_id=where(p), device_id_type=MESH,
+            )
+        return (copy, size, index, src_of, dst)
+
+    gradients = [
+        small(lambda p: dm_ref.at[lax.rem(p, 2)], dm_in, group_send.at[0], group_recv.at[0], in_group, group, me_group),
+        small(lambda p: bp_ref.at[p], bp_in, group_send.at[1], group_recv.at[1], in_group, group, me_group),
+        small(lambda p: en_ref.at[p // 2], en_in, group_send.at[2], group_recv.at[2], in_group, group, me_group),
+    ]
+    conds = [
+        small(lambda p, src=src: src, dst, sect_send.at[k], sect_recv.at[k], in_section, 4, section)
+        for k, (src, dst) in enumerate(
+            ((c_src, c_in), (ends_src, ends_all), (fmd_src, fmd_in), (cs_src, cs_all))
+        )
+    ]
+    hiddens = [small(lambda p: ph.at[p], ph_in, ph_send, ph_recv, in_dp, Z * X, me)]
+    news = [small(lambda p: news_src, news_out, news_send, news_recv, in_all, devices, me_all)]
+    norms = [small(lambda p: sq_src, sq_all, sq_send, sq_recv, in_all, devices, me_all)]
+
+    def own_copies(batch, first):
+        return [
+            pltpu.make_async_copy(src_of(index), dst.at[index], local_sem.at[first + k])
+            for k, (copy, size, index, src_of, dst) in enumerate(batch)
+        ]
+
+    def send_batch(batch, first):
+        for copy in own_copies(batch, first):
+            copy.start()
+        for copy, size, index, src_of, dst in batch:
+            @pl.loop(1, size)
+            def _(step):
+                copy(step, lax.rem(index + step, size), index).start()
+
+    def wait_batch(batch, first):
+        for copy in own_copies(batch, first):
+            copy.wait()
+        for copy, size, index, src_of, dst in batch:
+            @pl.loop(1, size)
+            def _(step):
+                p = lax.rem(index + size - step, size)
+                copy(step, p, p).wait_recv()
+                copy(step, p, p).wait_send()
+
+    def add_square(value):
+        sq_src[...] += jnp.sum(value * value)
+
+    def images_of():
+        cond = cond_ref[...]
+        cond_low = to_half(cond).astype(f32)
+        return jnp.where(section == 0, cond, cond_low), cond_low
+
+    def make_cond():
+        wait_batch(gradients, 0)
+        flat = dm_in[...].reshape(group * 48, 128)
+        row = lax.broadcasted_iota(jnp.int32, (group, group * 48), 0) * 48
+        column = lax.broadcasted_iota(jnp.int32, (group, group * 48), 1)
+        for k in range(5 * D // 128):
+            chosen = jnp.where(column == row + k, 1.0, 0.0).astype(BF)
+            dmat[:, 128 * k : 128 * (k + 1)] = to_half(matmul(chosen, flat))
+        news_src[...] = jnp.zeros_like(news_src)
+        news_src[0:SUM_ROWS] = jnp.sum(bp_in[...], axis=0)
+        ends_src[...] = jnp.sum(en_in[...], axis=0)
+        own_cond, cond_low = images_of()
+        d_mod, d_fm = dmat[:, : 3 * D], dmat[:, 3 * D :]
+        fmd_src[...] = d_fm
+        cs_src[...] = jnp.sum(d_mod.astype(f32), axis=0, keepdims=True)
+        d_silu = matmul_nt(d_mod, mod_ref[...])
+        d_silu = d_silu + (section == 3).astype(f32) * matmul_nt(d_fm, fm_ref[...])
+        c_src[...] = jnp.zeros_like(c_src)
+        c_src[:, :144] = silu_slope(own_cond) * d_silu
+        send_batch(conds, 3)
+        silu_own = to_half(jax.nn.silu(own_cond))
+        for k in range(3):
+            part_g = matmul_tn(silu_own, dmat[:, D * k : D * (k + 1)])
+            gmod_out[:, D * k : D * (k + 1)] = part_g
+            add_square(part_g)
+
+    once = (section == 0).astype(f32)
+
+    def make_hidden():
+        wait_batch(conds, 3)
+        total = to_half(c_in[3])
+        for slot in (2, 1, 0):
+            total = to_half(total.astype(f32) + c_in[slot])
+        dcond[...] = total
+        d_cond = dcond[:, :144]
+        for index in range(Z * X):
+            ph[index] = matmul(d_cond, two_ref[index])
+        send_batch(hiddens, 7)
+        own_cond, cond_low = images_of()
+        silu_low = to_half(jax.nn.silu(cond_low))
+        for k in range(2):
+            part_g = matmul_tn(silu_low, fmd_in[3, :, D * k : D * (k + 1)])
+            gfm_out[:, D * k : D * (k + 1)] = part_g
+            add_square(jnp.sqrt(once) * part_g)
+        fmsum_out[...] = jnp.sum(fmd_in[3].astype(f32), axis=0, keepdims=True)
+        part_g = matmul_tn(d_cond, one_hot(meta_ref[:, FREQ : FREQ + 1], gtab_out.shape[1]))
+        gtab_out[...] = part_g
+        add_square(once * part_g)
+        for index in range(Z * X):
+            part_g = matmul_tn(d_cond, hid_ref[index])
+            gtwo_out[index] = part_g
+            add_square(once * part_g)
+
+    def make_news():
+        wait_batch(hiddens, 7)
+        total = ph_in[0]
+        for index in range(1, Z * X):
+            total = total + ph_in[index]
+        d_pre = to_half(silu_slope(pre_ref[...]) * total)
+        part_g = matmul_tn(d_pre, to_half(meta_ref[:, :FREQ]))
+        gone_out[...] = part_g
+        add_square(once * part_g)
+        sums = jnp.sum(d_pre.astype(f32), axis=0, keepdims=True)
+        sums_cond = jnp.sum(dcond[...].astype(f32), axis=0, keepdims=True)
+        for k in range(2):
+            news_src[SUM_ROWS + k : SUM_ROWS + k + 1] = sums[:, 128 * k : 128 * (k + 1)]
+            news_src[SUM_ROWS + 2 + k : SUM_ROWS + 3 + k] = sums_cond[:, 128 * k : 128 * (k + 1)]
+        send_batch(news, 8)
+        first = (me == 0).astype(f32)
+        add_square(news_src[0:10])
+        add_square(once * sums)
+        add_square(once * sums_cond)
+        add_square(first * cs_src[...])
+        add_square(first * once * fmsum_out[...])
+        add_square(once * ends_all[0])
+        add_square(once * ends_all[3])
+
+    def dn_copy(k, slot, to_sib):
+        rows = pl.ds(SUM_CHUNKS[k][1], SUM_CHUNKS[k][2])
+        unit = slot * chunks + k
+        return pltpu.make_async_remote_copy(
+            src_ref=dn_out.at[slot, rows], dst_ref=dn_out.at[slot, rows],
+            send_sem=(sib_send if to_sib else y_send).at[unit],
+            recv_sem=(sib_recv if to_sib else y_recv).at[unit],
+            device_id={"section": sibling if to_sib else facing},
+            device_id_type=MESH,
+        )
 
     def each(distance, run):
         if distance == 0:
@@ -525,9 +691,12 @@
                     load(k, zz, True).start()
             each(distance, run)
 
-    pl.semaphore_wait(barrier, 1 + has_up.astype(jnp.int32) + has_down.astype(jnp.int32))
-
-    for which in range(2):
+    sq_src[...] = jnp.zeros_like(sq_src)
+    sq_rows[...] = jnp.zeros_like(sq_rows)
+    pl.semaphore_wait(barrier, devices - 1)
+    send_batch(gradients, 0)
+
+    for which in range(3):
         for distance in (3, 2, 1, 0):
             for k in range(chunks):
                 if SUM_CHUNKS[k][0] == which and not SUM_CHUNKS[k][3]:
@@ -582,7 +751,8 @@
         x_copy(k, z, other_of(k, z)).start()
 
     def finish(k):
-        dst = out.at[SUM_CHUNKS[k][0], part(k)]
+        which, rows = SUM_CHUNKS[k][0], SUM_CHUNKS[k][2]
+        dst = out.at[which - 1, part(k)] if which else acc_dn.at[pl.ds(0, rows)]
         load(k, z).wait()
         if SUM_CHUNKS[k][3]:
             total(k, dst, [own(k, z)])
@@ -593,18 +763,70 @@
             x_copy(k, z, hbm(k, z, 1 - x)).wait_recv()
             total(k, dst, [own(k, z), from_x(k, z)])
             add_z(dst, k, False)
-
-    straight = [k for k in range(chunks) if not SUM_CHUNKS[k][3]]
-    direct = [k for k in range(chunks) if SUM_CHUNKS[k][3]]
-    for which in range(2):
-        of = lambda group: [k for k in group if SUM_CHUNKS[k][0] == which]
-        for distance in (3, 2, 1):
-            for k in of(range(chunks)):
-                pass_on(k, distance)
-        for k in of(direct):
+        if not which:
+            total(k, dn_out.at[section, part(k)], [dst])
+            dn_copy(k, section, True).start()
+            dn_copy(k, section, False).start()
+
+        @pl.loop(0, rows // 16)
+        def _(step):
+            value = dst[pl.ds(pl.multiple_of(step * 16, 16), 16)]
+            sq_rows[...] += jnp.sum(value * value, axis=0, keepdims=True)
+
+    def of(which, direct=None):
+        return [
+            k for k in range(chunks)
+            if SUM_CHUNKS[k][0] == which and (direct is None or SUM_CHUNKS[k][3] == direct)
+        ]
+
+    def pass_all(which, distance):
+        for k in of(which):
+            pass_on(k, distance)
+
+    def finish_all(which):
+        for k in of(which, False) + of(which, True):
+            finish(k)
+
+    def direct_all(which):
+        for k in of(which, True):
             send_direct(k)
-    for k in straight + direct:
-        finish(k)
+
+    for distance in (3, 2, 1):
+        pass_all(0, distance)
+    make_cond()
+    pass_all(1, 3)
+    direct_all(0)
+    finish_all(0)
+    pass_all(1, 2)
+    make_hidden()
+    pass_all(1, 1)
+    for k in of(0):
+        dn_copy(k, facing, False).wait_recv()
+        dn_copy(k, facing, True).start()
+    pass_all(2, 3)
+    make_news()
+    direct_all(1)
+    finish_all(1)
+    pass_all(2, 2)
+    pass_all(2, 1)
+    direct_all(2)
+    finish_all(2)
+
+    @pl.loop(0, 144 // 16)
+    def _(step):
+        rows = pl.ds(pl.multiple_of(step * 16, 16), 16)
+        cross_src[rows] = to_half(jnp.where(core == 0, out[0, rows], out[1, rows]))
+
+    crossing = pltpu.make_async_remote_copy(
+        src_ref=cross_src, dst_ref=cross_out, send_sem=cross_sem.at[0], recv_sem=cross_sem.at[1],
+        device_id={"section": sibling}, device_id_type=MESH,
+    )
+    sq_src[...] += jnp.sum(sq_rows[...])
+    send_batch(norms, 9)
+    crossing.start()
+    wait_batch(norms, 9)
+    wait_batch(news, 8)
+    crossing.wait()
 
     for k in range(chunks):
         for distance in (3, 2, 1, 0):
@@ -618,35 +840,105 @@
                     if SUM_CHUNKS[k][3]:
                         z_copy(k, zz, up, True).wait_send()
             each(distance, run)
-
-
-def sum_gradients(first, second):
-    n = lax.axis_size("dp")
-    if not ring_fits(n, D // n):
-        total = lambda grad: lax.psum_scatter(grad, "dp", scatter_dimension=0, tiled=True)
-        return jnp.stack([total(first), total(second)]).astype(jnp.float32)
-    chunks = len(SUM_CHUNKS)
-    dma = lambda count: pltpu.SemaphoreType.DMA((count,))
-    ring = pltpu.VMEM((2, Z, 144, HALF), BF)
+        if not SUM_CHUNKS[k][0]:
+            dn_copy(k, section, True).wait_send()
+            dn_copy(k, section, False).wait_send()
+            dn_copy(k, facing, True).wait_send()
+            dn_copy(k, sibling, True).wait_recv()
+            dn_copy(k, lax.rem(sibling + 2, 4), True).wait_recv()
+
+
+def sum_gradients(g_dn, g_up, g_attn, d_mods, sums, ends, w_mod, w_fm, two_blocks, cond, pre, hidden, meta):
+    n, width = lax.axis_size("dp"), cond.shape[1]
+    f32 = jnp.float32
+    if not ring_fits(n, width):
+        return sum_plainly(g_dn, g_up, g_attn, d_mods, sums, ends, w_mod, w_fm, two_blocks, cond, pre, hidden, meta)
+    chunks, images, devices = len(SUM_CHUNKS), 2 * n, 4 * n
+    dma = lambda *count: pltpu.SemaphoreType.DMA(count)
+    ring = pltpu.VMEM((3, Z, 144, HALF), BF)
     short = [rows for start, rows, direct in CHUNKS if direct][0]
-    ring_o = pltpu.VMEM((2, Z, short, HALF), BF)
+    most = max(rows for start, rows, direct in CHUNKS)
+    ring_o = pltpu.VMEM((3, Z, short, HALF), BF)
+    hbm, vmem = pl.BlockSpec(memory_space=pl.ANY), pl.BlockSpec(memory_space=pltpu.VMEM)
+    like = jax.ShapeDtypeStruct
+    end_block = ends.shape[1:]
+    shapes = (
+        like((2, 144, HALF), f32), like((144, HALF), BF), like((4, 144, HALF), BF),
+        like((144, 3 * D), f32), like((144, 2 * D), f32), like((144, 1024), f32), like((WIDE, FREQ), f32),
+        like((n, 144, WIDE), f32), like((4,) + end_block, f32), like((devices, 24, 128), f32),
+        like((4, 1, 3 * D), f32), like((1, 2 * D), f32), like((devices, 8, 128), f32),
+    )
     return pl.pallas_call(
         sum_kernel,
-        out_shape=jax.ShapeDtypeStruct((2, 144, HALF), jnp.float32),
-        in_specs=[pl.BlockSpec(memory_space=pl.ANY)] * 2,
-        out_specs=pl.BlockSpec(memory_space=pltpu.VMEM),
+        out_shape=shapes,
+        in_specs=[hbm] * 3 + [vmem] * 10,
+        out_specs=(vmem,) * len(shapes),
         scratch_shapes=[
-            ring, ring_o, ring, pltpu.VMEM((2, short, HALF), BF),
-            ring, ring_o, ring, ring_o, pltpu.VMEM((short, HALF), jnp.float32),
+            ring, ring_o, ring, pltpu.VMEM((3, short, HALF), BF),
+            ring, ring_o, ring, ring_o, pltpu.VMEM((short, HALF), f32), pltpu.VMEM((most, HALF), f32),
+            pltpu.VMEM((images, 48, 128), BF), pltpu.VMEM((images, SUM_ROWS, 128), f32),
+            pltpu.VMEM((images,) + end_block, f32), pltpu.VMEM((images, 5 * D), BF),
+            pltpu.VMEM(end_block, f32), pltpu.VMEM((images, WIDE), f32), pltpu.VMEM((4, images, WIDE), f32),
+            pltpu.VMEM((images, 2 * D), BF), pltpu.VMEM((4, images, 2 * D), BF), pltpu.VMEM((1, 3 * D), f32),
+            pltpu.VMEM((images, WIDE), BF), pltpu.VMEM((n, images, WIDE), f32), pltpu.VMEM((n, images, WIDE), f32),
+            pltpu.VMEM((24, 128), f32), pltpu.VMEM((8, 128), f32), pltpu.VMEM((1, HALF), f32),
+            pltpu.VMEM((144, HALF), BF),
             dma(2 * chunks * Z), dma(chunks * Z), dma(chunks * Z),
             dma(2 * chunks * Z), dma(2 * chunks * Z), dma(2 * chunks * Z), dma(2 * chunks * Z),
+            dma(4 * chunks), dma(4 * chunks), dma(4 * chunks), dma(4 * chunks),
+            dma(3, images), dma(3, images), dma(4, 4), dma(4, 4),
+            dma(n), dma(n), dma(devices), dma(devices), dma(devices), dma(devices), dma(2), dma(10),
         ],
         compiler_params=pltpu.CompilerParams(
             collective_id=1, has_side_effects=True, vmem_limit_bytes=VMEM_BYTES
         ),
-        cost_estimate=pl.CostEstimate(flops=0, bytes_accessed=300_000_000, transcendentals=0),
+        cost_estimate=pl.CostEstimate(flops=0, bytes_accessed=400_000_000, transcendentals=0),
         name="sum_gradients",
-    )(first, second)
+    )(g_dn, g_up, g_attn, d_mods, sums, ends, w_mod, w_fm, two_blocks, cond, pre, hidden, meta)
+
+
+def sum_plainly(g_dn, g_up, g_attn, d_mods, sums, ends, w_mod, w_fm, two_blocks, cond, pre, hidden, meta):
+    n, width = lax.axis_size("dp"), cond.shape[1]
+    section, images, f32 = lax.axis_index("section"), 2 * n, jnp.float32
+    once = (section == 0).astype(f32)
+    anchor = (lax.axis_index("dp") == 0).astype(f32)
+    total = lambda grad: lax.psum_scatter(grad, "dp", scatter_dimension=0, tiled=True)
+    dn_own, out = total(g_dn), jnp.stack([total(g_up), total(g_attn)]).astype(f32)
+    dn_all = lax.all_gather(dn_own, "section")
+    cross = swap(to_half(jnp.where(lax.rem(section, 2) == 0, out[0], out[1])), 1)
+    d_mods, sums, ends = exchange(4, "stage", ("core", "each", "dp"), d_mods, sums, ends)
+    d_mods = d_mods.reshape(images, 48 * 128)
+    d_mod, d_fm = d_mods[:, : 3 * D], d_mods[:, 3 * D : 5 * D]
+    sums, ends = jnp.sum(sums, axis=0), jnp.sum(ends, axis=0)
+    cond_low = to_half(cond).astype(f32)
+    own_cond = jnp.where(section == 0, cond, cond_low)
+    d_silu = matmul_nt(d_mod, w_mod) + (section == 3).astype(f32) * matmul_nt(d_fm, w_fm)
+    c_own = jnp.pad(silu_slope(own_cond) * d_silu, ((0, 0), (0, WIDE - width)))
+    cs = column_sums(d_mod)[None]
+    c_all, ends_all, d_fm, cs_all = exchange(5, "section", ("all",) * 4, c_own, ends, d_fm, cs)
+    d_fm = d_fm[3]
+    d_cond = to_half(c_all[3])
+    for slot in (2, 1, 0):
+        d_cond = to_half(d_cond.astype(f32) + c_all[slot])
+    narrow = d_cond[:, :width]
+    part = jnp.einsum("iw,jwk->jik", narrow, two_blocks, preferred_element_type=f32)
+    (part,) = exchange(6, "dp", ("each",), part)
+    d_pre = to_half(silu_slope(pre) * jnp.sum(part, axis=0))
+    g_mod = matmul_tn(to_half(jax.nn.silu(own_cond)), d_mod)
+    g_fm = matmul_tn(to_half(jax.nn.silu(cond_low)), d_fm)
+    g_table = matmul_tn(narrow, one_hot(meta[:, FREQ : FREQ + 1], 1024))
+    g_one = matmul_tn(d_pre, to_half(meta[:, :FREQ]))
+    g_two = jnp.einsum("iw,jik->jwk", narrow, hidden, preferred_element_type=f32)
+    fm_sum = column_sums(d_fm)[None]
+    slices = [column_sums(value).reshape(2, 128) for value in (d_pre, d_cond)]
+    news = jnp.concatenate([sums, *slices, jnp.zeros((4, 128), f32)])
+    square = lambda value: jnp.sum(value * value)
+    squares = square(out) + square(dn_own.astype(f32)) + square(g_mod) + square(sums[:10])
+    squares = squares + anchor * square(cs) + anchor * once * square(fm_sum)
+    for value in (g_fm, g_table, g_one, g_two, ends_all[0], ends_all[3], *slices):
+        squares = squares + once * square(value)
+    news, squares = exchange(7, "every", ("all", "all"), news, jnp.broadcast_to(squares, (8, 128)))
+    return (out, cross, dn_all, g_mod, g_fm, g_table, g_one, g_two, ends_all, news, cs_all, fm_sum, squares)
 
 
 def exchange_kernel(axes, modes, *refs):
@@ -981,7 +1273,7 @@
 
 def collect_kernel(peers, flags_ref, *refs):
     tokens, d_pre_ref, mods, fm_ref, extra_ref = refs[:4], refs[4], refs[5:7], refs[7], refs[8]
-    sums_ref, mods_ref = refs[9:]
+    sums_ref, mods_ref, rows_ref = refs[9:]
     core, stage = flags_ref[0], flags_ref[1]
     ones = jnp.ones((8, PATCHES), BF)
     total = lambda value: matmul(ones, value)[0:1]
@@ -994,9 +1286,14 @@
     last = jnp.where(stage == 0, rows[5], extra_ref[0:1])
     for place, row in enumerate(rows[:4] + order + [rows[4], last, extra_ref[1:2]]):
         sums_ref[place : place + 1, :D] = row
+    rows_ref[...] = jnp.zeros_like(rows_ref)
     for k in range(2):
-        block = jnp.concatenate([mods[k][...], fm_ref[...]], axis=0)
-        mods_ref[k] = to_half(jnp.concatenate([block, jnp.zeros((16 - 5, D), jnp.float32)], axis=0))
+        for row in range(5):
+            source = mods[k][row : row + 1, :] if row < 3 else fm_ref[row - 3 : row - 2, :]
+            for part in range(D // 128):
+                at = row * (D // 128) + part
+                rows_ref[at : at + 1] = source[:, 128 * part : 128 * (part + 1)]
+        mods_ref[k] = to_half(rows_ref[...])
 
 
 def collect(flags, tokens, d_pre, mods, fm, extra):
@@ -1006,8 +1303,9 @@
         partial(collect_kernel, peers),
         out_shape=(
             jax.ShapeDtypeStruct((SUM_ROWS, 128 * max(peers, 9)), jnp.float32),
-            jax.ShapeDtypeStruct((2, 16, D), BF),
+            jax.ShapeDtypeStruct((2, 48, 128), BF),
         ),
+        scratch_shapes=[pltpu.VMEM((48, 128), jnp.float32)],
         in_specs=[pl.BlockSpec(memory_space=pltpu.SMEM)] + [vmem] * 9,
         out_specs=(vmem, vmem),
         compiler_params=pltpu.CompilerParams(vmem_limit_bytes=VMEM_BYTES),
@@ -1018,11 +1316,11 @@
 def final_step(x_out, fmod, w_head, b_head, target, counts, loss_scale):
     normed, inverse = normalized(x_out)
     xf_half = to_half(normed * (1.0 + fmod[1:2]) + fmod[0:1])
-    error = matmul(xf_half, w_head) + b_head - target
+    error = matmul_nt(xf_half, w_head) + b_head - target
     loss = counts * jnp.sum(error * error)
     d_pred = to_half(2.0 * loss_scale * counts * error)
     g_head = matmul_tn(xf_half, d_pred)
-    d_x, d_shift, d_scale = modulated_back(normed, inverse, fmod[1:2], matmul_nt(d_pred, w_head))
+    d_x, d_shift, d_scale = modulated_back(normed, inverse, fmod[1:2], matmul(d_pred, w_head))
     return (loss, d_x, jnp.stack([d_shift, d_scale]), g_head, column_sums(d_pred))
 
 
@@ -1062,31 +1360,25 @@
     dn_half = to_half(lax.dynamic_slice(downs, (stage, 0, core * HALF), (1, width, HALF))[0])
     at_one, at_two = NCLS + PATCH_IN, NCLS + PATCH_IN + FREQ
     w_two = stem_half[:, at_two:]
-    table = jnp.pad(stem_half[:, :NCLS], ((0, 0), (0, META - FREQ - NCLS)))
+    table = jnp.pad(stem_half[:, :NCLS], ((0, 0), (0, -NCLS % 128)))
     w_fm = tail_half[:, : 2 * D]
-    small = jnp.concatenate(
-        [stem_half[:, at_one:at_two], stem_half[:, NCLS:at_one], tail_half[:, 2 * D :]], axis=1
-    )
-    small = jnp.pad(small, ((0, 0), (0, -small.shape[1] % 128)))
+    to_wide = lambda value: jnp.pad(value, ((0, 0),) * (value.ndim - 1) + ((0, WIDE - width),))
+    ends = to_wide(jnp.concatenate([stem_half[:, NCLS:at_one], tail_half[:, 2 * D :]], axis=1).T)
+    w_one = jnp.pad(stem_half[:, at_one:at_two], ((0, WIDE - width), (0, 0)))
+    two_blocks = to_wide(w_two.reshape(width, n, width)).transpose(1, 0, 2)
     classes = jnp.where(null_mask > 0, NCLS - 1, labels)
-    lanes = jnp.arange(META - FREQ, dtype=jnp.int32)[None, :]
-    picks = (classes[:, None] == lanes).astype(jnp.float32)
-    picks = jnp.where(lanes == META - FREQ - 1, valid.astype(jnp.float32)[:, None], picks)
     freq = to_half(time_features(timesteps.astype(jnp.float32))).astype(jnp.float32)
-    meta = jnp.concatenate([freq, picks], axis=1)
-    meta = jnp.pad(meta, ((0, 8 - meta.shape[0]), (0, 0)))
-    b_two = lax.dynamic_slice_in_dim(biases, 32 * D + place * width, width)
-    w_blk, w_dn, meta, small, pre, cond, mods = gather_weights(
-        to_half(block_w[0]), dn_half, meta, small, w_two, table, mod_half_w, w_fm,
-        biases[None, 31 * D : 32 * D], b_two[None],
-    )
-    small = small.reshape(D, -1)
-    w_patch_all = small[:, FREQ : FREQ + PATCH_IN]
-    w_head_all = small[:, FREQ + PATCH_IN : FREQ + PATCH_IN + HEAD_OUT]
-    of_images = lambda value: value.reshape(n, 8, -1)[:, :2].reshape(2 * n, -1)
+    facts = jnp.stack([classes, valid], axis=1).astype(jnp.float32)
+    meta = jnp.concatenate([freq, facts, jnp.zeros((2, META - FREQ - 2), jnp.float32)], axis=1)
+    b_one, b_two = (lax.dynamic_slice_in_dim(biases, k * D + place * width, width)[None] for k in (31, 32))
+    w_blk, w_dn, meta, ends, pre_own, hidden_all, cond, mods = gather_weights(
+        to_half(block_w[0]), dn_half, meta, ends, w_one, two_blocks, table, mod_half_w, w_fm,
+        to_wide(b_one), b_two,
+    )
+    ends = ends[:, :, :width].transpose(1, 0, 2).reshape(ROWS_END, D)
+    w_patch_all, w_head_all = ends[:PATCH_IN], ends[PATCH_IN:]
     images = 2 * n
-    meta = of_images(meta)
-    count = jnp.sum(meta[:, META - 1])
+    count = jnp.sum(meta[:, FREQ + 1])
     loss_scale = 1.0 / (count * PATCHES * HEAD_OUT)
     mods = mods.reshape(2, 8 * PIECE)
     bias_of = lambda first, length: lax.dynamic_slice_in_dim(biases, first, length)
@@ -1102,23 +1394,13 @@
         bias_of(28 * D + D * stage, D)[None],
     )
 
-    freq = to_half(meta[:, :FREQ])
-    picks = to_half(meta[:, FREQ : FREQ + NCLS])
-    hidden_pre = of_images(pre).T
-    hidden_all = to_half(jax.nn.silu(hidden_pre))
-    cond = of_images(cond).T
-    cond_low = to_half(cond).astype(jnp.float32)
-    cond_own = jnp.where(section == 0, cond, cond_low)
-    silu_own = to_half(jax.nn.silu(cond_own))
-    silu_low = to_half(jax.nn.silu(cond_low))
-
     step = pick(timesteps, core).astype(jnp.float32)
     signal, spread = noise_levels(step)
     lat, noi = pick(latents, core)[None], pick(noise, core)[None]
     counts = pick(valid, core).astype(jnp.float32)
     tok_half = to_half(patchify(signal * lat + spread * noi))[0]
     target = jnp.concatenate([patchify(signal * noi - spread * lat), patchify(noi)], axis=2)[0]
-    x_first = matmul_nt(tok_half, w_patch_all) + biases[30 * D : 31 * D] + position_table(GRID // 2, D)
+    x_first = matmul(tok_half, w_patch_all) + biases[30 * D : 31 * D] + position_table(GRID // 2, D)
 
     x_hop = swap(stage_forward(False, x_first, weights)[0], 2)
     x_in = jnp.where(stage == 0, x_first, x_hop.astype(jnp.float32))
@@ -1137,7 +1419,6 @@
     act_sib, branch_sib, xm_sib, pre_sib = swap((act[:, HALF:], d_branch_b, xm_b, d_pre[:, HALF:]), 1)
     g_dn = to_half(matmul_tn(d_branch_b, act[:, :HALF]) + matmul_tn(branch_sib, act_sib))
     g_up = to_half(matmul_tn(xm_b, d_pre[:, :HALF]) + matmul_tn(xm_sib, pre_sib))
-    g_dn = lax.psum_scatter(g_dn, "dp", scatter_dimension=0, tiled=True)
 
     xa_sib, last_sib, one_sib, two_sib = swap(
         (
@@ -1158,97 +1439,54 @@
         ],
         axis=1,
     )
-    g_up, g_attn = sum_gradients(g_up, g_attn)
-    crossing = swap(to_half(jnp.where(even, g_up, g_attn)), 1).astype(jnp.float32)
-    g_blk = jnp.concatenate(
-        [jnp.where(even, g_attn, crossing), jnp.where(even, crossing, g_up)], axis=1
-    )
-    g_facing = swap(g_dn, 2)
-    g_sib, g_corner = swap((g_dn, g_facing), 1)
-    in_core = lambda own, sib: jnp.concatenate(
-        [jnp.where(even, own, sib), jnp.where(even, sib, own)], axis=1
-    ).astype(jnp.float32)
-    here, there = in_core(g_dn, g_sib), in_core(g_facing, g_corner)
-    down_both = jnp.where(stage == 0, jnp.stack([here, there]), jnp.stack([there, here]))
 
     extra = jnp.stack([jnp.pad(b_head, (0, D - HEAD_OUT)), jnp.pad(loss[None], (0, D - 1))])
     d_fmod = jnp.where(stage == 1, d_fmod, jnp.zeros_like(d_fmod))
-    own_biases, d_mods = collect(
+    own_sums, d_mods = collect(
         flags, (d_qkv, d_branch_a, d_branch_b, d_first), d_pre, (d_mod_a, d_mod_b), d_fmod, extra
     )
     g_patch = jnp.pad(matmul_tn(d_first, tok_half), ((0, 0), (0, HEAD_OUT - PATCH_IN)))
     end_rows = row_count(width * HEAD_OUT)
     own_ends = jnp.where(stage == 0, g_patch, g_head).reshape(n, width * HEAD_OUT)
     own_ends = jnp.pad(own_ends, ((0, 0), (0, end_rows * 128 - width * HEAD_OUT))).reshape(n, end_rows, 128)
-    own_biases = own_biases.reshape(SUM_ROWS, -1, 128).transpose(1, 0, 2)[: 2 * n]
-    d_mods, own_biases, own_ends = exchange(
-        4, "stage", ("core", "each", "dp"), d_mods, own_biases, own_ends
-    )
-    bias_piece = jnp.sum(own_biases, axis=0)
-    own_ends = jnp.sum(own_ends, axis=0)
-    d_mod_all = d_mods[:, :3].reshape(images, 3 * D)
-    d_fm_all = d_mods[:, 3:5].reshape(images, 2 * D)
-    g_mod = matmul(silu_own, d_mod_all)
-    c_own = matmul_nt(mod_half_w, d_mod_all)
-    c_own = c_own + matmul_nt(tail_half[:, : 2 * D], jnp.where(section == 3, d_fm_all, jnp.zeros_like(d_fm_all)))
-    c_own = silu_back(cond_own, c_own)
-    cond_rows = row_count(width * images)
-    c_all, end_pair, d_fm_all = exchange(
-        5, "section", ("all", "all", "all"), rows_of(c_own, cond_rows), own_ends, d_fm_all
-    )
-    d_fm_all = d_fm_all[3]
-    ends = [end_pair[k].reshape(-1)[: width * HEAD_OUT].reshape(width, HEAD_OUT) for k in (0, 3)]
-    g_fm = matmul(silu_low, d_fm_all)
-    c_all = [c_all[k].reshape(-1)[: width * images].reshape(width, images) for k in range(4)]
-    d_cond = to_half(c_all[3])
-    for slot in (2, 1, 0):
-        d_cond = to_half(d_cond.astype(jnp.float32) + c_all[slot])
-    part_hidden = matmul_tn(w_two, d_cond).reshape(n, width * images)
-    part_hidden = jnp.pad(part_hidden, ((0, 0), (0, cond_rows * 128 - width * images)))
-    (d_hidden,) = exchange(6, "dp", ("each",), part_hidden.reshape(n, cond_rows, 128))
-    d_hidden = jnp.sum(d_hidden, axis=0).reshape(-1)[: width * images].reshape(width, images)
-    pre_own = lax.dynamic_slice_in_dim(hidden_pre, place * width, width)
-    d_pre_one = to_half(silu_back(pre_own, d_hidden))
-    g_table = matmul(d_cond, picks)
-    g_one = matmul(d_pre_one, freq)
-    g_two = matmul_nt(d_cond, hidden_all)
-    g_stem = jnp.concatenate([g_table, ends[0][:, :PATCH_IN], g_one, g_two], axis=1)
+    own_sums = own_sums.reshape(SUM_ROWS, -1, 128).transpose(1, 0, 2)[: 2 * n]
+    halves, crossed, dn_all, g_mod, g_fm, g_table, g_one, g_two, ends_all, news, mod_sums, fm_sum, squares = (
+        sum_gradients(
+            g_dn, g_up, g_attn, d_mods, own_sums, own_ends, mod_half_w, w_fm, two_blocks, cond, pre_own,
+            hidden_all, meta,
+        )
+    )
+    crossed = crossed.astype(jnp.float32)
+    g_blk = jnp.concatenate(
+        [jnp.where(even, halves[1], crossed), jnp.where(even, crossed, halves[0])], axis=1
+    )
+    dn_all = dn_all.astype(jnp.float32)
+    down_both = jnp.stack([jnp.concatenate([dn_all[2 * k], dn_all[2 * k + 1]], axis=1) for k in range(2)])
+    ends = [
+        ends_all[k].reshape(-1)[: width * HEAD_OUT].reshape(width, HEAD_OUT) for k in (0, 3)
+    ]
+    g_two = g_two[:, :, :width].transpose(1, 0, 2).reshape(width, D)
+    g_stem = jnp.concatenate(
+        [g_table[:, :NCLS], ends[0][:, :PATCH_IN], g_one[:width], g_two], axis=1
+    )
     g_tail = jnp.concatenate([g_fm, ends[1]], axis=1)
 
-    square = lambda value: jnp.sum(value * value)
-    once = (section == 0).astype(jnp.float32)
-    squares = square(g_mod) + square(g_blk)
-    squares = squares + once * (square(down_both) + square(g_stem) + square(g_tail))
-    row_sums = lambda value: jnp.sum(value.astype(jnp.float32), axis=1)
-    mod_piece = 3 * D // n
-    mod_rows, slice_rows = row_count(mod_piece, 1), row_count(2 * width, 1)
-    bias_mod = lax.dynamic_slice_in_dim(column_sums(d_mod_all), place * mod_piece, mod_piece)
-    slices = jnp.concatenate([row_sums(d_pre_one), row_sums(d_cond)])
-    news = jnp.concatenate(
-        [bias_piece, rows_of(bias_mod, mod_rows), rows_of(slices, slice_rows), rows_of(squares[None], 1)]
-    )
-    news = jnp.pad(news, ((0, -news.shape[0] % 8), (0, 0)))
-    (news,) = exchange(7, "every", ("all",), news)
     news = news.reshape(n, 4, -1, 128)
-    piece = SUM_ROWS
-    first, second = piece + mod_rows, piece + mod_rows + slice_rows
     stages = []
     for k in range(2):
-        pieces = news[:, 2 * k : 2 * k + 2, :piece].reshape(2 * n, SUM_ROWS, 128)[: D // 128]
+        pieces = news[:, 2 * k : 2 * k + 2, :SUM_ROWS].reshape(2 * n, SUM_ROWS, 128)[: D // 128]
         stages.append(pieces.transpose(1, 0, 2).reshape(-1))
-    bias_mods = news[:, :, piece:first].reshape(n, 4, mod_rows * 128)[:, :, :mod_piece]
-    bias_mods = bias_mods.transpose(1, 0, 2).reshape(-1)
-    slices = news[:, 0, first:second].reshape(n, slice_rows * 128)[:, : 2 * width]
+    slices = news[:, 0, SUM_ROWS : SUM_ROWS + 4].reshape(n, 2, WIDE)[:, :, :width]
     bias_grad = jnp.concatenate(
-        [bias_mods]
+        [mod_sums.reshape(-1)]
         + [part[: 8 * D] for part in stages]
         + [part[8 * D : 9 * D] for part in stages]
         + [stages[0][9 * D : 10 * D]]
-        + [slices[:, :width].reshape(-1), slices[:, width:].reshape(-1)]
-        + [column_sums(d_fm_all), stages[1][9 * D : 9 * D + HEAD_OUT]]
+        + [slices[:, 0].reshape(-1), slices[:, 1].reshape(-1)]
+        + [fm_sum[0], stages[1][9 * D : 9 * D + HEAD_OUT]]
     )
     loss_sum = stages[1][10 * D]
-    grad_norm = jnp.sqrt(jnp.sum(news[:, :, second, 0]) + square(bias_grad))
+    grad_norm = jnp.sqrt(jnp.sum(squares[:, 0, 0]))
     factor = jnp.minimum(1.0, clip_limit / (grad_norm + 1e-06))
     mod_out = nesterov(mod_w, mod_m, mod_e, g_mod[None], factor)
     block_out = nesterov(block_w, block_m, block_e, g_blk[None], factor)

time: 765 us -> 736 us (0.962)
  Pallas kernels: 524 us -> 578 us
  other arithmetic: 80.7 us -> 53.6 us
  between operations: 24.1 us -> 6.85 us
  waiting for transfers between devices: 32.1 us -> 16.3 us
  matrix products: 36.8 us -> 26.3 us
  local copies, waits for them, and re-layouts: 53.5 us -> 44.6 us
    pallas_call x5 -> x1, Pallas kernels: 197 us -> 279 us  [sum_gradients(): pl.pallas_call(sum_kernel, out_shape=shapes, in_specs=[hbm] * 3 + [vmem]...]
    pallas_call x1, Pallas kernels: 220 us -> 193 us  [gather_weights(): pl.pallas_call(gather_kernel, out_shape=(jax.ShapeDtypeStruct((2, D, FF),...]
    ppermute x14 -> x10, waiting for transfers between devices: 32 us -> 16.3 us  [swap(): return lax.ppermute(array, 'section', [(k, k ^ by) for k in range(peers)])]
    reduce_sum x14 -> x2, other arithmetic: 13.8 us -> 2.92 us  [the longest x1 1.54 us: body(): grad_norm = jnp.sqrt(jnp.sum(squares[:, 0, 0]))]
    dot_general x11 -> x10, matrix products: 24.1 us -> 23.4 us  [matmul_tn(): lax.dot_general(left, right, (((0,), (0,)), ((), ())), preferred_element_...]
  transfers between devices with their start and end apart: 15 -> 10, of which waited for: 4 -> 2; matrix products, arithmetic and copies ran while one was open for 10% -> 5% of each run, Pallas kernels for 29% -> 5%
where the time goes in v6:
time: 736 us; the launch traced here: 731 us
  Pallas kernels  578 us (79%)
  other arithmetic  53.6 us (7%)
  local copies, waits for them, and re-layouts  44.6 us (6%)
  matrix products  26.3 us (4%)
  waiting for transfers between devices  16.3 us (2%)
    pallas_call x1, Pallas kernels, sum_gradients(): pl.pallas_call(sum_kernel, out_shape=shapes, in_specs=[hbm] * 3 + [vmem]...  279 us
    pallas_call x1, Pallas kernels, gather_weights(): pl.pallas_call(gather_kernel, out_shape=(jax.ShapeDtypeStruct((2, D, FF),...  193 us
    pallas_call x2, Pallas kernels, stage_backward(): pl.pallas_call(backward_kernel, out_shape=(like(D, BF), mods, mods, like(...  62.1 us
    pallas_call x2, Pallas kernels, stage_forward(): pl.pallas_call(partial(forward_kernel, save), out_shape=tuple(shapes), in...  39.6 us
    dot_general x10, matrix products, matmul_tn(): lax.dot_general(left, right, (((0,), (0,)), ((), ())), preferred_element_...  23.4 us
    ppermute x10, waiting for transfers between devices, swap(): return lax.ppermute(array, 'section', [(k, k ^ by) for k in range(peers)])  16.3 us
  transfers between devices with their start and end apart: 10, of which 2 were waited for; matrix products, arithmetic and copies ran while one was open for 5% of the time, Pallas kernels for 5%

profile of v6, /device:TPU:0, one launch (start us, length us, event | category | flops | bytes accessed | tf_op | source)
XLA Modules:
  0.0 730.8 jit_solution(2419768284650624173)
XLA Ops:
  12.7 2.2 fusion.16.dn_ref
  15.5 193.1 %gather_weights.1 = (bf16[2,1152,4608]{2,1,0:T(8,128)(2,1)}, bf16[2,1152,2304]{2,1,0:T(8,128)(2,1)}, f32[16,384]{1,0:T(8,128)}, bf16[8,48,256]{2,1,0:T(8,128)(2,...) custom-call(bf16[144,4608]{1,0:T(8,128)(2,1)} %convert_bitcast_fusion.1.blk_ref,, ...), custom_call_target="tpu_custom_call" | custom-call | bytes 400000000 | tf_op jit(solution)/shard_map/gather_weights/pallas_call | solution.py:403
  218.6 18.7 %stage_forward.2 = bf16[256,1152]{1,0:T(8,128)(2,1)} custom-call(s32[2]{0:T(128)} %pad_add_fusion.flags.flags_ref, f32[256,1152]{1,0:T(8,128)} %fusion.6.x_ref, f32[3,1152]{1,0:T(4,128)} %reshape.222.mod_a, f32[3,1152]{1,0:T(4,128)} %reshape.223.mod_m, f32[1,4608]{1,0:T(1,128)} %broadcast_in_dim.32.b_attn, f32[1,4608]{1,0:T(1,128)} %copy-done.55, ...), custom_call_target="tpu_custom_call" | custom-call | flops 16911433728 | bytes 31850496 | tf_op jit(solution)/shard_map/stage_forward/pallas_call | solution.py:1233
  237.3 1.6 collective-permute-start
  244.3 8.9 %collective-permute-done = bf16[256,1152]{1,0:T(8,128)(2,1)S(1)} collective-permute-done((bf16[256,1152]{1,0:T(8,128)(2,1)}, bf16[256,1152]{1,0:T(8,128)(2,1)S(1)}, u32[]{:S(2)}, u32[]{:S(2)}) %collective-permute-start) | collective-permute-done | bytes 589856 | tf_op jit(solution)/shard_map/ppermute | solution.py:1337
  254.3 20.9 %stage_forward.3 = (f32[256,1152]{1,0:T(8,128)}, bf16[256,1152]{1,0:T(8,128)(2,1)}, bf16[256,3456]{1,0:T(8,128)(2,1)}, bf16[256,1152]{1,0:T(8,128)(2,1)}, f32[25...) custom-call(s32[2]{0:T(128)} %pad_add_fusion.flags.flags_ref, ...), custom_call_target="tpu_custom_call" | custom-call | flops 16911433728 | bytes 31850496 | tf_op jit(solution)/shard_map/stage_forward/pallas_call | solution.py:1233
  280.4 31.1 %stage_backward.2 = (bf16[256,1152]{1,0:T(8,128)(2,1)}, f32[3,1152]{1,0:T(4,128)}, f32[3,1152]{1,0:T(4,128)}, bf16[256,1152]{1,0:T(8,128)(2,1)}, bf16[256,1152]{...) custom-call(s32[2]{0:T(128)} %pad_add_fusion.flags.flags_ref, ...), custom_call_target="tpu_custom_call" | custom-call | flops 16911433728 | bytes 31850496 | tf_op jit(solution)/shard_map/stage_backward/pallas_call | solution.py:1252
  311.5 1.6 collective-permute-start.1
  315.3 2.4 slice.211
  319.2 7.4 %collective-permute-done.1 = bf16[256,1152]{1,0:T(8,128)(2,1)S(1)} collective-permute-done((bf16[256,1152]{1,0:T(8,128)(2,1)}, bf16[256,1152]{1,0:T(8,128)(2,1)S(1)}, u32[]{:S(2)}, u32[]{:S(2)}) %collective-permute-start.1) | collective-permute-done | bytes 589856 | tf_op jit(solution)/shard_map/ppermute | solution.py:1337
  327.7 31.0 %stage_backward.3 = (bf16[256,1152]{1,0:T(8,128)(2,1)}, f32[3,1152]{1,0:T(4,128)}, f32[3,1152]{1,0:T(4,128)}, bf16[256,1152]{1,0:T(8,128)(2,1)}, bf16[256,1152]{...) custom-call(s32[2]{0:T(128)} %pad_add_fusion.flags.flags_ref, ...), custom_call_target="tpu_custom_call" | custom-call | flops 16911433728 | bytes 31850496 | tf_op jit(solution)/shard_map/stage_backward/pallas_call | solution.py:1252
  367.8 4.5 collect.1
  375.5 2.2 fusion.45
  379.1 2.1 fusion.3
  381.2 3.0 pad_maximum_fusion.g_attn
  384.1 3.0 fusion.43
  387.2 4.0 fusion.g_dn
  391.2 2.8 fusion.44
  394.0 5.0 fusion.1.g_up
  399.1 278.8 %sum_gradients.1 = (f32[2,144,2304]{2,1,0:T(8,128)}, bf16[144,2304]{1,0:T(8,128)(2,1)}, bf16[4,144,2304]{2,1,0:T(8,128)(2,1)}, f32[144,3456]{1,0:T(8,128)}, f32[...) custom-call(bf16[1152,2304]{1,0:T(8,128)(2,1)} %fusion.g_dn, ...), custom_call_target="tpu_custom_call" | custom-call | bytes 400000000 | tf_op jit(solution)/shard_map/sum_gradients/pallas_call | solution.py:871
  686.2 2.2 convert_element_type.161
  688.4 2.8 slice_bitcast_fusion.3
  692.8 1.7 fusion.35
  696.2 1.6 concatenate.67
  697.9 3.2 convert_bitcast_fusion.3
  701.1 4.7 fusion.9
  706.4 4.3 convert_bitcast_fusion
  710.8 3.5 fusion.4
  717.9 2.6 fusion.36
  720.6 1.9 multiply_add_fusion
  725.2 2.2 fusion.37
  727.4 2.0 multiply_add_fusion.2
  (300 shorter events, 66.8 us)
Async XLA Ops:
  15.5 198.1 %copy-start.51 = (f32[2,32,32,4]{2,3,1,0:T(4,128)S(1)}, f32[2,32,32,4]{2,3,1,0:T(4,128)}, u32[]{:S(2)}) copy-start(f32[2,32,32,4]{2,3,1,0:T(4,128)} %param.24) | copy-start | bytes 98308
  15.5 198.1 %copy-start.52 = (f32[2,32,32,4]{2,3,1,0:T(4,128)S(1)}, f32[2,32,32,4]{2,3,1,0:T(4,128)}, u32[]{:S(2)}) copy-start(f32[2,32,32,4]{2,3,1,0:T(4,128)} %param.25) | copy-start | bytes 98308
  237.3 15.9 %collective-permute-start = (bf16[256,1152]{1,0:T(8,128)(2,1)}, bf16[256,1152]{1,0:T(8,128)(2,1)S(1)}, u32[]{:S(2)}, u32[]{:S(2)}) collective-permute-start(bf16[256,1152]{1,0:T(8,128)(2,1)} %stage_forward.2), channel_id=1, source_target_pairs={{0,2},{1,3},{2,0},{3,1},{4,6},{5,7},{6,4},{7,5},{8,10},{9,11},{10,... | collective-permute-start | bytes 1769480 | tf_op jit(solution)/shard_map/ppermute | solution.py:1337
  240.4 12.8 %copy-start.24 = (f32[256,1152]{1,0:T(8,128)S(1)}, f32[256,1152]{1,0:T(8,128)}, u32[]{:S(2)}) copy-start(f32[256,1152]{1,0:T(8,128)} %fusion.6.x_ref) | copy-start | bytes 3538948
  280.4 33.4 %copy-start.12 = (bf16[256,1152]{1,0:T(8,128)(2,1)S(1)}, bf16[256,1152]{1,0:T(8,128)(2,1)}, u32[]{:S(2)}) copy-start(bf16[256,1152]{1,0:T(8,128)(2,1)} %get-tuple-element.84) | copy-start | bytes 1769476
  280.4 33.5 %copy-start.26 = (bf16[256,1152]{1,0:T(8,128)(2,1)S(1)}, bf16[256,1152]{1,0:T(8,128)(2,1)}, u32[]{:S(2)}) copy-start(bf16[256,1152]{1,0:T(8,128)(2,1)} %get-tuple-element.86) | copy-start | bytes 1769476
  311.5 15.1 %collective-permute-start.1 = (bf16[256,1152]{1,0:T(8,128)(2,1)}, bf16[256,1152]{1,0:T(8,128)(2,1)S(1)}, u32[]{:S(2)}, u32[]{:S(2)}) collective-permute-start(bf16[256,1152]{1,0:T(8,128)(2,1)} %get-tuple-element.79), channel_id=1, source_target_pairs={{0,2},{1,3},{2,0},{3,1},{4,6},{5,7},{6,4},{7,5},{8,10},{9,11},{10,... | collective-permute-start | bytes 1769480 | tf_op jit(solution)/shard_map/ppermute | solution.py:1337
  313.8 61.1 %collective-permute-start.6 = (bf16[256,1152]{1,0:T(8,128)(2,1)S(1)}, bf16[256,1152]{1,0:T(8,128)(2,1)}, u32[]{:S(2)}, u32[]{:S(2)}) collective-permute-start(bf16[256,1152]{1,0:T(8,128)(2,1)S(1)} %copy-done.12), channel_id=1, source_target_pairs={{0,1},{1,0},{2,3},{3,2},{4,5},{5,4},{6,7},{7,6},{8,9},{9,8},{10,11... | collective-permute-start | bytes 1769480 | tf_op jit(solution)/shard_map/ppermute | solution.py:1337
  314.8 11.8 %copy-start.25 = (f32[256,1152]{1,0:T(8,128)S(1)}, f32[256,1152]{1,0:T(8,128)}, u32[]{:S(2)}) copy-start(f32[256,1152]{1,0:T(8,128)} %subtract_multiply_fusion.d_ref) | copy-start | bytes 3538948
  314.8 64.0 %collective-permute-start.8 = (bf16[256,1152]{1,0:T(8,128)(2,1)}, bf16[256,1152]{1,0:T(8,128)(2,1)}, u32[]{:S(2)}, u32[]{:S(2)}) collective-permute-start(bf16[256,1152]{1,0:T(8,128)(2,1)} %broadcast_select_fusion), channel_id=1, source_target_pairs={{0,1},{1,0},{2,3},{3,2},{4,5},{5,4},{6,7},{7,6},{8,9},{9,8},{10,11... | collective-permute-start | bytes 1769480 | tf_op jit(solution)/shard_map/ppermute | solution.py:1337
  315.3 75.9 %collective-permute-start.4 = (bf16[256,1152]{1,0:T(8,128)(2,1)}, bf16[256,1152]{1,0:T(8,128)(2,1)}, u32[]{:S(2)}, u32[]{:S(2)}) collective-permute-start(bf16[256,1152]{1,0:T(8,128)(2,1)} %get-tuple-element.82), channel_id=1, source_target_pairs={{0,1},{1,0},{2,3},{3,2},{4,5},{5,4},{6,7},{7,6},{8,9},{9,8},{10,11... | collective-permute-start | bytes 1769480 | tf_op jit(solution)/shard_map/ppermute | solution.py:1337
  317.7 66.5 %collective-permute-start.3 = (bf16[256,2304]{1,0:T(8,128)(2,1)}, bf16[256,2304]{1,0:T(8,128)(2,1)}, u32[]{:S(2)}, u32[]{:S(2)}) collective-permute-start(bf16[256,2304]{1,0:T(8,128)(2,1)} %slice.211), channel_id=1, source_target_pairs={{0,1},{1,0},{2,3},{3,2},{4,5},{5,4},{6,7},{7,6},{8,9},{9,8},{10,11... | collective-permute-start | bytes 3538952 | tf_op jit(solution)/shard_map/ppermute | solution.py:1337
  365.7 9.3 %collective-permute-start.7 = (bf16[256,1152]{1,0:T(8,128)(2,1)}, bf16[256,1152]{1,0:T(8,128)(2,1)}, u32[]{:S(2)}, u32[]{:S(2)}) collective-permute-start(bf16[256,1152]{1,0:T(8,128)(2,1)} %get-tuple-element.143), channel_id=1, source_target_pairs={{0,1},{1,0},{2,3},{3,2},{4,5},{5,4},{6,7},{7,6},{8,9},{9,8},{10,11... | collective-permute-start | bytes 1769480 | tf_op jit(solution)/shard_map/ppermute | solution.py:1337
  367.8 6.0 copy-start.3
  367.8 6.0 copy-start.19
  367.8 6.0 copy-start.27
  374.9 9.2 %collective-permute-start.2 = (bf16[256,1152]{1,0:T(8,128)(2,1)S(1)}, bf16[256,1152]{1,0:T(8,128)(2,1)S(1)}, u32[]{:S(2)}, u32[]{:S(2)}) collective-permute-start(bf16[256,1152]{1,0:T(8,128)(2,1)S(1)} %copy-done.31), channel_id=1, source_target_pairs={{0,1},{1,0},{2,3},{3,2},{4,5},{5,4},{6,7},{7,6},{8,9},{9,8},{10,11... | collective-permute-start | bytes 1769480 | tf_op jit(solution)/shard_map/ppermute | solution.py:1337
  375.1 4.0 collective-permute-start.9
  379.0 12.2 %collective-permute-start.5 = (bf16[256,2304]{1,0:T(8,128)(2,1)S(1)}, bf16[256,2304]{1,0:T(8,128)(2,1)S(1)}, u32[]{:S(2)}, u32[]{:S(2)}) collective-permute-start(bf16[256,2304]{1,0:T(8,128)(2,1)S(1)} %copy-done.40), channel_id=1, source_target_pairs={{0,1},{1,0},{2,3},{3,2},{4,5},{5,4},{6,7},{7,6},{8,9},{9,8},{10,11... | collective-permute-start | bytes 3538952 | tf_op jit(solution)/shard_map/ppermute | solution.py:1337
  677.9 5.6 copy-start.53
  679.0 4.7 copy-start.39
  697.8 8.0 %copy-start.22 = (f32[144,2304]{1,0:T(8,128)S(1)}, f32[144,2304]{1,0:T(8,128)}, u32[]{:S(2)}) copy-start(f32[144,2304]{1,0:T(8,128)} %get-tuple-element.136) | copy-start | bytes 3981316
  697.8 8.0 %copy-start.23 = (f32[144,2304]{1,0:T(8,128)S(1)}, f32[144,2304]{1,0:T(8,128)}, u32[]{:S(2)}) copy-start(f32[144,2304]{1,0:T(8,128)} %get-tuple-element.139) | copy-start | bytes 3981316
  697.8 8.5 %slice-start = ((s8[5308416]{0:T(1024)(128)(4,1)}), s8[4194304]{0:T(1024)(128)(4,1)S(1)}, s32[]{:S(2)}) async-start(s8[5308416]{0:T(1024)(128)(4,1)} %bitcast.183), calls=%async_computation | async-start | bytes 8388608
  697.8 8.5 %slice-start.2 = ((s8[5308416]{0:T(1024)(128)(4,1)}), s8[4194304]{0:T(1024)(128)(4,1)S(1)}, s32[]{:S(2)}) async-start(s8[5308416]{0:T(1024)(128)(4,1)} %bitcast.186), calls=%async_computation.2 | async-start | bytes 8388608
  701.1 4.7 copy-start.17
  701.1 5.0 copy-start.20
  701.1 5.0 copy-start.21
  701.1 5.3 slice-start.1
  701.1 5.3 slice-start.3
  705.8 5.0 slice-start.4
  720.5 4.7 copy-start.35
  (45 other events, 120.6 us)

commit v7 on v6

--- a/solution.py
+++ b/solution.py
@@ -696,11 +696,23 @@
     pl.semaphore_wait(barrier, devices - 1)
     send_batch(gradients, 0)
 
-    for which in range(3):
-        for distance in (3, 2, 1, 0):
-            for k in range(chunks):
-                if SUM_CHUNKS[k][0] == which and not SUM_CHUNKS[k][3]:
-                    each(distance, lambda zz, up: x_copy(k, zz, hbm(k, zz, 1 - x)).start())
+    order = [
+        (k, distance) for which, distance in ((0, 3), (0, 2), (0, 1), (1, 3), (0, 0), (1, 2), (1, 1), (2, 3), (1, 0), (2, 2), (2, 1), (2, 0))
+        for k in range(chunks) if SUM_CHUNKS[k][0] == which and not SUM_CHUNKS[k][3]
+    ]
+    sent = []
+
+    def send_x(until):
+        while len(sent) < min(until, len(order)):
+            k, distance = order[len(sent)]
+            sent.append(1)
+            each(distance, lambda zz, up: x_copy(k, zz, hbm(k, zz, 1 - x)).start())
+
+    def after(k, distance):
+        if not SUM_CHUNKS[k][3]:
+            send_x(order.index((k, distance)) + 1 + 6)
+
+    send_x(6)
 
     def pass_on(k, distance):
         def run(zz, up):
@@ -782,10 +794,12 @@
     def pass_all(which, distance):
         for k in of(which):
             pass_on(k, distance)
+            after(k, distance)
 
     def finish_all(which):
         for k in of(which, False) + of(which, True):
             finish(k)
+            after(k, 0)
 
     def direct_all(which):
         for k in of(which, True):

time: 736 us -> 655 us (0.89)
  Pallas kernels: 578 us -> 497 us
    pallas_call x1, Pallas kernels: 279 us -> 198 us  [sum_gradients(): pl.pallas_call(sum_kernel, out_shape=shapes, in_specs=[hbm] * 3 + [vmem]...]
where the time goes in v7:
time: 655 us; the launch traced here: 650 us
  Pallas kernels  497 us (76%)
  other arithmetic  53.5 us (8%)
  local copies, waits for them, and re-layouts  44.6 us (7%)
  matrix products  26.3 us (4%)
  waiting for transfers between devices  16.5 us (3%)
  between operations  7.12 us (1%)
    pallas_call x1, Pallas kernels, sum_gradients(): pl.pallas_call(sum_kernel, out_shape=shapes, in_specs=[hbm] * 3 + [vmem]...  198 us
    pallas_call x1, Pallas kernels, gather_weights(): pl.pallas_call(gather_kernel, out_shape=(jax.ShapeDtypeStruct((2, D, FF),...  193 us
    pallas_call x2, Pallas kernels, stage_backward(): pl.pallas_call(backward_kernel, out_shape=(like(D, BF), mods, mods, like(...  62.3 us
    pallas_call x2, Pallas kernels, stage_forward(): pl.pallas_call(partial(forward_kernel, save), out_shape=tuple(shapes), in...  39.6 us
    dot_general x10, matrix products, matmul_tn(): lax.dot_general(left, right, (((0,), (0,)), ((), ())), preferred_element_...  23.4 us
    ppermute x10, waiting for transfers between devices, swap(): return lax.ppermute(array, 'section', [(k, k ^ by) for k in range(peers)])  16.5 us
  transfers between devices with their start and end apart: 10, of which 2 were waited for; matrix products, arithmetic and copies ran while one was open for 5% of the time, Pallas kernels for 5%

profile of v7, /device:TPU:0, one launch (start us, length us, event | category | flops | bytes accessed | tf_op | source)
XLA Modules:
  0.0 650.1 jit_solution(15927753000188042349)
XLA Ops:
  12.7 2.2 fusion.16.dn_ref
  15.5 193.1 %gather_weights.1 = (bf16[2,1152,4608]{2,1,0:T(8,128)(2,1)}, bf16[2,1152,2304]{2,1,0:T(8,128)(2,1)}, f32[16,384]{1,0:T(8,128)}, bf16[8,48,256]{2,1,0:T(8,128)(2,...) custom-call(bf16[144,4608]{1,0:T(8,128)(2,1)} %convert_bitcast_fusion.1.blk_ref,, ...), custom_call_target="tpu_custom_call" | custom-call | bytes 400000000 | tf_op jit(solution)/shard_map/gather_weights/pallas_call | solution.py:403
  218.6 18.5 %stage_forward.2 = bf16[256,1152]{1,0:T(8,128)(2,1)} custom-call(s32[2]{0:T(128)} %pad_add_fusion.flags.flags_ref, f32[256,1152]{1,0:T(8,128)} %fusion.6.x_ref, f32[3,1152]{1,0:T(4,128)} %reshape.222.mod_a, f32[3,1152]{1,0:T(4,128)} %reshape.223.mod_m, f32[1,4608]{1,0:T(1,128)} %broadcast_in_dim.32.b_attn, f32[1,4608]{1,0:T(1,128)} %copy-done.55, ...), custom_call_target="tpu_custom_call" | custom-call | flops 16911433728 | bytes 31850496 | tf_op jit(solution)/shard_map/stage_forward/pallas_call | solution.py:1247
  237.1 1.6 collective-permute-start
  244.1 8.9 %collective-permute-done = bf16[256,1152]{1,0:T(8,128)(2,1)S(1)} collective-permute-done((bf16[256,1152]{1,0:T(8,128)(2,1)}, bf16[256,1152]{1,0:T(8,128)(2,1)S(1)}, u32[]{:S(2)}, u32[]{:S(2)}) %collective-permute-start) | collective-permute-done | bytes 589856 | tf_op jit(solution)/shard_map/ppermute | solution.py:1351
  254.1 21.1 %stage_forward.3 = (f32[256,1152]{1,0:T(8,128)}, bf16[256,1152]{1,0:T(8,128)(2,1)}, bf16[256,3456]{1,0:T(8,128)(2,1)}, bf16[256,1152]{1,0:T(8,128)(2,1)}, f32[25...) custom-call(s32[2]{0:T(128)} %pad_add_fusion.flags.flags_ref, ...), custom_call_target="tpu_custom_call" | custom-call | flops 16911433728 | bytes 31850496 | tf_op jit(solution)/shard_map/stage_forward/pallas_call | solution.py:1247
  280.4 31.1 %stage_backward.2 = (bf16[256,1152]{1,0:T(8,128)(2,1)}, f32[3,1152]{1,0:T(4,128)}, f32[3,1152]{1,0:T(4,128)}, bf16[256,1152]{1,0:T(8,128)(2,1)}, bf16[256,1152]{...) custom-call(s32[2]{0:T(128)} %pad_add_fusion.flags.flags_ref, ...), custom_call_target="tpu_custom_call" | custom-call | flops 16911433728 | bytes 31850496 | tf_op jit(solution)/shard_map/stage_backward/pallas_call | solution.py:1266
  311.5 1.6 collective-permute-start.1
  315.3 2.4 slice.211
  319.0 7.6 %collective-permute-done.1 = bf16[256,1152]{1,0:T(8,128)(2,1)S(1)} collective-permute-done((bf16[256,1152]{1,0:T(8,128)(2,1)}, bf16[256,1152]{1,0:T(8,128)(2,1)S(1)}, u32[]{:S(2)}, u32[]{:S(2)}) %collective-permute-start.1) | collective-permute-done | bytes 589856 | tf_op jit(solution)/shard_map/ppermute | solution.py:1351
  327.7 31.2 %stage_backward.3 = (bf16[256,1152]{1,0:T(8,128)(2,1)}, f32[3,1152]{1,0:T(4,128)}, f32[3,1152]{1,0:T(4,128)}, bf16[256,1152]{1,0:T(8,128)(2,1)}, bf16[256,1152]{...) custom-call(s32[2]{0:T(128)} %pad_add_fusion.flags.flags_ref, ...), custom_call_target="tpu_custom_call" | custom-call | flops 16911433728 | bytes 31850496 | tf_op jit(solution)/shard_map/stage_backward/pallas_call | solution.py:1266
  368.0 4.5 collect.1
  375.7 2.2 fusion.45
  379.3 2.1 fusion.3
  381.4 2.9 pad_maximum_fusion.g_attn
  384.3 3.0 fusion.43
  387.4 4.0 fusion.g_dn
  391.4 2.8 fusion.44
  394.2 5.0 fusion.1.g_up
  399.3 197.6 %sum_gradients.1 = (f32[2,144,2304]{2,1,0:T(8,128)}, bf16[144,2304]{1,0:T(8,128)(2,1)}, bf16[4,144,2304]{2,1,0:T(8,128)(2,1)}, f32[144,3456]{1,0:T(8,128)}, f32[...) custom-call(bf16[1152,2304]{1,0:T(8,128)(2,1)} %fusion.g_dn, ...), custom_call_target="tpu_custom_call" | custom-call | bytes 400000000 | tf_op jit(solution)/shard_map/sum_gradients/pallas_call | solution.py:885
  605.1 2.2 convert_element_type.161
  607.4 2.8 slice_bitcast_fusion.3
  611.8 1.7 fusion.35
  615.1 1.6 concatenate.67
  616.8 3.2 convert_bitcast_fusion.3
  620.0 4.7 fusion.9
  625.4 4.4 convert_bitcast_fusion
  629.8 3.5 fusion.4
  636.9 2.6 fusion.36
  639.6 1.9 multiply_add_fusion
  644.2 2.2 fusion.37
  646.4 2.0 multiply_add_fusion.2
  (300 shorter events, 66.6 us)
Async XLA Ops:
  15.5 198.1 %copy-start.51 = (f32[2,32,32,4]{2,3,1,0:T(4,128)S(1)}, f32[2,32,32,4]{2,3,1,0:T(4,128)}, u32[]{:S(2)}) copy-start(f32[2,32,32,4]{2,3,1,0:T(4,128)} %param.24) | copy-start | bytes 98308
  15.5 198.1 %copy-start.52 = (f32[2,32,32,4]{2,3,1,0:T(4,128)S(1)}, f32[2,32,32,4]{2,3,1,0:T(4,128)}, u32[]{:S(2)}) copy-start(f32[2,32,32,4]{2,3,1,0:T(4,128)} %param.25) | copy-start | bytes 98308
  237.1 15.9 %collective-permute-start = (bf16[256,1152]{1,0:T(8,128)(2,1)}, bf16[256,1152]{1,0:T(8,128)(2,1)S(1)}, u32[]{:S(2)}, u32[]{:S(2)}) collective-permute-start(bf16[256,1152]{1,0:T(8,128)(2,1)} %stage_forward.2), channel_id=1, source_target_pairs={{0,2},{1,3},{2,0},{3,1},{4,6},{5,7},{6,4},{7,5},{8,10},{9,11},{10,... | collective-permute-start | bytes 1769480 | tf_op jit(solution)/shard_map/ppermute | solution.py:1351
  240.2 12.8 %copy-start.24 = (f32[256,1152]{1,0:T(8,128)S(1)}, f32[256,1152]{1,0:T(8,128)}, u32[]{:S(2)}) copy-start(f32[256,1152]{1,0:T(8,128)} %fusion.6.x_ref) | copy-start | bytes 3538948
  280.4 33.4 %copy-start.12 = (bf16[256,1152]{1,0:T(8,128)(2,1)S(1)}, bf16[256,1152]{1,0:T(8,128)(2,1)}, u32[]{:S(2)}) copy-start(bf16[256,1152]{1,0:T(8,128)(2,1)} %get-tuple-element.84) | copy-start | bytes 1769476
  280.4 33.5 %copy-start.26 = (bf16[256,1152]{1,0:T(8,128)(2,1)S(1)}, bf16[256,1152]{1,0:T(8,128)(2,1)}, u32[]{:S(2)}) copy-start(bf16[256,1152]{1,0:T(8,128)(2,1)} %get-tuple-element.86) | copy-start | bytes 1769476
  311.5 15.1 %collective-permute-start.1 = (bf16[256,1152]{1,0:T(8,128)(2,1)}, bf16[256,1152]{1,0:T(8,128)(2,1)S(1)}, u32[]{:S(2)}, u32[]{:S(2)}) collective-permute-start(bf16[256,1152]{1,0:T(8,128)(2,1)} %get-tuple-element.79), channel_id=1, source_target_pairs={{0,2},{1,3},{2,0},{3,1},{4,6},{5,7},{6,4},{7,5},{8,10},{9,11},{10,... | collective-permute-start | bytes 1769480 | tf_op jit(solution)/shard_map/ppermute | solution.py:1351
  313.8 61.3 %collective-permute-start.6 = (bf16[256,1152]{1,0:T(8,128)(2,1)S(1)}, bf16[256,1152]{1,0:T(8,128)(2,1)}, u32[]{:S(2)}, u32[]{:S(2)}) collective-permute-start(bf16[256,1152]{1,0:T(8,128)(2,1)S(1)} %copy-done.12), channel_id=1, source_target_pairs={{0,1},{1,0},{2,3},{3,2},{4,5},{5,4},{6,7},{7,6},{8,9},{9,8},{10,11... | collective-permute-start | bytes 1769480 | tf_op jit(solution)/shard_map/ppermute | solution.py:1351
  314.8 11.8 %copy-start.25 = (f32[256,1152]{1,0:T(8,128)S(1)}, f32[256,1152]{1,0:T(8,128)}, u32[]{:S(2)}) copy-start(f32[256,1152]{1,0:T(8,128)} %subtract_multiply_fusion.d_ref) | copy-start | bytes 3538948
  314.8 64.2 %collective-permute-start.8 = (bf16[256,1152]{1,0:T(8,128)(2,1)}, bf16[256,1152]{1,0:T(8,128)(2,1)}, u32[]{:S(2)}, u32[]{:S(2)}) collective-permute-start(bf16[256,1152]{1,0:T(8,128)(2,1)} %broadcast_select_fusion), channel_id=1, source_target_pairs={{0,1},{1,0},{2,3},{3,2},{4,5},{5,4},{6,7},{7,6},{8,9},{9,8},{10,11... | collective-permute-start | bytes 1769480 | tf_op jit(solution)/shard_map/ppermute | solution.py:1351
  315.3 76.1 %collective-permute-start.4 = (bf16[256,1152]{1,0:T(8,128)(2,1)}, bf16[256,1152]{1,0:T(8,128)(2,1)}, u32[]{:S(2)}, u32[]{:S(2)}) collective-permute-start(bf16[256,1152]{1,0:T(8,128)(2,1)} %get-tuple-element.82), channel_id=1, source_target_pairs={{0,1},{1,0},{2,3},{3,2},{4,5},{5,4},{6,7},{7,6},{8,9},{9,8},{10,11... | collective-permute-start | bytes 1769480 | tf_op jit(solution)/shard_map/ppermute | solution.py:1351
  317.7 66.7 %collective-permute-start.3 = (bf16[256,2304]{1,0:T(8,128)(2,1)}, bf16[256,2304]{1,0:T(8,128)(2,1)}, u32[]{:S(2)}, u32[]{:S(2)}) collective-permute-start(bf16[256,2304]{1,0:T(8,128)(2,1)} %slice.211), channel_id=1, source_target_pairs={{0,1},{1,0},{2,3},{3,2},{4,5},{5,4},{6,7},{7,6},{8,9},{9,8},{10,11... | collective-permute-start | bytes 3538952 | tf_op jit(solution)/shard_map/ppermute | solution.py:1351
  366.0 9.3 %collective-permute-start.7 = (bf16[256,1152]{1,0:T(8,128)(2,1)}, bf16[256,1152]{1,0:T(8,128)(2,1)}, u32[]{:S(2)}, u32[]{:S(2)}) collective-permute-start(bf16[256,1152]{1,0:T(8,128)(2,1)} %get-tuple-element.143), channel_id=1, source_target_pairs={{0,1},{1,0},{2,3},{3,2},{4,5},{5,4},{6,7},{7,6},{8,9},{9,8},{10,11... | collective-permute-start | bytes 1769480 | tf_op jit(solution)/shard_map/ppermute | solution.py:1351
  368.0 6.0 copy-start.3
  368.0 6.0 copy-start.19
  368.0 6.0 copy-start.27
  375.2 9.2 %collective-permute-start.2 = (bf16[256,1152]{1,0:T(8,128)(2,1)S(1)}, bf16[256,1152]{1,0:T(8,128)(2,1)S(1)}, u32[]{:S(2)}, u32[]{:S(2)}) collective-permute-start(bf16[256,1152]{1,0:T(8,128)(2,1)S(1)} %copy-done.31), channel_id=1, source_target_pairs={{0,1},{1,0},{2,3},{3,2},{4,5},{5,4},{6,7},{7,6},{8,9},{9,8},{10,11... | collective-permute-start | bytes 1769480 | tf_op jit(solution)/shard_map/ppermute | solution.py:1351
  375.3 4.0 collective-permute-start.9
  379.2 12.1 %collective-permute-start.5 = (bf16[256,2304]{1,0:T(8,128)(2,1)S(1)}, bf16[256,2304]{1,0:T(8,128)(2,1)S(1)}, u32[]{:S(2)}, u32[]{:S(2)}) collective-permute-start(bf16[256,2304]{1,0:T(8,128)(2,1)S(1)} %copy-done.40), channel_id=1, source_target_pairs={{0,1},{1,0},{2,3},{3,2},{4,5},{5,4},{6,7},{7,6},{8,9},{9,8},{10,11... | collective-permute-start | bytes 3538952 | tf_op jit(solution)/shard_map/ppermute | solution.py:1351
  596.9 5.6 copy-start.53
  597.9 4.7 copy-start.39
  616.7 8.0 %copy-start.22 = (f32[144,2304]{1,0:T(8,128)S(1)}, f32[144,2304]{1,0:T(8,128)}, u32[]{:S(2)}) copy-start(f32[144,2304]{1,0:T(8,128)} %get-tuple-element.136) | copy-start | bytes 3981316
  616.7 8.0 %copy-start.23 = (f32[144,2304]{1,0:T(8,128)S(1)}, f32[144,2304]{1,0:T(8,128)}, u32[]{:S(2)}) copy-start(f32[144,2304]{1,0:T(8,128)} %get-tuple-element.139) | copy-start | bytes 3981316
  616.8 8.5 %slice-start = ((s8[5308416]{0:T(1024)(128)(4,1)}), s8[4194304]{0:T(1024)(128)(4,1)S(1)}, s32[]{:S(2)}) async-start(s8[5308416]{0:T(1024)(128)(4,1)} %bitcast.183), calls=%async_computation | async-start | bytes 8388608
  616.8 8.5 %slice-start.2 = ((s8[5308416]{0:T(1024)(128)(4,1)}), s8[4194304]{0:T(1024)(128)(4,1)S(1)}, s32[]{:S(2)}) async-start(s8[5308416]{0:T(1024)(128)(4,1)} %bitcast.186), calls=%async_computation.2 | async-start | bytes 8388608
  620.0 4.7 copy-start.17
  620.0 5.0 copy-start.20
  620.0 5.0 copy-start.21
  620.0 5.3 slice-start.1
  620.0 5.3 slice-start.3
  624.7 5.1 slice-start.4
  639.6 4.7 copy-start.35
  (45 other events, 120.6 us)

commit v8 on v7

--- a/solution.py
+++ b/solution.py
@@ -96,7 +96,7 @@
 
 Z, X = 4, 2
 GATHER_CHUNKS = (
-    (0, 0, 48, False), (0, 48, 48, False), (0, 96, 48, False),
+    (0, 0, 48, True), (0, 48, 48, True), (0, 96, 48, False),
     (1, 0, 48, False), (1, 48, 48, False), (1, 96, 48, False),
 )
 CHUNKS = ((0, 16, True), (16, 32, False), (48, 32, False), (80, 32, False), (112, 32, False))
@@ -264,65 +264,47 @@
         own_part.start()
         send_all(part_copy, group, place_in)
 
-    def along(step, k, first_across):
-        shift = 1 - 2 * x if first_across else 0
-        crosses = (not first_across) and (not GATHER_CHUNKS[k][3])
-
-        @pl.when(z >= step)
-        def _():
-            owner = me - X * step + shift
-            arrived(owner, k)
-
-            @pl.when(has_up)
+    def along(step, k):
+        crosses = not (step == 1 and GATHER_CHUNKS[k][3])
+        for sign in (-1, 1):
+            @pl.when((z >= step) if sign < 0 else (z + step < Z))
             def _():
-                copy(owner, k, False, up_sem, me + X).start()
-
-            if crosses:
-                copy(owner, k, False, x_sem, across).start()
-            to_sibling(owner, k, False).start()
-
-        @pl.when(z + step < Z)
-        def _():
-            owner = me + X * step + shift
-            arrived(owner, k)
-
-            @pl.when(has_down)
-            def _():
-                copy(owner, k, False, down_sem, me - X).start()
-
-            if crosses:
-                copy(owner, k, False, x_sem, across).start()
-            to_sibling(owner, k, False).start()
+                owner = me + sign * X * step
+                arrived(owner, k)
+
+                @pl.when(has_up if sign < 0 else has_down)
+                def _():
+                    copy(owner, k, False, up_sem if sign < 0 else down_sem, me - sign * X).start()
+
+                if crosses:
+                    copy(owner, k, False, x_sem, across).start()
+                to_sibling(owner, k, False).start()
 
     def crossed(step, k):
-        direct = GATHER_CHUNKS[k][3]
         if step == 0:
-            owner = across
-            arrived(owner, k)
-            if direct:
+            arrived(across, k)
+            if GATHER_CHUNKS[k][3]:
                 @pl.when(has_up)
                 def _():
-                    copy(owner, k, False, up_sem, me + X).start()
+                    copy(across, k, False, up_sem, me + X).start()
 
                 @pl.when(has_down)
                 def _():
-                    copy(owner, k, False, down_sem, me - X).start()
-            to_sibling(owner, k, False).start()
-        elif not direct:
-            for sign in (-1, 1):
-                @pl.when((z >= step) if sign < 0 else (z + step < Z))
-                def _():
-                    owner = across + sign * X * step
-                    arrived(owner, k)
-                    to_sibling(owner, k, False).start()
+                    copy(across, k, False, down_sem, me - X).start()
+            to_sibling(across, k, False).start()
+            return
+        for sign in (-1, 1):
+            @pl.when((z >= step) if sign < 0 else (z + step < Z))
+            def _():
+                owner = across + sign * X * step
+                arrived(owner, k)
+                to_sibling(owner, k, False).start()
 
     for step in range(1, Z + 1):
         for k in range(chunks):
             if step < Z:
-                along(step, k, False)
+                along(step, k)
             crossed(step - 1, k)
-            if step < Z and GATHER_CHUNKS[k][3]:
-                along(step, k, True)
         if step == 1:
             make_hidden()
         if step == 2:
@@ -339,7 +321,7 @@
         mods_out[source_core] = total
 
     for k in range(chunks):
-        direct = GATHER_CHUNKS[k][3]
+        near = GATHER_CHUNKS[k][3]
         own_copy(k).wait()
         for column in range(2):
             base = me if column == 0 else across
@@ -358,7 +340,7 @@
                             device_id={"section": sibling},
                             device_id_type=MESH,
                         ).wait_recv()
-                        runs = column == 0 or direct
+                        runs = column == 0 or (near and step == 0)
                         if runs and (step == 0 or sign < 0):
                             @pl.when(has_up)
                             def _():
@@ -367,7 +349,7 @@
                             @pl.when(has_down)
                             def _():
                                 copy(owner, k, mine, down_sem, me - X).wait_send()
-                        if column == 0 and (step == 0 or not direct):
+                        if column == 0 and not (step == 1 and near):
                             copy(owner, k, mine, x_sem, across).wait_send()
 
 
@@ -438,10 +420,10 @@
 def sum_kernel(
     g_dn, g_up, g_attn, dm_ref, bp_ref, en_ref, mod_ref, fm_ref, two_ref, cond_ref, pre_ref, hid_ref, meta_ref,
     out, cross_out, dn_out, gmod_out, gfm_out, gtab_out, gone_out, gtwo_out,
-    ends_all, news_out, cs_all, fmsum_out, sq_all,
+    ends_all, news_out, cs_all, fmsum_out, sq_out,
     own_b, other_d, xb, xq, up_b, up_o, down_b, down_o, acc, acc_dn,
     dm_in, bp_in, en_in, dmat, ends_src, c_src, c_in, fmd_src, fmd_in, cs_src, dcond, ph, ph_in, news_src,
-    sq_src, sq_rows, cross_src,
+    sq_src, sq_all, sq_rows, cross_src,
     load_sem, x_send, x_recv, up_send, up_recv, down_send, down_recv,
     sib_send, sib_recv, y_send, y_recv, group_send, group_recv, sect_send, sect_recv,
     ph_send, ph_recv, news_send, news_recv, sq_send, sq_recv, cross_sem, local_sem,
@@ -576,7 +558,7 @@
         add_square(once * part_g)
         for index in range(Z * X):
             part_g = matmul_tn(d_cond, hid_ref[index])
-            gtwo_out[index] = part_g
+            gtwo_out[:, 144 * index : 144 * (index + 1)] = part_g[:, :144]
             add_square(once * part_g)
 
     def make_news():
@@ -839,6 +821,7 @@
     send_batch(norms, 9)
     crossing.start()
     wait_batch(norms, 9)
+    sq_out[...] = jnp.sum(sq_all[...], axis=0)
     wait_batch(news, 8)
     crossing.wait()
 
@@ -879,8 +862,8 @@
     shapes = (
         like((2, 144, HALF), f32), like((144, HALF), BF), like((4, 144, HALF), BF),
         like((144, 3 * D), f32), like((144, 2 * D), f32), like((144, 1024), f32), like((WIDE, FREQ), f32),
-        like((n, 144, WIDE), f32), like((4,) + end_block, f32), like((devices, 24, 128), f32),
-        like((4, 1, 3 * D), f32), like((1, 2 * D), f32), like((devices, 8, 128), f32),
+        like((144, D), f32), like((4,) + end_block, f32), like((devices, 24, 128), f32),
+        like((4, 1, 3 * D), f32), like((1, 2 * D), f32), like((8, 128), f32),
     )
     return pl.pallas_call(
         sum_kernel,
@@ -895,7 +878,8 @@
             pltpu.VMEM(end_block, f32), pltpu.VMEM((images, WIDE), f32), pltpu.VMEM((4, images, WIDE), f32),
             pltpu.VMEM((images, 2 * D), BF), pltpu.VMEM((4, images, 2 * D), BF), pltpu.VMEM((1, 3 * D), f32),
             pltpu.VMEM((images, WIDE), BF), pltpu.VMEM((n, images, WIDE), f32), pltpu.VMEM((n, images, WIDE), f32),
-            pltpu.VMEM((24, 128), f32), pltpu.VMEM((8, 128), f32), pltpu.VMEM((1, HALF), f32),
+            pltpu.VMEM((24, 128), f32), pltpu.VMEM((8, 128), f32), pltpu.VMEM((devices, 8, 128), f32),
+            pltpu.VMEM((1, HALF), f32),
             pltpu.VMEM((144, HALF), BF),
             dma(2 * chunks * Z), dma(chunks * Z), dma(chunks * Z),
             dma(2 * chunks * Z), dma(2 * chunks * Z), dma(2 * chunks * Z), dma(2 * chunks * Z),
@@ -942,7 +926,8 @@
     g_fm = matmul_tn(to_half(jax.nn.silu(cond_low)), d_fm)
     g_table = matmul_tn(narrow, one_hot(meta[:, FREQ : FREQ + 1], 1024))
     g_one = matmul_tn(d_pre, to_half(meta[:, :FREQ]))
-    g_two = jnp.einsum("iw,jik->jwk", narrow, hidden, preferred_element_type=f32)
+    g_two = jnp.einsum("iw,jik->wjk", narrow, hidden, preferred_element_type=f32)
+    g_two = g_two[:, :, :width].reshape(width, D)
     fm_sum = column_sums(d_fm)[None]
     slices = [column_sums(value).reshape(2, 128) for value in (d_pre, d_cond)]
     news = jnp.concatenate([sums, *slices, jnp.zeros((4, 128), f32)])
@@ -952,6 +937,7 @@
     for value in (g_fm, g_table, g_one, g_two, ends_all[0], ends_all[3], *slices):
         squares = squares + once * square(value)
     news, squares = exchange(7, "every", ("all", "all"), news, jnp.broadcast_to(squares, (8, 128)))
+    squares = jnp.sum(squares, axis=0)
     return (out, cross, dn_all, g_mod, g_fm, g_table, g_one, g_two, ends_all, news, cs_all, fm_sum, squares)
 
 
@@ -1096,8 +1082,9 @@
     save, flags, x_ref, mod_a, mod_m, b_attn, b_up, b_down, w_blk, w_dn, out_ref, *refs
 ):
     if save:
-        xm_ref, qkv_ref, att_ref, branch_a_ref, mid_ref, xm2_ref, branch_m_ref, pre_ref, act_ref = refs[:9]
-        wa, wu, wd, acc, sem = refs[9:]
+        xm_ref, qkv_ref, att_ref, last_ref, branch_a_ref, mid_ref, xm2_ref, branch_m_ref, pre_ref = refs[:9]
+        act_refs = refs[9:11]
+        wa, wu, wd, acc, sem = refs[11:]
     else:
         xm_ref, qkv_ref, att_ref, mid_ref, xm2_ref, wa, wu, wd, acc, sem = refs
     copies = weight_copies(
@@ -1129,6 +1116,7 @@
     branch = matmul(att_ref[...], wa[1, :, D:]) + b_attn[:, 3 * D :]
     if save:
         branch_a_ref[...] = branch
+        last_ref[...] = jnp.where(flags[0] == 0, att_ref[...], xm_ref[...])
     mid_ref[...] = to_half(x_ref[...] + mod_a[2:3] * branch).astype(jnp.float32)
     normed, unused = normalized(mid_ref[...])
     xm2_ref[...] = to_half(normed * (1.0 + mod_m[1:2]) + mod_m[0:1])
@@ -1144,7 +1132,7 @@
             act = to_half(pre * (0.5 * (1.0 + jnp.tanh(GELU_SCALE * cube))))
             if save:
                 pre_ref[:, part] = pre
-                act_ref[:, part] = act
+                act_refs[half][:, own] = act
             acc[...] += matmul_nt(act, wd[half, :, own])
     if save:
         branch_m_ref[...] = acc[...]
@@ -1154,7 +1142,7 @@
 
 def backward_kernel(
     flags, d_ref, x_ref, mid_ref, mod_a, mod_m, branch_a, branch_m, qkv_ref, pre_hbm, w_blk, w_dn,
-    d_in_ref, d_mod_a, d_mod_m, grad_a, grad_m, d_pre_ref, d_qkv_ref,
+    d_in_ref, d_mod_a, d_mod_m, grad_a, grad_m, d_pre_own, d_pre_sib, d_qkv_ref, right_own, right_sib,
     wa, wu, wd, pre_ref, acc, d_acc, d_att, sem,
 ):
     copies = weight_copies(
@@ -1187,7 +1175,7 @@
                 GELU_SCALE * (1.0 + (3.0 * 0.044715) * square)
             )
             d_pre = to_half(d_act * slope)
-            d_pre_ref[:, part] = d_pre
+            (d_pre_sib if half else d_pre_own)[:, own] = d_pre
             acc[...] += matmul_nt(d_pre, wu[half, :, own])
     normed, inverse = normalized(mid_ref[...])
     d_x, d_shift, d_scale = modulated_back(normed, inverse, mod_m[1:2], acc[...])
@@ -1212,6 +1200,11 @@
         d_acc[:, at(0)] += own_lanes(mask, matmul(d_scores, key) * SCALE)
         d_acc[:, at(1)] += own_lanes(mask, matmul_tn(d_scores, query) * SCALE)
     d_qkv_ref[...] = to_half(d_acc[...])
+    first = flags[0] == 0
+    pairs = ((d_qkv_ref[:, :D], d_qkv_ref[:, 2 * D :]), (d_qkv_ref[:, D : 2 * D], grad_a[...]))
+    for k, (one, two) in enumerate(pairs):
+        right_own[:, D * k : D * (k + 1)] = jnp.where(first, one, two)
+        right_sib[:, D * k : D * (k + 1)] = jnp.where(first, two, one)
     copies[6].wait()
     d_xm = matmul_nt(d_qkv_ref[:, 2 * D :], wa[1, :, :D]) + matmul_nt(d_qkv_ref[:, : 2 * D], wa[0])
     normed, inverse = normalized(x_ref[...])
@@ -1239,8 +1232,8 @@
     total = pltpu.VMEM((PATCHES, D), jnp.float32)
     f32 = jnp.float32
     if save:
-        shapes = [like(D, f32), like(D, BF), like(3 * D, BF), like(D, BF), like(D, f32), like(D, f32)]
-        shapes += [like(D, BF), like(D, f32), like(FF, f32), like(FF, BF)]
+        shapes = [like(D, f32), like(D, BF), like(3 * D, BF), like(D, BF), like(D, BF), like(D, f32), like(D, f32)]
+        shapes += [like(D, BF), like(D, f32), like(FF, f32), like(HALF, BF), like(HALF, BF)]
         scratch = []
     else:
         shapes, scratch = [like(D, BF)], [tokens, wide, tokens, total, tokens]
@@ -1258,16 +1251,17 @@
 
 def stage_backward(d_out, x_in, weights, kept):
     flags, mod_a, mod_m, w_blk, w_dn, b_attn, b_up, b_down = weights
-    xm_a, qkv, att, branch_a, x_mid, xm_m, branch_m, pre, act = kept
+    xm_a, qkv, att, last, branch_a, x_mid, xm_m, branch_m, pre, act_own, act_sib = kept
     vmem, hbm = pl.BlockSpec(memory_space=pltpu.VMEM), pl.BlockSpec(memory_space=pl.ANY)
     smem = pl.BlockSpec(memory_space=pltpu.SMEM)
     like = lambda columns, kind: jax.ShapeDtypeStruct((PATCHES, columns), kind)
     mods = jax.ShapeDtypeStruct((3, D), jnp.float32)
     return pl.pallas_call(
         backward_kernel,
-        out_shape=(like(D, BF), mods, mods, like(D, BF), like(D, BF), like(FF, BF), like(3 * D, BF)),
+        out_shape=(like(D, BF), mods, mods, like(D, BF), like(D, BF))
+        + (like(HALF, BF), like(HALF, BF), like(3 * D, BF), like(HALF, BF), like(HALF, BF)),
         in_specs=[smem] + [vmem] * 8 + [hbm] * 3,
-        out_specs=(vmem,) * 7,
+        out_specs=(vmem,) * 10,
         scratch_shapes=weight_scratch()
         + [
             pltpu.VMEM((PATCHES, FF), jnp.float32),
@@ -1282,24 +1276,89 @@
     )(flags, d_out, x_in, x_mid, mod_a, mod_m, branch_a, branch_m, qkv, pre, w_blk, w_dn)
 
 
+COLUMNS = 384
+
+
+def products_kernel(
+    flags, dn_own, dn_sib, up_own, up_sib, xa_own, xa_sib, att_own, last_sib,
+    act_own, act_sib, pre_own, pre_sib, right_own, right_sib,
+    g_dn, g_up, g_attn, t_dn, t_up, t_one, t_two,
+):
+    step = pl.program_id(0)
+
+    @pl.when(step == 0)
+    def _():
+        last_own = jnp.where(flags[0] == 0, xa_own[...], att_own[...])
+        for target, own, sib in (
+            (t_dn, dn_own[...], dn_sib), (t_up, up_own[...], up_sib),
+            (t_one, xa_own[...], xa_sib), (t_two, last_own, last_sib),
+        ):
+            target[:, :PATCHES] = own.T
+            target[:, PATCHES:] = sib[...].T
+
+    def product(left, own, sib):
+        return to_half(
+            matmul(left[:, :PATCHES], own[...]) + matmul(left[:, PATCHES:], sib[...])
+        )
+
+    g_dn[...] = product(t_dn, act_own, act_sib)
+    g_up[...] = product(t_up, pre_own, pre_sib)
+
+    @pl.when(step < D // COLUMNS)
+    def _():
+        g_attn[...] = product(t_one, right_own, right_sib)
+
+    @pl.when(step >= D // COLUMNS)
+    def _():
+        g_attn[...] = product(t_two, right_own, right_sib)
+
+
+def products(flags, lefts, rights):
+    left = whole_spec((PATCHES, D))
+    right = pl.BlockSpec((PATCHES, COLUMNS), lambda step: (0, step))
+    out = pl.BlockSpec((D, COLUMNS), lambda step: (0, step))
+    return pl.pallas_call(
+        products_kernel,
+        grid=(HALF // COLUMNS,),
+        out_shape=(jax.ShapeDtypeStruct((D, HALF), BF),) * 3,
+        in_specs=[pl.BlockSpec(memory_space=pltpu.SMEM)] + [left] * 8 + [right] * 6,
+        out_specs=(out,) * 3,
+        scratch_shapes=[pltpu.VMEM((D, 2 * PATCHES), BF)] * 4,
+        compiler_params=pltpu.CompilerParams(vmem_limit_bytes=VMEM_BYTES),
+        cost_estimate=pl.CostEstimate(
+            flops=12 * PATCHES * D * HALF, bytes_accessed=10 * D * HALF, transcendentals=0
+        ),
+        name="products",
+    )(flags, *lefts, *rights)
+
+
+def whole_spec(shape):
+    return pl.BlockSpec(shape, lambda step: (0,) * len(shape))
+
+
 SUM_ROWS = 16
 
 
-def collect_kernel(peers, flags_ref, *refs):
-    tokens, d_pre_ref, mods, fm_ref, extra_ref = refs[:4], refs[4], refs[5:7], refs[7], refs[8]
-    sums_ref, mods_ref, rows_ref = refs[9:]
+def collect_kernel(flags_ref, *refs):
+    tokens, d_pres, mods, fm_ref, extra_ref, tok_ref, head_ref = refs[:4], refs[4:6], refs[6:8], *refs[8:12]
+    sums_ref, mods_ref, ends_ref, rows_ref = refs[12:]
     core, stage = flags_ref[0], flags_ref[1]
     ones = jnp.ones((8, PATCHES), BF)
     total = lambda value: matmul(ones, value)[0:1]
     sums_ref[...] = jnp.zeros_like(sums_ref)
     rows = [total(tokens[0][:, D * k : D * (k + 1)]) for k in range(3)]
     rows += [total(ref[...]) for ref in tokens[1:]]
-    halves = [[total(d_pre_ref[:, D * k : D * (k + 1)]) for k in range(4)]]
-    own = halves[0]
+    halves = [[total(ref[:, D * k : D * (k + 1)]) for k in range(2)] for ref in d_pres]
+    own = halves[0] + halves[1]
     order = [jnp.where(core == 0, own[k], own[(k + 2) % 4]) for k in range(4)]
     last = jnp.where(stage == 0, rows[5], extra_ref[0:1])
     for place, row in enumerate(rows[:4] + order + [rows[4], last, extra_ref[1:2]]):
         sums_ref[place : place + 1, :D] = row
+    ends = jnp.where(stage == 0, matmul_tn(tok_ref[...], tokens[3][...]), head_ref[...])
+    ends_ref[...] = jnp.zeros_like(ends_ref)
+    width = D // ends_ref.shape[0]
+    for index in range(ends_ref.shape[0]):
+        ends_ref[index, :, :width] = ends[:, width * index : width * (index + 1)]
     rows_ref[...] = jnp.zeros_like(rows_ref)
     for k in range(2):
         for row in range(5):
@@ -1310,21 +1369,22 @@
         mods_ref[k] = to_half(rows_ref[...])
 
 
-def collect(flags, tokens, d_pre, mods, fm, extra):
-    peers = 2 * lax.axis_size("dp")
+def collect(flags, tokens, d_pres, mods, fm, extra, tok, g_head):
+    n = lax.axis_size("dp")
     vmem = pl.BlockSpec(memory_space=pltpu.VMEM)
     return pl.pallas_call(
-        partial(collect_kernel, peers),
+        collect_kernel,
         out_shape=(
-            jax.ShapeDtypeStruct((SUM_ROWS, 128 * max(peers, 9)), jnp.float32),
+            jax.ShapeDtypeStruct((SUM_ROWS, 128 * max(2 * n, 9)), jnp.float32),
             jax.ShapeDtypeStruct((2, 48, 128), BF),
+            jax.ShapeDtypeStruct((n, HEAD_OUT, WIDE), jnp.float32),
         ),
         scratch_shapes=[pltpu.VMEM((48, 128), jnp.float32)],
-        in_specs=[pl.BlockSpec(memory_space=pltpu.SMEM)] + [vmem] * 9,
-        out_specs=(vmem, vmem),
+        in_specs=[pl.BlockSpec(memory_space=pltpu.SMEM)] + [vmem] * 12,
+        out_specs=(vmem,) * 3,
         compiler_params=pltpu.CompilerParams(vmem_limit_bytes=VMEM_BYTES),
         name="collect",
-    )(flags, *tokens, d_pre, *mods, fm, extra)
+    )(flags, *tokens, *d_pres, *mods, fm, extra, tok, g_head)
 
 
 def final_step(x_out, fmod, w_head, b_head, target, counts, loss_scale):
@@ -1333,7 +1393,7 @@
     error = matmul_nt(xf_half, w_head) + b_head - target
     loss = counts * jnp.sum(error * error)
     d_pred = to_half(2.0 * loss_scale * counts * error)
-    g_head = matmul_tn(xf_half, d_pred)
+    g_head = matmul_tn(d_pred, xf_half)
     d_x, d_shift, d_scale = modulated_back(normed, inverse, fmod[1:2], matmul(d_pred, w_head))
     return (loss, d_x, jnp.stack([d_shift, d_scale]), g_head, column_sums(d_pred))
 
@@ -1422,47 +1482,28 @@
     loss, d_final, d_fmod, g_head, b_head = final_step(
         x_out, fmod, w_head_all, biases[35 * D :], target, counts, loss_scale
     )
-    xm_a, qkv, attended, branch_a, x_mid, xm_b, branch_b, pre, act = kept
+    xm_a, qkv, attended, last_sib, branch_a, x_mid, xm_b, branch_b, pre, act_own, act_sib = kept
     d_hop = swap(stage_backward(d_final, x_in, weights, kept)[0], 2)
     d_out = jnp.where(stage == 1, d_final, d_hop.astype(jnp.float32))
-    d_first, d_mod_a, d_mod_b, d_branch_a, d_branch_b, d_pre, d_qkv = stage_backward(
-        d_out, x_in, weights, kept
-    )
-    d_query, d_key, d_value = (d_qkv[:, D * k : D * (k + 1)] for k in range(3))
-
-    act_sib, branch_sib, xm_sib, pre_sib = swap((act[:, HALF:], d_branch_b, xm_b, d_pre[:, HALF:]), 1)
-    g_dn = to_half(matmul_tn(d_branch_b, act[:, :HALF]) + matmul_tn(branch_sib, act_sib))
-    g_up = to_half(matmul_tn(xm_b, d_pre[:, :HALF]) + matmul_tn(xm_sib, pre_sib))
-
-    xa_sib, last_sib, one_sib, two_sib = swap(
-        (
-            xm_a,
-            jnp.where(even, attended, xm_a),
-            jnp.where(even, d_value, d_query),
-            jnp.where(even, d_branch_a, d_key),
-        ),
-        1,
-    )
-    last = jnp.where(even, xm_a, attended)
-    one = jnp.where(even, d_query, d_value)
-    two = jnp.where(even, d_key, d_branch_a)
-    g_attn = jnp.concatenate(
-        [
-            to_half(matmul_tn(xm_a, one) + matmul_tn(xa_sib, one_sib)),
-            to_half(matmul_tn(last, two) + matmul_tn(last_sib, two_sib)),
-        ],
-        axis=1,
+    d_first, d_mod_a, d_mod_b, d_branch_a, d_branch_b, d_pre_own, d_pre_sib, d_qkv, right_own, right_sib = (
+        stage_backward(d_out, x_in, weights, kept)
+    )
+
+    act_come, xb_come, xa_come, last_come = swap((act_sib, xm_b, xm_a, last_sib), 1)
+    branch_come, pre_come, right_come = swap((d_branch_b, d_pre_sib, right_sib), 1)
+    g_dn, g_up, g_attn = products(
+        flags,
+        (d_branch_b, branch_come, xm_b, xb_come, xm_a, xa_come, attended, last_come),
+        (act_own, act_come, d_pre_own, pre_come, right_own, right_come),
     )
 
     extra = jnp.stack([jnp.pad(b_head, (0, D - HEAD_OUT)), jnp.pad(loss[None], (0, D - 1))])
     d_fmod = jnp.where(stage == 1, d_fmod, jnp.zeros_like(d_fmod))
-    own_sums, d_mods = collect(
-        flags, (d_qkv, d_branch_a, d_branch_b, d_first), d_pre, (d_mod_a, d_mod_b), d_fmod, extra
-    )
-    g_patch = jnp.pad(matmul_tn(d_first, tok_half), ((0, 0), (0, HEAD_OUT - PATCH_IN)))
-    end_rows = row_count(width * HEAD_OUT)
-    own_ends = jnp.where(stage == 0, g_patch, g_head).reshape(n, width * HEAD_OUT)
-    own_ends = jnp.pad(own_ends, ((0, 0), (0, end_rows * 128 - width * HEAD_OUT))).reshape(n, end_rows, 128)
+    tok_wide = jnp.pad(tok_half, ((0, 0), (0, HEAD_OUT - PATCH_IN)))
+    own_sums, d_mods, own_ends = collect(
+        flags, (d_qkv, d_branch_a, d_branch_b, d_first), (d_pre_own, d_pre_sib), (d_mod_a, d_mod_b), d_fmod,
+        extra, tok_wide, g_head,
+    )
     own_sums = own_sums.reshape(SUM_ROWS, -1, 128).transpose(1, 0, 2)[: 2 * n]
     halves, crossed, dn_all, g_mod, g_fm, g_table, g_one, g_two, ends_all, news, mod_sums, fm_sum, squares = (
         sum_gradients(
@@ -1476,10 +1517,7 @@
     )
     dn_all = dn_all.astype(jnp.float32)
     down_both = jnp.stack([jnp.concatenate([dn_all[2 * k], dn_all[2 * k + 1]], axis=1) for k in range(2)])
-    ends = [
-        ends_all[k].reshape(-1)[: width * HEAD_OUT].reshape(width, HEAD_OUT) for k in (0, 3)
-    ]
-    g_two = g_two[:, :, :width].transpose(1, 0, 2).reshape(width, D)
+    ends = [ends_all[k, :, :width].T for k in (0, 3)]
     g_stem = jnp.concatenate(
         [g_table[:, :NCLS], ends[0][:, :PATCH_IN], g_one[:width], g_two], axis=1
     )
@@ -1500,7 +1538,7 @@
         + [fm_sum[0], stages[1][9 * D : 9 * D + HEAD_OUT]]
     )
     loss_sum = stages[1][10 * D]
-    grad_norm = jnp.sqrt(jnp.sum(squares[:, 0, 0]))
+    grad_norm = jnp.sqrt(squares[0, 0])
     factor = jnp.minimum(1.0, clip_limit / (grad_norm + 1e-06))
     mod_out = nesterov(mod_w, mod_m, mod_e, g_mod[None], factor)
     block_out = nesterov(block_w, block_m, block_e, g_blk[None], factor)

time: 655 us -> 644 us (0.983)
  matrix products: 26.3 us -> 3.88 us
  Pallas kernels: 497 us -> 509 us
    dot_general x10 -> x1, matrix products: 23.4 us -> 0.88 us  [matmul_tn(): lax.dot_general(left, right, (((0,), (0,)), ((), ())), preferred_element_...]
    pallas_call x1 -> x2, Pallas kernels: 4.47 us -> 23.6 us  [the longest x1 19.1 us: products(): pl.pallas_call(products_kernel, grid=(HALF // COLUMNS,), out_shape=(jax.S...]
    pallas_call x1, Pallas kernels: 193 us -> 183 us  [gather_weights(): pl.pallas_call(gather_kernel, out_shape=(jax.ShapeDtypeStruct((2, D, FF),...]
    ppermute x10 -> x9, waiting for transfers between devices: 16.5 us -> 18.5 us  [swap(): return lax.ppermute(array, 'section', [(k, k ^ by) for k in range(peers)])]
  transfers between devices with their start and end apart: 10 -> 9, of which waited for: 2 -> 2; matrix products, arithmetic and copies ran while one was open for 5% -> 2% of each run, Pallas kernels for 5% -> 6%
where the time goes in v8:
time: 644 us; the launch traced here: 639 us
  Pallas kernels  509 us (79%)
  other arithmetic  53.5 us (8%)
  local copies, waits for them, and re-layouts  42.8 us (7%)
  waiting for transfers between devices  18.5 us (3%)
  between operations  6.77 us (1%)
    pallas_call x1, Pallas kernels, sum_gradients(): pl.pallas_call(sum_kernel, out_shape=shapes, in_specs=[hbm] * 3 + [vmem]...  200 us
    pallas_call x1, Pallas kernels, gather_weights(): pl.pallas_call(gather_kernel, out_shape=(jax.ShapeDtypeStruct((2, D, FF),...  183 us
    pallas_call x2, Pallas kernels, stage_backward(): pl.pallas_call(backward_kernel, out_shape=(like(D, BF), mods, mods, like(...  62.4 us
    pallas_call x2, Pallas kernels, stage_forward(): pl.pallas_call(partial(forward_kernel, save), out_shape=tuple(shapes), in...  40 us
    pallas_call x1, Pallas kernels, products(): pl.pallas_call(products_kernel, grid=(HALF // COLUMNS,), out_shape=(jax.S...  19.1 us
    ppermute x9, waiting for transfers between devices, swap(): return lax.ppermute(array, 'section', [(k, k ^ by) for k in range(peers)])  18.5 us
  transfers between devices with their start and end apart: 9, of which 2 were waited for; matrix products, arithmetic and copies ran while one was open for 2% of the time, Pallas kernels for 6%

profile of v8, /device:TPU:0, one launch (start us, length us, event | category | flops | bytes accessed | tf_op | source)
XLA Modules:
  0.0 638.8 jit_solution(14133603674110589719)
XLA Ops:
  0.7 1.5 bitcast_convert_fusion
  12.7 2.2 fusion.10.dn_ref
  15.5 182.9 %gather_weights.1 = (bf16[2,1152,4608]{2,1,0:T(8,128)(2,1)}, bf16[2,1152,2304]{2,1,0:T(8,128)(2,1)}, f32[16,384]{1,0:T(8,128)}, bf16[8,48,256]{2,1,0:T(8,128)(2,...) custom-call(bf16[144,4608]{1,0:T(8,128)(2,1)} %convert_bitcast_fusion.1.blk_ref,, ...), custom_call_target="tpu_custom_call" | custom-call | bytes 400000000 | tf_op jit(solution)/shard_map/gather_weights/pallas_call | solution.py:385
  208.5 18.7 %stage_forward.2 = bf16[256,1152]{1,0:T(8,128)(2,1)} custom-call(s32[2]{0:T(128)} %pad_add_fusion.flags.flags_ref, f32[256,1152]{1,0:T(8,128)} %fusion.2.x_ref, f32[3,1152]{1,0:T(4,128)} %reshape.204.mod_a, f32[3,1152]{1,0:T(4,128)} %reshape.205.mod_m, f32[1,4608]{1,0:T(1,128)} %broadcast_in_dim.32.b_attn, f32[1,4608]{1,0:T(1,128)} %copy-done.41, ...), custom_call_target="tpu_custom_call" | custom-call | flops 16911433728 | bytes 31850496 | tf_op jit(solution)/shard_map/stage_forward/pallas_call | solution.py:1240
  227.2 1.6 collective-permute-start
  231.4 1.5 copy.67
  237.8 5.4 collective-permute-done
  243.2 2.2 convert_select_fusion.3.x_ref
  245.4 21.3 %stage_forward.3 = (f32[256,1152]{1,0:T(8,128)}, bf16[256,1152]{1,0:T(8,128)(2,1)}, bf16[256,3456]{1,0:T(8,128)(2,1)}, bf16[256,1152]{1,0:T(8,128)(2,1)}, bf16[2...) custom-call(s32[2]{0:T(128)} %pad_add_fusion.flags.flags_ref, ...), custom_call_target="tpu_custom_call" | custom-call | flops 16911433728 | bytes 31850496 | tf_op jit(solution)/shard_map/stage_forward/pallas_call | solution.py:1240
  272.0 31.3 %stage_backward.2 = (bf16[256,1152]{1,0:T(8,128)(2,1)}, f32[3,1152]{1,0:T(4,128)}, f32[3,1152]{1,0:T(4,128)}, bf16[256,1152]{1,0:T(8,128)(2,1)}, bf16[256,1152]{...) custom-call(s32[2]{0:T(128)} %pad_add_fusion.flags.flags_ref, ...), custom_call_target="tpu_custom_call" | custom-call | flops 16911433728 | bytes 31850496 | tf_op jit(solution)/shard_map/stage_backward/pallas_call | solution.py:1259
  303.2 1.6 collective-permute-start.1
  305.3 13.1 %collective-permute-done.1 = bf16[256,1152]{1,0:T(8,128)(2,1)} collective-permute-done((bf16[256,1152]{1,0:T(8,128)(2,1)}, bf16[256,1152]{1,0:T(8,128)(2,1)}, u32[]{:S(2)}, u32[]{:S(2)}) %collective-permute-start.1) | collective-permute-done | bytes 589856 | tf_op jit(solution)/shard_map/ppermute | solution.py:1411
  318.4 2.2 convert_select_fusion.2.d_ref
  320.6 31.2 %stage_backward.3 = (bf16[256,1152]{1,0:T(8,128)(2,1)}, f32[3,1152]{1,0:T(4,128)}, f32[3,1152]{1,0:T(4,128)}, bf16[256,1152]{1,0:T(8,128)(2,1)}, bf16[256,1152]{...) custom-call(s32[2]{0:T(128)} %pad_add_fusion.flags.flags_ref, ...), custom_call_target="tpu_custom_call" | custom-call | flops 16911433728 | bytes 31850496 | tf_op jit(solution)/shard_map/stage_backward/pallas_call | solution.py:1259
  356.0 4.5 collect.1
  360.5 1.6 bitcast_bitcast_fusion.bp_ref
  362.1 19.1 %products.1 = (bf16[1152,2304]{1,0:T(8,128)(2,1)}, bf16[1152,2304]{1,0:T(8,128)(2,1)}, bf16[1152,2304]{1,0:T(8,128)(2,1)}) custom-call(s32[2]{0:T(128)} %pad_add_fusion.flags.flags_ref, bf16[256,1152]{1,0:T(8,128)(2,1)} %get-tuple-element.89.dn_own.refs_2_, bf16[256,1152]{1,0:T(8,128)(2,1)} %collective-permute-done.2.dn_sib, ...), custom_call_target="tpu_custom_call" | custom-call | flops 8153726976 | bytes 26542080 | tf_op jit(solution)/shard_map/products/pallas_call | solution.py:1320
  381.2 199.6 %sum_gradients.1 = (f32[2,144,2304]{2,1,0:T(8,128)}, bf16[144,2304]{1,0:T(8,128)(2,1)}, bf16[4,144,2304]{2,1,0:T(8,128)(2,1)}, f32[144,3456]{1,0:T(8,128)}, f32[...) custom-call(bf16[1152,2304]{1,0:T(8,128)(2,1)} %get-tuple-element.10, ...), custom_call_target="tpu_custom_call" | custom-call | bytes 400000000 | tf_op jit(solution)/shard_map/sum_gradients/pallas_call | solution.py:868
  589.7 2.2 convert_element_type.143
  592.0 2.8 slice_bitcast_fusion.3
  596.4 1.7 fusion.20
  598.1 1.6 multiply_add_fusion.3
  599.7 2.5 concatenate.63
  602.2 3.6 convert_bitcast_fusion.3
  605.9 3.9 fusion.5
  611.9 4.1 convert_bitcast_fusion
  616.0 7.9 %fusion = f32[2,4608,144]{1,2,0:T(8,128)} fusion(f32[2,144,4608]{2,1,0:T(8,128)S(1)} %get-tuple-element.144, f32[2,4608,144]{1,2,0:T(8,128)} %param.38), kind=kLoop, calls=%fused_computation.2 | loop fusion | flops 3981312 | bytes 15925248 | tf_op jit(solution)/shard_map/transpose | solution.py:1545
  624.2 1.5 copy-done.3
  626.5 2.6 fusion.21
  629.1 1.9 multiply_add_fusion
  633.2 2.2 fusion.22
  635.3 1.9 multiply_add_fusion.2
  (248 shorter events, 50.1 us)
Async XLA Ops:
  4.4 3.3 copy-start.45
  4.4 3.4 copy-start.46
  4.4 3.5 copy-start.5
  15.5 187.9 %copy-start.38 = (f32[2,32,32,4]{2,3,1,0:T(4,128)S(1)}, f32[2,32,32,4]{2,3,1,0:T(4,128)}, u32[]{:S(2)}) copy-start(f32[2,32,32,4]{2,3,1,0:T(4,128)} %param.24) | copy-start | bytes 98308
  15.5 187.9 %copy-start.39 = (f32[2,32,32,4]{2,3,1,0:T(4,128)S(1)}, f32[2,32,32,4]{2,3,1,0:T(4,128)}, u32[]{:S(2)}) copy-start(f32[2,32,32,4]{2,3,1,0:T(4,128)} %param.25) | copy-start | bytes 98308
  227.2 16.0 %collective-permute-start = (bf16[256,1152]{1,0:T(8,128)(2,1)}, bf16[256,1152]{1,0:T(8,128)(2,1)}, u32[]{:S(2)}, u32[]{:S(2)}) collective-permute-start(bf16[256,1152]{1,0:T(8,128)(2,1)} %stage_forward.2), channel_id=1, source_target_pairs={{0,2},{1,3},{2,0},{3,1},{4,6},{5,7},{6,4},{7,5},{8,10},{9,11},{10,... | collective-permute-start | bytes 1769480 | tf_op jit(solution)/shard_map/ppermute | solution.py:1411
  230.3 12.9 %copy-start.18 = (f32[256,1152]{1,0:T(8,128)S(1)}, f32[256,1152]{1,0:T(8,128)}, u32[]{:S(2)}) copy-start(f32[256,1152]{1,0:T(8,128)} %fusion.2.x_ref) | copy-start | bytes 3538948
  272.0 46.5 %copy-start.19 = (f32[256,1152]{1,0:T(8,128)S(1)}, f32[256,1152]{1,0:T(8,128)}, u32[]{:S(2)}) copy-start(f32[256,1152]{1,0:T(8,128)} %subtract_multiply_fusion.d_ref) | copy-start | bytes 3538948
  303.2 15.2 %collective-permute-start.1 = (bf16[256,1152]{1,0:T(8,128)(2,1)}, bf16[256,1152]{1,0:T(8,128)(2,1)}, u32[]{:S(2)}, u32[]{:S(2)}) collective-permute-start(bf16[256,1152]{1,0:T(8,128)(2,1)} %get-tuple-element.88), channel_id=1, source_target_pairs={{0,2},{1,3},{2,0},{3,1},{4,6},{5,7},{6,4},{7,5},{8,10},{9,11},{10,... | collective-permute-start | bytes 1769480 | tf_op jit(solution)/shard_map/ppermute | solution.py:1411
  304.8 57.3 %collective-permute-start.6 = (bf16[256,2304]{1,0:T(8,128)(2,1)}, bf16[256,2304]{1,0:T(8,128)(2,1)}, u32[]{:S(2)}, u32[]{:S(2)}) collective-permute-start(bf16[256,2304]{1,0:T(8,128)(2,1)} %get-tuple-element.95), channel_id=1, source_target_pairs={{0,1},{1,0},{2,3},{3,2},{4,5},{5,4},{6,7},{7,6},{8,9},{9,8},{10,11... | collective-permute-start | bytes 3538952 | tf_op jit(solution)/shard_map/ppermute | solution.py:1411
  304.8 49.0 %collective-permute-start.3 = (bf16[256,1152]{1,0:T(8,128)(2,1)}, bf16[256,1152]{1,0:T(8,128)(2,1)}, u32[]{:S(2)}, u32[]{:S(2)}) collective-permute-start(bf16[256,1152]{1,0:T(8,128)(2,1)} %get-tuple-element.90.up_own), channel_id=1, source_target_pairs={{0,1},{1,0},{2,3},{3,2},{4,5},{5,4},{6,7},{7,6},{8,9},{9,8},{10,11... | collective-permute-start | bytes 1769480 | tf_op jit(solution)/shard_map/ppermute | solution.py:1411
  305.3 48.7 %collective-permute-start.4 = (bf16[256,1152]{1,0:T(8,128)(2,1)}, bf16[256,1152]{1,0:T(8,128)(2,1)}, u32[]{:S(2)}, u32[]{:S(2)}) collective-permute-start(bf16[256,1152]{1,0:T(8,128)(2,1)} %get-tuple-element.91.xa_own), channel_id=1, source_target_pairs={{0,1},{1,0},{2,3},{3,2},{4,5},{5,4},{6,7},{7,6},{8,9},{9,8},{10,11... | collective-permute-start | bytes 1769480 | tf_op jit(solution)/shard_map/ppermute | solution.py:1411
  320.6 34.4 %copy-start.13 = (bf16[256,1152]{1,0:T(8,128)(2,1)S(1)}, bf16[256,1152]{1,0:T(8,128)(2,1)}, u32[]{:S(2)}) copy-start(bf16[256,1152]{1,0:T(8,128)(2,1)} %copy-done.12) | copy-start | bytes 1769476
  351.8 10.3 %collective-permute-start.7 = (bf16[256,2304]{1,0:T(8,128)(2,1)}, bf16[256,2304]{1,0:T(8,128)(2,1)}, u32[]{:S(2)}, u32[]{:S(2)}) collective-permute-start(bf16[256,2304]{1,0:T(8,128)(2,1)} %get-tuple-element.97.refs_5_), channel_id=1, source_target_pairs={{0,1},{1,0},{2,3},{3,2},{4,5},{5,4},{6,7},{7,6},{8,9},{9,8},{10,11... | collective-permute-start | bytes 3538952 | tf_op jit(solution)/shard_map/ppermute | solution.py:1411
  351.9 10.2 %collective-permute-start.8 = (bf16[256,2304]{1,0:T(8,128)(2,1)}, bf16[256,2304]{1,0:T(8,128)(2,1)}, u32[]{:S(2)}, u32[]{:S(2)}) collective-permute-start(bf16[256,2304]{1,0:T(8,128)(2,1)} %get-tuple-element.99), channel_id=1, source_target_pairs={{0,1},{1,0},{2,3},{3,2},{4,5},{5,4},{6,7},{7,6},{8,9},{9,8},{10,11... | collective-permute-start | bytes 3538952 | tf_op jit(solution)/shard_map/ppermute | solution.py:1411
  353.9 8.2 %collective-permute-start.5 = (bf16[256,1152]{1,0:T(8,128)(2,1)}, bf16[256,1152]{1,0:T(8,128)(2,1)}, u32[]{:S(2)}, u32[]{:S(2)}) collective-permute-start(bf16[256,1152]{1,0:T(8,128)(2,1)} %get-tuple-element.93), channel_id=1, source_target_pairs={{0,1},{1,0},{2,3},{3,2},{4,5},{5,4},{6,7},{7,6},{8,9},{9,8},{10,11... | collective-permute-start | bytes 1769480 | tf_op jit(solution)/shard_map/ppermute | solution.py:1411
  354.0 8.1 %collective-permute-start.2 = (bf16[256,1152]{1,0:T(8,128)(2,1)}, bf16[256,1152]{1,0:T(8,128)(2,1)}, u32[]{:S(2)}, u32[]{:S(2)}) collective-permute-start(bf16[256,1152]{1,0:T(8,128)(2,1)} %get-tuple-element.89.dn_own.refs_2_), channel_id=1, source_target_pairs={{0,1},{1,0},{2,3},{3,2},{4,5},{5,4},{6,7},{7,6},{8,9},{9,8},{10,11... | collective-permute-start | bytes 1769480 | tf_op jit(solution)/shard_map/ppermute | solution.py:1411
  583.3 5.7 copy-start.37
  591.9 3.6 copy-start.36
  591.9 4.3 copy-start.8
  592.0 4.3 copy-start.26
  602.2 7.6 %copy-start.16 = (f32[144,2304]{1,0:T(8,128)S(1)}, f32[144,2304]{1,0:T(8,128)}, u32[]{:S(2)}) copy-start(f32[144,2304]{1,0:T(8,128)} %get-tuple-element.154) | copy-start | bytes 3981316
  602.2 7.6 %copy-start.17 = (f32[144,2304]{1,0:T(8,128)S(1)}, f32[144,2304]{1,0:T(8,128)}, u32[]{:S(2)}) copy-start(f32[144,2304]{1,0:T(8,128)} %get-tuple-element.157) | copy-start | bytes 3981316
  602.2 9.6 %slice-start = ((s8[5308416]{0:T(1024)(128)(4,1)}), s8[4194304]{0:T(1024)(128)(4,1)S(1)}, s32[]{:S(2)}) async-start(s8[5308416]{0:T(1024)(128)(4,1)} %bitcast.172), calls=%async_computation | async-start | bytes 8388608
  602.2 9.6 %slice-start.2 = ((s8[5308416]{0:T(1024)(128)(4,1)}), s8[4194304]{0:T(1024)(128)(4,1)S(1)}, s32[]{:S(2)}) async-start(s8[5308416]{0:T(1024)(128)(4,1)} %bitcast.175), calls=%async_computation.2 | async-start | bytes 8388608
  605.8 4.0 copy-start.11
  605.8 6.0 slice-start.1
  605.9 6.0 slice-start.3
  616.0 7.9 %copy-start = (f32[2,144,4608]{2,1,0:T(8,128)}, f32[2,144,4608]{2,1,0:T(8,128)S(1)}, u32[]{:S(2)}) copy-start(f32[2,144,4608]{2,1,0:T(8,128)S(1)} %get-tuple-element.144) | copy-start | bytes 15925252
  616.0 7.9 %copy-start.21 = (f32[2,144,2304]{2,1,0:T(8,128)S(1)}, f32[2,144,2304]{2,1,0:T(8,128)}, u32[]{:S(2)}) copy-start(f32[2,144,2304]{2,1,0:T(8,128)} %get-tuple-element.117) | copy-start | bytes 7962628
  616.0 7.9 %copy-start.29 = (bf16[144,2304]{1,0:T(8,128)(2,1)S(1)}, bf16[144,2304]{1,0:T(8,128)(2,1)}, u32[]{:S(2)}) copy-start(bf16[144,2304]{1,0:T(8,128)(2,1)} %get-tuple-element.118) | copy-start | bytes 1990660
  629.1 4.1 copy-start.25
  (28 other events, 59.1 us)

commit v9 on v8

--- a/solution.py
+++ b/solution.py
@@ -116,9 +116,9 @@
 
 
 def gather_kernel(
-    blk_ref, dn_ref, meta_ref, ends_ref, one_ref, two_ref, table_ref, mod_ref, fm_ref, b_one, b_two,
-    out_blk, out_dn, meta_out, ends_out, pre_out, hidden_out, cond_out, mods_out,
-    metas, hidden, part, parts, arrived_parts,
+    blk_hbm, dn_hbm, stem_hbm, mod_hbm, tail_hbm, meta_ref, ends_ref, b_one, b_two,
+    out_blk, out_dn, meta_out, ends_out, pre_out, hidden_out, cond_out, mods_out, mod_ref, fm_ref, two_ref,
+    blk_f, dn_f, stem_f, mod_f, tail_f, blk_ref, dn_ref, one_ref, table_ref, load_sem, metas, hidden, part, parts, arrived_parts,
     meta_send, meta_recv, ends_send, ends_recv, hid_send, hid_recv, part_send, part_recv, local_sem,
     up_sem, down_sem, x_sem, sib_sem, recv_sem, sib_recv, own_sem,
 ):
@@ -134,6 +134,15 @@
     where = lambda p: {"dp": p // 2, "section": low + lax.rem(p, 2)}
     has_up, has_down = z < Z - 1, z > 0
 
+    stage_rows = dn_hbm.at[section // 2, :, pl.ds(pl.multiple_of(core * HALF, 128), HALF)]
+    loads = [
+        pltpu.make_async_copy(src, dst, load_sem.at[k])
+        for k, (src, dst) in enumerate(
+            ((blk_hbm, blk_f), (stage_rows, dn_f), (stem_hbm, stem_f), (mod_hbm, mod_f), (tail_hbm, tail_f))
+        )
+    ]
+    for copy_in in loads:
+        copy_in.start()
     barrier = pltpu.get_barrier_semaphore()
 
     @pl.loop(1, group)
@@ -220,6 +229,17 @@
     def arrived(owner, k):
         copy(owner, k, False, x_sem, across).wait_recv()
 
+    for which in range(2):
+        loads[which].wait()
+
+        @pl.loop(0, 144 // 16)
+        def _(step):
+            rows = pl.ds(pl.multiple_of(step * 16, 16), 16)
+            if which:
+                dn_ref[rows] = to_half(dn_f[rows])
+            else:
+                blk_ref[rows] = to_half(blk_f[rows])
+
     for k in range(chunks):
         @pl.when(has_up)
         def _():
@@ -234,6 +254,18 @@
         to_sibling(me, k, True).start()
 
     send_all(ends_copy, Z * X, me)
+
+    at_one, at_two = NCLS + PATCH_IN, NCLS + PATCH_IN + FREQ
+    for copy_in in loads[2:]:
+        copy_in.wait()
+    for ref in (table_ref, one_ref, two_ref):
+        ref[...] = jnp.zeros_like(ref)
+    table_ref[:, :NCLS] = to_half(stem_f[:, :NCLS])
+    one_ref[:144] = to_half(stem_f[:, at_one:at_two])
+    for index in range(Z * X):
+        two_ref[index, :, :144] = to_half(stem_f[:, at_two + 144 * index : at_two + 144 * (index + 1)])
+    mod_ref[...] = to_half(mod_f[...])
+    fm_ref[...] = to_half(tail_f[:, : 2 * D])
 
     def make_hidden():
         own_meta.wait()
@@ -353,15 +385,23 @@
                             copy(owner, k, mine, x_sem, across).wait_send()
 
 
-def gather_weights(blk, dn, meta, ends, w_one, w_two, table, w_mod, w_fm, b_one, b_two):
-    n, width = lax.axis_size("dp"), blk.shape[0]
+def gather_weights(block, downs, stems, mod, tail, meta, ends, b_one, b_two):
+    n, width = lax.axis_size("dp"), block.shape[0]
     section = lax.axis_index("section")
     if not ring_fits(n, width):
         both = lambda own, sib: jnp.where(
             lax.rem(section, 2) == 0, jnp.stack([own, sib]), jnp.stack([sib, own])
         )
-        blk = lax.all_gather(blk, "dp", axis=0, tiled=True)
-        dn = lax.all_gather(dn, "dp", axis=0, tiled=True)
+        core = lax.rem(section, 2)
+        dn = lax.dynamic_slice(downs, (section // 2, 0, core * HALF), (1, width, HALF))[0]
+        blk = lax.all_gather(to_half(block), "dp", axis=0, tiled=True)
+        dn = lax.all_gather(to_half(dn), "dp", axis=0, tiled=True)
+        at_one, at_two = NCLS + PATCH_IN, NCLS + PATCH_IN + FREQ
+        stem, w_mod, w_fm = to_half(stems), to_half(mod), to_half(tail[:, : 2 * D])
+        table = jnp.pad(stem[:, :NCLS], ((0, 0), (0, -NCLS % 128)))
+        w_one = jnp.pad(stem[:, at_one:at_two], ((0, WIDE - width), (0, 0)))
+        w_two = stem[:, at_two:].reshape(width, n, width).transpose(1, 0, 2)
+        w_two = jnp.pad(w_two, ((0, 0), (0, 0), (0, WIDE - width)))
         meta, ends = exchange(2, "dp", ("all", "all"), meta, ends)
         meta = meta.reshape(2 * n, META)
         pre = matmul_nt(to_half(meta[:, :FREQ]), w_one) + b_one
@@ -377,7 +417,8 @@
         parts = jnp.pad(jnp.concatenate(parts, axis=1), ((0, 0), (0, 8 * PIECE - 5 * D)))
         (parts,) = exchange(3, "stage", ("each",), parts.reshape(2 * n, 8, PIECE))
         mods = jnp.sum(parts.reshape(n, 2, 8, PIECE), axis=0)
-        return (both(blk, swap(blk, 1)), both(dn, swap(dn, 1)), meta, ends, pre, hidden, cond, mods)
+        own = (both(blk, swap(blk, 1)), both(dn, swap(dn, 1)), meta, ends, pre, hidden, cond, mods)
+        return own + (w_mod, w_fm, w_two)
     units, images = n * len(GATHER_CHUNKS), 2 * n
     hbm, vmem = pl.BlockSpec(memory_space=pl.ANY), pl.BlockSpec(memory_space=pltpu.VMEM)
     dma = lambda count: pltpu.SemaphoreType.DMA((count,))
@@ -389,10 +430,16 @@
             jax.ShapeDtypeStruct((images, META), f32), jax.ShapeDtypeStruct((n,) + ends.shape, BF),
             jax.ShapeDtypeStruct((images, WIDE), f32), jax.ShapeDtypeStruct((n, images, WIDE), BF),
             jax.ShapeDtypeStruct((images, width), f32), jax.ShapeDtypeStruct((2, 8, PIECE), f32),
+            jax.ShapeDtypeStruct((width, 3 * D), BF), jax.ShapeDtypeStruct((width, 2 * D), BF),
+            jax.ShapeDtypeStruct((n, width, WIDE), BF),
         ),
-        in_specs=[hbm] * 2 + [vmem] * 9,
-        out_specs=(hbm, hbm) + (vmem,) * 6,
+        in_specs=[hbm] * 5 + [vmem] * 4,
+        out_specs=(hbm, hbm) + (vmem,) * 9,
         scratch_shapes=[
+            pltpu.VMEM((width, FF), f32), pltpu.VMEM((width, HALF), f32), pltpu.VMEM(stems.shape, f32),
+            pltpu.VMEM((width, 3 * D), f32), pltpu.VMEM(tail.shape, f32),
+            pltpu.VMEM((width, FF), BF), pltpu.VMEM((width, HALF), BF), pltpu.VMEM((WIDE, FREQ), BF),
+            pltpu.VMEM((width, 1024), BF), dma(5),
             pltpu.VMEM((n, 2, META), f32), pltpu.VMEM((images, WIDE), BF),
             pltpu.VMEM((images, 8 * PIECE), f32),
             pltpu.VMEM((images, 8, PIECE), f32), pltpu.VMEM((images, 8, PIECE), f32),
@@ -405,7 +452,7 @@
         ),
         cost_estimate=pl.CostEstimate(flops=0, bytes_accessed=400_000_000, transcendentals=0),
         name="gather_weights",
-    )(blk, dn, meta, ends, w_one, w_two, table, w_mod, w_fm, b_one, b_two)
+    )(block, downs, stems, mod, tail, meta, ends, b_one, b_two)
 
 
 VMEM_BYTES = 60 * 1024 * 1024
@@ -1406,6 +1453,61 @@
     return (weight_new, moment_new, average_new, weight_new.astype(jnp.bfloat16))
 
 
+def down_update_kernel(factor, weight, moment, average, grad, *outs):
+    values = nesterov(
+        weight[...], moment[...], average[...], grad[...].astype(jnp.float32), factor[0]
+    )
+    for out, value in zip(outs, values):
+        out[...] = value
+
+
+def updated(like):
+    f32 = jax.ShapeDtypeStruct(like.shape, jnp.float32)
+    return (f32, f32, f32, jax.ShapeDtypeStruct(like.shape, BF))
+
+
+def down_update(factor, weight, moment, average, grads):
+    width = weight.shape[1]
+    rows = width
+    state = pl.BlockSpec((1, rows, HALF), lambda l, h, r: (l, r, h))
+    return pl.pallas_call(
+        down_update_kernel,
+        grid=(LAYERS, 2, width // rows),
+        out_shape=updated(weight),
+        in_specs=[pl.BlockSpec(memory_space=pltpu.SMEM), state, state, state]
+        + [pl.BlockSpec((1, rows, HALF), lambda l, h, r: (2 * l + h, r, 0))],
+        out_specs=(state,) * 4,
+        compiler_params=pltpu.CompilerParams(vmem_limit_bytes=VMEM_BYTES),
+        cost_estimate=pl.CostEstimate(flops=10 * weight.size, bytes_accessed=28 * weight.size, transcendentals=0),
+        name="down_update",
+    )(factor, weight, moment, average, grads)
+
+
+def stem_update_kernel(factor, weight, moment, average, g_table, g_patch, g_one, g_two, *outs):
+    width, first = weight.shape[0], 0
+    for grad, length in ((g_table, NCLS), (g_patch, PATCH_IN), (g_one, FREQ), (g_two, D)):
+        part = slice(first, first + length)
+        values = nesterov(
+            weight[:, part], moment[:, part], average[:, part], grad[:width, :length], factor[0]
+        )
+        for out, value in zip(outs, values):
+            out[:, part] = value
+        first += length
+
+
+def stem_update(factor, weight, moment, average, *grads):
+    vmem = pl.BlockSpec(memory_space=pltpu.VMEM)
+    return pl.pallas_call(
+        stem_update_kernel,
+        out_shape=updated(weight),
+        in_specs=[pl.BlockSpec(memory_space=pltpu.SMEM)] + [vmem] * 7,
+        out_specs=(vmem,) * 4,
+        compiler_params=pltpu.CompilerParams(vmem_limit_bytes=VMEM_BYTES),
+        cost_estimate=pl.CostEstimate(flops=10 * weight.size, bytes_accessed=30 * weight.size, transcendentals=0),
+        name="stem_update",
+    )(factor, weight, moment, average, *grads)
+
+
 def swap(array, by):
     peers = lax.axis_size("section")
     return lax.ppermute(array, "section", [(k, k ^ by) for k in range(peers)])
@@ -1430,24 +1532,16 @@
 
     flags = jnp.stack([core, stage]).astype(jnp.int32)
     downs, stems = jnp.swapaxes(down_w, 1, 2), stem_w.T
-    stem_half, tail_half, mod_half_w = to_half(stems), to_half(tail_w), to_half(mod_w[0])
-    dn_half = to_half(lax.dynamic_slice(downs, (stage, 0, core * HALF), (1, width, HALF))[0])
-    at_one, at_two = NCLS + PATCH_IN, NCLS + PATCH_IN + FREQ
-    w_two = stem_half[:, at_two:]
-    table = jnp.pad(stem_half[:, :NCLS], ((0, 0), (0, -NCLS % 128)))
-    w_fm = tail_half[:, : 2 * D]
     to_wide = lambda value: jnp.pad(value, ((0, 0),) * (value.ndim - 1) + ((0, WIDE - width),))
-    ends = to_wide(jnp.concatenate([stem_half[:, NCLS:at_one], tail_half[:, 2 * D :]], axis=1).T)
-    w_one = jnp.pad(stem_half[:, at_one:at_two], ((0, WIDE - width), (0, 0)))
-    two_blocks = to_wide(w_two.reshape(width, n, width)).transpose(1, 0, 2)
+    ends = jnp.concatenate([stems[:, NCLS : NCLS + PATCH_IN], tail_w[:, 2 * D :]], axis=1)
+    ends = to_wide(to_half(ends).T)
     classes = jnp.where(null_mask > 0, NCLS - 1, labels)
     freq = to_half(time_features(timesteps.astype(jnp.float32))).astype(jnp.float32)
     facts = jnp.stack([classes, valid], axis=1).astype(jnp.float32)
     meta = jnp.concatenate([freq, facts, jnp.zeros((2, META - FREQ - 2), jnp.float32)], axis=1)
     b_one, b_two = (lax.dynamic_slice_in_dim(biases, k * D + place * width, width)[None] for k in (31, 32))
-    w_blk, w_dn, meta, ends, pre_own, hidden_all, cond, mods = gather_weights(
-        to_half(block_w[0]), dn_half, meta, ends, w_one, two_blocks, table, mod_half_w, w_fm,
-        to_wide(b_one), b_two,
+    w_blk, w_dn, meta, ends, pre_own, hidden_all, cond, mods, mod_half_w, w_fm, two_blocks = gather_weights(
+        block_w[0], downs, stems, mod_w[0], tail_w, meta, ends, to_wide(b_one), b_two
     )
     ends = ends[:, :, :width].transpose(1, 0, 2).reshape(ROWS_END, D)
     w_patch_all, w_head_all = ends[:PATCH_IN], ends[PATCH_IN:]
@@ -1515,12 +1609,7 @@
     g_blk = jnp.concatenate(
         [jnp.where(even, halves[1], crossed), jnp.where(even, crossed, halves[0])], axis=1
     )
-    dn_all = dn_all.astype(jnp.float32)
-    down_both = jnp.stack([jnp.concatenate([dn_all[2 * k], dn_all[2 * k + 1]], axis=1) for k in range(2)])
     ends = [ends_all[k, :, :width].T for k in (0, 3)]
-    g_stem = jnp.concatenate(
-        [g_table[:, :NCLS], ends[0][:, :PATCH_IN], g_one[:width], g_two], axis=1
-    )
     g_tail = jnp.concatenate([g_fm, ends[1]], axis=1)
 
     news = news.reshape(n, 4, -1, 128)
@@ -1543,8 +1632,12 @@
     mod_out = nesterov(mod_w, mod_m, mod_e, g_mod[None], factor)
     block_out = nesterov(block_w, block_m, block_e, g_blk[None], factor)
     flip = lambda value: jnp.swapaxes(value, 1, 2)
-    down_out = tuple(map(flip, nesterov(downs, flip(down_m), flip(down_e), down_both, factor)))
-    stem_out = tuple(value.T for value in nesterov(stems, stem_m.T, stem_e.T, g_stem, factor))
+    scalar = factor.reshape(1)
+    down_out = tuple(map(flip, down_update(scalar, downs, flip(down_m), flip(down_e), dn_all)))
+    stem_out = stem_update(
+        scalar, stems, stem_m.T, stem_e.T, g_table, ends[0][:, :PATCH_IN], g_one, g_two
+    )
+    stem_out = tuple(value.T for value in stem_out)
     tail_out = nesterov(tail_w, tail_m, tail_e, g_tail, factor)
     bias_out = nesterov(biases, bias_m, bias_e, bias_grad, factor)
     return (

time: 644 us -> 649 us (level)
  other arithmetic: 53.5 us -> 30.3 us
  Pallas kernels: 509 us -> 527 us
  local copies, waits for them, and re-layouts: 42.8 us -> 49.7 us
    transpose x5 -> x1, other arithmetic: 19.7 us -> 0.01 us  [body(): ends = to_wide(to_half(ends).T)]
    pallas_call x0 -> x2, Pallas kernels: none -> 18.7 us  [the longest x1 12.9 us: down_update(): pl.pallas_call(down_update_kernel, grid=(LAYERS, 2, width // rows), out_s...]
    unnamed x114 -> x76, local copies, waits for them, and re-layouts: 8.62 us -> 21.9 us
  transfers between devices with their start and end apart: 9 -> 9, of which waited for: 2 -> 2; matrix products, arithmetic and copies ran while one was open for 2% -> 1% of each run, Pallas kernels for 6% -> 6%
where the time goes in v9:
time: 649 us; the launch traced here: 644 us
  Pallas kernels  527 us (81%)
  local copies, waits for them, and re-layouts  49.7 us (8%)
  other arithmetic  30.3 us (5%)
  waiting for transfers between devices  21.9 us (3%)
    pallas_call x1, Pallas kernels, sum_gradients(): pl.pallas_call(sum_kernel, out_shape=shapes, in_specs=[hbm] * 3 + [vmem]...  200 us
    pallas_call x1, Pallas kernels, gather_weights(): pl.pallas_call(gather_kernel, out_shape=(jax.ShapeDtypeStruct((2, D, FF),...  183 us
    pallas_call x2, Pallas kernels, stage_backward(): pl.pallas_call(backward_kernel, out_shape=(like(D, BF), mods, mods, like(...  62.4 us
    pallas_call x2, Pallas kernels, stage_forward(): pl.pallas_call(partial(forward_kernel, save), out_shape=tuple(shapes), in...  40 us
    unnamed x76, local copies, waits for them, and re-layouts  21.9 us
    ppermute x9, waiting for transfers between devices, swap(): return lax.ppermute(array, 'section', [(k, k ^ by) for k in range(peers)])  21.9 us
    pallas_call x1, Pallas kernels, products(): pl.pallas_call(products_kernel, grid=(HALF // COLUMNS,), out_shape=(jax.S...  19.1 us
  transfers between devices with their start and end apart: 9, of which 2 were waited for; matrix products, arithmetic and copies ran while one was open for 1% of the time, Pallas kernels for 6%

profile of v9, /device:TPU:0, one launch (start us, length us, event | category | flops | bytes accessed | tf_op | source)
XLA Modules:
  0.0 644.3 jit_solution(14795027620314189248)
XLA Ops:
  8.3 182.9 %gather_weights.1 = (bf16[2,1152,4608]{2,1,0:T(8,128)(2,1)}, bf16[2,1152,2304]{2,1,0:T(8,128)(2,1)}, f32[16,384]{1,0:T(8,128)}, bf16[8,48,256]{2,1,0:T(8,128)(2,...) custom-call(f32[144,4608]{1,0:T(8,128)} %bitcast.124, ...), custom_call_target="tpu_custom_call" | custom-call | bytes 400000000 | tf_op jit(solution)/shard_map/gather_weights/pallas_call | solution.py:426
  200.5 18.7 %stage_forward.2 = bf16[256,1152]{1,0:T(8,128)(2,1)} custom-call(s32[2]{0:T(128)} %pad_add_fusion.flags.flags_ref, f32[256,1152]{1,0:T(8,128)} %fusion.x_ref, f32[3,1152]{1,0:T(4,128)} %reshape.200.mod_a, f32[3,1152]{1,0:T(4,128)} %reshape.201.mod_m, f32[1,4608]{1,0:T(1,128)} %broadcast_in_dim.32.b_attn, f32[1,4608]{1,0:T(1,128)} %copy-done.26, ...), custom_call_target="tpu_custom_call" | custom-call | flops 16911433728 | bytes 31850496 | tf_op jit(solution)/shard_map/stage_forward/pallas_call | solution.py:1287
  219.2 1.6 collective-permute-start
  224.1 1.4 slice_reduce_fusion.5
  226.2 8.9 %collective-permute-done = bf16[256,1152]{1,0:T(8,128)(2,1)S(1)} collective-permute-done((bf16[256,1152]{1,0:T(8,128)(2,1)}, bf16[256,1152]{1,0:T(8,128)(2,1)S(1)}, u32[]{:S(2)}, u32[]{:S(2)}) %collective-permute-start) | collective-permute-done | bytes 589856 | tf_op jit(solution)/shard_map/ppermute | solution.py:1513
  236.2 21.3 %stage_forward.3 = (f32[256,1152]{1,0:T(8,128)}, bf16[256,1152]{1,0:T(8,128)(2,1)}, bf16[256,3456]{1,0:T(8,128)(2,1)}, bf16[256,1152]{1,0:T(8,128)(2,1)}, bf16[2...) custom-call(s32[2]{0:T(128)} %pad_add_fusion.flags.flags_ref, ...), custom_call_target="tpu_custom_call" | custom-call | flops 16911433728 | bytes 31850496 | tf_op jit(solution)/shard_map/stage_forward/pallas_call | solution.py:1287
  257.5 1.5 reduce_sum.81
  261.4 1.4 subtract_multiply_fusion.d_ref
  262.8 31.3 %stage_backward.2 = (bf16[256,1152]{1,0:T(8,128)(2,1)}, f32[3,1152]{1,0:T(4,128)}, f32[3,1152]{1,0:T(4,128)}, bf16[256,1152]{1,0:T(8,128)(2,1)}, bf16[256,1152]{...) custom-call(s32[2]{0:T(128)} %pad_add_fusion.flags.flags_ref, ...), custom_call_target="tpu_custom_call" | custom-call | flops 16911433728 | bytes 31850496 | tf_op jit(solution)/shard_map/stage_backward/pallas_call | solution.py:1306
  294.1 1.6 collective-permute-start.1
  296.2 13.0 %collective-permute-done.1 = bf16[256,1152]{1,0:T(8,128)(2,1)S(1)} collective-permute-done((bf16[256,1152]{1,0:T(8,128)(2,1)}, bf16[256,1152]{1,0:T(8,128)(2,1)S(1)}, u32[]{:S(2)}, u32[]{:S(2)}) %collective-permute-start.1) | collective-permute-done | bytes 589856 | tf_op jit(solution)/shard_map/ppermute | solution.py:1513
  310.3 31.1 %stage_backward.3 = (bf16[256,1152]{1,0:T(8,128)(2,1)}, f32[3,1152]{1,0:T(4,128)}, f32[3,1152]{1,0:T(4,128)}, bf16[256,1152]{1,0:T(8,128)(2,1)}, bf16[256,1152]{...) custom-call(s32[2]{0:T(128)} %pad_add_fusion.flags.flags_ref, ...), custom_call_target="tpu_custom_call" | custom-call | flops 16911433728 | bytes 31850496 | tf_op jit(solution)/shard_map/stage_backward/pallas_call | solution.py:1306
  345.6 4.5 collect.1
  350.1 1.6 bitcast_bitcast_fusion.bp_ref
  352.9 19.1 %products.1 = (bf16[1152,2304]{1,0:T(8,128)(2,1)}, bf16[1152,2304]{1,0:T(8,128)(2,1)}, bf16[1152,2304]{1,0:T(8,128)(2,1)}) custom-call(s32[2]{0:T(128)} %pad_add_fusion.flags.flags_ref, bf16[256,1152]{1,0:T(8,128)(2,1)} %get-tuple-element.100.dn_own.refs_2_, bf16[256,1152]{1,0:T(8,128)(2,1)} %copy-done.29, bf16[256,1152]{1,0:T(8,128)(2,1)} %get-tuple-element.101.up_own, ...), custom_call_target="tpu_custom_call" | custom-call | flops 8153726976 | bytes 26542080 | tf_op jit(solution)/shard_map/products/pallas_call | solution.py:1367
  372.0 199.5 %sum_gradients.1 = (f32[2,144,2304]{2,1,0:T(8,128)}, bf16[144,2304]{1,0:T(8,128)(2,1)}, bf16[4,144,2304]{2,1,0:T(8,128)(2,1)}, f32[144,3456]{1,0:T(8,128)}, f32[...) custom-call(bf16[1152,2304]{1,0:T(8,128)(2,1)} %get-tuple-element.11, ...), custom_call_target="tpu_custom_call" | custom-call | bytes 400000000 | tf_op jit(solution)/shard_map/sum_gradients/pallas_call | solution.py:915
  576.3 1.5 slice.159
  577.8 1.6 reduce.4
  579.4 1.5 reshape.210
  581.5 1.5 constant_dynamic-update-slice_fusion
  582.9 1.4 constant_dynamic-update-slice_fusion.6
  584.3 1.4 constant_dynamic-update-slice_fusion.5
  600.5 1.8 fusion.14
  602.3 1.7 multiply_add_fusion.5
  604.0 3.1 fusion.15
  610.3 1.5 copy-done.1
  612.6 2.6 fusion.16
  615.2 1.9 multiply_add_fusion
  619.9 2.2 fusion.17
  622.0 2.0 multiply_add_fusion.2
  624.1 12.9 %down_update.1 = (f32[2,144,4608]{2,1,0:T(8,128)}, f32[2,144,4608]{2,1,0:T(8,128)}, f32[2,144,4608]{2,1,0:T(8,128)}, bf16[2,144,4608]{2,1,0:T(8,128)(2,1)}) custom-call(f32[1]{0:T(128)} %bitcast.35.factor, f32[2,144,4608]{2,1,0:T(8,128)} %bitcast.123, f32[2,144,4608]{2,1,0:T(8,128)} %bitcast.129, f32[2,144,4608]{2,1,0:T(8,128)} %bitcast.130, ...), custom_call_target="tpu_custom_call" | custom-call | flops 13271040 | bytes 37158912 | tf_op jit(solution)/shard_map/down_update/pallas_call | solution.py:1473
  636.9 5.8 stem_update.1
  (189 shorter events, 54.1 us)
Async XLA Ops:
  8.3 183.9 %copy-start.20 = (f32[40352]{0:T(1024)S(1)}, f32[40352]{0:T(1024)}, u32[]{:S(2)}) copy-start(f32[40352]{0:T(1024)} %param.45) | copy-start | bytes 484228
  8.3 185.4 %copy-start.30 = (s32[2]{0:T(128)S(1)}, s32[2]{0:T(128)}, u32[]{:S(2)}) copy-start(s32[2]{0:T(128)} %param.26) | copy-start | bytes 28
  8.3 186.8 %copy-start.24 = (f32[2,32,32,4]{2,3,1,0:T(4,128)S(1)}, f32[2,32,32,4]{2,3,1,0:T(4,128)}, u32[]{:S(2)}) copy-start(f32[2,32,32,4]{2,3,1,0:T(4,128)} %param.24) | copy-start | bytes 98308
  8.3 186.8 %copy-start.25 = (f32[2,32,32,4]{2,3,1,0:T(4,128)S(1)}, f32[2,32,32,4]{2,3,1,0:T(4,128)}, u32[]{:S(2)}) copy-start(f32[2,32,32,4]{2,3,1,0:T(4,128)} %param.25) | copy-start | bytes 98308
  191.2 5.0 copy-start.23
  196.2 25.1 %copy-start.17 = (bf16[48,8,144]{2,0,1:T(8,128)(2,1)}, bf16[48,8,144]{2,0,1:T(8,128)(2,1)S(1)}, u32[]{:S(2)}) copy-start(bf16[48,8,144]{2,0,1:T(8,128)(2,1)S(1)} %slice_bitcast_fusion) | copy-start | bytes 331780
  200.5 20.3 %copy-start.31 = (s32[2]{0:T(128)S(1)}, s32[2]{0:T(128)}, u32[]{:S(2)}) copy-start(s32[2]{0:T(128)} %param.29) | copy-start | bytes 28
  219.2 15.9 %collective-permute-start = (bf16[256,1152]{1,0:T(8,128)(2,1)}, bf16[256,1152]{1,0:T(8,128)(2,1)S(1)}, u32[]{:S(2)}, u32[]{:S(2)}) collective-permute-start(bf16[256,1152]{1,0:T(8,128)(2,1)} %stage_forward.2), channel_id=1, source_target_pairs={{0,2},{1,3},{2,0},{3,1},{4,6},{5,7},{6,4},{7,5},{8,10},{9,11},{10,... | collective-permute-start | bytes 1769480 | tf_op jit(solution)/shard_map/ppermute | solution.py:1513
  221.7 13.4 %copy-start.7 = (f32[256,1152]{1,0:T(8,128)S(1)}, f32[256,1152]{1,0:T(8,128)}, u32[]{:S(2)}) copy-start(f32[256,1152]{1,0:T(8,128)} %fusion.x_ref) | copy-start | bytes 3538948
  262.8 33.4 %copy-start.28 = (bf16[256,1152]{1,0:T(8,128)(2,1)S(1)}, bf16[256,1152]{1,0:T(8,128)(2,1)}, u32[]{:S(2)}) copy-start(bf16[256,1152]{1,0:T(8,128)(2,1)} %get-tuple-element.102.xa_own) | copy-start | bytes 1769476
  262.8 46.4 %copy-start.8 = (f32[256,1152]{1,0:T(8,128)S(1)}, f32[256,1152]{1,0:T(8,128)}, u32[]{:S(2)}) copy-start(f32[256,1152]{1,0:T(8,128)} %subtract_multiply_fusion.d_ref) | copy-start | bytes 3538948
  294.1 15.1 %collective-permute-start.1 = (bf16[256,1152]{1,0:T(8,128)(2,1)}, bf16[256,1152]{1,0:T(8,128)(2,1)S(1)}, u32[]{:S(2)}, u32[]{:S(2)}) collective-permute-start(bf16[256,1152]{1,0:T(8,128)(2,1)} %get-tuple-element.99), channel_id=1, source_target_pairs={{0,2},{1,3},{2,0},{3,1},{4,6},{5,7},{6,4},{7,5},{8,10},{9,11},{10,... | collective-permute-start | bytes 1769480 | tf_op jit(solution)/shard_map/ppermute | solution.py:1513
  295.7 56.1 %collective-permute-start.6 = (bf16[256,2304]{1,0:T(8,128)(2,1)}, bf16[256,2304]{1,0:T(8,128)(2,1)}, u32[]{:S(2)}, u32[]{:S(2)}) collective-permute-start(bf16[256,2304]{1,0:T(8,128)(2,1)} %get-tuple-element.106), channel_id=1, source_target_pairs={{0,1},{1,0},{2,3},{3,2},{4,5},{5,4},{6,7},{7,6},{8,9},{9,8},{10,11... | collective-permute-start | bytes 3538952 | tf_op jit(solution)/shard_map/ppermute | solution.py:1513
  295.7 47.8 %collective-permute-start.3 = (bf16[256,1152]{1,0:T(8,128)(2,1)}, bf16[256,1152]{1,0:T(8,128)(2,1)}, u32[]{:S(2)}, u32[]{:S(2)}) collective-permute-start(bf16[256,1152]{1,0:T(8,128)(2,1)} %get-tuple-element.101.up_own), channel_id=1, source_target_pairs={{0,1},{1,0},{2,3},{3,2},{4,5},{5,4},{6,7},{7,6},{8,9},{9,8},{10,11... | collective-permute-start | bytes 1769480 | tf_op jit(solution)/shard_map/ppermute | solution.py:1513
  296.2 47.5 %collective-permute-start.4 = (bf16[256,1152]{1,0:T(8,128)(2,1)S(1)}, bf16[256,1152]{1,0:T(8,128)(2,1)}, u32[]{:S(2)}, u32[]{:S(2)}) collective-permute-start(bf16[256,1152]{1,0:T(8,128)(2,1)S(1)} %copy-done.28), channel_id=1, source_target_pairs={{0,1},{1,0},{2,3},{3,2},{4,5},{5,4},{6,7},{7,6},{8,9},{9,8},{10,11... | collective-permute-start | bytes 1769480 | tf_op jit(solution)/shard_map/ppermute | solution.py:1513
  341.4 10.3 %collective-permute-start.7 = (bf16[256,2304]{1,0:T(8,128)(2,1)}, bf16[256,2304]{1,0:T(8,128)(2,1)S(1)}, u32[]{:S(2)}, u32[]{:S(2)}) collective-permute-start(bf16[256,2304]{1,0:T(8,128)(2,1)} %get-tuple-element.108.refs_5_), channel_id=1, source_target_pairs={{0,1},{1,0},{2,3},{3,2},{4,5},{5,4},{6,7},{7,6},{8,9},{9,8},{10,11... | collective-permute-start | bytes 3538952 | tf_op jit(solution)/shard_map/ppermute | solution.py:1513
  341.5 10.3 %collective-permute-start.8 = (bf16[256,2304]{1,0:T(8,128)(2,1)}, bf16[256,2304]{1,0:T(8,128)(2,1)}, u32[]{:S(2)}, u32[]{:S(2)}) collective-permute-start(bf16[256,2304]{1,0:T(8,128)(2,1)} %get-tuple-element.110), channel_id=1, source_target_pairs={{0,1},{1,0},{2,3},{3,2},{4,5},{5,4},{6,7},{7,6},{8,9},{9,8},{10,11... | collective-permute-start | bytes 3538952 | tf_op jit(solution)/shard_map/ppermute | solution.py:1513
  343.5 8.2 %collective-permute-start.5 = (bf16[256,1152]{1,0:T(8,128)(2,1)}, bf16[256,1152]{1,0:T(8,128)(2,1)}, u32[]{:S(2)}, u32[]{:S(2)}) collective-permute-start(bf16[256,1152]{1,0:T(8,128)(2,1)} %get-tuple-element.104), channel_id=1, source_target_pairs={{0,1},{1,0},{2,3},{3,2},{4,5},{5,4},{6,7},{7,6},{8,9},{9,8},{10,11... | collective-permute-start | bytes 1769480 | tf_op jit(solution)/shard_map/ppermute | solution.py:1513
  343.7 8.1 %collective-permute-start.2 = (bf16[256,1152]{1,0:T(8,128)(2,1)}, bf16[256,1152]{1,0:T(8,128)(2,1)S(1)}, u32[]{:S(2)}, u32[]{:S(2)}) collective-permute-start(bf16[256,1152]{1,0:T(8,128)(2,1)} %get-tuple-element.100.dn_own.refs_2_), channel_id=1, source_target_pairs={{0,1},{1,0},{2,3},{3,2},{4,5},{5,4},{6,7},{7,6},{8,9},{9,8},{10,11... | collective-permute-start | bytes 1769480 | tf_op jit(solution)/shard_map/ppermute | solution.py:1513
  571.6 3.2 copy-start.22
  575.0 28.9 %copy-start.15 = (f32[144,2336]{1,0:T(8,128)S(1)}, f32[144,2336]{1,0:T(8,128)}, u32[]{:S(2)}) copy-start(f32[144,2336]{1,0:T(8,128)} %param.43) | copy-start | bytes 4036612
  575.7 28.3 %copy-start.5 = (f32[144,2336]{1,0:T(8,128)S(1)}, f32[144,2336]{1,0:T(8,128)}, u32[]{:S(2)}) copy-start(f32[144,2336]{1,0:T(8,128)} %tail_hbm.1) | copy-start | bytes 4036612
  602.3 4.8 copy-start.19
  604.0 3.2 copy-start.16
  607.1 2.8 copy-start.10
  607.1 2.9 copy-start.18
  610.0 2.5 copy-start.9
  612.6 2.6 copy-start.11
  615.2 2.7 copy-start.2
  615.2 3.0 copy-start.3
  615.2 4.1 copy-start.12
  615.2 4.7 copy-start.14
  (10 other events, 14.8 us)

commit v10 on v9

--- a/solution.py
+++ b/solution.py
@@ -467,10 +467,10 @@
 def sum_kernel(
     g_dn, g_up, g_attn, dm_ref, bp_ref, en_ref, mod_ref, fm_ref, two_ref, cond_ref, pre_ref, hid_ref, meta_ref,
     out, cross_out, dn_out, gmod_out, gfm_out, gtab_out, gone_out, gtwo_out,
-    ends_all, news_out, cs_all, fmsum_out, sq_out,
+    ends_all, bias_out, sq_out,
     own_b, other_d, xb, xq, up_b, up_o, down_b, down_o, acc, acc_dn,
     dm_in, bp_in, en_in, dmat, ends_src, c_src, c_in, fmd_src, fmd_in, cs_src, dcond, ph, ph_in, news_src,
-    sq_src, sq_all, sq_rows, cross_src,
+    sq_src, sq_all, sq_rows, cross_src, news_out, cs_all, fmsum_out,
     load_sem, x_send, x_recv, up_send, up_recv, down_send, down_recv,
     sib_send, sib_recv, y_send, y_recv, group_send, group_recv, sect_send, sect_recv,
     ph_send, ph_recv, news_send, news_recv, sq_send, sq_recv, cross_sem, local_sem,
@@ -632,6 +632,32 @@
         add_square(once * ends_all[0])
         add_square(once * ends_all[3])
 
+    def make_biases():
+        wait_batch(news, 8)
+        bias_out[...] = jnp.zeros_like(bias_out)
+        for slot in range(4):
+            for k in range(3):
+                row = 3 * slot + k
+                bias_out[row : row + 1] = cs_all[slot, :, D * k : D * (k + 1)]
+        for side in range(2):
+            for block in range(D // 128):
+                part = slice(128 * block, 128 * (block + 1))
+                device = (block // 2) * 4 + 2 * side + block % 2
+                bias_out[12 + 8 * side : 20 + 8 * side, part] = news_out[device, 0:8]
+                bias_out[28 + side : 29 + side, part] = news_out[device, 8:9]
+                row = 35 if side else 30
+                bias_out[row : row + 1, part] = news_out[device, 9:10]
+                if side:
+                    bias_out[36:37, part] = news_out[device, 10:11]
+        for index in range(Z * X):
+            first = 144 * index
+            for k in range(2):
+                at = SUM_ROWS + 2 * k
+                bias_out[31 + k : 32 + k, first : first + 128] = news_out[4 * index, at : at + 1]
+                bias_out[31 + k : 32 + k, first + 128 : first + 144] = news_out[4 * index, at + 1 : at + 2, :16]
+        for k in range(2):
+            bias_out[33 + k : 34 + k] = fmsum_out[:, D * k : D * (k + 1)]
+
     def dn_copy(k, slot, to_sib):
         rows = pl.ds(SUM_CHUNKS[k][1], SUM_CHUNKS[k][2])
         unit = slot * chunks + k
@@ -852,6 +878,7 @@
     finish_all(1)
     pass_all(2, 2)
     pass_all(2, 1)
+    make_biases()
     direct_all(2)
     finish_all(2)
 
@@ -869,7 +896,6 @@
     crossing.start()
     wait_batch(norms, 9)
     sq_out[...] = jnp.sum(sq_all[...], axis=0)
-    wait_batch(news, 8)
     crossing.wait()
 
     for k in range(chunks):
@@ -909,8 +935,7 @@
     shapes = (
         like((2, 144, HALF), f32), like((144, HALF), BF), like((4, 144, HALF), BF),
         like((144, 3 * D), f32), like((144, 2 * D), f32), like((144, 1024), f32), like((WIDE, FREQ), f32),
-        like((144, D), f32), like((4,) + end_block, f32), like((devices, 24, 128), f32),
-        like((4, 1, 3 * D), f32), like((1, 2 * D), f32), like((8, 128), f32),
+        like((144, D), f32), like((4,) + end_block, f32), like((40, D), f32), like((8, 128), f32),
     )
     return pl.pallas_call(
         sum_kernel,
@@ -927,7 +952,8 @@
             pltpu.VMEM((images, WIDE), BF), pltpu.VMEM((n, images, WIDE), f32), pltpu.VMEM((n, images, WIDE), f32),
             pltpu.VMEM((24, 128), f32), pltpu.VMEM((8, 128), f32), pltpu.VMEM((devices, 8, 128), f32),
             pltpu.VMEM((1, HALF), f32),
-            pltpu.VMEM((144, HALF), BF),
+            pltpu.VMEM((144, HALF), BF), pltpu.VMEM((devices, 24, 128), f32), pltpu.VMEM((4, 1, 3 * D), f32),
+            pltpu.VMEM((1, 2 * D), f32),
             dma(2 * chunks * Z), dma(chunks * Z), dma(chunks * Z),
             dma(2 * chunks * Z), dma(2 * chunks * Z), dma(2 * chunks * Z), dma(2 * chunks * Z),
             dma(4 * chunks), dma(4 * chunks), dma(4 * chunks), dma(4 * chunks),
@@ -985,7 +1011,21 @@
         squares = squares + once * square(value)
     news, squares = exchange(7, "every", ("all", "all"), news, jnp.broadcast_to(squares, (8, 128)))
     squares = jnp.sum(squares, axis=0)
-    return (out, cross, dn_all, g_mod, g_fm, g_table, g_one, g_two, ends_all, news, cs_all, fm_sum, squares)
+    news = news.reshape(n, 4, -1, 128)
+    stages = []
+    for k in range(2):
+        pieces = news[:, 2 * k : 2 * k + 2, :SUM_ROWS].reshape(2 * n, SUM_ROWS, 128)[: D // 128]
+        stages.append(pieces.transpose(1, 0, 2).reshape(-1))
+    slices = news[:, 0, SUM_ROWS : SUM_ROWS + 4].reshape(n, 2, WIDE)[:, :, :width]
+    bias_rows = jnp.concatenate(
+        [cs_all.reshape(-1)]
+        + [part[: 8 * D] for part in stages]
+        + [part[8 * D : 9 * D] for part in stages]
+        + [stages[0][9 * D : 10 * D]]
+        + [slices[:, 0].reshape(-1), slices[:, 1].reshape(-1)]
+        + [fm_sum[0], stages[1][9 * D : 11 * D], jnp.zeros((3 * D,), f32)]
+    ).reshape(40, D)
+    return (out, cross, dn_all, g_mod, g_fm, g_table, g_one, g_two, ends_all, bias_rows, squares)
 
 
 def exchange_kernel(axes, modes, *refs):
@@ -1599,7 +1639,7 @@
         extra, tok_wide, g_head,
     )
     own_sums = own_sums.reshape(SUM_ROWS, -1, 128).transpose(1, 0, 2)[: 2 * n]
-    halves, crossed, dn_all, g_mod, g_fm, g_table, g_one, g_two, ends_all, news, mod_sums, fm_sum, squares = (
+    halves, crossed, dn_all, g_mod, g_fm, g_table, g_one, g_two, ends_all, biases_new, squares = (
         sum_gradients(
             g_dn, g_up, g_attn, d_mods, own_sums, own_ends, mod_half_w, w_fm, two_blocks, cond, pre_own,
             hidden_all, meta,
@@ -1612,21 +1652,7 @@
     ends = [ends_all[k, :, :width].T for k in (0, 3)]
     g_tail = jnp.concatenate([g_fm, ends[1]], axis=1)
 
-    news = news.reshape(n, 4, -1, 128)
-    stages = []
-    for k in range(2):
-        pieces = news[:, 2 * k : 2 * k + 2, :SUM_ROWS].reshape(2 * n, SUM_ROWS, 128)[: D // 128]
-        stages.append(pieces.transpose(1, 0, 2).reshape(-1))
-    slices = news[:, 0, SUM_ROWS : SUM_ROWS + 4].reshape(n, 2, WIDE)[:, :, :width]
-    bias_grad = jnp.concatenate(
-        [mod_sums.reshape(-1)]
-        + [part[: 8 * D] for part in stages]
-        + [part[8 * D : 9 * D] for part in stages]
-        + [stages[0][9 * D : 10 * D]]
-        + [slices[:, 0].reshape(-1), slices[:, 1].reshape(-1)]
-        + [fm_sum[0], stages[1][9 * D : 9 * D + HEAD_OUT]]
-    )
-    loss_sum = stages[1][10 * D]
+    bias_grad, loss_sum = biases_new.reshape(-1)[:NBIAS], biases_new[36, 0]
     grad_norm = jnp.sqrt(squares[0, 0])
     factor = jnp.minimum(1.0, clip_limit / (grad_norm + 1e-06))
     mod_out = nesterov(mod_w, mod_m, mod_e, g_mod[None], factor)

time: 649 us -> 626 us (0.965)
  local copies, waits for them, and re-layouts: 49.7 us -> 30.6 us
    unnamed x76 -> x65, local copies, waits for them, and re-layouts: 21.9 us -> 9.07 us
where the time goes in v10:
time: 626 us; the launch traced here: 622 us
  Pallas kernels  527 us (84%)
  local copies, waits for them, and re-layouts  30.6 us (5%)
  other arithmetic  27.5 us (4%)
  waiting for transfers between devices  21.9 us (3%)
  between operations  6.32 us (1%)
    pallas_call x1, Pallas kernels, sum_gradients(): pl.pallas_call(sum_kernel, out_shape=shapes, in_specs=[hbm] * 3 + [vmem]...  199 us
    pallas_call x1, Pallas kernels, gather_weights(): pl.pallas_call(gather_kernel, out_shape=(jax.ShapeDtypeStruct((2, D, FF),...  183 us
    pallas_call x2, Pallas kernels, stage_backward(): pl.pallas_call(backward_kernel, out_shape=(like(D, BF), mods, mods, like(...  62.4 us
    pallas_call x2, Pallas kernels, stage_forward(): pl.pallas_call(partial(forward_kernel, save), out_shape=tuple(shapes), in...  40 us
    ppermute x9, waiting for transfers between devices, swap(): return lax.ppermute(array, 'section', [(k, k ^ by) for k in range(peers)])  21.9 us
    pallas_call x1, Pallas kernels, products(): pl.pallas_call(products_kernel, grid=(HALF // COLUMNS,), out_shape=(jax.S...  19.1 us
    pallas_call x1, Pallas kernels, down_update(): pl.pallas_call(down_update_kernel, grid=(LAYERS, 2, width // rows), out_s...  12.9 us
  transfers between devices with their start and end apart: 9, of which 2 were waited for; matrix products, arithmetic and copies ran while one was open for 1% of the time, Pallas kernels for 6%

profile of v10, /device:TPU:0, one launch (start us, length us, event | category | flops | bytes accessed | tf_op | source)
XLA Modules:
  0.0 621.9 jit_solution(15295131567636352362)
XLA Ops:
  4.9 1.3 fusion.17
  8.3 182.8 %gather_weights.1 = (bf16[2,1152,4608]{2,1,0:T(8,128)(2,1)}, bf16[2,1152,2304]{2,1,0:T(8,128)(2,1)}, f32[16,384]{1,0:T(8,128)}, bf16[8,48,256]{2,1,0:T(8,128)(2,...) custom-call(f32[144,4608]{1,0:T(8,128)} %bitcast.105, ...), custom_call_target="tpu_custom_call" | custom-call | bytes 400000000 | tf_op jit(solution)/shard_map/gather_weights/pallas_call | solution.py:426
  199.0 1.4 fusion.x_ref
  200.4 18.7 %stage_forward.2 = bf16[256,1152]{1,0:T(8,128)(2,1)} custom-call(s32[2]{0:T(128)} %pad_add_fusion.flags.flags_ref, f32[256,1152]{1,0:T(8,128)} %fusion.x_ref, f32[3,1152]{1,0:T(4,128)} %reshape.182.mod_a, f32[3,1152]{1,0:T(4,128)} %reshape.183.mod_m, f32[1,4608]{1,0:T(1,128)} %broadcast_in_dim.32.b_attn, f32[1,4608]{1,0:T(1,128)} %copy-done.25, ...), custom_call_target="tpu_custom_call" | custom-call | flops 16911433728 | bytes 31850496 | tf_op jit(solution)/shard_map/stage_forward/pallas_call | solution.py:1327
  219.1 1.6 collective-permute-start
  224.0 1.4 slice_reduce_fusion.3
  226.1 8.9 %collective-permute-done = bf16[256,1152]{1,0:T(8,128)(2,1)S(1)} collective-permute-done((bf16[256,1152]{1,0:T(8,128)(2,1)}, bf16[256,1152]{1,0:T(8,128)(2,1)S(1)}, u32[]{:S(2)}, u32[]{:S(2)}) %collective-permute-start) | collective-permute-done | bytes 589856 | tf_op jit(solution)/shard_map/ppermute | solution.py:1553
  236.1 21.3 %stage_forward.3 = (f32[256,1152]{1,0:T(8,128)}, bf16[256,1152]{1,0:T(8,128)(2,1)}, bf16[256,3456]{1,0:T(8,128)(2,1)}, bf16[256,1152]{1,0:T(8,128)(2,1)}, bf16[2...) custom-call(s32[2]{0:T(128)} %pad_add_fusion.flags.flags_ref, ...), custom_call_target="tpu_custom_call" | custom-call | flops 16911433728 | bytes 31850496 | tf_op jit(solution)/shard_map/stage_forward/pallas_call | solution.py:1327
  257.4 1.5 reduce_sum.81
  261.3 1.4 subtract_multiply_fusion.d_ref
  262.7 31.3 %stage_backward.2 = (bf16[256,1152]{1,0:T(8,128)(2,1)}, f32[3,1152]{1,0:T(4,128)}, f32[3,1152]{1,0:T(4,128)}, bf16[256,1152]{1,0:T(8,128)(2,1)}, bf16[256,1152]{...) custom-call(s32[2]{0:T(128)} %pad_add_fusion.flags.flags_ref, ...), custom_call_target="tpu_custom_call" | custom-call | flops 16911433728 | bytes 31850496 | tf_op jit(solution)/shard_map/stage_backward/pallas_call | solution.py:1346
  294.0 1.6 collective-permute-start.1
  296.1 13.0 %collective-permute-done.1 = bf16[256,1152]{1,0:T(8,128)(2,1)S(1)} collective-permute-done((bf16[256,1152]{1,0:T(8,128)(2,1)}, bf16[256,1152]{1,0:T(8,128)(2,1)S(1)}, u32[]{:S(2)}, u32[]{:S(2)}) %collective-permute-start.1) | collective-permute-done | bytes 589856 | tf_op jit(solution)/shard_map/ppermute | solution.py:1553
  310.2 31.1 %stage_backward.3 = (bf16[256,1152]{1,0:T(8,128)(2,1)}, f32[3,1152]{1,0:T(4,128)}, f32[3,1152]{1,0:T(4,128)}, bf16[256,1152]{1,0:T(8,128)(2,1)}, bf16[256,1152]{...) custom-call(s32[2]{0:T(128)} %pad_add_fusion.flags.flags_ref, ...), custom_call_target="tpu_custom_call" | custom-call | flops 16911433728 | bytes 31850496 | tf_op jit(solution)/shard_map/stage_backward/pallas_call | solution.py:1346
  345.4 4.5 collect.1
  350.0 1.6 bitcast_bitcast_fusion.bp_ref
  352.8 19.1 %products.1 = (bf16[1152,2304]{1,0:T(8,128)(2,1)}, bf16[1152,2304]{1,0:T(8,128)(2,1)}, bf16[1152,2304]{1,0:T(8,128)(2,1)}) custom-call(s32[2]{0:T(128)} %pad_add_fusion.flags.flags_ref, bf16[256,1152]{1,0:T(8,128)(2,1)} %get-tuple-element.98.dn_own.refs_2_, bf16[256,1152]{1,0:T(8,128)(2,1)} %copy-done.28, bf16[256,1152]{1,0:T(8,128)(2,1)} %get-tuple-element.99.up_own, ...), custom_call_target="tpu_custom_call" | custom-call | flops 8153726976 | bytes 26542080 | tf_op jit(solution)/shard_map/products/pallas_call | solution.py:1407
  371.9 199.3 %sum_gradients.1 = (f32[2,144,2304]{2,1,0:T(8,128)}, bf16[144,2304]{1,0:T(8,128)(2,1)}, bf16[4,144,2304]{2,1,0:T(8,128)(2,1)}, f32[144,3456]{1,0:T(8,128)}, f32[...) custom-call(bf16[1152,2304]{1,0:T(8,128)(2,1)} %get-tuple-element.10, ...), custom_call_target="tpu_custom_call" | custom-call | bytes 400000000 | tf_op jit(solution)/shard_map/sum_gradients/pallas_call | solution.py:940
  574.1 1.2 slice.93
  575.3 1.2 slice.94
  578.6 1.7 fusion.11
  580.3 1.7 multiply_add_fusion.5
  582.0 2.7 fusion.12
  584.7 1.3 multiply_add_fusion.3
  586.3 1.2 copy-done.10
  587.9 1.5 copy-done.1
  590.2 2.6 fusion.13
  592.8 1.9 multiply_add_fusion
  597.5 2.2 fusion.14
  599.6 2.0 multiply_add_fusion.2
  601.7 12.9 %down_update.1 = (f32[2,144,4608]{2,1,0:T(8,128)}, f32[2,144,4608]{2,1,0:T(8,128)}, f32[2,144,4608]{2,1,0:T(8,128)}, bf16[2,144,4608]{2,1,0:T(8,128)(2,1)}) custom-call(f32[1]{0:T(128)} %bitcast.32.factor, f32[2,144,4608]{2,1,0:T(8,128)} %bitcast.104, f32[2,144,4608]{2,1,0:T(8,128)} %bitcast.110, f32[2,144,4608]{2,1,0:T(8,128)} %bitcast.111, ...), custom_call_target="tpu_custom_call" | custom-call | flops 13271040 | bytes 37158912 | tf_op jit(solution)/shard_map/down_update/pallas_call | solution.py:1513
  614.5 5.8 stem_update.1
  (159 shorter events, 33.8 us)
Async XLA Ops:
  8.3 183.9 %copy-start.21 = (f32[40352]{0:T(1024)S(1)}, f32[40352]{0:T(1024)}, u32[]{:S(2)}) copy-start(f32[40352]{0:T(1024)} %param.45) | copy-start | bytes 484228
  8.3 185.3 %copy-start.29 = (s32[2]{0:T(128)S(1)}, s32[2]{0:T(128)}, u32[]{:S(2)}) copy-start(s32[2]{0:T(128)} %param.26) | copy-start | bytes 28
  8.3 186.7 %copy-start.23 = (f32[2,32,32,4]{2,3,1,0:T(4,128)S(1)}, f32[2,32,32,4]{2,3,1,0:T(4,128)}, u32[]{:S(2)}) copy-start(f32[2,32,32,4]{2,3,1,0:T(4,128)} %param.24) | copy-start | bytes 98308
  8.3 186.7 %copy-start.24 = (f32[2,32,32,4]{2,3,1,0:T(4,128)S(1)}, f32[2,32,32,4]{2,3,1,0:T(4,128)}, u32[]{:S(2)}) copy-start(f32[2,32,32,4]{2,3,1,0:T(4,128)} %param.25) | copy-start | bytes 98308
  191.2 5.0 copy-start.22
  196.2 25.1 %copy-start.18 = (bf16[48,8,144]{2,0,1:T(8,128)(2,1)}, bf16[48,8,144]{2,0,1:T(8,128)(2,1)S(1)}, u32[]{:S(2)}) copy-start(bf16[48,8,144]{2,0,1:T(8,128)(2,1)S(1)} %slice_bitcast_fusion) | copy-start | bytes 331780
  200.4 20.3 %copy-start.30 = (s32[2]{0:T(128)S(1)}, s32[2]{0:T(128)}, u32[]{:S(2)}) copy-start(s32[2]{0:T(128)} %param.29) | copy-start | bytes 28
  219.1 15.9 %collective-permute-start = (bf16[256,1152]{1,0:T(8,128)(2,1)}, bf16[256,1152]{1,0:T(8,128)(2,1)S(1)}, u32[]{:S(2)}, u32[]{:S(2)}) collective-permute-start(bf16[256,1152]{1,0:T(8,128)(2,1)} %stage_forward.2), channel_id=1, source_target_pairs={{0,2},{1,3},{2,0},{3,1},{4,6},{5,7},{6,4},{7,5},{8,10},{9,11},{10,... | collective-permute-start | bytes 1769480 | tf_op jit(solution)/shard_map/ppermute | solution.py:1553
  221.6 13.4 %copy-start.7 = (f32[256,1152]{1,0:T(8,128)S(1)}, f32[256,1152]{1,0:T(8,128)}, u32[]{:S(2)}) copy-start(f32[256,1152]{1,0:T(8,128)} %fusion.x_ref) | copy-start | bytes 3538948
  262.7 33.4 %copy-start.27 = (bf16[256,1152]{1,0:T(8,128)(2,1)S(1)}, bf16[256,1152]{1,0:T(8,128)(2,1)}, u32[]{:S(2)}) copy-start(bf16[256,1152]{1,0:T(8,128)(2,1)} %get-tuple-element.100.xa_own) | copy-start | bytes 1769476
  262.7 46.4 %copy-start.8 = (f32[256,1152]{1,0:T(8,128)S(1)}, f32[256,1152]{1,0:T(8,128)}, u32[]{:S(2)}) copy-start(f32[256,1152]{1,0:T(8,128)} %subtract_multiply_fusion.d_ref) | copy-start | bytes 3538948
  294.0 15.1 %collective-permute-start.1 = (bf16[256,1152]{1,0:T(8,128)(2,1)}, bf16[256,1152]{1,0:T(8,128)(2,1)S(1)}, u32[]{:S(2)}, u32[]{:S(2)}) collective-permute-start(bf16[256,1152]{1,0:T(8,128)(2,1)} %get-tuple-element.97), channel_id=1, source_target_pairs={{0,2},{1,3},{2,0},{3,1},{4,6},{5,7},{6,4},{7,5},{8,10},{9,11},{10,... | collective-permute-start | bytes 1769480 | tf_op jit(solution)/shard_map/ppermute | solution.py:1553
  295.6 56.0 %collective-permute-start.6 = (bf16[256,2304]{1,0:T(8,128)(2,1)}, bf16[256,2304]{1,0:T(8,128)(2,1)}, u32[]{:S(2)}, u32[]{:S(2)}) collective-permute-start(bf16[256,2304]{1,0:T(8,128)(2,1)} %get-tuple-element.104), channel_id=1, source_target_pairs={{0,1},{1,0},{2,3},{3,2},{4,5},{5,4},{6,7},{7,6},{8,9},{9,8},{10,11... | collective-permute-start | bytes 3538952 | tf_op jit(solution)/shard_map/ppermute | solution.py:1553
  295.6 47.8 %collective-permute-start.3 = (bf16[256,1152]{1,0:T(8,128)(2,1)}, bf16[256,1152]{1,0:T(8,128)(2,1)}, u32[]{:S(2)}, u32[]{:S(2)}) collective-permute-start(bf16[256,1152]{1,0:T(8,128)(2,1)} %get-tuple-element.99.up_own), channel_id=1, source_target_pairs={{0,1},{1,0},{2,3},{3,2},{4,5},{5,4},{6,7},{7,6},{8,9},{9,8},{10,11... | collective-permute-start | bytes 1769480 | tf_op jit(solution)/shard_map/ppermute | solution.py:1553
  296.1 47.4 %collective-permute-start.4 = (bf16[256,1152]{1,0:T(8,128)(2,1)S(1)}, bf16[256,1152]{1,0:T(8,128)(2,1)}, u32[]{:S(2)}, u32[]{:S(2)}) collective-permute-start(bf16[256,1152]{1,0:T(8,128)(2,1)S(1)} %copy-done.27), channel_id=1, source_target_pairs={{0,1},{1,0},{2,3},{3,2},{4,5},{5,4},{6,7},{7,6},{8,9},{9,8},{10,11... | collective-permute-start | bytes 1769480 | tf_op jit(solution)/shard_map/ppermute | solution.py:1553
  341.3 10.3 %collective-permute-start.7 = (bf16[256,2304]{1,0:T(8,128)(2,1)}, bf16[256,2304]{1,0:T(8,128)(2,1)S(1)}, u32[]{:S(2)}, u32[]{:S(2)}) collective-permute-start(bf16[256,2304]{1,0:T(8,128)(2,1)} %get-tuple-element.106.refs_5_), channel_id=1, source_target_pairs={{0,1},{1,0},{2,3},{3,2},{4,5},{5,4},{6,7},{7,6},{8,9},{9,8},{10,11... | collective-permute-start | bytes 3538952 | tf_op jit(solution)/shard_map/ppermute | solution.py:1553
  341.4 10.2 %collective-permute-start.8 = (bf16[256,2304]{1,0:T(8,128)(2,1)}, bf16[256,2304]{1,0:T(8,128)(2,1)}, u32[]{:S(2)}, u32[]{:S(2)}) collective-permute-start(bf16[256,2304]{1,0:T(8,128)(2,1)} %get-tuple-element.108), channel_id=1, source_target_pairs={{0,1},{1,0},{2,3},{3,2},{4,5},{5,4},{6,7},{7,6},{8,9},{9,8},{10,11... | collective-permute-start | bytes 3538952 | tf_op jit(solution)/shard_map/ppermute | solution.py:1553
  343.4 8.2 %collective-permute-start.5 = (bf16[256,1152]{1,0:T(8,128)(2,1)}, bf16[256,1152]{1,0:T(8,128)(2,1)}, u32[]{:S(2)}, u32[]{:S(2)}) collective-permute-start(bf16[256,1152]{1,0:T(8,128)(2,1)} %get-tuple-element.102), channel_id=1, source_target_pairs={{0,1},{1,0},{2,3},{3,2},{4,5},{5,4},{6,7},{7,6},{8,9},{9,8},{10,11... | collective-permute-start | bytes 1769480 | tf_op jit(solution)/shard_map/ppermute | solution.py:1553
  343.5 8.1 %collective-permute-start.2 = (bf16[256,1152]{1,0:T(8,128)(2,1)}, bf16[256,1152]{1,0:T(8,128)(2,1)S(1)}, u32[]{:S(2)}, u32[]{:S(2)}) collective-permute-start(bf16[256,1152]{1,0:T(8,128)(2,1)} %get-tuple-element.98.dn_own.refs_2_), channel_id=1, source_target_pairs={{0,1},{1,0},{2,3},{3,2},{4,5},{5,4},{6,7},{7,6},{8,9},{9,8},{10,11... | collective-permute-start | bytes 1769480 | tf_op jit(solution)/shard_map/ppermute | solution.py:1553
  371.9 210.1 %copy-start.15 = (f32[144,2336]{1,0:T(8,128)S(1)}, f32[144,2336]{1,0:T(8,128)}, u32[]{:S(2)}) copy-start(f32[144,2336]{1,0:T(8,128)} %param.43) | copy-start | bytes 4036612
  571.2 10.8 %copy-start.5 = (f32[144,2336]{1,0:T(8,128)S(1)}, f32[144,2336]{1,0:T(8,128)}, u32[]{:S(2)}) copy-start(f32[144,2336]{1,0:T(8,128)} %tail_hbm.1) | copy-start | bytes 4036612
  577.9 4.0 copy-start.17
  580.3 4.4 copy-start.20
  582.0 2.8 copy-start.16
  584.7 2.8 copy-start.10
  584.7 2.9 copy-start.19
  587.6 2.5 copy-start.9
  590.2 2.6 copy-start.11
  592.8 2.7 copy-start.2
  592.8 3.0 copy-start.3
  592.8 4.1 copy-start.12
  592.8 4.7 copy-start.14
  (9 other events, 14.2 us)

commit v11 on v10

--- a/solution.py
+++ b/solution.py
@@ -1336,20 +1336,22 @@
     )(flags, x_in, mod_a, mod_m, b_attn, b_up, b_down, w_blk, w_dn)
 
 
-def stage_backward(d_out, x_in, weights, kept):
+def stage_backward(full, d_out, x_in, weights, kept):
     flags, mod_a, mod_m, w_blk, w_dn, b_attn, b_up, b_down = weights
     xm_a, qkv, att, last, branch_a, x_mid, xm_m, branch_m, pre, act_own, act_sib = kept
     vmem, hbm = pl.BlockSpec(memory_space=pltpu.VMEM), pl.BlockSpec(memory_space=pl.ANY)
     smem = pl.BlockSpec(memory_space=pltpu.SMEM)
     like = lambda columns, kind: jax.ShapeDtypeStruct((PATCHES, columns), kind)
     mods = jax.ShapeDtypeStruct((3, D), jnp.float32)
+    rest = (mods, mods, like(D, BF), like(D, BF), like(HALF, BF), like(HALF, BF), like(3 * D, BF))
+    rest += (like(HALF, BF), like(HALF, BF))
     return pl.pallas_call(
         backward_kernel,
-        out_shape=(like(D, BF), mods, mods, like(D, BF), like(D, BF))
-        + (like(HALF, BF), like(HALF, BF), like(3 * D, BF), like(HALF, BF), like(HALF, BF)),
+        out_shape=(like(D, BF),) + (rest if full else ()),
         in_specs=[smem] + [vmem] * 8 + [hbm] * 3,
-        out_specs=(vmem,) * 10,
-        scratch_shapes=weight_scratch()
+        out_specs=(vmem,) * (1 + len(rest) if full else 1),
+        scratch_shapes=([] if full else [pltpu.VMEM(each.shape, each.dtype) for each in rest])
+        + weight_scratch()
         + [
             pltpu.VMEM((PATCHES, FF), jnp.float32),
             pltpu.VMEM((PATCHES, D), jnp.float32),
@@ -1363,7 +1365,7 @@
     )(flags, d_out, x_in, x_mid, mod_a, mod_m, branch_a, branch_m, qkv, pre, w_blk, w_dn)
 
 
-COLUMNS = 384
+COLUMNS = 1152
 
 
 def products_kernel(
@@ -1617,10 +1619,10 @@
         x_out, fmod, w_head_all, biases[35 * D :], target, counts, loss_scale
     )
     xm_a, qkv, attended, last_sib, branch_a, x_mid, xm_b, branch_b, pre, act_own, act_sib = kept
-    d_hop = swap(stage_backward(d_final, x_in, weights, kept)[0], 2)
+    d_hop = swap(stage_backward(False, d_final, x_in, weights, kept)[0], 2)
     d_out = jnp.where(stage == 1, d_final, d_hop.astype(jnp.float32))
     d_first, d_mod_a, d_mod_b, d_branch_a, d_branch_b, d_pre_own, d_pre_sib, d_qkv, right_own, right_sib = (
-        stage_backward(d_out, x_in, weights, kept)
+        stage_backward(True, d_out, x_in, weights, kept)
     )
 
     act_come, xb_come, xa_come, last_come = swap((act_sib, xm_b, xm_a, last_sib), 1)

time: 626 us -> 626 us (level)
  transfers between devices with their start and end apart: 9 -> 9, of which waited for: 2 -> 2; matrix products, arithmetic and copies ran while one was open for 1% -> 2% of each run, Pallas kernels for 6% -> 6%
where the time goes in v11:
time: 626 us; the launch traced here: 622 us
  Pallas kernels  526 us (84%)
  local copies, waits for them, and re-layouts  30.6 us (5%)
  other arithmetic  28.1 us (4%)
  waiting for transfers between devices  21.9 us (3%)
    pallas_call x1, Pallas kernels, sum_gradients(): pl.pallas_call(sum_kernel, out_shape=shapes, in_specs=[hbm] * 3 + [vmem]...  199 us
    pallas_call x1, Pallas kernels, gather_weights(): pl.pallas_call(gather_kernel, out_shape=(jax.ShapeDtypeStruct((2, D, FF),...  183 us
    pallas_call x2, Pallas kernels, stage_backward(): pl.pallas_call(backward_kernel, out_shape=(like(D, BF),) + (rest if full...  62.5 us
    pallas_call x2, Pallas kernels, stage_forward(): pl.pallas_call(partial(forward_kernel, save), out_shape=tuple(shapes), in...  39.8 us
    ppermute x9, waiting for transfers between devices, swap(): return lax.ppermute(array, 'section', [(k, k ^ by) for k in range(peers)])  21.9 us
    pallas_call x1, Pallas kernels, products(): pl.pallas_call(products_kernel, grid=(HALF // COLUMNS,), out_shape=(jax.S...  18.6 us
    pallas_call x1, Pallas kernels, down_update(): pl.pallas_call(down_update_kernel, grid=(LAYERS, 2, width // rows), out_s...  12.9 us
  transfers between devices with their start and end apart: 9, of which 2 were waited for; matrix products, arithmetic and copies ran while one was open for 2% of the time, Pallas kernels for 6%

profile of v11, /device:TPU:0, one launch (start us, length us, event | category | flops | bytes accessed | tf_op | source)
XLA Modules:
  0.0 621.8 jit_solution(1872341269811798449)
XLA Ops:
  4.9 1.3 fusion.17
  8.3 182.8 %gather_weights.1 = (bf16[2,1152,4608]{2,1,0:T(8,128)(2,1)}, bf16[2,1152,2304]{2,1,0:T(8,128)(2,1)}, f32[16,384]{1,0:T(8,128)}, bf16[8,48,256]{2,1,0:T(8,128)(2,...) custom-call(f32[144,4608]{1,0:T(8,128)} %bitcast.105, ...), custom_call_target="tpu_custom_call" | custom-call | bytes 400000000 | tf_op jit(solution)/shard_map/gather_weights/pallas_call | solution.py:426
  199.0 1.4 fusion.x_ref
  200.4 18.5 %stage_forward.2 = bf16[256,1152]{1,0:T(8,128)(2,1)} custom-call(s32[2]{0:T(128)} %pad_add_fusion.flags.flags_ref, f32[256,1152]{1,0:T(8,128)} %fusion.x_ref, f32[3,1152]{1,0:T(4,128)} %reshape.182.mod_a, f32[3,1152]{1,0:T(4,128)} %reshape.183.mod_m, f32[1,4608]{1,0:T(1,128)} %broadcast_in_dim.32.b_attn, f32[1,4608]{1,0:T(1,128)} %copy-done.25, ...), custom_call_target="tpu_custom_call" | custom-call | flops 16911433728 | bytes 31850496 | tf_op jit(solution)/shard_map/stage_forward/pallas_call | solution.py:1327
  218.9 1.6 collective-permute-start
  223.8 1.4 slice_reduce_fusion.3
  225.8 8.9 %collective-permute-done = bf16[256,1152]{1,0:T(8,128)(2,1)S(1)} collective-permute-done((bf16[256,1152]{1,0:T(8,128)(2,1)}, bf16[256,1152]{1,0:T(8,128)(2,1)S(1)}, u32[]{:S(2)}, u32[]{:S(2)}) %collective-permute-start) | collective-permute-done | bytes 589856 | tf_op jit(solution)/shard_map/ppermute | solution.py:1555
  235.9 21.4 %stage_forward.3 = (f32[256,1152]{1,0:T(8,128)}, bf16[256,1152]{1,0:T(8,128)(2,1)}, bf16[256,3456]{1,0:T(8,128)(2,1)}, bf16[256,1152]{1,0:T(8,128)(2,1)}, bf16[2...) custom-call(s32[2]{0:T(128)} %pad_add_fusion.flags.flags_ref, ...), custom_call_target="tpu_custom_call" | custom-call | flops 16911433728 | bytes 31850496 | tf_op jit(solution)/shard_map/stage_forward/pallas_call | solution.py:1327
  257.2 1.5 reduce_sum.81
  261.0 1.4 subtract_multiply_fusion.d_ref
  262.4 31.2 %stage_backward.2 = bf16[256,1152]{1,0:T(8,128)(2,1)} custom-call(s32[2]{0:T(128)} %pad_add_fusion.flags.flags_ref, f32[256,1152]{1,0:T(8,128)} %subtract_multiply_fusion.d_ref, f32[256,1152]{1,0:T(8,128)} %convert_select_fusion.3.x_ref, f32[256,1152]{1,0:T(8,128)} %get-tuple-element.91.mid_ref, f32[3,1152]{1,0:T(4,128)} %reshape.182.mod_a, ...), custom_call_target="tpu_custom_call" | custom-call | flops 16911433728 | bytes 31850496 | tf_op jit(solution)/shard_map/stage_backward/pallas_call | solution.py:1348
  293.6 1.6 collective-permute-start.1
  295.7 13.0 %collective-permute-done.1 = bf16[256,1152]{1,0:T(8,128)(2,1)S(1)} collective-permute-done((bf16[256,1152]{1,0:T(8,128)(2,1)}, bf16[256,1152]{1,0:T(8,128)(2,1)S(1)}, u32[]{:S(2)}, u32[]{:S(2)}) %collective-permute-start.1) | collective-permute-done | bytes 589856 | tf_op jit(solution)/shard_map/ppermute | solution.py:1555
  309.8 31.4 %stage_backward.3 = (bf16[256,1152]{1,0:T(8,128)(2,1)}, f32[3,1152]{1,0:T(4,128)}, f32[3,1152]{1,0:T(4,128)}, bf16[256,1152]{1,0:T(8,128)(2,1)}, bf16[256,1152]{...) custom-call(s32[2]{0:T(128)} %pad_add_fusion.flags.flags_ref, ...), custom_call_target="tpu_custom_call" | custom-call | flops 16911433728 | bytes 31850496 | tf_op jit(solution)/shard_map/stage_backward/pallas_call | solution.py:1348
  345.8 4.5 collect.1
  350.4 1.6 bitcast_bitcast_fusion.bp_ref
  353.2 18.6 %products.1 = (bf16[1152,2304]{1,0:T(8,128)(2,1)}, bf16[1152,2304]{1,0:T(8,128)(2,1)}, bf16[1152,2304]{1,0:T(8,128)(2,1)}) custom-call(s32[2]{0:T(128)} %pad_add_fusion.flags.flags_ref, bf16[256,1152]{1,0:T(8,128)(2,1)} %get-tuple-element.96.dn_own.refs_2_, bf16[256,1152]{1,0:T(8,128)(2,1)} %copy-done.28, bf16[256,1152]{1,0:T(8,128)(2,1)} %get-tuple-element.97.up_own, ...), custom_call_target="tpu_custom_call" | custom-call | flops 8153726976 | bytes 26542080 | tf_op jit(solution)/shard_map/products/pallas_call | solution.py:1409
  371.8 199.4 %sum_gradients.1 = (f32[2,144,2304]{2,1,0:T(8,128)}, bf16[144,2304]{1,0:T(8,128)(2,1)}, bf16[4,144,2304]{2,1,0:T(8,128)(2,1)}, f32[144,3456]{1,0:T(8,128)}, f32[...) custom-call(bf16[1152,2304]{1,0:T(8,128)(2,1)} %get-tuple-element.10, ...), custom_call_target="tpu_custom_call" | custom-call | bytes 400000000 | tf_op jit(solution)/shard_map/sum_gradients/pallas_call | solution.py:940
  574.2 1.2 slice.93
  575.4 1.2 slice.94
  578.6 1.7 fusion.11
  580.4 1.7 multiply_add_fusion.5
  582.1 2.7 fusion.12
  584.8 1.3 multiply_add_fusion.3
  586.3 1.2 copy-done.10
  587.9 1.5 copy-done.1
  590.3 2.6 fusion.13
  592.9 1.9 multiply_add_fusion
  597.5 2.2 fusion.14
  599.7 2.0 multiply_add_fusion.2
  601.8 12.9 %down_update.1 = (f32[2,144,4608]{2,1,0:T(8,128)}, f32[2,144,4608]{2,1,0:T(8,128)}, f32[2,144,4608]{2,1,0:T(8,128)}, bf16[2,144,4608]{2,1,0:T(8,128)(2,1)}) custom-call(f32[1]{0:T(128)} %bitcast.32.factor, f32[2,144,4608]{2,1,0:T(8,128)} %bitcast.104, f32[2,144,4608]{2,1,0:T(8,128)} %bitcast.110, f32[2,144,4608]{2,1,0:T(8,128)} %bitcast.111, ...), custom_call_target="tpu_custom_call" | custom-call | flops 13271040 | bytes 37158912 | tf_op jit(solution)/shard_map/down_update/pallas_call | solution.py:1515
  614.6 5.8 stem_update.1
  (160 shorter events, 34.3 us)
Async XLA Ops:
  8.3 183.9 %copy-start.21 = (f32[40352]{0:T(1024)S(1)}, f32[40352]{0:T(1024)}, u32[]{:S(2)}) copy-start(f32[40352]{0:T(1024)} %param.45) | copy-start | bytes 484228
  8.3 185.3 %copy-start.29 = (s32[2]{0:T(128)S(1)}, s32[2]{0:T(128)}, u32[]{:S(2)}) copy-start(s32[2]{0:T(128)} %param.26) | copy-start | bytes 28
  8.3 186.7 %copy-start.23 = (f32[2,32,32,4]{2,3,1,0:T(4,128)S(1)}, f32[2,32,32,4]{2,3,1,0:T(4,128)}, u32[]{:S(2)}) copy-start(f32[2,32,32,4]{2,3,1,0:T(4,128)} %param.24) | copy-start | bytes 98308
  8.3 186.7 %copy-start.24 = (f32[2,32,32,4]{2,3,1,0:T(4,128)S(1)}, f32[2,32,32,4]{2,3,1,0:T(4,128)}, u32[]{:S(2)}) copy-start(f32[2,32,32,4]{2,3,1,0:T(4,128)} %param.25) | copy-start | bytes 98308
  191.2 5.0 copy-start.22
  196.2 24.9 %copy-start.18 = (bf16[48,8,144]{2,0,1:T(8,128)(2,1)}, bf16[48,8,144]{2,0,1:T(8,128)(2,1)S(1)}, u32[]{:S(2)}) copy-start(bf16[48,8,144]{2,0,1:T(8,128)(2,1)S(1)} %slice_bitcast_fusion) | copy-start | bytes 331780
  200.4 20.1 %copy-start.30 = (s32[2]{0:T(128)S(1)}, s32[2]{0:T(128)}, u32[]{:S(2)}) copy-start(s32[2]{0:T(128)} %param.29) | copy-start | bytes 28
  218.9 15.9 %collective-permute-start = (bf16[256,1152]{1,0:T(8,128)(2,1)}, bf16[256,1152]{1,0:T(8,128)(2,1)S(1)}, u32[]{:S(2)}, u32[]{:S(2)}) collective-permute-start(bf16[256,1152]{1,0:T(8,128)(2,1)} %stage_forward.2), channel_id=1, source_target_pairs={{0,2},{1,3},{2,0},{3,1},{4,6},{5,7},{6,4},{7,5},{8,10},{9,11},{10,... | collective-permute-start | bytes 1769480 | tf_op jit(solution)/shard_map/ppermute | solution.py:1555
  221.3 13.4 %copy-start.7 = (f32[256,1152]{1,0:T(8,128)S(1)}, f32[256,1152]{1,0:T(8,128)}, u32[]{:S(2)}) copy-start(f32[256,1152]{1,0:T(8,128)} %fusion.x_ref) | copy-start | bytes 3538948
  262.4 33.3 %copy-start.27 = (bf16[256,1152]{1,0:T(8,128)(2,1)S(1)}, bf16[256,1152]{1,0:T(8,128)(2,1)}, u32[]{:S(2)}) copy-start(bf16[256,1152]{1,0:T(8,128)(2,1)} %get-tuple-element.98.xa_own) | copy-start | bytes 1769476
  262.4 46.3 %copy-start.8 = (f32[256,1152]{1,0:T(8,128)S(1)}, f32[256,1152]{1,0:T(8,128)}, u32[]{:S(2)}) copy-start(f32[256,1152]{1,0:T(8,128)} %subtract_multiply_fusion.d_ref) | copy-start | bytes 3538948
  293.6 15.1 %collective-permute-start.1 = (bf16[256,1152]{1,0:T(8,128)(2,1)}, bf16[256,1152]{1,0:T(8,128)(2,1)S(1)}, u32[]{:S(2)}, u32[]{:S(2)}) collective-permute-start(bf16[256,1152]{1,0:T(8,128)(2,1)} %stage_backward.2), channel_id=1, source_target_pairs={{0,2},{1,3},{2,0},{3,1},{4,6},{5,7},{6,4},{7,5},{8,10},{9,11},{10,... | collective-permute-start | bytes 1769480 | tf_op jit(solution)/shard_map/ppermute | solution.py:1555
  295.2 56.8 %collective-permute-start.6 = (bf16[256,2304]{1,0:T(8,128)(2,1)}, bf16[256,2304]{1,0:T(8,128)(2,1)}, u32[]{:S(2)}, u32[]{:S(2)}) collective-permute-start(bf16[256,2304]{1,0:T(8,128)(2,1)} %get-tuple-element.102), channel_id=1, source_target_pairs={{0,1},{1,0},{2,3},{3,2},{4,5},{5,4},{6,7},{7,6},{8,9},{9,8},{10,11... | collective-permute-start | bytes 3538952 | tf_op jit(solution)/shard_map/ppermute | solution.py:1555
  295.2 48.6 %collective-permute-start.3 = (bf16[256,1152]{1,0:T(8,128)(2,1)}, bf16[256,1152]{1,0:T(8,128)(2,1)}, u32[]{:S(2)}, u32[]{:S(2)}) collective-permute-start(bf16[256,1152]{1,0:T(8,128)(2,1)} %get-tuple-element.97.up_own), channel_id=1, source_target_pairs={{0,1},{1,0},{2,3},{3,2},{4,5},{5,4},{6,7},{7,6},{8,9},{9,8},{10,11... | collective-permute-start | bytes 1769480 | tf_op jit(solution)/shard_map/ppermute | solution.py:1555
  295.7 48.2 %collective-permute-start.4 = (bf16[256,1152]{1,0:T(8,128)(2,1)S(1)}, bf16[256,1152]{1,0:T(8,128)(2,1)}, u32[]{:S(2)}, u32[]{:S(2)}) collective-permute-start(bf16[256,1152]{1,0:T(8,128)(2,1)S(1)} %copy-done.27), channel_id=1, source_target_pairs={{0,1},{1,0},{2,3},{3,2},{4,5},{5,4},{6,7},{7,6},{8,9},{9,8},{10,11... | collective-permute-start | bytes 1769480 | tf_op jit(solution)/shard_map/ppermute | solution.py:1555
  341.1 10.8 %collective-permute-start.7 = (bf16[256,2304]{1,0:T(8,128)(2,1)}, bf16[256,2304]{1,0:T(8,128)(2,1)S(1)}, u32[]{:S(2)}, u32[]{:S(2)}) collective-permute-start(bf16[256,2304]{1,0:T(8,128)(2,1)} %get-tuple-element.104.refs_5_), channel_id=1, source_target_pairs={{0,1},{1,0},{2,3},{3,2},{4,5},{5,4},{6,7},{7,6},{8,9},{9,8},{10,11... | collective-permute-start | bytes 3538952 | tf_op jit(solution)/shard_map/ppermute | solution.py:1555
  341.2 10.8 %collective-permute-start.8 = (bf16[256,2304]{1,0:T(8,128)(2,1)}, bf16[256,2304]{1,0:T(8,128)(2,1)}, u32[]{:S(2)}, u32[]{:S(2)}) collective-permute-start(bf16[256,2304]{1,0:T(8,128)(2,1)} %get-tuple-element.106), channel_id=1, source_target_pairs={{0,1},{1,0},{2,3},{3,2},{4,5},{5,4},{6,7},{7,6},{8,9},{9,8},{10,11... | collective-permute-start | bytes 3538952 | tf_op jit(solution)/shard_map/ppermute | solution.py:1555
  343.8 8.1 %collective-permute-start.5 = (bf16[256,1152]{1,0:T(8,128)(2,1)}, bf16[256,1152]{1,0:T(8,128)(2,1)}, u32[]{:S(2)}, u32[]{:S(2)}) collective-permute-start(bf16[256,1152]{1,0:T(8,128)(2,1)} %get-tuple-element.100), channel_id=1, source_target_pairs={{0,1},{1,0},{2,3},{3,2},{4,5},{5,4},{6,7},{7,6},{8,9},{9,8},{10,11... | collective-permute-start | bytes 1769480 | tf_op jit(solution)/shard_map/ppermute | solution.py:1555
  343.9 8.0 %collective-permute-start.2 = (bf16[256,1152]{1,0:T(8,128)(2,1)}, bf16[256,1152]{1,0:T(8,128)(2,1)S(1)}, u32[]{:S(2)}, u32[]{:S(2)}) collective-permute-start(bf16[256,1152]{1,0:T(8,128)(2,1)} %get-tuple-element.96.dn_own.refs_2_), channel_id=1, source_target_pairs={{0,1},{1,0},{2,3},{3,2},{4,5},{5,4},{6,7},{7,6},{8,9},{9,8},{10,11... | collective-permute-start | bytes 1769480 | tf_op jit(solution)/shard_map/ppermute | solution.py:1555
  371.8 210.3 %copy-start.15 = (f32[144,2336]{1,0:T(8,128)S(1)}, f32[144,2336]{1,0:T(8,128)}, u32[]{:S(2)}) copy-start(f32[144,2336]{1,0:T(8,128)} %param.43) | copy-start | bytes 4036612
  571.2 10.8 %copy-start.5 = (f32[144,2336]{1,0:T(8,128)S(1)}, f32[144,2336]{1,0:T(8,128)}, u32[]{:S(2)}) copy-start(f32[144,2336]{1,0:T(8,128)} %tail_hbm.1) | copy-start | bytes 4036612
  578.0 4.0 copy-start.17
  580.4 4.4 copy-start.20
  582.1 2.8 copy-start.16
  584.8 2.8 copy-start.10
  584.8 2.9 copy-start.19
  587.7 2.5 copy-start.9
  590.3 2.6 copy-start.11
  592.9 2.7 copy-start.2
  592.9 3.0 copy-start.3
  592.9 4.1 copy-start.12
  592.9 4.7 copy-start.14
  (9 other events, 14.2 us)

commit v12 on v10

--- a/solution.py
+++ b/solution.py
@@ -1440,7 +1440,8 @@
     order = [jnp.where(core == 0, own[k], own[(k + 2) % 4]) for k in range(4)]
     last = jnp.where(stage == 0, rows[5], extra_ref[0:1])
     for place, row in enumerate(rows[:4] + order + [rows[4], last, extra_ref[1:2]]):
-        sums_ref[place : place + 1, :D] = row
+        for block in range(D // 128):
+            sums_ref[block, place : place + 1] = row[:, 128 * block : 128 * (block + 1)]
     ends = jnp.where(stage == 0, matmul_tn(tok_ref[...], tokens[3][...]), head_ref[...])
     ends_ref[...] = jnp.zeros_like(ends_ref)
     width = D // ends_ref.shape[0]
@@ -1462,7 +1463,7 @@
     return pl.pallas_call(
         collect_kernel,
         out_shape=(
-            jax.ShapeDtypeStruct((SUM_ROWS, 128 * max(2 * n, 9)), jnp.float32),
+            jax.ShapeDtypeStruct((2 * n, SUM_ROWS, 128), jnp.float32),
             jax.ShapeDtypeStruct((2, 48, 128), BF),
             jax.ShapeDtypeStruct((n, HEAD_OUT, WIDE), jnp.float32),
         ),
@@ -1638,7 +1639,6 @@
         flags, (d_qkv, d_branch_a, d_branch_b, d_first), (d_pre_own, d_pre_sib), (d_mod_a, d_mod_b), d_fmod,
         extra, tok_wide, g_head,
     )
-    own_sums = own_sums.reshape(SUM_ROWS, -1, 128).transpose(1, 0, 2)[: 2 * n]
     halves, crossed, dn_all, g_mod, g_fm, g_table, g_one, g_two, ends_all, biases_new, squares = (
         sum_gradients(
             g_dn, g_up, g_attn, d_mods, own_sums, own_ends, mod_half_w, w_fm, two_blocks, cond, pre_own,

time: 626 us -> 624 us (level)
  no operation moved by 1% of the time
where the time goes in v12:
time: 624 us; the launch traced here: 620 us
  Pallas kernels  527 us (84%)
  local copies, waits for them, and re-layouts  29 us (5%)
  other arithmetic  27.5 us (4%)
  waiting for transfers between devices  21.9 us (4%)
  between operations  6.32 us (1%)
    pallas_call x1, Pallas kernels, sum_gradients(): pl.pallas_call(sum_kernel, out_shape=shapes, in_specs=[hbm] * 3 + [vmem]...  199 us
    pallas_call x1, Pallas kernels, gather_weights(): pl.pallas_call(gather_kernel, out_shape=(jax.ShapeDtypeStruct((2, D, FF),...  183 us
    pallas_call x2, Pallas kernels, stage_backward(): pl.pallas_call(backward_kernel, out_shape=(like(D, BF), mods, mods, like(...  62.4 us
    pallas_call x2, Pallas kernels, stage_forward(): pl.pallas_call(partial(forward_kernel, save), out_shape=tuple(shapes), in...  40 us
    ppermute x9, waiting for transfers between devices, swap(): return lax.ppermute(array, 'section', [(k, k ^ by) for k in range(peers)])  21.9 us
    pallas_call x1, Pallas kernels, products(): pl.pallas_call(products_kernel, grid=(HALF // COLUMNS,), out_shape=(jax.S...  19.1 us
    pallas_call x1, Pallas kernels, down_update(): pl.pallas_call(down_update_kernel, grid=(LAYERS, 2, width // rows), out_s...  12.9 us
  transfers between devices with their start and end apart: 9, of which 2 were waited for; matrix products, arithmetic and copies ran while one was open for 1% of the time, Pallas kernels for 6%

profile of v12, /device:TPU:0, one launch (start us, length us, event | category | flops | bytes accessed | tf_op | source)
XLA Modules:
  0.0 620.3 jit_solution(4791230222243923239)
XLA Ops:
  4.9 1.3 fusion.17
  8.3 182.8 %gather_weights.1 = (bf16[2,1152,4608]{2,1,0:T(8,128)(2,1)}, bf16[2,1152,2304]{2,1,0:T(8,128)(2,1)}, f32[16,384]{1,0:T(8,128)}, bf16[8,48,256]{2,1,0:T(8,128)(2,...) custom-call(f32[144,4608]{1,0:T(8,128)} %bitcast.98, ...), custom_call_target="tpu_custom_call" | custom-call | bytes 400000000 | tf_op jit(solution)/shard_map/gather_weights/pallas_call | solution.py:426
  199.0 1.4 fusion.x_ref
  200.4 18.7 %stage_forward.2 = bf16[256,1152]{1,0:T(8,128)(2,1)} custom-call(s32[2]{0:T(128)} %pad_add_fusion.flags.flags_ref, f32[256,1152]{1,0:T(8,128)} %fusion.x_ref, f32[3,1152]{1,0:T(4,128)} %reshape.179.mod_a, f32[3,1152]{1,0:T(4,128)} %reshape.180.mod_m, f32[1,4608]{1,0:T(1,128)} %broadcast_in_dim.32.b_attn, f32[1,4608]{1,0:T(1,128)} %copy-done.25, ...), custom_call_target="tpu_custom_call" | custom-call | flops 16911433728 | bytes 31850496 | tf_op jit(solution)/shard_map/stage_forward/pallas_call | solution.py:1327
  219.1 1.6 collective-permute-start
  224.0 1.4 slice_reduce_fusion.3
  226.1 8.9 %collective-permute-done = bf16[256,1152]{1,0:T(8,128)(2,1)S(1)} collective-permute-done((bf16[256,1152]{1,0:T(8,128)(2,1)}, bf16[256,1152]{1,0:T(8,128)(2,1)S(1)}, u32[]{:S(2)}, u32[]{:S(2)}) %collective-permute-start) | collective-permute-done | bytes 589856 | tf_op jit(solution)/shard_map/ppermute | solution.py:1554
  235.0 1.1 convert_select_fusion.3.x_ref
  236.1 21.3 %stage_forward.3 = (f32[256,1152]{1,0:T(8,128)}, bf16[256,1152]{1,0:T(8,128)(2,1)}, bf16[256,3456]{1,0:T(8,128)(2,1)}, bf16[256,1152]{1,0:T(8,128)(2,1)}, bf16[2...) custom-call(s32[2]{0:T(128)} %pad_add_fusion.flags.flags_ref, ...), custom_call_target="tpu_custom_call" | custom-call | flops 16911433728 | bytes 31850496 | tf_op jit(solution)/shard_map/stage_forward/pallas_call | solution.py:1327
  257.4 1.5 reduce_sum.81
  261.3 1.4 subtract_multiply_fusion.d_ref
  262.7 31.3 %stage_backward.2 = (bf16[256,1152]{1,0:T(8,128)(2,1)}, f32[3,1152]{1,0:T(4,128)}, f32[3,1152]{1,0:T(4,128)}, bf16[256,1152]{1,0:T(8,128)(2,1)}, bf16[256,1152]{...) custom-call(s32[2]{0:T(128)} %pad_add_fusion.flags.flags_ref, ...), custom_call_target="tpu_custom_call" | custom-call | flops 16911433728 | bytes 31850496 | tf_op jit(solution)/shard_map/stage_backward/pallas_call | solution.py:1346
  294.0 1.6 collective-permute-start.1
  296.1 13.0 %collective-permute-done.1 = bf16[256,1152]{1,0:T(8,128)(2,1)S(1)} collective-permute-done((bf16[256,1152]{1,0:T(8,128)(2,1)}, bf16[256,1152]{1,0:T(8,128)(2,1)S(1)}, u32[]{:S(2)}, u32[]{:S(2)}) %collective-permute-start.1) | collective-permute-done | bytes 589856 | tf_op jit(solution)/shard_map/ppermute | solution.py:1554
  310.2 31.1 %stage_backward.3 = (bf16[256,1152]{1,0:T(8,128)(2,1)}, f32[3,1152]{1,0:T(4,128)}, f32[3,1152]{1,0:T(4,128)}, bf16[256,1152]{1,0:T(8,128)(2,1)}, bf16[256,1152]{...) custom-call(s32[2]{0:T(128)} %pad_add_fusion.flags.flags_ref, ...), custom_call_target="tpu_custom_call" | custom-call | flops 16911433728 | bytes 31850496 | tf_op jit(solution)/shard_map/stage_backward/pallas_call | solution.py:1346
  345.4 4.5 collect.1
  351.1 19.1 %products.1 = (bf16[1152,2304]{1,0:T(8,128)(2,1)}, bf16[1152,2304]{1,0:T(8,128)(2,1)}, bf16[1152,2304]{1,0:T(8,128)(2,1)}) custom-call(s32[2]{0:T(128)} %pad_add_fusion.flags.flags_ref, bf16[256,1152]{1,0:T(8,128)(2,1)} %get-tuple-element.98.dn_own.refs_2_, bf16[256,1152]{1,0:T(8,128)(2,1)} %copy-done.28, bf16[256,1152]{1,0:T(8,128)(2,1)} %get-tuple-element.99.up_own, ...), custom_call_target="tpu_custom_call" | custom-call | flops 8153726976 | bytes 26542080 | tf_op jit(solution)/shard_map/products/pallas_call | solution.py:1407
  370.2 199.3 %sum_gradients.1 = (f32[2,144,2304]{2,1,0:T(8,128)}, bf16[144,2304]{1,0:T(8,128)(2,1)}, bf16[4,144,2304]{2,1,0:T(8,128)(2,1)}, f32[144,3456]{1,0:T(8,128)}, f32[...) custom-call(bf16[1152,2304]{1,0:T(8,128)(2,1)} %get-tuple-element.10, ...), custom_call_target="tpu_custom_call" | custom-call | bytes 400000000 | tf_op jit(solution)/shard_map/sum_gradients/pallas_call | solution.py:940
  572.5 1.2 slice.93
  573.6 1.2 slice.94
  576.9 1.7 fusion.11
  578.7 1.7 multiply_add_fusion.5
  580.4 2.7 fusion.12
  583.1 1.3 multiply_add_fusion.3
  584.6 1.2 copy-done.10
  586.2 1.5 copy-done.1
  588.6 2.6 fusion.13
  591.2 1.9 multiply_add_fusion
  595.8 2.2 fusion.14
  598.0 2.0 multiply_add_fusion.2
  600.0 12.9 %down_update.1 = (f32[2,144,4608]{2,1,0:T(8,128)}, f32[2,144,4608]{2,1,0:T(8,128)}, f32[2,144,4608]{2,1,0:T(8,128)}, bf16[2,144,4608]{2,1,0:T(8,128)(2,1)}) custom-call(f32[1]{0:T(128)} %bitcast.31.factor, f32[2,144,4608]{2,1,0:T(8,128)} %bitcast.97, f32[2,144,4608]{2,1,0:T(8,128)} %bitcast.103, f32[2,144,4608]{2,1,0:T(8,128)} %bitcast.104, ...), custom_call_target="tpu_custom_call" | custom-call | flops 13271040 | bytes 37158912 | tf_op jit(solution)/shard_map/down_update/pallas_call | solution.py:1514
  612.9 5.8 stem_update.1
  (158 shorter events, 32.6 us)
Async XLA Ops:
  8.3 183.9 %copy-start.21 = (f32[40352]{0:T(1024)S(1)}, f32[40352]{0:T(1024)}, u32[]{:S(2)}) copy-start(f32[40352]{0:T(1024)} %param.45) | copy-start | bytes 484228
  8.3 185.3 %copy-start.29 = (s32[2]{0:T(128)S(1)}, s32[2]{0:T(128)}, u32[]{:S(2)}) copy-start(s32[2]{0:T(128)} %param.26) | copy-start | bytes 28
  8.3 186.7 %copy-start.23 = (f32[2,32,32,4]{2,3,1,0:T(4,128)S(1)}, f32[2,32,32,4]{2,3,1,0:T(4,128)}, u32[]{:S(2)}) copy-start(f32[2,32,32,4]{2,3,1,0:T(4,128)} %param.24) | copy-start | bytes 98308
  8.3 186.7 %copy-start.24 = (f32[2,32,32,4]{2,3,1,0:T(4,128)S(1)}, f32[2,32,32,4]{2,3,1,0:T(4,128)}, u32[]{:S(2)}) copy-start(f32[2,32,32,4]{2,3,1,0:T(4,128)} %param.25) | copy-start | bytes 98308
  191.2 5.0 copy-start.22
  196.2 25.1 %copy-start.18 = (bf16[48,8,144]{2,0,1:T(8,128)(2,1)}, bf16[48,8,144]{2,0,1:T(8,128)(2,1)S(1)}, u32[]{:S(2)}) copy-start(bf16[48,8,144]{2,0,1:T(8,128)(2,1)S(1)} %slice_bitcast_fusion) | copy-start | bytes 331780
  200.4 20.3 %copy-start.30 = (s32[2]{0:T(128)S(1)}, s32[2]{0:T(128)}, u32[]{:S(2)}) copy-start(s32[2]{0:T(128)} %param.29) | copy-start | bytes 28
  219.1 15.9 %collective-permute-start = (bf16[256,1152]{1,0:T(8,128)(2,1)}, bf16[256,1152]{1,0:T(8,128)(2,1)S(1)}, u32[]{:S(2)}, u32[]{:S(2)}) collective-permute-start(bf16[256,1152]{1,0:T(8,128)(2,1)} %stage_forward.2), channel_id=1, source_target_pairs={{0,2},{1,3},{2,0},{3,1},{4,6},{5,7},{6,4},{7,5},{8,10},{9,11},{10,... | collective-permute-start | bytes 1769480 | tf_op jit(solution)/shard_map/ppermute | solution.py:1554
  221.6 13.4 %copy-start.7 = (f32[256,1152]{1,0:T(8,128)S(1)}, f32[256,1152]{1,0:T(8,128)}, u32[]{:S(2)}) copy-start(f32[256,1152]{1,0:T(8,128)} %fusion.x_ref) | copy-start | bytes 3538948
  262.7 33.4 %copy-start.27 = (bf16[256,1152]{1,0:T(8,128)(2,1)S(1)}, bf16[256,1152]{1,0:T(8,128)(2,1)}, u32[]{:S(2)}) copy-start(bf16[256,1152]{1,0:T(8,128)(2,1)} %get-tuple-element.100.xa_own) | copy-start | bytes 1769476
  262.7 46.4 %copy-start.8 = (f32[256,1152]{1,0:T(8,128)S(1)}, f32[256,1152]{1,0:T(8,128)}, u32[]{:S(2)}) copy-start(f32[256,1152]{1,0:T(8,128)} %subtract_multiply_fusion.d_ref) | copy-start | bytes 3538948
  294.0 15.1 %collective-permute-start.1 = (bf16[256,1152]{1,0:T(8,128)(2,1)}, bf16[256,1152]{1,0:T(8,128)(2,1)S(1)}, u32[]{:S(2)}, u32[]{:S(2)}) collective-permute-start(bf16[256,1152]{1,0:T(8,128)(2,1)} %get-tuple-element.97), channel_id=1, source_target_pairs={{0,2},{1,3},{2,0},{3,1},{4,6},{5,7},{6,4},{7,5},{8,10},{9,11},{10,... | collective-permute-start | bytes 1769480 | tf_op jit(solution)/shard_map/ppermute | solution.py:1554
  295.6 54.4 %collective-permute-start.6 = (bf16[256,2304]{1,0:T(8,128)(2,1)}, bf16[256,2304]{1,0:T(8,128)(2,1)}, u32[]{:S(2)}, u32[]{:S(2)}) collective-permute-start(bf16[256,2304]{1,0:T(8,128)(2,1)} %get-tuple-element.104), channel_id=1, source_target_pairs={{0,1},{1,0},{2,3},{3,2},{4,5},{5,4},{6,7},{7,6},{8,9},{9,8},{10,11... | collective-permute-start | bytes 3538952 | tf_op jit(solution)/shard_map/ppermute | solution.py:1554
  295.6 46.3 %collective-permute-start.3 = (bf16[256,1152]{1,0:T(8,128)(2,1)}, bf16[256,1152]{1,0:T(8,128)(2,1)}, u32[]{:S(2)}, u32[]{:S(2)}) collective-permute-start(bf16[256,1152]{1,0:T(8,128)(2,1)} %get-tuple-element.99.up_own), channel_id=1, source_target_pairs={{0,1},{1,0},{2,3},{3,2},{4,5},{5,4},{6,7},{7,6},{8,9},{9,8},{10,11... | collective-permute-start | bytes 1769480 | tf_op jit(solution)/shard_map/ppermute | solution.py:1554
  296.1 45.9 %collective-permute-start.4 = (bf16[256,1152]{1,0:T(8,128)(2,1)S(1)}, bf16[256,1152]{1,0:T(8,128)(2,1)}, u32[]{:S(2)}, u32[]{:S(2)}) collective-permute-start(bf16[256,1152]{1,0:T(8,128)(2,1)S(1)} %copy-done.27), channel_id=1, source_target_pairs={{0,1},{1,0},{2,3},{3,2},{4,5},{5,4},{6,7},{7,6},{8,9},{9,8},{10,11... | collective-permute-start | bytes 1769480 | tf_op jit(solution)/shard_map/ppermute | solution.py:1554
  341.3 8.6 %collective-permute-start.7 = (bf16[256,2304]{1,0:T(8,128)(2,1)}, bf16[256,2304]{1,0:T(8,128)(2,1)S(1)}, u32[]{:S(2)}, u32[]{:S(2)}) collective-permute-start(bf16[256,2304]{1,0:T(8,128)(2,1)} %get-tuple-element.106.refs_5_), channel_id=1, source_target_pairs={{0,1},{1,0},{2,3},{3,2},{4,5},{5,4},{6,7},{7,6},{8,9},{9,8},{10,11... | collective-permute-start | bytes 3538952 | tf_op jit(solution)/shard_map/ppermute | solution.py:1554
  341.4 8.6 %collective-permute-start.8 = (bf16[256,2304]{1,0:T(8,128)(2,1)}, bf16[256,2304]{1,0:T(8,128)(2,1)}, u32[]{:S(2)}, u32[]{:S(2)}) collective-permute-start(bf16[256,2304]{1,0:T(8,128)(2,1)} %get-tuple-element.108), channel_id=1, source_target_pairs={{0,1},{1,0},{2,3},{3,2},{4,5},{5,4},{6,7},{7,6},{8,9},{9,8},{10,11... | collective-permute-start | bytes 3538952 | tf_op jit(solution)/shard_map/ppermute | solution.py:1554
  341.9 8.0 %collective-permute-start.5 = (bf16[256,1152]{1,0:T(8,128)(2,1)}, bf16[256,1152]{1,0:T(8,128)(2,1)}, u32[]{:S(2)}, u32[]{:S(2)}) collective-permute-start(bf16[256,1152]{1,0:T(8,128)(2,1)} %get-tuple-element.102), channel_id=1, source_target_pairs={{0,1},{1,0},{2,3},{3,2},{4,5},{5,4},{6,7},{7,6},{8,9},{9,8},{10,11... | collective-permute-start | bytes 1769480 | tf_op jit(solution)/shard_map/ppermute | solution.py:1554
  342.0 7.9 %collective-permute-start.2 = (bf16[256,1152]{1,0:T(8,128)(2,1)}, bf16[256,1152]{1,0:T(8,128)(2,1)S(1)}, u32[]{:S(2)}, u32[]{:S(2)}) collective-permute-start(bf16[256,1152]{1,0:T(8,128)(2,1)} %get-tuple-element.98.dn_own.refs_2_), channel_id=1, source_target_pairs={{0,1},{1,0},{2,3},{3,2},{4,5},{5,4},{6,7},{7,6},{8,9},{9,8},{10,11... | collective-permute-start | bytes 1769480 | tf_op jit(solution)/shard_map/ppermute | solution.py:1554
  370.2 210.1 %copy-start.15 = (f32[144,2336]{1,0:T(8,128)S(1)}, f32[144,2336]{1,0:T(8,128)}, u32[]{:S(2)}) copy-start(f32[144,2336]{1,0:T(8,128)} %param.43) | copy-start | bytes 4036612
  569.5 10.8 %copy-start.5 = (f32[144,2336]{1,0:T(8,128)S(1)}, f32[144,2336]{1,0:T(8,128)}, u32[]{:S(2)}) copy-start(f32[144,2336]{1,0:T(8,128)} %tail_hbm.1) | copy-start | bytes 4036612
  576.3 4.0 copy-start.17
  578.7 4.4 copy-start.20
  580.3 2.8 copy-start.16
  583.1 2.8 copy-start.10
  583.1 2.9 copy-start.19
  586.0 2.5 copy-start.9
  588.5 2.6 copy-start.11
  591.2 2.7 copy-start.2
  591.2 3.0 copy-start.3
  591.2 4.1 copy-start.12
  591.2 4.7 copy-start.14
  (9 other events, 14.2 us)
